TPU v7x, 32 devices: a whole 2x2x4 slice. The times are simulated.
32 devices in a mesh: row: 8 (over z, y), col: 4 (over x, core).
Axes of the slice: x: 2, y: 2, z: 4, core: 2. Of those that a mesh axis runs over, the one named last changes fastest.
Arguments:
- blocks: bfloat16 [512, 3, 128, 128], P(('row', 'col')), may hold values from -0.3984375 to 0.3984375
- rows: int32 [512, 3], P(('row', 'col')), may hold values from 0 to 63, as said below
- counts: int32 [512], P(('row', 'col')), may hold values from 1 to 3
- sketch: bfloat16 [65536, 128], P(('row', 'col')), may hold values from -6 to 6
- weights: float32 [8192], replicated, may hold values from 0.35 to 2.8
Outputs:
- basis_out: float32 [8192, 128], P(('row', 'col'))
- right_factors: bfloat16 [65536, 128], P(('row', 'col'))
Inputs may be any that keep to these rules, and one draw needn't show every extreme that they name: `rows`: the 3 entries of each document block are distinct feature blocks.
All inputs are finite; a program needn't handle non-finite values.
Results may differ from a plain program's by a relative error of at most 0.0049.
Values may be sent and summed in bfloat16 or wider, within the bound.
No kernel may reach another device: no remote copies, remote signals or barrier semaphores. Data moves between devices by JAX's collectives and lax.ppermute only.
A program may use at most 64 MiB of HBM per device.

v0:
```python
import jax
import jax.numpy as jnp
from jax import lax
from jax.sharding import PartitionSpec as P

HIGHEST = lax.Precision.HIGHEST


def body(blocks, rows, counts, sketch, weights):
    doc_blocks = blocks.shape[0]
    slot_count = blocks.shape[1]
    block_width = blocks.shape[2]
    columns = sketch.shape[1]
    features = weights.shape[0]
    feature_blocks = features // block_width
    in_use = lax.broadcasted_iota(jnp.int32, (doc_blocks, slot_count), 1) < counts[:, None]
    segment_ids = jnp.where(in_use, rows, feature_blocks).reshape(-1)
    row_count = lax.axis_size("row")
    col_count = lax.axis_size("col")
    flat_rows = features // (row_count * col_count)
    band_rows = features // row_count
    band_weights = lax.dynamic_slice_in_dim(weights, lax.axis_index("row") * band_rows, band_rows)[
        :, None
    ]
    width_now = sketch.shape[1]
    tiles_docs = sketch.reshape(doc_blocks, block_width, width_now)
    terms = jnp.einsum("dsfk,dkl->dsfl", blocks, tiles_docs, preferred_element_type=jnp.float32)
    terms = terms.reshape(doc_blocks * slot_count, block_width, width_now)
    summed = jax.ops.segment_sum(terms, segment_ids, num_segments=feature_blocks + 1)
    local_terms = summed[:feature_blocks].reshape(features, sketch.shape[1])
    row_partial = lax.psum_scatter(local_terms, "row", scatter_dimension=0, tiled=True)
    band_summed = lax.psum(row_partial, "col") * band_weights
    chol_factor = jnp.linalg.cholesky(
        lax.psum(jnp.dot(band_summed.T, band_summed, precision=HIGHEST), "row") / features
    )
    inverse = jax.scipy.linalg.solve_triangular(
        chol_factor, jnp.eye(columns, dtype=jnp.float32), lower=True
    )
    current = jnp.dot(band_summed, inverse.T, precision=HIGHEST)
    weighted = (current * band_weights).astype(jnp.bfloat16)
    gathered = lax.all_gather(weighted, "row", axis=0, tiled=True)
    width_now = gathered.shape[1]
    picked = gathered.reshape(feature_blocks, block_width, width_now)[rows]
    picked = jnp.where(in_use[:, :, None, None], picked, jnp.zeros((), gathered.dtype))
    product = jnp.einsum("dsfl,dsfk->dkl", picked, blocks, preferred_element_type=jnp.float32)
    factors = product.reshape(doc_blocks * block_width, width_now).astype(jnp.bfloat16)
    basis_out = lax.dynamic_slice_in_dim(current, lax.axis_index("col") * flat_rows, flat_rows)
    return (basis_out, factors)


def solution(mesh):
    placed = (
        P(("row", "col"), None, None, None),
        P(("row", "col"), None),
        P(("row", "col")),
        P(("row", "col"), None),
        P(),
    )
    return jax.shard_map(
        body,
        mesh=mesh,
        in_specs=placed,
        out_specs=(P(("row", "col"), None), P(("row", "col"), None)),
        check_vma=False,
    )
```

profile of v0, /device:TPU:0, one launch (start us, length us, event | category | flops | bytes accessed | tf_op | source)
XLA Modules:
  0.0 314.4 jit_solution(17388687398177355012)
XLA Ops:
  7.2 0.8 compare_select_fusion
  8.2 0.4 copy-done
  8.6 3.3 %fusion.21 = f32[16,3,128,128]{3,2,1,0:T(8,128)} fusion(bf16[16,3,128,128]{3,2,1,0:T(8,128)(2,1)S(1)} %copy-done, bf16[16,128,128,1]{2,1,3,0:T(8,128)(2,1)} %bitcast.34), kind=kOutput, calls=%fused_computation.32 | convolution fusion | flops 201326592 | bytes 5242880 | tf_op jit(solution)/shard_map/dsfk,dkl->dsfl/dot_general | solution.py:27
  11.9 2.5 broadcast_in_dim.27
  14.4 10.2 %scatter_fusion = f32[65,128,128]{2,1,0:T(8,128)} fusion(f32[65,128,128]{2,1,0:T(8,128)} %broadcast_in_dim.27, s32[48]{0:T(128)S(1)} %reshape.61, f32[48,128,128]{2,1,0:T(8,128)} %bitcast.31), kind=kCustom, calls=%fused_computation.1 | custom fusion | flops 786432 | bytes 9437376 | tf_op jit(solution)/shard_map/scatter-add | solution.py:29
  24.5 4.7 %slice.18 = f32[64,128,128]{2,1,0:T(8,128)} slice(f32[65,128,128]{2,1,0:T(8,128)} %scatter_fusion), slice={[0:64], [0:128], [0:128]} | slice | bytes 8388608 | tf_op jit(solution)/shard_map/slice | solution.py:30
  29.2 90.7 %reduce-scatter.2.cloned.1.call-done = f32[1024,128]{1,0:T(8,128)} async-done(((f32[8192,128]{1,0:T(8,128)}), f32[1024,128]{1,0:T(8,128)}) %reduce-scatter.2.cloned.1.call-update) | async-done | bytes 524304 | tf_op jit(solution)/shard_map/reduce_scatter | solution.py:31
  120.0 0.7 dynamic_slice.6
  120.7 34.6 %all-reduce.3.cloned.1.call-done = f32[1024,128]{1,0:T(8,128)} async-done(((f32[1024,128]{1,0:T(8,128)}), f32[1024,128]{1,0:T(8,128)}) %all-reduce.3.cloned.1.call-update) | async-done | bytes 524304 | tf_op jit(solution)/shard_map/psum | solution.py:32
  155.4 3.2 %fusion.12 = f32[128,128]{0,1:T(8,128)} fusion(f32[1024,128]{1,0:T(8,128)} %all-reduce.3.cloned.1.call-done, f32[1024]{0:T(1024)S(1)} %dynamic_slice.6), kind=kOutput, calls=%fused_computation.11 | convolution fusion | flops 201457664 | bytes 593920 | tf_op jit(solution)/shard_map/dot_general | solution.py:34
  158.6 69.6 %all-reduce.5.cloned.1.call-done = f32[128,128]{0,1:T(8,128)} async-done(((f32[128,128]{0,1:T(8,128)}), f32[128,128]{0,1:T(8,128)}) %all-reduce.5.cloned.1.call-update) | async-done | bytes 65552 | tf_op jit(solution)/shard_map/psum | solution.py:34
  228.2 0.8 broadcast_multiply_fusion
  229.1 0.9 fusion.19
  230.0 11.7 %cholesky.17 = f32[128,128]{1,0:T(8,128)S(1)} custom-call(f32[128,128]{1,0:T(8,128)S(1)} %fusion.19), custom_call_target="Cholesky" | custom-call | tf_op jit(solution)/shard_map/jit(cholesky)/cholesky | solution.py:33
  241.8 0.6 compare_reduce_fusion
  242.4 0.7 fusion.16
  243.1 9.8 %custom-call.7 = f32[1,128,128]{1,2,0:T(8,128)S(1)} custom-call(f32[1,128,128]{2,1,0:T(8,128)S(1)} %fusion.16), custom_call_target="InvertDiagBlocksLowerTriangular" | custom-call | tf_op jit(solution)/shard_map/jit(_solve_triangular)/triangular_solve | solution.py:36
  252.9 0.2 fusion.17
  253.1 1.3 multiply_convert_fusion
  254.7 0.1 copy.16
  254.8 0.7 constant_dynamic-slice_fusion
  255.5 48.4 %all-gather.2.cloned.1.call-done = bf16[8192,128]{1,0:T(8,128)(2,1)} async-done(((bf16[1024,128]{1,0:T(8,128)(2,1)}), bf16[8192,128]{1,0:T(8,128)(2,1)}) %all-gather.2.cloned.1.call-update) | async-done | bytes 2097168 | tf_op jit(solution)/shard_map/all_gather | solution.py:41
  303.9 2.4 gather_fusion
  306.3 1.5 fusion.6
  (21 shorter events, 0.7 us)
Async XLA Ops:
  7.2 1.4 copy-start
  7.2 112.8 %reduce-scatter.2.cloned.1.call-start = ((), (), s32[]{:S(2)}) async-start(), calls=%async_computation.1 | async-start | bytes 4718592 | tf_op jit(solution)/shard_map/reduce_scatter | solution.py:31
  29.2 126.2 %all-reduce.3.cloned.1.call-start = ((), (), s32[]{:S(2)}) async-start(), calls=%async_computation.2 | async-start | bytes 1048576 | tf_op jit(solution)/shard_map/psum | solution.py:32
  120.0 108.2 %all-reduce.5.cloned.1.call-start = ((), (), s32[]{:S(2)}) async-start(), calls=%async_computation.3 | async-start | bytes 131072 | tf_op jit(solution)/shard_map/psum | solution.py:34
  120.0 134.6 %copy-start.2 = (s32[16]{0:T(128)S(1)}, s32[16]{0:T(128)}, u32[]{:S(2)}) copy-start(s32[16]{0:T(128)} %param.7) | copy-start | bytes 196
  155.4 97.8 %copy-start.1 = (f32[1024,128]{1,0:T(8,128)S(1)}, f32[1024,128]{1,0:T(8,128)}, u32[]{:S(2)}) copy-start(f32[1024,128]{1,0:T(8,128)} %all-reduce.3.cloned.1.call-done) | copy-start | bytes 1572868
  158.6 145.3 %all-gather.2.cloned.1.call-start = ((), (), s32[]{:S(2)}) async-start(), calls=%async_computation.4 | async-start | bytes 2359296 | tf_op jit(solution)/shard_map/all_gather | solution.py:41
Sparse Core Ops, SparseCore 0:
  29.3 90.5 reduce-scatter.1
  122.4 32.8 all-reduce.2
  159.7 68.4 all-reduce.4
  254.6 49.2 all-gather.1
where the time goes:
time: 315 us; the launch traced here: 314 us
  waiting for transfers between devices  243 us (77%)
  other arithmetic  35.5 us (11%)
  between operations  13.9 us (4%)
  local copies, waits for them, and re-layouts  11.9 us (4%)
  matrix products  9.56 us (3%)
    reduce_scatter x1, waiting for transfers between devices, body(): lax.psum_scatter(local_terms, 'row', scatter_dimension=0, tiled=True)  90.7 us
    psum x1, waiting for transfers between devices, body(): lax.psum(jnp.dot(band_summed.T, band_summed, precision=HIGHEST), 'row')  69.6 us
    all_gather x1, waiting for transfers between devices, body(): gathered = lax.all_gather(weighted, 'row', axis=0, tiled=True)  48.4 us
    psum x1, waiting for transfers between devices, body(): band_summed = lax.psum(row_partial, 'col') * band_weights  34.6 us
    another operation x3, other arithmetic, body(): jnp.linalg.cholesky(lax.psum(jnp.dot(band_summed.T, band_summed, precisio...  12.4 us
    another operation x2, other arithmetic, body(): jax.scipy.linalg.solve_triangular(chol_factor, jnp.eye(columns, dtype=jnp...  10.5 us
    scatter-add x1, other arithmetic, body(): jax.ops.segment_sum(terms, segment_ids, num_segments=feature_blocks + 1)  10.2 us
  transfers between devices with their start and end apart: 4, of which 4 were waited for; matrix products, arithmetic and copies ran while one was open for 1% of the time, Pallas kernels for 0%

commit v1 on v0

v1 whole, which is shorter than its diff:
```python
import functools

import jax
import jax.numpy as jnp
from jax import lax
from jax.experimental import pallas as pl
from jax.experimental.pallas import tpu as pltpu
from jax.sharding import PartitionSpec as P

F32 = jnp.float32
BF16 = jnp.bfloat16
HIGHEST = lax.Precision.HIGHEST
AXES = ("row", "col")
VMEM_BYTES = 48 * 1024 * 1024


def whole():
    return pl.BlockSpec(memory_space=pltpu.VMEM)


def scalars():
    return pl.BlockSpec(memory_space=pltpu.SMEM)


class Plan:
    def __init__(self, rows, cols, features, block):
        self.count = rows * cols
        self.cols = cols
        self.plane_bits = cols.bit_length() - 1
        self.plane = cols
        self.rest = self.count // 2 // cols
        assert self.plane * self.rest * 2 == self.count and self.count & (self.count - 1) == 0
        self.flat = features // self.count
        self.piece = min(self.flat, block)
        self.pieces = block // self.piece
        self.per_slice = self.flat // self.piece

    def me(self):
        return lax.axis_index("row") * self.cols + lax.axis_index("col")

    def start(self, me, feature_block, piece):
        unit = feature_block * self.pieces + piece
        owner = unit // self.per_slice if self.per_slice > 1 else unit
        inside = unit - owner * self.per_slice
        apart = owner ^ me
        core = apart & 1
        plane = (apart >> 1) & (self.plane - 1)
        rest = apart >> (1 + self.plane_bits)
        at = (core * self.plane + plane) * self.rest + rest
        return pl.multiple_of(at * self.flat + inside * self.piece, self.piece)

    def swap(self, value, mask):
        return lax.ppermute(value, AXES, [(d, d ^ mask) for d in range(self.count)])


def sum_kernel(plan, rows_ref, counts_ref, blocks_ref, sketch_ref, keep_ref, send_ref, total_ref):
    me = plan.me()
    documents, slots, block, _ = blocks_ref.shape
    half = keep_ref.shape[0]
    total_ref[...] = jnp.zeros_like(total_ref)
    for d in range(documents):
        docs = sketch_ref[d * block : (d + 1) * block, :]
        for s in range(slots):
            def add(d=d, s=s, docs=docs):
                term = jnp.dot(blocks_ref[d, s], docs, preferred_element_type=F32)
                for p in range(plan.pieces):
                    at = pl.ds(plan.start(me, rows_ref[d, s], p), plan.piece)
                    total_ref[at, :] += term[p * plan.piece : (p + 1) * plan.piece]

            pl.when(s < counts_ref[d])(add)
    keep_ref[...] = total_ref[:half, :]
    send_ref[...] = total_ref[half:, :].astype(BF16)


def tiles_kernel(rows_ref, counts_ref, blocks_ref, weights_ref, out_ref):
    documents, slots, block, _ = blocks_ref.shape
    for d in range(documents):
        for s in range(slots):
            scale = weights_ref[pl.ds(rows_ref[d, s], 1), :]
            scale = jnp.where(s < counts_ref[d], scale, 0.0)
            tile = blocks_ref[d, s].T.astype(F32) * scale
            out_ref[d, :, s * block : (s + 1) * block] = tile.astype(BF16)


def split(value):
    high = value.astype(BF16)
    return high, (value - high.astype(F32)).astype(BF16)


def dot_t(a, b):
    return lax.dot_general(a, b, (((1,), (1,)), ((), ())), preferred_element_type=F32)


def dot_t3(a, b):
    a_high, a_low = split(a)
    b_high, b_low = split(b)
    return dot_t(a_high, b_high) + (dot_t(a_high, b_low) + dot_t(a_low, b_high))


def gram_kernel(own_ref, other_ref, gram_ref, *, features):
    total = jnp.zeros(gram_ref.shape, F32)
    for ref in (own_ref, other_ref):
        step = min(1024, ref.shape[0])
        for at in range(0, ref.shape[0], step):
            part = ref[at : at + step, :]
            total += lax.dot_general(part, part, (((0,), (0,)), ((), ())), preferred_element_type=F32)
    gram_ref[...] = total * (1.0 / features)


def last_kernel(plan, rows_ref, tiles_ref, own_ref, other_ref, mine_ref, inverse_ref, basis_ref, factors_ref, all_ref):
    me = plan.me()
    documents, block, _ = tiles_ref.shape
    half = own_ref.shape[0]
    slots = tiles_ref.shape[2] // block
    inverse = inverse_ref[...]
    basis_ref[...] = dot_t3(mine_ref[...], inverse)
    all_ref[:half, :] = own_ref[...]
    all_ref[half:, :] = other_ref[...]
    for d in range(documents):
        picked = []
        for s in range(slots):
            for p in range(plan.pieces):
                at = pl.ds(plan.start(me, rows_ref[d, s], p), plan.piece)
                picked.append(all_ref[at, :])
        product = jnp.dot(tiles_ref[d], jnp.concatenate(picked, axis=0), preferred_element_type=F32)
        factors_ref[d * block : (d + 1) * block, :] = dot_t3(product, inverse).astype(BF16)


def body(plan, blocks, rows, counts, sketch, weights):
    documents, slots, block, _ = blocks.shape
    columns = sketch.shape[1]
    features = weights.shape[0]
    half = features // 2
    flat, plane, rest = plan.flat, plan.plane, plan.rest
    params = pltpu.CompilerParams(vmem_limit_bytes=VMEM_BYTES)
    shape = jax.ShapeDtypeStruct

    keep, send = pl.pallas_call(
        functools.partial(sum_kernel, plan),
        out_shape=(shape((half, columns), F32), shape((half, columns), BF16)),
        in_specs=[scalars(), scalars(), whole(), whole()],
        out_specs=(whole(), whole()),
        scratch_shapes=[pltpu.VMEM((features, columns), F32)],
        compiler_params=params,
        name="local_sum",
    )(rows, counts, blocks, sketch)

    got = plan.swap(send, 1)
    keep = keep.reshape(plane, rest * flat, columns)
    got = got.reshape(plane, rest * flat, columns)
    sent = [plan.swap((keep[p] + got[p].astype(F32)).astype(BF16), p << 1) for p in range(1, plane)]
    held = keep[0] + got[0].astype(F32)
    for part in sent:
        held = held + part.astype(F32)
    held = held.reshape(rest, flat, columns)
    step = 1 + plan.plane_bits
    sent = [plan.swap(held[q].astype(BF16), q << step) for q in range(1, rest)]
    mine = held[0]
    for part in sent:
        mine = mine + part.astype(F32)
    mine = mine * lax.dynamic_slice_in_dim(weights, plan.me() * flat, flat)[:, None]

    tiles = pl.pallas_call(
        tiles_kernel,
        out_shape=shape((documents, block, slots * block), BF16),
        in_specs=[scalars(), scalars(), whole(), whole()],
        out_specs=whole(),
        compiler_params=params,
        name="tiles",
    )(rows, counts, blocks, weights.reshape(features // block, block))

    rounded = mine.astype(BF16)
    near = jnp.concatenate([rounded] + [plan.swap(rounded, q << step) for q in range(1, rest)], axis=0)
    own = jnp.concatenate([near] + [plan.swap(near, p << 1) for p in range(1, plane)], axis=0)
    other = plan.swap(own, 1)

    gram = pl.pallas_call(
        functools.partial(gram_kernel, features=features),
        out_shape=shape((columns, columns), F32),
        in_specs=[whole(), whole()],
        out_specs=whole(),
        compiler_params=params,
        name="gram",
    )(own, other)
    factor = jnp.linalg.cholesky(gram, symmetrize_input=False)
    inverse = jax.scipy.linalg.solve_triangular(factor, jnp.eye(columns, dtype=F32), lower=True)
    return pl.pallas_call(
        functools.partial(last_kernel, plan),
        out_shape=(shape((flat, columns), F32), shape((documents * block, columns), BF16)),
        in_specs=[scalars()] + [whole()] * 5,
        out_specs=(whole(), whole()),
        scratch_shapes=[pltpu.VMEM((features, columns), BF16)],
        compiler_params=params,
        name="factors",
    )(rows, tiles, own, other, mine, inverse)


def solution(mesh):
    placed = (
        P(AXES, None, None, None),
        P(AXES, None),
        P(AXES),
        P(AXES, None),
        P(),
    )

    def run(blocks, rows, counts, sketch, weights):
        plan = Plan(mesh.shape["row"], mesh.shape["col"], weights.shape[0], blocks.shape[2])
        return jax.shard_map(
            functools.partial(body, plan),
            mesh=mesh,
            in_specs=placed,
            out_specs=(P(AXES, None), P(AXES, None)),
            check_vma=False,
        )(blocks, rows, counts, sketch, weights)

    return run
```

time: 315 us -> 95.3 us (0.30)
  waiting for transfers between devices: 243 us -> 33.9 us
  starting transfers between devices: 0.16 us -> 16.9 us
  between operations: 13.9 us -> 0.83 us
  other arithmetic: 35.5 us -> 23.3 us
  Pallas kernels: 0 us -> 12 us
  matrix products: 9.56 us -> 0.25 us
  local copies, waits for them, and re-layouts: 11.9 us -> 7.53 us
    psum x2 -> x0, waiting for transfers between devices: 104 us -> none  [the longest x1 69.6 us: body(): lax.psum(jnp.dot(band_summed.T, band_summed, precision=HIGHEST), 'row')]
    reduce_scatter x1 -> x0, waiting for transfers between devices: 90.7 us -> none  [body(): lax.psum_scatter(local_terms, 'row', scatter_dimension=0, tiled=True)]
    all_gather x1 -> x0, waiting for transfers between devices: 48.4 us -> none  [body(): gathered = lax.all_gather(weighted, 'row', axis=0, tiled=True)]
    ppermute x0 -> x14, waiting for transfers between devices: none -> 33.9 us  [swap(): return lax.ppermute(value, AXES, [(d, d ^ mask) for d in range(self.count)])]
    ppermute x0 -> x14, starting transfers between devices: none -> 16.9 us  [swap(): return lax.ppermute(value, AXES, [(d, d ^ mask) for d in range(self.count)])]
    pallas_call x0 -> x4, Pallas kernels: none -> 12 us  [the longest x1 6.23 us: body(): pl.pallas_call(functools.partial(sum_kernel, plan), out_shape=(shape((hal...]
    scatter-add x1 -> x0, other arithmetic: 10.2 us -> none  [body(): jax.ops.segment_sum(terms, segment_ids, num_segments=feature_blocks + 1)]
    dot_general x4 -> x0, matrix products: 9.31 us -> none  [the longest x1 3.28 us: body(): jnp.einsum('dsfk,dkl->dsfl', blocks, tiles_docs, preferred_element_type=j...]
  transfers between devices with their start and end apart: 4 -> 14, of which waited for: 4 -> 11; matrix products, arithmetic and copies ran while one was open for 1% -> 0% of each run, Pallas kernels for 0% -> 1%
where the time goes in v1:
time: 95.3 us; the launch traced here: 94.7 us
  waiting for transfers between devices  33.9 us (36%)
  other arithmetic  23.3 us (24%)
  starting transfers between devices  16.9 us (18%)
  Pallas kernels  12 us (13%)
  local copies, waits for them, and re-layouts  7.53 us (8%)
    ppermute x14, waiting for transfers between devices, swap(): return lax.ppermute(value, AXES, [(d, d ^ mask) for d in range(self.count)])  33.9 us
    ppermute x14, starting transfers between devices, swap(): return lax.ppermute(value, AXES, [(d, d ^ mask) for d in range(self.count)])  16.9 us
    another operation x3, other arithmetic, body(): factor = jnp.linalg.cholesky(gram, symmetrize_input=False)  12.4 us
    another operation x2, other arithmetic, body(): jax.scipy.linalg.solve_triangular(factor, jnp.eye(columns, dtype=F32), lo...  10.5 us
    unnamed x26, local copies, waits for them, and re-layouts  7.4 us
    pallas_call x1, Pallas kernels, body(): pl.pallas_call(functools.partial(sum_kernel, plan), out_shape=(shape((hal...  6.23 us
    pallas_call x1, Pallas kernels, body(): pl.pallas_call(functools.partial(last_kernel, plan), out_shape=(shape((fl...  3.91 us
  transfers between devices with their start and end apart: 14, of which 11 were waited for; matrix products, arithmetic and copies ran while one was open for 0% of the time, Pallas kernels for 1%

profile of v1, /device:TPU:0, one launch (start us, length us, event | category | flops | bytes accessed | tf_op | source)
XLA Modules:
  0.0 94.7 jit_solution(10357221744362405501)
XLA Ops:
  1.4 1.4 %copy-done = bf16[16,3,128,128]{3,2,1,0:T(8,128)(2,1)S(1)} copy-done((bf16[16,3,128,128]{3,2,1,0:T(8,128)(2,1)S(1)}, bf16[16,3,128,128]{3,2,1,0:T(8,128)(2,1)}, u32[]{:S(2)}) %copy-start) | copy-done | bytes 1572888
  4.5 6.2 %local_sum.1 = (f32[4096,128]{1,0:T(8,128)S(1)}, bf16[4096,128]{1,0:T(8,128)(2,1)S(1)}) custom-call(s32[16,3]{1,0:T(8,128)S(1)} %copy.9.rows_ref, s32[16]{0:T(128)S(1)} %copy-done.8, bf16[16,3,128,128]{3,2,1,0:T(8,128)(2,1)S(1)} %copy-done, bf16[2048,128]{1,0:T(8,128)(2,1)S(1)} %copy-done.6), custom_call_target="tpu_custom_call" | custom-call | tf_op jit(solution)/shard_map/local_sum/pallas_call | solution.py:138
  10.8 2.6 %collective-permute-done = bf16[4096,128]{1,0:T(8,128)(2,1)S(1)} collective-permute-done((bf16[4096,128]{1,0:T(8,128)(2,1)S(1)}, bf16[4096,128]{1,0:T(8,128)(2,1)S(1)}, u32[]{:S(2)}, u32[]{:S(2)}) %collective-permute-start) | collective-permute-done | bytes 1048608 | tf_op jit(solution)/shard_map/ppermute | solution.py:53
  13.6 2.4 %collective-permute-start.1 = (bf16[1024,128]{1,0:T(8,128)(2,1)S(1)}, bf16[1024,128]{1,0:T(8,128)(2,1)S(1)}, u32[]{:S(2)}, u32[]{:S(2)}) collective-permute-start(bf16[1024,128]{1,0:T(8,128)(2,1)S(1)} %get-tuple-element.11), channel_id=1, source_target_pairs={{0,2},{1,3},{2,0},{3,1},{4,6},{5,7},{6,4},{7,5},{8,10},{9,11},{10,... | collective-permute-start | bytes 786440 | tf_op jit(solution)/shard_map/ppermute | solution.py:53
  17.6 5.5 %collective-permute-done.1 = bf16[1024,128]{1,0:T(8,128)(2,1)S(1)} collective-permute-done((bf16[1024,128]{1,0:T(8,128)(2,1)S(1)}, bf16[1024,128]{1,0:T(8,128)(2,1)S(1)}, u32[]{:S(2)}, u32[]{:S(2)}) %collective-permute-start.1) | collective-permute-done | bytes 262176 | tf_op jit(solution)/shard_map/ppermute | solution.py:53
  23.2 6.6 %collective-permute-done.2 = bf16[1024,128]{1,0:T(8,128)(2,1)S(1)} collective-permute-done((bf16[1024,128]{1,0:T(8,128)(2,1)S(1)}, bf16[1024,128]{1,0:T(8,128)(2,1)S(1)}, u32[]{:S(2)}, u32[]{:S(2)}) %collective-permute-start.2) | collective-permute-done | bytes 262176 | tf_op jit(solution)/shard_map/ppermute | solution.py:53
  30.0 2.3 %collective-permute-start.4 = (bf16[256,128]{1,0:T(8,128)(2,1)S(1)}, bf16[256,128]{1,0:T(8,128)(2,1)S(1)}, u32[]{:S(2)}, u32[]{:S(2)}) collective-permute-start(bf16[256,128]{1,0:T(8,128)(2,1)S(1)} %get-tuple-element.14), channel_id=1, source_target_pairs={{0,8},{1,9},{2,10},{3,11},{4,12},{5,13},{6,14},{7,15},{8,0},{9,1},... | collective-permute-start | bytes 196616 | tf_op jit(solution)/shard_map/ppermute | solution.py:53
  32.3 1.6 %collective-permute-start.5 = (bf16[256,128]{1,0:T(8,128)(2,1)S(1)}, bf16[256,128]{1,0:T(8,128)(2,1)S(1)}, u32[]{:S(2)}, u32[]{:S(2)}) collective-permute-start(bf16[256,128]{1,0:T(8,128)(2,1)S(1)} %get-tuple-element.16), channel_id=1, source_target_pairs={{0,16},{1,17},{2,18},{3,19},{4,20},{5,21},{6,22},{7,23},{8,24},{9,... | collective-permute-start | bytes 196616 | tf_op jit(solution)/shard_map/ppermute | solution.py:53
  35.3 3.3 %collective-permute-done.5 = bf16[256,128]{1,0:T(8,128)(2,1)S(1)} collective-permute-done((bf16[256,128]{1,0:T(8,128)(2,1)S(1)}, bf16[256,128]{1,0:T(8,128)(2,1)S(1)}, u32[]{:S(2)}, u32[]{:S(2)}) %collective-permute-start.5) | collective-permute-done | bytes 65568 | tf_op jit(solution)/shard_map/ppermute | solution.py:53
  38.6 1.4 %collective-permute-done.6 = bf16[256,128]{1,0:T(8,128)(2,1)S(1)} collective-permute-done((bf16[256,128]{1,0:T(8,128)(2,1)S(1)}, bf16[256,128]{1,0:T(8,128)(2,1)S(1)}, u32[]{:S(2)}, u32[]{:S(2)}) %collective-permute-start.6) | collective-permute-done | bytes 65568 | tf_op jit(solution)/shard_map/ppermute | solution.py:53
  40.2 2.2 %collective-permute-start.8 = (bf16[256,128]{1,0:T(8,128)(2,1)S(1)}, bf16[256,128]{1,0:T(8,128)(2,1)S(1)}, u32[]{:S(2)}, u32[]{:S(2)}) collective-permute-start(bf16[256,128]{1,0:T(8,128)(2,1)S(1)} %get-tuple-element.7), channel_id=1, source_target_pairs={{0,16},{1,17},{2,18},{3,19},{4,20},{5,21},{6,22},{7,23},{8,24},{9,... | collective-permute-start | bytes 196616 | tf_op jit(solution)/shard_map/ppermute | solution.py:53
  42.4 2.1 %collective-permute-start.9 = (bf16[256,128]{1,0:T(8,128)(2,1)S(1)}, bf16[256,128]{1,0:T(8,128)(2,1)S(1)}, u32[]{:S(2)}, u32[]{:S(2)}) collective-permute-start(bf16[256,128]{1,0:T(8,128)(2,1)S(1)} %get-tuple-element.7), channel_id=1, source_target_pairs={{0,24},{1,25},{2,26},{3,27},{4,28},{5,29},{6,30},{7,31},{8,16},{9,... | collective-permute-start | bytes 196616 | tf_op jit(solution)/shard_map/ppermute | solution.py:53
  44.6 1.3 %collective-permute-done.8 = bf16[256,128]{1,0:T(8,128)(2,1)S(1)} collective-permute-done((bf16[256,128]{1,0:T(8,128)(2,1)S(1)}, bf16[256,128]{1,0:T(8,128)(2,1)S(1)}, u32[]{:S(2)}, u32[]{:S(2)}) %collective-permute-start.8) | collective-permute-done | bytes 65568 | tf_op jit(solution)/shard_map/ppermute | solution.py:53
  45.9 2.6 %collective-permute-done.9 = bf16[256,128]{1,0:T(8,128)(2,1)S(1)} collective-permute-done((bf16[256,128]{1,0:T(8,128)(2,1)S(1)}, bf16[256,128]{1,0:T(8,128)(2,1)S(1)}, u32[]{:S(2)}, u32[]{:S(2)}) %collective-permute-start.9) | collective-permute-done | bytes 65568 | tf_op jit(solution)/shard_map/ppermute | solution.py:53
  48.5 1.4 %collective-permute-start.10 = (bf16[1024,128]{1,0:T(8,128)(2,1)S(1)}, bf16[1024,128]{1,0:T(8,128)(2,1)S(1)}, u32[]{:S(2)}, u32[]{:S(2)}) collective-permute-start(bf16[1024,128]{1,0:T(8,128)(2,1)S(1)} %pad_maximum_fusion), channel_id=1, source_target_pairs={{0,2},{1,3},{2,0},{3,1},{4,6},{5,7},{6,4},{7,5},{8,10},{9,11},{10,... | collective-permute-start | bytes 786440 | tf_op jit(solution)/shard_map/ppermute | solution.py:53
  50.2 1.9 %collective-permute-start.12 = (bf16[1024,128]{1,0:T(8,128)(2,1)S(1)}, bf16[1024,128]{1,0:T(8,128)(2,1)S(1)}, u32[]{:S(2)}, u32[]{:S(2)}) collective-permute-start(bf16[1024,128]{1,0:T(8,128)(2,1)S(1)} %pad_maximum_fusion), channel_id=1, source_target_pairs={{0,6},{1,7},{2,4},{3,5},{4,2},{5,3},{6,0},{7,1},{8,14},{9,15},{10,... | collective-permute-start | bytes 786440 | tf_op jit(solution)/shard_map/ppermute | solution.py:53
  52.1 4.5 %collective-permute-done.10 = bf16[1024,128]{1,0:T(8,128)(2,1)S(1)} collective-permute-done((bf16[1024,128]{1,0:T(8,128)(2,1)S(1)}, bf16[1024,128]{1,0:T(8,128)(2,1)S(1)}, u32[]{:S(2)}, u32[]{:S(2)}) %collective-permute-start.10) | collective-permute-done | bytes 262176 | tf_op jit(solution)/shard_map/ppermute | solution.py:53
  56.6 4.1 %collective-permute-done.11 = bf16[1024,128]{1,0:T(8,128)(2,1)S(1)} collective-permute-done((bf16[1024,128]{1,0:T(8,128)(2,1)S(1)}, bf16[1024,128]{1,0:T(8,128)(2,1)S(1)}, u32[]{:S(2)}, u32[]{:S(2)}) %collective-permute-start.11) | collective-permute-done | bytes 262176 | tf_op jit(solution)/shard_map/ppermute | solution.py:53
  62.0 1.5 %collective-permute-done.13.other_ref = bf16[4096,128]{1,0:T(8,128)(2,1)S(1)} collective-permute-done((bf16[4096,128]{1,0:T(8,128)(2,1)S(1)}, bf16[4096,128]{1,0:T(8,128)(2,1)S(1)}, u32[]{:S(2)}, u32[]{:S(2)}) %collective-permute-start.13) | collective-permute-done | bytes 1048608 | tf_op jit(solution)/shard_map/ppermute | solution.py:53
  65.2 11.7 %cholesky.17 = f32[128,128]{1,0:T(8,128)S(1)} custom-call(f32[128,128]{1,0:T(8,128)S(1)} %gram.1), custom_call_target="Cholesky" | custom-call | tf_op jit(solution)/shard_map/jit(cholesky)/cholesky | solution.py:185
  78.3 9.8 %custom-call.7 = f32[1,128,128]{1,2,0:T(8,128)S(1)} custom-call(f32[1,128,128]{2,1,0:T(8,128)S(1)} %fusion.3), custom_call_target="InvertDiagBlocksLowerTriangular" | custom-call | tf_op jit(solution)/shard_map/jit(_solve_triangular)/triangular_solve | solution.py:186
  88.4 1.2 %copy-done.3 = bf16[4096,128]{1,0:T(8,128)(2,1)S(1)} copy-done((bf16[4096,128]{1,0:T(8,128)(2,1)S(1)}, bf16[4096,128]{1,0:T(8,128)(2,1)}, u32[]{:S(2)}) %copy-start.3) | copy-done | bytes 1048600
  89.6 1.2 %copy-done.5 = bf16[4096,128]{1,0:T(8,128)(2,1)S(1)} copy-done((bf16[4096,128]{1,0:T(8,128)(2,1)S(1)}, bf16[4096,128]{1,0:T(8,128)(2,1)}, u32[]{:S(2)}) %copy-start.5) | copy-done | bytes 1048600
  90.8 3.9 %factors.1 = (f32[256,128]{1,0:T(8,128)}, bf16[2048,128]{1,0:T(8,128)(2,1)}) custom-call(s32[16,3]{1,0:T(8,128)S(1)} %copy.9.rows_ref, bf16[16,128,384]{2,1,0:T(8,128)(2,1)S(1)} %tiles.1.tiles_ref, bf16[4096,128]{1,0:T(8,128)(2,1)S(1)} %copy-done.3, bf16[4096,128]{1,0:T(8,128)(2,1)S(1)} %copy-done.5, f32[256,128]{1,0:T(8,128)S(1)} %get-tuple-element.8.mine_ref, ...), custom_call_target="tpu_custom_call" | custom-call | tf_op jit(solution)/shard_map/factors/pallas_call | solution.py:187
  (47 shorter events, 10.9 us)
Async XLA Ops:
  1.4 1.4 %copy-start = (bf16[16,3,128,128]{3,2,1,0:T(8,128)(2,1)S(1)}, bf16[16,3,128,128]{3,2,1,0:T(8,128)(2,1)}, u32[]{:S(2)}) copy-start(bf16[16,3,128,128]{3,2,1,0:T(8,128)(2,1)} %blocks_ref.3) | copy-start | bytes 4718596
  2.8 1.0 %copy-start.6 = (bf16[2048,128]{1,0:T(8,128)(2,1)S(1)}, bf16[2048,128]{1,0:T(8,128)(2,1)}, u32[]{:S(2)}) copy-start(bf16[2048,128]{1,0:T(8,128)(2,1)} %sketch_ref.1) | copy-start | bytes 1572868
  3.8 0.7 copy-start.8
  10.7 2.7 %collective-permute-start = (bf16[4096,128]{1,0:T(8,128)(2,1)S(1)}, bf16[4096,128]{1,0:T(8,128)(2,1)S(1)}, u32[]{:S(2)}, u32[]{:S(2)}) collective-permute-start(bf16[4096,128]{1,0:T(8,128)(2,1)S(1)} %get-tuple-element.5), channel_id=1, source_target_pairs={{0,1},{1,0},{2,3},{3,2},{4,5},{5,4},{6,7},{7,6},{8,9},{9,8},{10,11... | collective-permute-start | bytes 3145736 | tf_op jit(solution)/shard_map/ppermute | solution.py:53
  13.6 21.1 %copy-start.7 = (f32[8192]{0:T(1024)S(1)}, f32[8192]{0:T(1024)}, u32[]{:S(2)}) copy-start(f32[8192]{0:T(1024)} %param.9) | copy-start | bytes 98308
  13.6 9.5 %collective-permute-start.1 = (bf16[1024,128]{1,0:T(8,128)(2,1)S(1)}, bf16[1024,128]{1,0:T(8,128)(2,1)S(1)}, u32[]{:S(2)}, u32[]{:S(2)}) collective-permute-start(bf16[1024,128]{1,0:T(8,128)(2,1)S(1)} %get-tuple-element.11), channel_id=1, source_target_pairs={{0,2},{1,3},{2,0},{3,1},{4,6},{5,7},{6,4},{7,5},{8,10},{9,11},{10,... | collective-permute-start | bytes 786440 | tf_op jit(solution)/shard_map/ppermute | solution.py:53
  16.1 13.7 %collective-permute-start.2 = (bf16[1024,128]{1,0:T(8,128)(2,1)S(1)}, bf16[1024,128]{1,0:T(8,128)(2,1)S(1)}, u32[]{:S(2)}, u32[]{:S(2)}) collective-permute-start(bf16[1024,128]{1,0:T(8,128)(2,1)S(1)} %get-tuple-element.13), channel_id=1, source_target_pairs={{0,4},{1,5},{2,6},{3,7},{4,0},{5,1},{6,2},{7,3},{8,12},{9,13},{10,... | collective-permute-start | bytes 786440 | tf_op jit(solution)/shard_map/ppermute | solution.py:53
  17.2 12.6 %collective-permute-start.3 = (bf16[1024,128]{1,0:T(8,128)(2,1)S(1)}, bf16[1024,128]{1,0:T(8,128)(2,1)S(1)}, u32[]{:S(2)}, u32[]{:S(2)}) collective-permute-start(bf16[1024,128]{1,0:T(8,128)(2,1)S(1)} %get-tuple-element.12), channel_id=1, source_target_pairs={{0,6},{1,7},{2,4},{3,5},{4,2},{5,3},{6,0},{7,1},{8,14},{9,15},{10,... | collective-permute-start | bytes 786440 | tf_op jit(solution)/shard_map/ppermute | solution.py:53
  29.9 30.9 %copy-start.1 = (bf16[16,3,128,128]{3,2,1,0:T(8,128)(2,1)S(1)}, bf16[16,3,128,128]{3,2,1,0:T(8,128)(2,1)}, u32[]{:S(2)}) copy-start(bf16[16,3,128,128]{3,2,1,0:T(8,128)(2,1)} %blocks_ref.3) | copy-start | bytes 4718596
  29.9 30.9 %copy-start.9 = (s32[16]{0:T(128)S(1)}, s32[16]{0:T(128)}, u32[]{:S(2)}) copy-start(s32[16]{0:T(128)} %counts_ref.3) | copy-start | bytes 196
  30.0 5.3 %collective-permute-start.4 = (bf16[256,128]{1,0:T(8,128)(2,1)S(1)}, bf16[256,128]{1,0:T(8,128)(2,1)S(1)}, u32[]{:S(2)}, u32[]{:S(2)}) collective-permute-start(bf16[256,128]{1,0:T(8,128)(2,1)S(1)} %get-tuple-element.14), channel_id=1, source_target_pairs={{0,8},{1,9},{2,10},{3,11},{4,12},{5,13},{6,14},{7,15},{8,0},{9,1},... | collective-permute-start | bytes 196616 | tf_op jit(solution)/shard_map/ppermute | solution.py:53
  32.3 6.3 %collective-permute-start.5 = (bf16[256,128]{1,0:T(8,128)(2,1)S(1)}, bf16[256,128]{1,0:T(8,128)(2,1)S(1)}, u32[]{:S(2)}, u32[]{:S(2)}) collective-permute-start(bf16[256,128]{1,0:T(8,128)(2,1)S(1)} %get-tuple-element.16), channel_id=1, source_target_pairs={{0,16},{1,17},{2,18},{3,19},{4,20},{5,21},{6,22},{7,23},{8,24},{9,... | collective-permute-start | bytes 196616 | tf_op jit(solution)/shard_map/ppermute | solution.py:53
  33.9 6.1 %collective-permute-start.6 = (bf16[256,128]{1,0:T(8,128)(2,1)S(1)}, bf16[256,128]{1,0:T(8,128)(2,1)S(1)}, u32[]{:S(2)}, u32[]{:S(2)}) collective-permute-start(bf16[256,128]{1,0:T(8,128)(2,1)S(1)} %get-tuple-element.15), channel_id=1, source_target_pairs={{0,24},{1,25},{2,26},{3,27},{4,28},{5,29},{6,30},{7,31},{8,16},{9,... | collective-permute-start | bytes 196616 | tf_op jit(solution)/shard_map/ppermute | solution.py:53
  40.1 4.5 %collective-permute-start.7 = (bf16[256,128]{1,0:T(8,128)(2,1)S(1)}, bf16[256,128]{1,0:T(8,128)(2,1)S(1)}, u32[]{:S(2)}, u32[]{:S(2)}) collective-permute-start(bf16[256,128]{1,0:T(8,128)(2,1)S(1)} %get-tuple-element.7), channel_id=1, source_target_pairs={{0,8},{1,9},{2,10},{3,11},{4,12},{5,13},{6,14},{7,15},{8,0},{9,1},... | collective-permute-start | bytes 196616 | tf_op jit(solution)/shard_map/ppermute | solution.py:53
  40.2 5.7 %collective-permute-start.8 = (bf16[256,128]{1,0:T(8,128)(2,1)S(1)}, bf16[256,128]{1,0:T(8,128)(2,1)S(1)}, u32[]{:S(2)}, u32[]{:S(2)}) collective-permute-start(bf16[256,128]{1,0:T(8,128)(2,1)S(1)} %get-tuple-element.7), channel_id=1, source_target_pairs={{0,16},{1,17},{2,18},{3,19},{4,20},{5,21},{6,22},{7,23},{8,24},{9,... | collective-permute-start | bytes 196616 | tf_op jit(solution)/shard_map/ppermute | solution.py:53
  42.4 6.1 %collective-permute-start.9 = (bf16[256,128]{1,0:T(8,128)(2,1)S(1)}, bf16[256,128]{1,0:T(8,128)(2,1)S(1)}, u32[]{:S(2)}, u32[]{:S(2)}) collective-permute-start(bf16[256,128]{1,0:T(8,128)(2,1)S(1)} %get-tuple-element.7), channel_id=1, source_target_pairs={{0,24},{1,25},{2,26},{3,27},{4,28},{5,29},{6,30},{7,31},{8,16},{9,... | collective-permute-start | bytes 196616 | tf_op jit(solution)/shard_map/ppermute | solution.py:53
  48.5 8.1 %collective-permute-start.10 = (bf16[1024,128]{1,0:T(8,128)(2,1)S(1)}, bf16[1024,128]{1,0:T(8,128)(2,1)S(1)}, u32[]{:S(2)}, u32[]{:S(2)}) collective-permute-start(bf16[1024,128]{1,0:T(8,128)(2,1)S(1)} %pad_maximum_fusion), channel_id=1, source_target_pairs={{0,2},{1,3},{2,0},{3,1},{4,6},{5,7},{6,4},{7,5},{8,10},{9,11},{10,... | collective-permute-start | bytes 786440 | tf_op jit(solution)/shard_map/ppermute | solution.py:53
  49.9 10.8 %collective-permute-start.11 = (bf16[1024,128]{1,0:T(8,128)(2,1)S(1)}, bf16[1024,128]{1,0:T(8,128)(2,1)S(1)}, u32[]{:S(2)}, u32[]{:S(2)}) collective-permute-start(bf16[1024,128]{1,0:T(8,128)(2,1)S(1)} %pad_maximum_fusion), channel_id=1, source_target_pairs={{0,4},{1,5},{2,6},{3,7},{4,0},{5,1},{6,2},{7,3},{8,12},{9,13},{10,... | collective-permute-start | bytes 786440 | tf_op jit(solution)/shard_map/ppermute | solution.py:53
  50.2 10.5 %collective-permute-start.12 = (bf16[1024,128]{1,0:T(8,128)(2,1)S(1)}, bf16[1024,128]{1,0:T(8,128)(2,1)S(1)}, u32[]{:S(2)}, u32[]{:S(2)}) collective-permute-start(bf16[1024,128]{1,0:T(8,128)(2,1)S(1)} %pad_maximum_fusion), channel_id=1, source_target_pairs={{0,6},{1,7},{2,4},{3,5},{4,2},{5,3},{6,0},{7,1},{8,14},{9,15},{10,... | collective-permute-start | bytes 786440 | tf_op jit(solution)/shard_map/ppermute | solution.py:53
  60.8 2.7 %copy-start.2 = (bf16[4096,128]{1,0:T(8,128)(2,1)}, bf16[4096,128]{1,0:T(8,128)(2,1)S(1)}, u32[]{:S(2)}) copy-start(bf16[4096,128]{1,0:T(8,128)(2,1)S(1)} %constant_dynamic-update-slice_fusion.own_ref) | copy-start | bytes 3145732
  60.8 2.7 %collective-permute-start.13 = (bf16[4096,128]{1,0:T(8,128)(2,1)S(1)}, bf16[4096,128]{1,0:T(8,128)(2,1)S(1)}, u32[]{:S(2)}, u32[]{:S(2)}) collective-permute-start(bf16[4096,128]{1,0:T(8,128)(2,1)S(1)} %constant_dynamic-update-slice_fusion.own_ref), channel_id=1, source_target_pairs={{0,1},{1,0},{2,3},{3,2},{4,5},{5,4},{6,7},{7,6},{8,9},{9,8},{10,11... | collective-permute-start | bytes 3145736 | tf_op jit(solution)/shard_map/ppermute | solution.py:53
  64.3 1.0 %copy-start.4 = (bf16[4096,128]{1,0:T(8,128)(2,1)}, bf16[4096,128]{1,0:T(8,128)(2,1)S(1)}, u32[]{:S(2)}) copy-start(bf16[4096,128]{1,0:T(8,128)(2,1)S(1)} %collective-permute-done.13.other_ref) | copy-start | bytes 3145732
  88.4 1.2 %copy-start.3 = (bf16[4096,128]{1,0:T(8,128)(2,1)S(1)}, bf16[4096,128]{1,0:T(8,128)(2,1)}, u32[]{:S(2)}) copy-start(bf16[4096,128]{1,0:T(8,128)(2,1)} %copy-done.2) | copy-start | bytes 3145732
  89.6 1.2 %copy-start.5 = (bf16[4096,128]{1,0:T(8,128)(2,1)S(1)}, bf16[4096,128]{1,0:T(8,128)(2,1)}, u32[]{:S(2)}) copy-start(bf16[4096,128]{1,0:T(8,128)(2,1)} %copy-done.4) | copy-start | bytes 3145732

commit v2 on v1

--- a/solution.py
+++ b/solution.py
@@ -9,7 +9,6 @@
 
 F32 = jnp.float32
 BF16 = jnp.bfloat16
-HIGHEST = lax.Precision.HIGHEST
 AXES = ("row", "col")
 VMEM_BYTES = 48 * 1024 * 1024
 
@@ -53,33 +52,47 @@
         return lax.ppermute(value, AXES, [(d, d ^ mask) for d in range(self.count)])
 
 
-def sum_kernel(plan, rows_ref, counts_ref, blocks_ref, sketch_ref, keep_ref, send_ref, total_ref):
+def sum_kernel(plan, rows_ref, counts_ref, blocks_ref, sketch_ref, total_ref, send_ref, tiles_ref, docs_ref, sems):
     me = plan.me()
-    documents, slots, block, _ = blocks_ref.shape
-    half = keep_ref.shape[0]
+    documents, slots, block, _ = tiles_ref.shape
+    half = send_ref.shape[0]
+    parts = sems.shape[0]
+    per = documents // parts
+    copies = []
+    for c in range(parts):
+        tiles_at = pl.ds(c * per, per)
+        docs_at = pl.ds(c * per * block, per * block)
+        pair = (
+            pltpu.make_async_copy(blocks_ref.at[tiles_at], tiles_ref.at[tiles_at], sems.at[c, 0]),
+            pltpu.make_async_copy(sketch_ref.at[docs_at], docs_ref.at[docs_at], sems.at[c, 1]),
+        )
+        for copy in pair:
+            copy.start()
+        copies.append(pair)
     total_ref[...] = jnp.zeros_like(total_ref)
-    for d in range(documents):
-        docs = sketch_ref[d * block : (d + 1) * block, :]
-        for s in range(slots):
-            def add(d=d, s=s, docs=docs):
-                term = jnp.dot(blocks_ref[d, s], docs, preferred_element_type=F32)
+    for c in range(parts):
+        for copy in copies[c]:
+            copy.wait()
+        for d in range(c * per, (c + 1) * per):
+            docs = docs_ref[d * block : (d + 1) * block, :]
+            terms = jnp.dot(tiles_ref[d].reshape(slots * block, block), docs, preferred_element_type=F32)
+            for s in range(slots):
+                term = jnp.where(s < counts_ref[d], terms[s * block : (s + 1) * block], 0.0)
                 for p in range(plan.pieces):
-                    at = pl.ds(plan.start(me, rows_ref[d, s], p), plan.piece)
+                    at = pl.ds(plan.start(me, rows_ref[s, d], p), plan.piece)
                     total_ref[at, :] += term[p * plan.piece : (p + 1) * plan.piece]
-
-            pl.when(s < counts_ref[d])(add)
-    keep_ref[...] = total_ref[:half, :]
     send_ref[...] = total_ref[half:, :].astype(BF16)
 
 
-def tiles_kernel(rows_ref, counts_ref, blocks_ref, weights_ref, out_ref):
+def tiles_kernel(rows_ref, counts_ref, blocks_ref, weights_ref, high_ref, low_ref):
     documents, slots, block, _ = blocks_ref.shape
     for d in range(documents):
         for s in range(slots):
-            scale = weights_ref[pl.ds(rows_ref[d, s], 1), :]
+            scale = weights_ref[pl.ds(rows_ref[s, d], 1), :]
             scale = jnp.where(s < counts_ref[d], scale, 0.0)
-            tile = blocks_ref[d, s].T.astype(F32) * scale
-            out_ref[d, :, s * block : (s + 1) * block] = tile.astype(BF16)
+            high, low = split(blocks_ref[d, s].T.astype(F32) * scale)
+            high_ref[d, :, s * block : (s + 1) * block] = high
+            low_ref[d, :, s * block : (s + 1) * block] = low
 
 
 def split(value):
@@ -97,32 +110,96 @@
     return dot_t(a_high, b_high) + (dot_t(a_high, b_low) + dot_t(a_low, b_high))
 
 
-def gram_kernel(own_ref, other_ref, gram_ref, *, features):
-    total = jnp.zeros(gram_ref.shape, F32)
-    for ref in (own_ref, other_ref):
-        step = min(1024, ref.shape[0])
-        for at in range(0, ref.shape[0], step):
+def dot3(a, b):
+    a_high, a_low = split(a)
+    b_high, b_low = split(b)
+    return dot(a_high, b_high) + (dot(a_high, b_low) + dot(a_low, b_high))
+
+
+def dot(a, b):
+    return jnp.dot(a, b, preferred_element_type=F32)
+
+
+def dot1(a, b):
+    return dot(a.astype(BF16), b.astype(BF16))
+
+
+def dot_t1(a, b):
+    return dot_t(a.astype(BF16), b.astype(BF16))
+
+
+def eliminate(gram_ref, inverse_ref):
+    size = gram_ref.shape[0]
+    lane = lax.broadcasted_iota(jnp.int32, (size, size), 1)
+    line = lax.broadcasted_iota(jnp.int32, (size, 1), 0)
+    first = lax.broadcasted_iota(jnp.int32, (1, size), 1)
+    inverse_ref[...] = jnp.where(lane == line, 1.0, 0.0)
+
+    def step(j, carry):
+        values = gram_ref[...]
+        pivot_row = gram_ref[pl.ds(j, 1), :]
+        pivot = jnp.sum(jnp.where(first == j, pivot_row, 0.0), axis=1, keepdims=True)
+        scale = 1.0 / jnp.sqrt(pivot)
+        column = jnp.sum(jnp.where(lane == j, values, 0.0), axis=1, keepdims=True)
+        column = jnp.where(line > j, column * scale, 0.0)
+        gram_ref[...] = values - column * (pivot_row * scale)
+        own_row = inverse_ref[pl.ds(j, 1), :] * scale
+        inverse_ref[...] = jnp.where(line == j, own_row, inverse_ref[...] - column * own_row)
+        return carry
+
+    lax.fori_loop(0, size, step, 0)
+
+
+def invert_factor(gram, gram_ref, inverse_ref):
+    size = gram.shape[0]
+    line = lax.broadcasted_iota(jnp.int32, (size, size), 0)
+    lane = lax.broadcasted_iota(jnp.int32, (size, size), 1)
+    same = line == lane
+    eye = jnp.where(same, 1.0, 0.0)
+    take = jnp.where(line > lane, 1.0, jnp.where(same, 0.5, 0.0))
+    diagonal = jnp.where(same, gram, 0.0)
+    down = 1.0 / jnp.sqrt(jnp.sum(diagonal, axis=1, keepdims=True))
+    across = 1.0 / jnp.sqrt(jnp.sum(diagonal, axis=0, keepdims=True))
+    beyond = gram * down * across - eye
+    factor = eye - take * beyond
+    for product, product_t in ((dot1, dot_t1), (dot1, dot_t1), (dot3, dot_t3), (dot3, dot_t3)):
+        left = factor - eye + product(factor, beyond)
+        residual = factor.T - eye + product_t(left, factor)
+        factor = factor - product(take * residual, factor)
+    inverse_ref[...] = factor * across
+    worst = jnp.max(jnp.sum(jnp.abs(residual), axis=1))
+
+    @pl.when(jnp.logical_not(worst < 1e-3))
+    def _():
+        gram_ref[...] = gram
+        eliminate(gram_ref, inverse_ref)
+
+
+def last_kernel(
+    plan, features, rows_ref, high_ref, low_ref, own_ref, other_ref, mine_ref, basis_ref, factors_ref, all_ref, gram_ref, inverse_ref
+):
+    me = plan.me()
+    documents, block, _ = high_ref.shape
+    half = own_ref.shape[0]
+    slots = high_ref.shape[2] // block
+    gram = jnp.zeros(gram_ref.shape, F32)
+    step = min(1024, half)
+    for base, ref in ((0, own_ref), (half, other_ref)):
+        for at in range(0, half, step):
             part = ref[at : at + step, :]
-            total += lax.dot_general(part, part, (((0,), (0,)), ((), ())), preferred_element_type=F32)
-    gram_ref[...] = total * (1.0 / features)
-
-
-def last_kernel(plan, rows_ref, tiles_ref, own_ref, other_ref, mine_ref, inverse_ref, basis_ref, factors_ref, all_ref):
-    me = plan.me()
-    documents, block, _ = tiles_ref.shape
-    half = own_ref.shape[0]
-    slots = tiles_ref.shape[2] // block
+            all_ref[base + at : base + at + step, :] = part
+            gram += lax.dot_general(part, part, (((0,), (0,)), ((), ())), preferred_element_type=F32)
+    invert_factor(gram * (1.0 / features), gram_ref, inverse_ref)
     inverse = inverse_ref[...]
     basis_ref[...] = dot_t3(mine_ref[...], inverse)
-    all_ref[:half, :] = own_ref[...]
-    all_ref[half:, :] = other_ref[...]
     for d in range(documents):
         picked = []
         for s in range(slots):
             for p in range(plan.pieces):
-                at = pl.ds(plan.start(me, rows_ref[d, s], p), plan.piece)
+                at = pl.ds(plan.start(me, rows_ref[s, d], p), plan.piece)
                 picked.append(all_ref[at, :])
-        product = jnp.dot(tiles_ref[d], jnp.concatenate(picked, axis=0), preferred_element_type=F32)
+        picked = jnp.concatenate(picked, axis=0)
+        product = dot(high_ref[d], picked) + dot(low_ref[d], picked)
         factors_ref[d * block : (d + 1) * block, :] = dot_t3(product, inverse).astype(BF16)
 
 
@@ -135,15 +212,22 @@
     params = pltpu.CompilerParams(vmem_limit_bytes=VMEM_BYTES)
     shape = jax.ShapeDtypeStruct
 
+    rows = rows.T
+    parts = min(4, documents)
     keep, send = pl.pallas_call(
         functools.partial(sum_kernel, plan),
-        out_shape=(shape((half, columns), F32), shape((half, columns), BF16)),
-        in_specs=[scalars(), scalars(), whole(), whole()],
+        out_shape=(shape((features, columns), F32), shape((half, columns), BF16)),
+        in_specs=[scalars(), scalars(), pl.BlockSpec(memory_space=pltpu.HBM), pl.BlockSpec(memory_space=pltpu.HBM)],
         out_specs=(whole(), whole()),
-        scratch_shapes=[pltpu.VMEM((features, columns), F32)],
+        scratch_shapes=[
+            pltpu.VMEM(blocks.shape, BF16),
+            pltpu.VMEM(sketch.shape, BF16),
+            pltpu.SemaphoreType.DMA((parts, 2)),
+        ],
         compiler_params=params,
         name="local_sum",
     )(rows, counts, blocks, sketch)
+    keep = keep[:half]
 
     got = plan.swap(send, 1)
     keep = keep.reshape(plane, rest * flat, columns)
@@ -160,12 +244,14 @@
         mine = mine + part.astype(F32)
     mine = mine * lax.dynamic_slice_in_dim(weights, plan.me() * flat, flat)[:, None]
 
-    tiles = pl.pallas_call(
+    tiles_shape = shape((documents, block, slots * block), BF16)
+    high, low = pl.pallas_call(
         tiles_kernel,
-        out_shape=shape((documents, block, slots * block), BF16),
+        out_shape=(tiles_shape, tiles_shape),
         in_specs=[scalars(), scalars(), whole(), whole()],
-        out_specs=whole(),
+        out_specs=(whole(), whole()),
         compiler_params=params,
+        cost_estimate=pl.CostEstimate(flops=1 << 20, bytes_accessed=16 << 20, transcendentals=0),
         name="tiles",
     )(rows, counts, blocks, weights.reshape(features // block, block))
 
@@ -174,25 +260,19 @@
     own = jnp.concatenate([near] + [plan.swap(near, p << 1) for p in range(1, plane)], axis=0)
     other = plan.swap(own, 1)
 
-    gram = pl.pallas_call(
-        functools.partial(gram_kernel, features=features),
-        out_shape=shape((columns, columns), F32),
-        in_specs=[whole(), whole()],
-        out_specs=whole(),
-        compiler_params=params,
-        name="gram",
-    )(own, other)
-    factor = jnp.linalg.cholesky(gram, symmetrize_input=False)
-    inverse = jax.scipy.linalg.solve_triangular(factor, jnp.eye(columns, dtype=F32), lower=True)
     return pl.pallas_call(
-        functools.partial(last_kernel, plan),
+        functools.partial(last_kernel, plan, features),
         out_shape=(shape((flat, columns), F32), shape((documents * block, columns), BF16)),
         in_specs=[scalars()] + [whole()] * 5,
         out_specs=(whole(), whole()),
-        scratch_shapes=[pltpu.VMEM((features, columns), BF16)],
+        scratch_shapes=[
+            pltpu.VMEM((features, columns), BF16),
+            pltpu.VMEM((columns, columns), F32),
+            pltpu.VMEM((columns, columns), F32),
+        ],
         compiler_params=params,
         name="factors",
-    )(rows, tiles, own, other, mine, inverse)
+    )(rows, high, low, own, other, mine)
 
 
 def solution(mesh):

time: 95.3 us -> 86.8 us (0.911)
  other arithmetic: 23.3 us -> 2.99 us
  Pallas kernels: 12 us -> 27.9 us
  local copies, waits for them, and re-layouts: 7.53 us -> 4.03 us
    another operation x5 -> x0, other arithmetic: 22.9 us -> none  [the longest x3 12.4 us: body(): factor = jnp.linalg.cholesky(gram, symmetrize_input=False)]
    pallas_call x4 -> x3, Pallas kernels: 12 us -> 27.9 us  [the longest x1 21.2 us: body(): pl.pallas_call(functools.partial(last_kernel, plan, features), out_shape=...]
    unnamed x26 -> x21, local copies, waits for them, and re-layouts: 7.4 us -> 3.9 us
    convert_element_type x1, other arithmetic: 0.16 us -> 1.66 us  [body(): (keep[p] + got[p].astype(F32)).astype(BF16)]
    another operation x1, other arithmetic: 0.16 us -> 1.21 us  [run(): jax.shard_map(functools.partial(body, plan), mesh=mesh, in_specs=placed,...]
  transfers between devices with their start and end apart: 14 -> 14, of which waited for: 11 -> 12; matrix products, arithmetic and copies ran while one was open for 0% -> 0% of each run, Pallas kernels for 1% -> 2%
where the time goes in v2:
time: 86.8 us; the launch traced here: 86.5 us
  waiting for transfers between devices  33.3 us (38%)
  Pallas kernels  27.9 us (32%)
  starting transfers between devices  17.5 us (20%)
  local copies, waits for them, and re-layouts  4.03 us (5%)
  other arithmetic  2.99 us (3%)
    ppermute x14, waiting for transfers between devices, swap(): return lax.ppermute(value, AXES, [(d, d ^ mask) for d in range(self.count)])  33.3 us
    pallas_call x1, Pallas kernels, body(): pl.pallas_call(functools.partial(last_kernel, plan, features), out_shape=...  21.2 us
    ppermute x14, starting transfers between devices, swap(): return lax.ppermute(value, AXES, [(d, d ^ mask) for d in range(self.count)])  17.5 us
    pallas_call x1, Pallas kernels, body(): pl.pallas_call(functools.partial(sum_kernel, plan), out_shape=(shape((fea...  5.39 us
    unnamed x21, local copies, waits for them, and re-layouts  3.9 us
  transfers between devices with their start and end apart: 14, of which 12 were waited for; matrix products, arithmetic and copies ran while one was open for 0% of the time, Pallas kernels for 2%

profile of v2, /device:TPU:0, one launch (start us, length us, event | category | flops | bytes accessed | tf_op | source)
XLA Modules:
  0.0 86.5 jit_solution(6586092720340489657)
XLA Ops:
  0.6 1.4 %copy-done = bf16[16,3,128,128]{3,2,1,0:T(8,128)(2,1)S(1)} copy-done((bf16[16,3,128,128]{3,2,1,0:T(8,128)(2,1)S(1)}, bf16[16,3,128,128]{3,2,1,0:T(8,128)(2,1)}, u32[]{:S(2)}) %copy-start) | copy-done | bytes 1572888
  2.0 1.0 %copy-done.2 = bf16[2048,128]{1,0:T(8,128)(2,1)S(1)} copy-done((bf16[2048,128]{1,0:T(8,128)(2,1)S(1)}, bf16[2048,128]{1,0:T(8,128)(2,1)}, u32[]{:S(2)}) %copy-start.2) | copy-done | bytes 524312
  4.4 5.4 %local_sum.1 = (f32[8192,128]{1,0:T(8,128)}, bf16[4096,128]{1,0:T(8,128)(2,1)S(1)}) custom-call(s32[3,16]{1,0:T(4,128)S(1)} %bitcast.3, s32[16]{0:T(128)S(1)} %copy-done.6, bf16[16,3,128,128]{3,2,1,0:T(8,128)(2,1)S(1)} %copy-done, bf16[2048,128]{1,0:T(8,128)(2,1)S(1)} %copy-done.2), custom_call_target="tpu_custom_call" | custom-call | tf_op jit(solution)/shard_map/local_sum/pallas_call | solution.py:217
  10.3 2.3 %collective-permute-done = bf16[4096,128]{1,0:T(8,128)(2,1)S(1)} collective-permute-done((bf16[4096,128]{1,0:T(8,128)(2,1)S(1)}, bf16[4096,128]{1,0:T(8,128)(2,1)S(1)}, u32[]{:S(2)}, u32[]{:S(2)}) %collective-permute-start) | collective-permute-done | bytes 1048608 | tf_op jit(solution)/shard_map/ppermute | solution.py:52
  12.6 1.7 %add_convert_fusion.2 = (bf16[1024,128]{1,0:T(8,128)(2,1)S(1)}, bf16[1024,128]{1,0:T(8,128)(2,1)S(1)}, bf16[1024,128]{1,0:T(8,128)(2,1)S(1)}) fusion(f32[8192,128]{1,0:T(8,128)} %get-tuple-element.8, bf16[4096,128]{1,0:T(8,128)(2,1)S(1)} %collective-permute-done), kind=kLoop, calls=%fused_computation.3 | loop fusion | flops 1179648 | bytes 3145728 | tf_op jit(solution)/shard_map/convert_element_type | solution.py:235
  14.3 2.9 %collective-permute-start.1 = (bf16[1024,128]{1,0:T(8,128)(2,1)S(1)}, bf16[1024,128]{1,0:T(8,128)(2,1)S(1)}, u32[]{:S(2)}, u32[]{:S(2)}) collective-permute-start(bf16[1024,128]{1,0:T(8,128)(2,1)S(1)} %get-tuple-element.15), channel_id=1, source_target_pairs={{0,2},{1,3},{2,0},{3,1},{4,6},{5,7},{6,4},{7,5},{8,10},{9,11},{10,... | collective-permute-start | bytes 786440 | tf_op jit(solution)/shard_map/ppermute | solution.py:52
  17.2 1.5 %collective-permute-start.2 = (bf16[1024,128]{1,0:T(8,128)(2,1)S(1)}, bf16[1024,128]{1,0:T(8,128)(2,1)S(1)}, u32[]{:S(2)}, u32[]{:S(2)}) collective-permute-start(bf16[1024,128]{1,0:T(8,128)(2,1)S(1)} %get-tuple-element.17), channel_id=1, source_target_pairs={{0,4},{1,5},{2,6},{3,7},{4,0},{5,1},{6,2},{7,3},{8,12},{9,13},{10,... | collective-permute-start | bytes 786440 | tf_op jit(solution)/shard_map/ppermute | solution.py:52
  18.8 5.5 %collective-permute-done.1 = bf16[1024,128]{1,0:T(8,128)(2,1)S(1)} collective-permute-done((bf16[1024,128]{1,0:T(8,128)(2,1)S(1)}, bf16[1024,128]{1,0:T(8,128)(2,1)S(1)}, u32[]{:S(2)}, u32[]{:S(2)}) %collective-permute-start.1) | collective-permute-done | bytes 262176 | tf_op jit(solution)/shard_map/ppermute | solution.py:52
  24.3 6.6 %collective-permute-done.2 = bf16[1024,128]{1,0:T(8,128)(2,1)S(1)} collective-permute-done((bf16[1024,128]{1,0:T(8,128)(2,1)S(1)}, bf16[1024,128]{1,0:T(8,128)(2,1)S(1)}, u32[]{:S(2)}, u32[]{:S(2)}) %collective-permute-start.2) | collective-permute-done | bytes 262176 | tf_op jit(solution)/shard_map/ppermute | solution.py:52
  30.9 1.2 %fusion.4 = (bf16[1024,128]{1,0:T(8,128)(2,1)S(1)}, f32[1024,128]{1,0:T(8,128)S(1)}) fusion(bf16[1024,128]{1,0:T(8,128)(2,1)S(1)} %collective-permute-done.3, bf16[1024,128]{1,0:T(8,128)(2,1)S(1)} %collective-permute-done.2, bf16[1024,128]{1,0:T(8,128)(2,1)S(1)} %collective-permute-done.1, bf16[4096,128]{1,0:T(8,128)(2,1)S(1)} %collective-permute-done, ...), kind=kLoop, calls=%fused_computation.16 | loop fusion | flops 1179648 | bytes 2359296 | tf_op jit(solution)/shard_map/convert.2 | solution.py:289
  32.1 1.6 %collective-permute-start.4 = (bf16[256,128]{1,0:T(8,128)(2,1)S(1)}, bf16[256,128]{1,0:T(8,128)(2,1)S(1)}, u32[]{:S(2)}, u32[]{:S(2)}) collective-permute-start(bf16[256,128]{1,0:T(8,128)(2,1)S(1)} %get-tuple-element.18), channel_id=1, source_target_pairs={{0,8},{1,9},{2,10},{3,11},{4,12},{5,13},{6,14},{7,15},{8,0},{9,1},... | collective-permute-start | bytes 196616 | tf_op jit(solution)/shard_map/ppermute | solution.py:52
  33.8 2.6 %collective-permute-start.5 = (bf16[256,128]{1,0:T(8,128)(2,1)S(1)}, bf16[256,128]{1,0:T(8,128)(2,1)S(1)}, u32[]{:S(2)}, u32[]{:S(2)}) collective-permute-start(bf16[256,128]{1,0:T(8,128)(2,1)S(1)} %get-tuple-element.20), channel_id=1, source_target_pairs={{0,16},{1,17},{2,18},{3,19},{4,20},{5,21},{6,22},{7,23},{8,24},{9,... | collective-permute-start | bytes 196616 | tf_op jit(solution)/shard_map/ppermute | solution.py:52
  37.1 3.2 %collective-permute-done.5 = bf16[256,128]{1,0:T(8,128)(2,1)S(1)} collective-permute-done((bf16[256,128]{1,0:T(8,128)(2,1)S(1)}, bf16[256,128]{1,0:T(8,128)(2,1)S(1)}, u32[]{:S(2)}, u32[]{:S(2)}) %collective-permute-start.5) | collective-permute-done | bytes 65568 | tf_op jit(solution)/shard_map/ppermute | solution.py:52
  40.4 2.1 %collective-permute-done.6 = bf16[256,128]{1,0:T(8,128)(2,1)S(1)} collective-permute-done((bf16[256,128]{1,0:T(8,128)(2,1)S(1)}, bf16[256,128]{1,0:T(8,128)(2,1)S(1)}, u32[]{:S(2)}, u32[]{:S(2)}) %collective-permute-start.6) | collective-permute-done | bytes 65568 | tf_op jit(solution)/shard_map/ppermute | solution.py:52
  42.6 1.6 %collective-permute-start.8 = (bf16[256,128]{1,0:T(8,128)(2,1)S(1)}, bf16[256,128]{1,0:T(8,128)(2,1)S(1)}, u32[]{:S(2)}, u32[]{:S(2)}) collective-permute-start(bf16[256,128]{1,0:T(8,128)(2,1)S(1)} %get-tuple-element.11), channel_id=1, source_target_pairs={{0,16},{1,17},{2,18},{3,19},{4,20},{5,21},{6,22},{7,23},{8,24},{9,... | collective-permute-start | bytes 196616 | tf_op jit(solution)/shard_map/ppermute | solution.py:52
  44.2 2.8 %collective-permute-start.9 = (bf16[256,128]{1,0:T(8,128)(2,1)S(1)}, bf16[256,128]{1,0:T(8,128)(2,1)S(1)}, u32[]{:S(2)}, u32[]{:S(2)}) collective-permute-start(bf16[256,128]{1,0:T(8,128)(2,1)S(1)} %get-tuple-element.11), channel_id=1, source_target_pairs={{0,24},{1,25},{2,26},{3,27},{4,28},{5,29},{6,30},{7,31},{8,16},{9,... | collective-permute-start | bytes 196616 | tf_op jit(solution)/shard_map/ppermute | solution.py:52
  47.9 2.5 %collective-permute-done.9 = bf16[256,128]{1,0:T(8,128)(2,1)S(1)} collective-permute-done((bf16[256,128]{1,0:T(8,128)(2,1)S(1)}, bf16[256,128]{1,0:T(8,128)(2,1)S(1)}, u32[]{:S(2)}, u32[]{:S(2)}) %collective-permute-start.9) | collective-permute-done | bytes 65568 | tf_op jit(solution)/shard_map/ppermute | solution.py:52
  50.4 1.6 %collective-permute-start.10 = (bf16[1024,128]{1,0:T(8,128)(2,1)S(1)}, bf16[1024,128]{1,0:T(8,128)(2,1)S(1)}, u32[]{:S(2)}, u32[]{:S(2)}) collective-permute-start(bf16[1024,128]{1,0:T(8,128)(2,1)S(1)} %pad_maximum_fusion), channel_id=1, source_target_pairs={{0,2},{1,3},{2,0},{3,1},{4,6},{5,7},{6,4},{7,5},{8,10},{9,11},{10,... | collective-permute-start | bytes 786440 | tf_op jit(solution)/shard_map/ppermute | solution.py:52
  52.4 1.5 %collective-permute-start.12 = (bf16[1024,128]{1,0:T(8,128)(2,1)S(1)}, bf16[1024,128]{1,0:T(8,128)(2,1)S(1)}, u32[]{:S(2)}, u32[]{:S(2)}) collective-permute-start(bf16[1024,128]{1,0:T(8,128)(2,1)S(1)} %pad_maximum_fusion), channel_id=1, source_target_pairs={{0,6},{1,7},{2,4},{3,5},{4,2},{5,3},{6,0},{7,1},{8,14},{9,15},{10,... | collective-permute-start | bytes 786440 | tf_op jit(solution)/shard_map/ppermute | solution.py:52
  54.0 4.3 %collective-permute-done.10 = bf16[1024,128]{1,0:T(8,128)(2,1)S(1)} collective-permute-done((bf16[1024,128]{1,0:T(8,128)(2,1)S(1)}, bf16[1024,128]{1,0:T(8,128)(2,1)S(1)}, u32[]{:S(2)}, u32[]{:S(2)}) %collective-permute-start.10) | collective-permute-done | bytes 262176 | tf_op jit(solution)/shard_map/ppermute | solution.py:52
  58.3 4.2 %collective-permute-done.11 = bf16[1024,128]{1,0:T(8,128)(2,1)S(1)} collective-permute-done((bf16[1024,128]{1,0:T(8,128)(2,1)S(1)}, bf16[1024,128]{1,0:T(8,128)(2,1)S(1)}, u32[]{:S(2)}, u32[]{:S(2)}) %collective-permute-start.11) | collective-permute-done | bytes 262176 | tf_op jit(solution)/shard_map/ppermute | solution.py:52
  62.7 1.3 %tiles.1 = (bf16[16,128,384]{2,1,0:T(8,128)(2,1)S(1)}, bf16[16,128,384]{2,1,0:T(8,128)(2,1)S(1)}) custom-call(s32[3,16]{1,0:T(4,128)S(1)} %bitcast.4, s32[16]{0:T(128)S(1)} %copy-done.7, bf16[16,3,128,128]{3,2,1,0:T(8,128)(2,1)S(1)} %copy-done.1, f32[64,128]{1,0:T(8,128)S(1)} %bitcast.2), custom_call_target="tpu_custom_call" | custom-call | flops 1048576 | bytes 16777216 | tf_op jit(solution)/shard_map/tiles/pallas_call | solution.py:248
  64.0 1.3 %collective-permute-done.13.other_ref = bf16[4096,128]{1,0:T(8,128)(2,1)S(1)} collective-permute-done((bf16[4096,128]{1,0:T(8,128)(2,1)S(1)}, bf16[4096,128]{1,0:T(8,128)(2,1)S(1)}, u32[]{:S(2)}, u32[]{:S(2)}) %collective-permute-start.13) | collective-permute-done | bytes 1048608 | tf_op jit(solution)/shard_map/ppermute | solution.py:52
  65.3 21.2 %factors.1 = (f32[256,128]{1,0:T(8,128)}, bf16[2048,128]{1,0:T(8,128)(2,1)}) custom-call(s32[3,16]{1,0:T(4,128)S(1)} %bitcast.5, bf16[16,128,384]{2,1,0:T(8,128)(2,1)S(1)} %get-tuple-element.6.high_ref, bf16[16,128,384]{2,1,0:T(8,128)(2,1)S(1)} %get-tuple-element.7.low_ref, bf16[4096,128]{1,0:T(8,128)(2,1)S(1)} %constant_dynamic-update-slice_fusion.own_ref, ...), custom_call_target="tpu_custom_call" | custom-call | tf_op jit(solution)/shard_map/factors/pallas_call | solution.py:263
  (35 shorter events, 4.4 us)
Async XLA Ops:
  0.6 1.4 %copy-start = (bf16[16,3,128,128]{3,2,1,0:T(8,128)(2,1)S(1)}, bf16[16,3,128,128]{3,2,1,0:T(8,128)(2,1)}, u32[]{:S(2)}) copy-start(bf16[16,3,128,128]{3,2,1,0:T(8,128)(2,1)} %blocks_ref.3) | copy-start | bytes 4718596
  2.0 1.0 %copy-start.2 = (bf16[2048,128]{1,0:T(8,128)(2,1)S(1)}, bf16[2048,128]{1,0:T(8,128)(2,1)}, u32[]{:S(2)}) copy-start(bf16[2048,128]{1,0:T(8,128)(2,1)} %sketch_ref.1) | copy-start | bytes 1572868
  3.1 0.7 copy-start.4
  3.8 0.7 copy-start.6
  4.4 32.2 %copy-start.3 = (f32[8192]{0:T(1024)S(1)}, f32[8192]{0:T(1024)}, u32[]{:S(2)}) copy-start(f32[8192]{0:T(1024)} %param.9) | copy-start | bytes 98308
  9.8 2.8 %collective-permute-start = (bf16[4096,128]{1,0:T(8,128)(2,1)S(1)}, bf16[4096,128]{1,0:T(8,128)(2,1)S(1)}, u32[]{:S(2)}, u32[]{:S(2)}) collective-permute-start(bf16[4096,128]{1,0:T(8,128)(2,1)S(1)} %get-tuple-element.9), channel_id=1, source_target_pairs={{0,1},{1,0},{2,3},{3,2},{4,5},{5,4},{6,7},{7,6},{8,9},{9,8},{10,11... | collective-permute-start | bytes 3145736 | tf_op jit(solution)/shard_map/ppermute | solution.py:52
  12.6 50.0 %copy-start.1 = (bf16[16,3,128,128]{3,2,1,0:T(8,128)(2,1)S(1)}, bf16[16,3,128,128]{3,2,1,0:T(8,128)(2,1)}, u32[]{:S(2)}) copy-start(bf16[16,3,128,128]{3,2,1,0:T(8,128)(2,1)} %blocks_ref.3) | copy-start | bytes 4718596
  12.6 50.0 %copy-start.5 = (s32[16,3]{0,1:T(4,128)S(1)}, s32[16,3]{0,1:T(4,128)}, u32[]{:S(2)}) copy-start(s32[16,3]{0,1:T(4,128)} %param.6) | copy-start | bytes 580
  12.6 50.0 %copy-start.7 = (s32[16]{0:T(128)S(1)}, s32[16]{0:T(128)}, u32[]{:S(2)}) copy-start(s32[16]{0:T(128)} %counts_ref.3) | copy-start | bytes 196
  14.3 10.0 %collective-permute-start.1 = (bf16[1024,128]{1,0:T(8,128)(2,1)S(1)}, bf16[1024,128]{1,0:T(8,128)(2,1)S(1)}, u32[]{:S(2)}, u32[]{:S(2)}) collective-permute-start(bf16[1024,128]{1,0:T(8,128)(2,1)S(1)} %get-tuple-element.15), channel_id=1, source_target_pairs={{0,2},{1,3},{2,0},{3,1},{4,6},{5,7},{6,4},{7,5},{8,10},{9,11},{10,... | collective-permute-start | bytes 786440 | tf_op jit(solution)/shard_map/ppermute | solution.py:52
  17.2 13.7 %collective-permute-start.2 = (bf16[1024,128]{1,0:T(8,128)(2,1)S(1)}, bf16[1024,128]{1,0:T(8,128)(2,1)S(1)}, u32[]{:S(2)}, u32[]{:S(2)}) collective-permute-start(bf16[1024,128]{1,0:T(8,128)(2,1)S(1)} %get-tuple-element.17), channel_id=1, source_target_pairs={{0,4},{1,5},{2,6},{3,7},{4,0},{5,1},{6,2},{7,3},{8,12},{9,13},{10,... | collective-permute-start | bytes 786440 | tf_op jit(solution)/shard_map/ppermute | solution.py:52
  18.7 12.2 %collective-permute-start.3 = (bf16[1024,128]{1,0:T(8,128)(2,1)S(1)}, bf16[1024,128]{1,0:T(8,128)(2,1)S(1)}, u32[]{:S(2)}, u32[]{:S(2)}) collective-permute-start(bf16[1024,128]{1,0:T(8,128)(2,1)S(1)} %get-tuple-element.16), channel_id=1, source_target_pairs={{0,6},{1,7},{2,4},{3,5},{4,2},{5,3},{6,0},{7,1},{8,14},{9,15},{10,... | collective-permute-start | bytes 786440 | tf_op jit(solution)/shard_map/ppermute | solution.py:52
  32.1 5.0 %collective-permute-start.4 = (bf16[256,128]{1,0:T(8,128)(2,1)S(1)}, bf16[256,128]{1,0:T(8,128)(2,1)S(1)}, u32[]{:S(2)}, u32[]{:S(2)}) collective-permute-start(bf16[256,128]{1,0:T(8,128)(2,1)S(1)} %get-tuple-element.18), channel_id=1, source_target_pairs={{0,8},{1,9},{2,10},{3,11},{4,12},{5,13},{6,14},{7,15},{8,0},{9,1},... | collective-permute-start | bytes 196616 | tf_op jit(solution)/shard_map/ppermute | solution.py:52
  33.8 6.6 %collective-permute-start.5 = (bf16[256,128]{1,0:T(8,128)(2,1)S(1)}, bf16[256,128]{1,0:T(8,128)(2,1)S(1)}, u32[]{:S(2)}, u32[]{:S(2)}) collective-permute-start(bf16[256,128]{1,0:T(8,128)(2,1)S(1)} %get-tuple-element.20), channel_id=1, source_target_pairs={{0,16},{1,17},{2,18},{3,19},{4,20},{5,21},{6,22},{7,23},{8,24},{9,... | collective-permute-start | bytes 196616 | tf_op jit(solution)/shard_map/ppermute | solution.py:52
  36.4 6.1 %collective-permute-start.6 = (bf16[256,128]{1,0:T(8,128)(2,1)S(1)}, bf16[256,128]{1,0:T(8,128)(2,1)S(1)}, u32[]{:S(2)}, u32[]{:S(2)}) collective-permute-start(bf16[256,128]{1,0:T(8,128)(2,1)S(1)} %get-tuple-element.19), channel_id=1, source_target_pairs={{0,24},{1,25},{2,26},{3,27},{4,28},{5,29},{6,30},{7,31},{8,16},{9,... | collective-permute-start | bytes 196616 | tf_op jit(solution)/shard_map/ppermute | solution.py:52
  42.5 4.6 %collective-permute-start.7 = (bf16[256,128]{1,0:T(8,128)(2,1)S(1)}, bf16[256,128]{1,0:T(8,128)(2,1)S(1)}, u32[]{:S(2)}, u32[]{:S(2)}) collective-permute-start(bf16[256,128]{1,0:T(8,128)(2,1)S(1)} %get-tuple-element.11), channel_id=1, source_target_pairs={{0,8},{1,9},{2,10},{3,11},{4,12},{5,13},{6,14},{7,15},{8,0},{9,1},... | collective-permute-start | bytes 196616 | tf_op jit(solution)/shard_map/ppermute | solution.py:52
  42.6 5.2 %collective-permute-start.8 = (bf16[256,128]{1,0:T(8,128)(2,1)S(1)}, bf16[256,128]{1,0:T(8,128)(2,1)S(1)}, u32[]{:S(2)}, u32[]{:S(2)}) collective-permute-start(bf16[256,128]{1,0:T(8,128)(2,1)S(1)} %get-tuple-element.11), channel_id=1, source_target_pairs={{0,16},{1,17},{2,18},{3,19},{4,20},{5,21},{6,22},{7,23},{8,24},{9,... | collective-permute-start | bytes 196616 | tf_op jit(solution)/shard_map/ppermute | solution.py:52
  44.2 6.1 %collective-permute-start.9 = (bf16[256,128]{1,0:T(8,128)(2,1)S(1)}, bf16[256,128]{1,0:T(8,128)(2,1)S(1)}, u32[]{:S(2)}, u32[]{:S(2)}) collective-permute-start(bf16[256,128]{1,0:T(8,128)(2,1)S(1)} %get-tuple-element.11), channel_id=1, source_target_pairs={{0,24},{1,25},{2,26},{3,27},{4,28},{5,29},{6,30},{7,31},{8,16},{9,... | collective-permute-start | bytes 196616 | tf_op jit(solution)/shard_map/ppermute | solution.py:52
  50.4 7.9 %collective-permute-start.10 = (bf16[1024,128]{1,0:T(8,128)(2,1)S(1)}, bf16[1024,128]{1,0:T(8,128)(2,1)S(1)}, u32[]{:S(2)}, u32[]{:S(2)}) collective-permute-start(bf16[1024,128]{1,0:T(8,128)(2,1)S(1)} %pad_maximum_fusion), channel_id=1, source_target_pairs={{0,2},{1,3},{2,0},{3,1},{4,6},{5,7},{6,4},{7,5},{8,10},{9,11},{10,... | collective-permute-start | bytes 786440 | tf_op jit(solution)/shard_map/ppermute | solution.py:52
  51.9 10.5 %collective-permute-start.11 = (bf16[1024,128]{1,0:T(8,128)(2,1)S(1)}, bf16[1024,128]{1,0:T(8,128)(2,1)S(1)}, u32[]{:S(2)}, u32[]{:S(2)}) collective-permute-start(bf16[1024,128]{1,0:T(8,128)(2,1)S(1)} %pad_maximum_fusion), channel_id=1, source_target_pairs={{0,4},{1,5},{2,6},{3,7},{4,0},{5,1},{6,2},{7,3},{8,12},{9,13},{10,... | collective-permute-start | bytes 786440 | tf_op jit(solution)/shard_map/ppermute | solution.py:52
  52.4 10.1 %collective-permute-start.12 = (bf16[1024,128]{1,0:T(8,128)(2,1)S(1)}, bf16[1024,128]{1,0:T(8,128)(2,1)S(1)}, u32[]{:S(2)}, u32[]{:S(2)}) collective-permute-start(bf16[1024,128]{1,0:T(8,128)(2,1)S(1)} %pad_maximum_fusion), channel_id=1, source_target_pairs={{0,6},{1,7},{2,4},{3,5},{4,2},{5,3},{6,0},{7,1},{8,14},{9,15},{10,... | collective-permute-start | bytes 786440 | tf_op jit(solution)/shard_map/ppermute | solution.py:52
  62.6 2.7 %collective-permute-start.13 = (bf16[4096,128]{1,0:T(8,128)(2,1)S(1)}, bf16[4096,128]{1,0:T(8,128)(2,1)S(1)}, u32[]{:S(2)}, u32[]{:S(2)}) collective-permute-start(bf16[4096,128]{1,0:T(8,128)(2,1)S(1)} %constant_dynamic-update-slice_fusion.own_ref), channel_id=1, source_target_pairs={{0,1},{1,0},{2,3},{3,2},{4,5},{5,4},{6,7},{7,6},{8,9},{9,8},{10,11... | collective-permute-start | bytes 3145736 | tf_op jit(solution)/shard_map/ppermute | solution.py:52

commit v3 on v2

--- a/solution.py
+++ b/solution.py
@@ -17,6 +17,10 @@
     return pl.BlockSpec(memory_space=pltpu.VMEM)
 
 
+def in_hbm(value):
+    return pltpu.with_memory_space_constraint(value, pltpu.HBM)
+
+
 def scalars():
     return pl.BlockSpec(memory_space=pltpu.SMEM)
 
@@ -25,34 +29,42 @@
     def __init__(self, rows, cols, features, block):
         self.count = rows * cols
         self.cols = cols
-        self.plane_bits = cols.bit_length() - 1
-        self.plane = cols
-        self.rest = self.count // 2 // cols
-        assert self.plane * self.rest * 2 == self.count and self.count & (self.count - 1) == 0
+        self.steps = self.count.bit_length() - 2
+        assert 1 << (self.steps + 1) == self.count and self.steps >= 2
+        bits = list(range(1, self.steps + 1))
+        self.order = (bits[:-2] + [bits[-1], bits[-2]], [bits[-2]] + bits[:-2] + [bits[-1]])
         self.flat = features // self.count
         self.piece = min(self.flat, block)
         self.pieces = block // self.piece
-        self.per_slice = self.flat // self.piece
+        per_slice = self.flat // self.piece
+        self.slice_bits = per_slice.bit_length() - 1
+        assert 1 << self.slice_bits == per_slice and self.piece * self.pieces == block
 
     def me(self):
         return lax.axis_index("row") * self.cols + lax.axis_index("col")
 
     def start(self, me, feature_block, piece):
         unit = feature_block * self.pieces + piece
-        owner = unit // self.per_slice if self.per_slice > 1 else unit
-        inside = unit - owner * self.per_slice
+        owner = unit >> self.slice_bits
+        inside = unit & ((1 << self.slice_bits) - 1)
         apart = owner ^ me
-        core = apart & 1
-        plane = (apart >> 1) & (self.plane - 1)
-        rest = apart >> (1 + self.plane_bits)
-        at = (core * self.plane + plane) * self.rest + rest
-        return pl.multiple_of(at * self.flat + inside * self.piece, self.piece)
-
-    def swap(self, value, mask):
-        return lax.ppermute(value, AXES, [(d, d ^ mask) for d in range(self.count)])
-
-
-def sum_kernel(plan, rows_ref, counts_ref, blocks_ref, sketch_ref, total_ref, send_ref, tiles_ref, docs_ref, sems):
+        places = []
+        for order in self.order:
+            place = apart & 1
+            for bit in order:
+                place = (place << 1) | ((apart >> bit) & 1)
+            places.append(place)
+        place = jnp.where((owner & 1) == 0, places[0], places[1])
+        return pl.multiple_of(place * self.flat + inside * self.piece, self.piece)
+
+    def swap(self, value, step):
+        return lax.ppermute(value, AXES, [(d, d ^ (1 << self.order[d & 1][step])) for d in range(self.count)])
+
+    def swap_cores(self, value):
+        return lax.ppermute(value, AXES, [(d, d ^ 1) for d in range(self.count)])
+
+
+def sum_kernel(plan, rows_ref, counts_ref, blocks_ref, sketch_ref, keep_ref, send_ref, total_ref, tiles_ref, docs_ref, sems):
     me = plan.me()
     documents, slots, block, _ = tiles_ref.shape
     half = send_ref.shape[0]
@@ -81,6 +93,7 @@
                 for p in range(plan.pieces):
                     at = pl.ds(plan.start(me, rows_ref[s, d], p), plan.piece)
                     total_ref[at, :] += term[p * plan.piece : (p + 1) * plan.piece]
+    keep_ref[...] = total_ref[:half, :]
     send_ref[...] = total_ref[half:, :].astype(BF16)
 
 
@@ -208,7 +221,7 @@
     columns = sketch.shape[1]
     features = weights.shape[0]
     half = features // 2
-    flat, plane, rest = plan.flat, plan.plane, plan.rest
+    flat = plan.flat
     params = pltpu.CompilerParams(vmem_limit_bytes=VMEM_BYTES)
     shape = jax.ShapeDtypeStruct
 
@@ -216,32 +229,25 @@
     parts = min(4, documents)
     keep, send = pl.pallas_call(
         functools.partial(sum_kernel, plan),
-        out_shape=(shape((features, columns), F32), shape((half, columns), BF16)),
+        out_shape=(pltpu.VMEM((half, columns), F32), pltpu.VMEM((half, columns), BF16)),
         in_specs=[scalars(), scalars(), pl.BlockSpec(memory_space=pltpu.HBM), pl.BlockSpec(memory_space=pltpu.HBM)],
         out_specs=(whole(), whole()),
         scratch_shapes=[
+            pltpu.VMEM((features, columns), F32),
             pltpu.VMEM(blocks.shape, BF16),
             pltpu.VMEM(sketch.shape, BF16),
             pltpu.SemaphoreType.DMA((parts, 2)),
         ],
-        compiler_params=params,
+        compiler_params=pltpu.CompilerParams(vmem_limit_bytes=VMEM_BYTES),
         name="local_sum",
-    )(rows, counts, blocks, sketch)
-    keep = keep[:half]
-
-    got = plan.swap(send, 1)
-    keep = keep.reshape(plane, rest * flat, columns)
-    got = got.reshape(plane, rest * flat, columns)
-    sent = [plan.swap((keep[p] + got[p].astype(F32)).astype(BF16), p << 1) for p in range(1, plane)]
-    held = keep[0] + got[0].astype(F32)
-    for part in sent:
-        held = held + part.astype(F32)
-    held = held.reshape(rest, flat, columns)
-    step = 1 + plan.plane_bits
-    sent = [plan.swap(held[q].astype(BF16), q << step) for q in range(1, rest)]
-    mine = held[0]
-    for part in sent:
-        mine = mine + part.astype(F32)
+    )(in_hbm(rows), in_hbm(counts), in_hbm(blocks), in_hbm(sketch))
+    got = plan.swap_cores(send)
+    for k in range(plan.steps):
+        held = keep + got.astype(F32)
+        middle = held.shape[0] // 2
+        keep = held[:middle]
+        got = plan.swap(held[middle:].astype(BF16), k)
+    mine = keep + got.astype(F32)
     mine = mine * lax.dynamic_slice_in_dim(weights, plan.me() * flat, flat)[:, None]
 
     tiles_shape = shape((documents, block, slots * block), BF16)
@@ -255,10 +261,10 @@
         name="tiles",
     )(rows, counts, blocks, weights.reshape(features // block, block))
 
-    rounded = mine.astype(BF16)
-    near = jnp.concatenate([rounded] + [plan.swap(rounded, q << step) for q in range(1, rest)], axis=0)
-    own = jnp.concatenate([near] + [plan.swap(near, p << 1) for p in range(1, plane)], axis=0)
-    other = plan.swap(own, 1)
+    own = mine.astype(BF16)
+    for k in reversed(range(plan.steps)):
+        own = jnp.concatenate([own, plan.swap(own, k)], axis=0)
+    other = plan.swap_cores(own)
 
     return pl.pallas_call(
         functools.partial(last_kernel, plan, features),

time: 86.8 us -> 88.6 us (1.021)
  starting transfers between devices: 17.5 us -> 24.3 us
  local copies, waits for them, and re-layouts: 4.03 us -> 0.33 us
  waiting for transfers between devices: 33.3 us -> 36.9 us
  other arithmetic: 2.99 us -> 0.54 us
  Pallas kernels: 27.9 us -> 25.6 us
    ppermute x14 -> x10, starting transfers between devices: 17.5 us -> 24.3 us  [the longest x8 23.7 us: swap(): lax.ppermute(value, AXES, [(d, d ^ 1 << self.order[d & 1][step]) for d in...]
    unnamed x21 -> x11, local copies, waits for them, and re-layouts: 3.9 us -> 0.08 us
    ppermute x14 -> x10, waiting for transfers between devices: 33.3 us -> 36.9 us  [the longest x8 33.3 us: swap(): lax.ppermute(value, AXES, [(d, d ^ 1 << self.order[d & 1][step]) for d in...]
    pallas_call x1, Pallas kernels: 5.39 us -> 3.13 us  [body(): pl.pallas_call(functools.partial(sum_kernel, plan), out_shape=(pltpu.VMEM...]
    convert_element_type x1 -> x0, other arithmetic: 1.66 us -> none  [body(): (keep[p] + got[p].astype(F32)).astype(BF16)]
    another operation x1 -> x0, other arithmetic: 1.21 us -> none  [run(): jax.shard_map(functools.partial(body, plan), mesh=mesh, in_specs=placed,...]
  transfers between devices with their start and end apart: 14 -> 10, of which waited for: 12 -> 10; matrix products, arithmetic and copies ran while one was open for 0% -> 0% of each run, Pallas kernels for 2% -> 1%
where the time goes in v3:
time: 88.6 us; the launch traced here: 88.5 us
  waiting for transfers between devices  36.9 us (42%)
  Pallas kernels  25.6 us (29%)
  starting transfers between devices  24.3 us (27%)
    ppermute x8, waiting for transfers between devices, swap(): lax.ppermute(value, AXES, [(d, d ^ 1 << self.order[d & 1][step]) for d in...  33.3 us
    ppermute x8, starting transfers between devices, swap(): lax.ppermute(value, AXES, [(d, d ^ 1 << self.order[d & 1][step]) for d in...  23.7 us
    pallas_call x1, Pallas kernels, body(): pl.pallas_call(functools.partial(last_kernel, plan, features), out_shape=...  21.2 us
    ppermute x2, waiting for transfers between devices, swap_cores(): return lax.ppermute(value, AXES, [(d, d ^ 1) for d in range(self.count)])  3.59 us
    pallas_call x1, Pallas kernels, body(): pl.pallas_call(functools.partial(sum_kernel, plan), out_shape=(pltpu.VMEM...  3.13 us
  transfers between devices with their start and end apart: 10, of which 10 were waited for; matrix products, arithmetic and copies ran while one was open for 0% of the time, Pallas kernels for 1%

profile of v3, /device:TPU:0, one launch (start us, length us, event | category | flops | bytes accessed | tf_op | source)
XLA Modules:
  0.0 88.5 jit_solution(16517974633069011723)
XLA Ops:
  0.6 3.1 %local_sum.1 = (f32[4096,128]{1,0:T(8,128)S(1)}, bf16[4096,128]{1,0:T(8,128)(2,1)S(1)}) custom-call(s32[3,16]{1,0:T(4,128)} %bitcast.3, s32[16]{0:T(128)} %counts_ref.3, bf16[16,3,128,128]{3,2,1,0:T(8,128)(2,1)} %blocks_ref.3, bf16[2048,128]{1,0:T(8,128)(2,1)} %sketch_ref.1), custom_call_target="tpu_custom_call" | custom-call | tf_op jit(solution)/shard_map/local_sum/pallas_call | solution.py:230
  3.8 0.5 collective-permute-start
  4.3 2.3 %collective-permute-done = bf16[4096,128]{1,0:T(8,128)(2,1)S(1)} collective-permute-done((bf16[4096,128]{1,0:T(8,128)(2,1)S(1)}, bf16[4096,128]{1,0:T(8,128)(2,1)S(1)}, u32[]{:S(2)}, u32[]{:S(2)}) %collective-permute-start) | collective-permute-done | bytes 1048608 | tf_op jit(solution)/shard_map/ppermute | solution.py:64
  6.6 0.2 convert_add_fusion
  6.8 2.9 %collective-permute-start.1 = (bf16[2048,128]{1,0:T(8,128)(2,1)S(1)}, bf16[2048,128]{1,0:T(8,128)(2,1)S(1)}, u32[]{:S(2)}, u32[]{:S(2)}) collective-permute-start(bf16[2048,128]{1,0:T(8,128)(2,1)S(1)} %slice.54), channel_id=1, source_target_pairs={{0,2},{1,9},{2,0},{3,11},{4,6},{5,13},{6,4},{7,15},{8,10},{9,1},{1... | collective-permute-start | bytes 1572872 | tf_op jit(solution)/shard_map/ppermute | solution.py:61
  9.7 7.2 %collective-permute-done.1 = bf16[2048,128]{1,0:T(8,128)(2,1)S(1)} collective-permute-done((bf16[2048,128]{1,0:T(8,128)(2,1)S(1)}, bf16[2048,128]{1,0:T(8,128)(2,1)S(1)}, u32[]{:S(2)}, u32[]{:S(2)}) %collective-permute-start.1) | collective-permute-done | bytes 524320 | tf_op jit(solution)/shard_map/ppermute | solution.py:61
  16.9 0.1 slice_add_fusion
  17.1 2.1 %collective-permute-start.2 = (bf16[1024,128]{1,0:T(8,128)(2,1)S(1)}, bf16[1024,128]{1,0:T(8,128)(2,1)S(1)}, u32[]{:S(2)}, u32[]{:S(2)}) collective-permute-start(bf16[1024,128]{1,0:T(8,128)(2,1)S(1)} %slice.55), channel_id=1, source_target_pairs={{0,4},{1,3},{2,6},{3,1},{4,0},{5,7},{6,2},{7,5},{8,12},{9,11},{10,... | collective-permute-start | bytes 786440 | tf_op jit(solution)/shard_map/ppermute | solution.py:61
  19.2 4.4 %collective-permute-done.2 = bf16[1024,128]{1,0:T(8,128)(2,1)S(1)} collective-permute-done((bf16[1024,128]{1,0:T(8,128)(2,1)S(1)}, bf16[1024,128]{1,0:T(8,128)(2,1)S(1)}, u32[]{:S(2)}, u32[]{:S(2)}) %collective-permute-start.2) | collective-permute-done | bytes 262176 | tf_op jit(solution)/shard_map/ppermute | solution.py:61
  23.6 3.2 %collective-permute-start.3 = (bf16[512,128]{1,0:T(8,128)(2,1)S(1)}, bf16[512,128]{1,0:T(8,128)(2,1)S(1)}, u32[]{:S(2)}, u32[]{:S(2)}) collective-permute-start(bf16[512,128]{1,0:T(8,128)(2,1)S(1)} %slice.56), channel_id=1, source_target_pairs={{0,16},{1,5},{2,18},{3,7},{4,20},{5,1},{6,22},{7,3},{8,24},{9,13},... | collective-permute-start | bytes 393224 | tf_op jit(solution)/shard_map/ppermute | solution.py:61
  26.8 3.0 %collective-permute-done.3 = bf16[512,128]{1,0:T(8,128)(2,1)S(1)} collective-permute-done((bf16[512,128]{1,0:T(8,128)(2,1)S(1)}, bf16[512,128]{1,0:T(8,128)(2,1)S(1)}, u32[]{:S(2)}, u32[]{:S(2)}) %collective-permute-start.3) | collective-permute-done | bytes 131104 | tf_op jit(solution)/shard_map/ppermute | solution.py:61
  29.8 3.9 %collective-permute-start.4 = (bf16[256,128]{1,0:T(8,128)(2,1)S(1)}, bf16[256,128]{1,0:T(8,128)(2,1)S(1)}, u32[]{:S(2)}, u32[]{:S(2)}) collective-permute-start(bf16[256,128]{1,0:T(8,128)(2,1)S(1)} %slice.57), channel_id=1, source_target_pairs={{0,8},{1,17},{2,10},{3,19},{4,12},{5,21},{6,14},{7,23},{8,0},{9,25... | collective-permute-start | bytes 196616 | tf_op jit(solution)/shard_map/ppermute | solution.py:61
  33.7 2.2 %collective-permute-done.4 = bf16[256,128]{1,0:T(8,128)(2,1)S(1)} collective-permute-done((bf16[256,128]{1,0:T(8,128)(2,1)S(1)}, bf16[256,128]{1,0:T(8,128)(2,1)S(1)}, u32[]{:S(2)}, u32[]{:S(2)}) %collective-permute-start.4) | collective-permute-done | bytes 65568 | tf_op jit(solution)/shard_map/ppermute | solution.py:61
  36.0 2.1 %collective-permute-start.5 = (bf16[256,128]{1,0:T(8,128)(2,1)S(1)}, bf16[256,128]{1,0:T(8,128)(2,1)S(1)}, u32[]{:S(2)}, u32[]{:S(2)}) collective-permute-start(bf16[256,128]{1,0:T(8,128)(2,1)S(1)} %get-tuple-element.11), channel_id=1, source_target_pairs={{0,8},{1,17},{2,10},{3,19},{4,12},{5,21},{6,14},{7,23},{8,0},{9,25... | collective-permute-start | bytes 196616 | tf_op jit(solution)/shard_map/ppermute | solution.py:61
  38.1 2.2 %collective-permute-done.5 = bf16[256,128]{1,0:T(8,128)(2,1)S(1)} collective-permute-done((bf16[256,128]{1,0:T(8,128)(2,1)S(1)}, bf16[256,128]{1,0:T(8,128)(2,1)S(1)}, u32[]{:S(2)}, u32[]{:S(2)}) %collective-permute-start.5) | collective-permute-done | bytes 65568 | tf_op jit(solution)/shard_map/ppermute | solution.py:61
  40.3 3.6 %collective-permute-start.6 = (bf16[512,128]{1,0:T(8,128)(2,1)S(1)}, bf16[512,128]{1,0:T(8,128)(2,1)S(1)}, u32[]{:S(2)}, u32[]{:S(2)}) collective-permute-start(bf16[512,128]{1,0:T(8,128)(2,1)S(1)} %pad_maximum_fusion.2), channel_id=1, source_target_pairs={{0,16},{1,5},{2,18},{3,7},{4,20},{5,1},{6,22},{7,3},{8,24},{9,13},... | collective-permute-start | bytes 393224 | tf_op jit(solution)/shard_map/ppermute | solution.py:61
  44.0 2.9 %collective-permute-done.6 = bf16[512,128]{1,0:T(8,128)(2,1)S(1)} collective-permute-done((bf16[512,128]{1,0:T(8,128)(2,1)S(1)}, bf16[512,128]{1,0:T(8,128)(2,1)S(1)}, u32[]{:S(2)}, u32[]{:S(2)}) %collective-permute-start.6) | collective-permute-done | bytes 131104 | tf_op jit(solution)/shard_map/ppermute | solution.py:61
  47.0 3.9 %collective-permute-start.7 = (bf16[1024,128]{1,0:T(8,128)(2,1)S(1)}, bf16[1024,128]{1,0:T(8,128)(2,1)S(1)}, u32[]{:S(2)}, u32[]{:S(2)}) collective-permute-start(bf16[1024,128]{1,0:T(8,128)(2,1)S(1)} %pad_maximum_fusion.1), channel_id=1, source_target_pairs={{0,4},{1,3},{2,6},{3,1},{4,0},{5,7},{6,2},{7,5},{8,12},{9,11},{10,... | collective-permute-start | bytes 786440 | tf_op jit(solution)/shard_map/ppermute | solution.py:61
  50.8 4.4 %collective-permute-done.7 = bf16[1024,128]{1,0:T(8,128)(2,1)S(1)} collective-permute-done((bf16[1024,128]{1,0:T(8,128)(2,1)S(1)}, bf16[1024,128]{1,0:T(8,128)(2,1)S(1)}, u32[]{:S(2)}, u32[]{:S(2)}) %collective-permute-start.7) | collective-permute-done | bytes 262176 | tf_op jit(solution)/shard_map/ppermute | solution.py:61
  55.2 2.1 %collective-permute-start.8 = (bf16[2048,128]{1,0:T(8,128)(2,1)S(1)}, bf16[2048,128]{1,0:T(8,128)(2,1)S(1)}, u32[]{:S(2)}, u32[]{:S(2)}) collective-permute-start(bf16[2048,128]{1,0:T(8,128)(2,1)S(1)} %pad_maximum_fusion), channel_id=1, source_target_pairs={{0,2},{1,9},{2,0},{3,11},{4,6},{5,13},{6,4},{7,15},{8,10},{9,1},{1... | collective-permute-start | bytes 1572872 | tf_op jit(solution)/shard_map/ppermute | solution.py:61
  57.3 7.1 %collective-permute-done.8 = bf16[2048,128]{1,0:T(8,128)(2,1)S(1)} collective-permute-done((bf16[2048,128]{1,0:T(8,128)(2,1)S(1)}, bf16[2048,128]{1,0:T(8,128)(2,1)S(1)}, u32[]{:S(2)}, u32[]{:S(2)}) %collective-permute-start.8) | collective-permute-done | bytes 524320 | tf_op jit(solution)/shard_map/ppermute | solution.py:61
  64.6 1.3 %tiles.1 = (bf16[16,128,384]{2,1,0:T(8,128)(2,1)S(1)}, bf16[16,128,384]{2,1,0:T(8,128)(2,1)S(1)}) custom-call(s32[3,16]{1,0:T(4,128)S(1)} %bitcast.4, s32[16]{0:T(128)S(1)} %copy-done.3, bf16[16,3,128,128]{3,2,1,0:T(8,128)(2,1)S(1)} %copy-done, f32[64,128]{1,0:T(8,128)S(1)} %bitcast.2), custom_call_target="tpu_custom_call" | custom-call | flops 1048576 | bytes 16777216 | tf_op jit(solution)/shard_map/tiles/pallas_call | solution.py:254
  65.9 1.3 %collective-permute-done.9.other_ref = bf16[4096,128]{1,0:T(8,128)(2,1)S(1)} collective-permute-done((bf16[4096,128]{1,0:T(8,128)(2,1)S(1)}, bf16[4096,128]{1,0:T(8,128)(2,1)S(1)}, u32[]{:S(2)}, u32[]{:S(2)}) %collective-permute-start.9) | collective-permute-done | bytes 1048608 | tf_op jit(solution)/shard_map/ppermute | solution.py:64
  67.2 21.2 %factors.1 = (f32[256,128]{1,0:T(8,128)}, bf16[2048,128]{1,0:T(8,128)(2,1)}) custom-call(s32[3,16]{1,0:T(4,128)S(1)} %bitcast.5, bf16[16,128,384]{2,1,0:T(8,128)(2,1)S(1)} %get-tuple-element.6.high_ref, bf16[16,128,384]{2,1,0:T(8,128)(2,1)S(1)} %get-tuple-element.7.low_ref, bf16[4096,128]{1,0:T(8,128)(2,1)S(1)} %constant_dynamic-update-slice_fusion.own_ref, ...), custom_call_target="tpu_custom_call" | custom-call | tf_op jit(solution)/shard_map/factors/pallas_call | solution.py:269
  (24 shorter events, 0.6 us)
Async XLA Ops:
  3.8 2.8 %collective-permute-start = (bf16[4096,128]{1,0:T(8,128)(2,1)S(1)}, bf16[4096,128]{1,0:T(8,128)(2,1)S(1)}, u32[]{:S(2)}, u32[]{:S(2)}) collective-permute-start(bf16[4096,128]{1,0:T(8,128)(2,1)S(1)} %get-tuple-element.9), channel_id=1, source_target_pairs={{0,1},{1,0},{2,3},{3,2},{4,5},{5,4},{6,7},{7,6},{8,9},{9,8},{10,11... | collective-permute-start | bytes 3145736 | tf_op jit(solution)/shard_map/ppermute | solution.py:64
  6.8 10.1 %collective-permute-start.1 = (bf16[2048,128]{1,0:T(8,128)(2,1)S(1)}, bf16[2048,128]{1,0:T(8,128)(2,1)S(1)}, u32[]{:S(2)}, u32[]{:S(2)}) collective-permute-start(bf16[2048,128]{1,0:T(8,128)(2,1)S(1)} %slice.54), channel_id=1, source_target_pairs={{0,2},{1,9},{2,0},{3,11},{4,6},{5,13},{6,4},{7,15},{8,10},{9,1},{1... | collective-permute-start | bytes 1572872 | tf_op jit(solution)/shard_map/ppermute | solution.py:61
  17.0 16.6 %copy-start.1 = (f32[8192]{0:T(1024)S(1)}, f32[8192]{0:T(1024)}, u32[]{:S(2)}) copy-start(f32[8192]{0:T(1024)} %param.9) | copy-start | bytes 98308
  17.1 6.5 %collective-permute-start.2 = (bf16[1024,128]{1,0:T(8,128)(2,1)S(1)}, bf16[1024,128]{1,0:T(8,128)(2,1)S(1)}, u32[]{:S(2)}, u32[]{:S(2)}) collective-permute-start(bf16[1024,128]{1,0:T(8,128)(2,1)S(1)} %slice.55), channel_id=1, source_target_pairs={{0,4},{1,3},{2,6},{3,1},{4,0},{5,7},{6,2},{7,5},{8,12},{9,11},{10,... | collective-permute-start | bytes 786440 | tf_op jit(solution)/shard_map/ppermute | solution.py:61
  23.6 6.1 %collective-permute-start.3 = (bf16[512,128]{1,0:T(8,128)(2,1)S(1)}, bf16[512,128]{1,0:T(8,128)(2,1)S(1)}, u32[]{:S(2)}, u32[]{:S(2)}) collective-permute-start(bf16[512,128]{1,0:T(8,128)(2,1)S(1)} %slice.56), channel_id=1, source_target_pairs={{0,16},{1,5},{2,18},{3,7},{4,20},{5,1},{6,22},{7,3},{8,24},{9,13},... | collective-permute-start | bytes 393224 | tf_op jit(solution)/shard_map/ppermute | solution.py:61
  29.8 6.1 %collective-permute-start.4 = (bf16[256,128]{1,0:T(8,128)(2,1)S(1)}, bf16[256,128]{1,0:T(8,128)(2,1)S(1)}, u32[]{:S(2)}, u32[]{:S(2)}) collective-permute-start(bf16[256,128]{1,0:T(8,128)(2,1)S(1)} %slice.57), channel_id=1, source_target_pairs={{0,8},{1,17},{2,10},{3,19},{4,12},{5,21},{6,14},{7,23},{8,0},{9,25... | collective-permute-start | bytes 196616 | tf_op jit(solution)/shard_map/ppermute | solution.py:61
  33.7 30.9 %copy-start = (bf16[16,3,128,128]{3,2,1,0:T(8,128)(2,1)S(1)}, bf16[16,3,128,128]{3,2,1,0:T(8,128)(2,1)}, u32[]{:S(2)}) copy-start(bf16[16,3,128,128]{3,2,1,0:T(8,128)(2,1)} %blocks_ref.3) | copy-start | bytes 4718596
  33.7 30.9 %copy-start.2 = (s32[16,3]{0,1:T(4,128)S(1)}, s32[16,3]{0,1:T(4,128)}, u32[]{:S(2)}) copy-start(s32[16,3]{0,1:T(4,128)} %param.6) | copy-start | bytes 580
  33.7 30.9 %copy-start.3 = (s32[16]{0:T(128)S(1)}, s32[16]{0:T(128)}, u32[]{:S(2)}) copy-start(s32[16]{0:T(128)} %counts_ref.3) | copy-start | bytes 196
  36.0 4.3 %collective-permute-start.5 = (bf16[256,128]{1,0:T(8,128)(2,1)S(1)}, bf16[256,128]{1,0:T(8,128)(2,1)S(1)}, u32[]{:S(2)}, u32[]{:S(2)}) collective-permute-start(bf16[256,128]{1,0:T(8,128)(2,1)S(1)} %get-tuple-element.11), channel_id=1, source_target_pairs={{0,8},{1,17},{2,10},{3,19},{4,12},{5,21},{6,14},{7,23},{8,0},{9,25... | collective-permute-start | bytes 196616 | tf_op jit(solution)/shard_map/ppermute | solution.py:61
  40.3 6.6 %collective-permute-start.6 = (bf16[512,128]{1,0:T(8,128)(2,1)S(1)}, bf16[512,128]{1,0:T(8,128)(2,1)S(1)}, u32[]{:S(2)}, u32[]{:S(2)}) collective-permute-start(bf16[512,128]{1,0:T(8,128)(2,1)S(1)} %pad_maximum_fusion.2), channel_id=1, source_target_pairs={{0,16},{1,5},{2,18},{3,7},{4,20},{5,1},{6,22},{7,3},{8,24},{9,13},... | collective-permute-start | bytes 393224 | tf_op jit(solution)/shard_map/ppermute | solution.py:61
  47.0 8.2 %collective-permute-start.7 = (bf16[1024,128]{1,0:T(8,128)(2,1)S(1)}, bf16[1024,128]{1,0:T(8,128)(2,1)S(1)}, u32[]{:S(2)}, u32[]{:S(2)}) collective-permute-start(bf16[1024,128]{1,0:T(8,128)(2,1)S(1)} %pad_maximum_fusion.1), channel_id=1, source_target_pairs={{0,4},{1,3},{2,6},{3,1},{4,0},{5,7},{6,2},{7,5},{8,12},{9,11},{10,... | collective-permute-start | bytes 786440 | tf_op jit(solution)/shard_map/ppermute | solution.py:61
  55.2 9.2 %collective-permute-start.8 = (bf16[2048,128]{1,0:T(8,128)(2,1)S(1)}, bf16[2048,128]{1,0:T(8,128)(2,1)S(1)}, u32[]{:S(2)}, u32[]{:S(2)}) collective-permute-start(bf16[2048,128]{1,0:T(8,128)(2,1)S(1)} %pad_maximum_fusion), channel_id=1, source_target_pairs={{0,2},{1,9},{2,0},{3,11},{4,6},{5,13},{6,4},{7,15},{8,10},{9,1},{1... | collective-permute-start | bytes 1572872 | tf_op jit(solution)/shard_map/ppermute | solution.py:61
  64.5 2.7 %collective-permute-start.9 = (bf16[4096,128]{1,0:T(8,128)(2,1)S(1)}, bf16[4096,128]{1,0:T(8,128)(2,1)S(1)}, u32[]{:S(2)}, u32[]{:S(2)}) collective-permute-start(bf16[4096,128]{1,0:T(8,128)(2,1)S(1)} %constant_dynamic-update-slice_fusion.own_ref), channel_id=1, source_target_pairs={{0,1},{1,0},{2,3},{3,2},{4,5},{5,4},{6,7},{7,6},{8,9},{9,8},{10,11... | collective-permute-start | bytes 3145736 | tf_op jit(solution)/shard_map/ppermute | solution.py:64

commit v4 on v3

--- a/solution.py
+++ b/solution.py
@@ -29,16 +29,26 @@
     def __init__(self, rows, cols, features, block):
         self.count = rows * cols
         self.cols = cols
-        self.steps = self.count.bit_length() - 2
-        assert 1 << (self.steps + 1) == self.count and self.steps >= 2
-        bits = list(range(1, self.steps + 1))
-        self.order = (bits[:-2] + [bits[-1], bits[-2]], [bits[-2]] + bits[:-2] + [bits[-1]])
+        self.plane = cols
+        self.line = rows // 2
+        self.plane_bits = cols.bit_length() - 1
+        assert self.plane * self.line * 2 == self.count and self.count & (self.count - 1) == 0
+        self.turned = (False, self.plane == self.line)
         self.flat = features // self.count
         self.piece = min(self.flat, block)
         self.pieces = block // self.piece
         per_slice = self.flat // self.piece
         self.slice_bits = per_slice.bit_length() - 1
         assert 1 << self.slice_bits == per_slice and self.piece * self.pieces == block
+        planes, lines = [], []
+        for core in (0, 1):
+            first = [[(z * self.plane + p) * 2 + core for p in range(self.plane)] for z in range(self.line)]
+            second = [[(z * self.plane + p) * 2 + core for z in range(self.line)] for p in range(self.plane)]
+            if self.turned[core]:
+                first, second = second, first
+            planes += first
+            lines += second
+        self.groups = (planes, lines)
 
     def me(self):
         return lax.axis_index("row") * self.cols + lax.axis_index("col")
@@ -47,18 +57,16 @@
         unit = feature_block * self.pieces + piece
         owner = unit >> self.slice_bits
         inside = unit & ((1 << self.slice_bits) - 1)
-        apart = owner ^ me
-        places = []
-        for order in self.order:
-            place = apart & 1
-            for bit in order:
-                place = (place << 1) | ((apart >> bit) & 1)
-            places.append(place)
-        place = jnp.where((owner & 1) == 0, places[0], places[1])
+        plane = (owner >> 1) & (self.plane - 1)
+        line = owner >> (1 + self.plane_bits)
+        place = plane * self.line + line
+        if self.turned[1]:
+            place = jnp.where((owner & 1) == 0, place, line * self.plane + plane)
+        place = place + ((owner ^ me) & 1) * (self.count // 2)
         return pl.multiple_of(place * self.flat + inside * self.piece, self.piece)
 
-    def swap(self, value, step):
-        return lax.ppermute(value, AXES, [(d, d ^ (1 << self.order[d & 1][step])) for d in range(self.count)])
+    def exchange(self, value, stage):
+        return lax.all_to_all(value, AXES, 0, 0, axis_index_groups=self.groups[stage], tiled=True)
 
     def swap_cores(self, value):
         return lax.ppermute(value, AXES, [(d, d ^ 1) for d in range(self.count)])
@@ -242,12 +250,12 @@
         name="local_sum",
     )(in_hbm(rows), in_hbm(counts), in_hbm(blocks), in_hbm(sketch))
     got = plan.swap_cores(send)
-    for k in range(plan.steps):
-        held = keep + got.astype(F32)
-        middle = held.shape[0] // 2
-        keep = held[:middle]
-        got = plan.swap(held[middle:].astype(BF16), k)
     mine = keep + got.astype(F32)
+    for stage, members in ((0, plan.plane), (1, plan.line)):
+        parts = plan.exchange(mine.astype(BF16).reshape(members, -1, columns), stage)
+        mine = parts[0].astype(F32)
+        for j in range(1, members):
+            mine = mine + parts[j].astype(F32)
     mine = mine * lax.dynamic_slice_in_dim(weights, plan.me() * flat, flat)[:, None]
 
     tiles_shape = shape((documents, block, slots * block), BF16)
@@ -262,8 +270,8 @@
     )(rows, counts, blocks, weights.reshape(features // block, block))
 
     own = mine.astype(BF16)
-    for k in reversed(range(plan.steps)):
-        own = jnp.concatenate([own, plan.swap(own, k)], axis=0)
+    for stage, members in ((1, plan.line), (0, plan.plane)):
+        own = plan.exchange(jnp.broadcast_to(own, (members,) + own.shape), stage).reshape(-1, columns)
     other = plan.swap_cores(own)
 
     return pl.pallas_call(

time: 88.6 us -> 84.7 us (0.956)
  blocking collectives: 0 us -> 37.7 us
  waiting for transfers between devices: 36.9 us -> 9.95 us
  starting transfers between devices: 24.3 us -> 8.94 us
    all_to_all x0 -> x3, blocking collectives: none -> 37.7 us  [exchange(): lax.all_to_all(value, AXES, 0, 0, axis_index_groups=self.groups[stage], t...]
    ppermute x8 -> x0, waiting for transfers between devices: 33.3 us -> none  [swap(): lax.ppermute(value, AXES, [(d, d ^ 1 << self.order[d & 1][step]) for d in...]
    ppermute x8 -> x0, starting transfers between devices: 23.7 us -> none  [swap(): lax.ppermute(value, AXES, [(d, d ^ 1 << self.order[d & 1][step]) for d in...]
    all_to_all x0 -> x1, waiting for transfers between devices: none -> 6.7 us  [exchange(): lax.all_to_all(value, AXES, 0, 0, axis_index_groups=self.groups[stage], t...]
    all_to_all x0 -> x1, starting transfers between devices: none -> 4.87 us  [exchange(): lax.all_to_all(value, AXES, 0, 0, axis_index_groups=self.groups[stage], t...]
    ppermute x2, starting transfers between devices: 0.59 us -> 4.07 us  [swap_cores(): return lax.ppermute(value, AXES, [(d, d ^ 1) for d in range(self.count)])]
  transfers between devices with their start and end apart: 10 -> 3, of which waited for: 10 -> 3; matrix products, arithmetic and copies ran while one was open for 0% -> 0% of each run, Pallas kernels for 1% -> 2%
where the time goes in v4:
time: 84.7 us; the launch traced here: 84.3 us
  blocking collectives  37.7 us (45%)
  Pallas kernels  25.6 us (30%)
  waiting for transfers between devices  9.95 us (12%)
  starting transfers between devices  8.94 us (11%)
  other arithmetic  1.15 us (1%)
    all_to_all x3, blocking collectives, exchange(): lax.all_to_all(value, AXES, 0, 0, axis_index_groups=self.groups[stage], t...  37.7 us
    pallas_call x1, Pallas kernels, body(): pl.pallas_call(functools.partial(last_kernel, plan, features), out_shape=...  21.2 us
    all_to_all x1, waiting for transfers between devices, exchange(): lax.all_to_all(value, AXES, 0, 0, axis_index_groups=self.groups[stage], t...  6.7 us
    all_to_all x1, starting transfers between devices, exchange(): lax.all_to_all(value, AXES, 0, 0, axis_index_groups=self.groups[stage], t...  4.87 us
    ppermute x2, starting transfers between devices, swap_cores(): return lax.ppermute(value, AXES, [(d, d ^ 1) for d in range(self.count)])  4.07 us
    ppermute x2, waiting for transfers between devices, swap_cores(): return lax.ppermute(value, AXES, [(d, d ^ 1) for d in range(self.count)])  3.25 us
    pallas_call x1, Pallas kernels, body(): pl.pallas_call(functools.partial(sum_kernel, plan), out_shape=(pltpu.VMEM...  3.13 us
  transfers between devices with their start and end apart: 3, of which 3 were waited for; matrix products, arithmetic and copies ran while one was open for 0% of the time, Pallas kernels for 2%

profile of v4, /device:TPU:0, one launch (start us, length us, event | category | flops | bytes accessed | tf_op | source)
XLA Modules:
  0.0 84.3 jit_solution(6131567335019520542)
XLA Ops:
  0.6 3.1 %local_sum.1 = (f32[4096,128]{1,0:T(8,128)S(1)}, bf16[4096,128]{1,0:T(8,128)(2,1)S(1)}) custom-call(s32[3,16]{1,0:T(4,128)} %bitcast.12, s32[16]{0:T(128)} %counts_ref.3, bf16[16,3,128,128]{3,2,1,0:T(8,128)(2,1)} %blocks_ref.3, bf16[2048,128]{1,0:T(8,128)(2,1)} %sketch_ref.1), custom_call_target="tpu_custom_call" | custom-call | tf_op jit(solution)/shard_map/local_sum/pallas_call | solution.py:238
  3.8 0.5 collective-permute-start
  4.3 2.3 %collective-permute-done = bf16[4096,128]{1,0:T(8,128)(2,1)S(1)} collective-permute-done((bf16[4096,128]{1,0:T(8,128)(2,1)S(1)}, bf16[4096,128]{1,0:T(8,128)(2,1)S(1)}, u32[]{:S(2)}, u32[]{:S(2)}) %collective-permute-start) | collective-permute-done | bytes 1048608 | tf_op jit(solution)/shard_map/ppermute | solution.py:72
  6.6 0.2 add_convert_fusion
  6.8 0.0 copy-start.1
  6.8 14.8 %all_to_all.20 = bf16[4,1024,128]{2,1,0:T(8,128)(2,1)S(1)} all-to-all(bf16[4,1024,128]{2,1,0:T(8,128)(2,1)S(1)} %bitcast.15), channel_id=1, replica_groups={{0,2,4,6},{8,10,12,14},{16,18,20,22},{24,26,28,30},{1,9,17,25},{3,11,19..., dimensions={0} | all-to-all | bytes 2097152 | tf_op jit(solution)/shard_map/all_to_all | solution.py:69
  21.6 0.8 add_convert_fusion.1
  22.5 4.9 %all-to-all-start.1 = ((bf16[4,256,128]{2,1,0:T(8,128)(2,1)}), bf16[4,256,128]{2,1,0:T(8,128)(2,1)S(1)}, u32[]{:S(2)}, u32[]{:S(2)}) async-start(bf16[4,256,128]{2,1,0:T(8,128)(2,1)} %bitcast.3), calls=%async_computation.1 | async-start | bytes 524288 | tf_op jit(solution)/shard_map/all_to_all | solution.py:69
  27.3 0.0 copy-done.1
  27.3 0.1 dynamic_slice.3
  27.4 6.7 %all-to-all-done.1 = bf16[4,256,128]{2,1,0:T(8,128)(2,1)S(1)} async-done(((bf16[4,256,128]{2,1,0:T(8,128)(2,1)}), bf16[4,256,128]{2,1,0:T(8,128)(2,1)S(1)}, u32[]{:S(2)}, u32[]{:S(2)}) %all-to-all-start.1) | async-done | bytes 262176 | tf_op jit(solution)/shard_map/all_to_all | solution.py:69
  34.1 0.1 fusion
  34.2 0.0 copy-start
  34.2 0.0 copy-start.2
  34.2 0.0 copy-start.3
  34.3 10.5 %all_to_all.21 = bf16[4,256,128]{2,1,0:T(8,128)(2,1)S(1)} all-to-all(bf16[4,256,128]{2,1,0:T(8,128)(2,1)S(1)} %broadcast_in_dim.7), channel_id=1, replica_groups={{0,8,16,24},{2,10,18,26},{4,12,20,28},{6,14,22,30},{1,3,5,7},{9,11,13,1..., dimensions={0} | all-to-all | bytes 524288 | tf_op jit(solution)/shard_map/all_to_all | solution.py:69
  44.8 0.1 broadcast_in_dim.8
  44.9 12.4 %all_to_all.22 = bf16[4,1024,128]{2,1,0:T(8,128)(2,1)S(1)} all-to-all(bf16[4,1024,128]{2,1,0:T(8,128)(2,1)S(1)} %broadcast_in_dim.8), channel_id=1, replica_groups={{0,2,4,6},{8,10,12,14},{16,18,20,22},{24,26,28,30},{1,9,17,25},{3,11,19..., dimensions={0} | all-to-all | bytes 2097152 | tf_op jit(solution)/shard_map/all_to_all | solution.py:69
  57.3 3.6 %collective-permute-start.1 = (bf16[4096,128]{1,0:T(8,128)(2,1)S(1)}, bf16[4096,128]{1,0:T(8,128)(2,1)S(1)}, u32[]{:S(2)}, u32[]{:S(2)}) collective-permute-start(bf16[4096,128]{1,0:T(8,128)(2,1)S(1)} %bitcast.9), channel_id=1, source_target_pairs={{0,1},{1,0},{2,3},{3,2},{4,5},{5,4},{6,7},{7,6},{8,9},{9,8},{10,11... | collective-permute-start | bytes 3145736 | tf_op jit(solution)/shard_map/ppermute | solution.py:72
  60.8 0.0 copy-done
  60.8 0.0 copy-done.2
  60.9 1.3 %tiles.1 = (bf16[16,128,384]{2,1,0:T(8,128)(2,1)S(1)}, bf16[16,128,384]{2,1,0:T(8,128)(2,1)S(1)}) custom-call(s32[3,16]{1,0:T(4,128)S(1)} %bitcast.13, s32[16]{0:T(128)S(1)} %copy-done.3, bf16[16,3,128,128]{3,2,1,0:T(8,128)(2,1)S(1)} %copy-done, f32[64,128]{1,0:T(8,128)S(1)} %bitcast.11), custom_call_target="tpu_custom_call" | custom-call | flops 1048576 | bytes 16777216 | tf_op jit(solution)/shard_map/tiles/pallas_call | solution.py:262
  62.2 1.0 %collective-permute-done.1.other_ref = bf16[4096,128]{1,0:T(8,128)(2,1)S(1)} collective-permute-done((bf16[4096,128]{1,0:T(8,128)(2,1)S(1)}, bf16[4096,128]{1,0:T(8,128)(2,1)S(1)}, u32[]{:S(2)}, u32[]{:S(2)}) %collective-permute-start.1) | collective-permute-done | bytes 1048608 | tf_op jit(solution)/shard_map/ppermute | solution.py:72
  63.1 21.2 %factors.1 = (f32[256,128]{1,0:T(8,128)}, bf16[2048,128]{1,0:T(8,128)(2,1)}) custom-call(s32[3,16]{1,0:T(4,128)S(1)} %bitcast.14, bf16[16,128,384]{2,1,0:T(8,128)(2,1)S(1)} %get-tuple-element.6.high_ref, bf16[16,128,384]{2,1,0:T(8,128)(2,1)S(1)} %get-tuple-element.7.low_ref, bf16[4096,128]{1,0:T(8,128)(2,1)S(1)} %bitcast.10, ...), custom_call_target="tpu_custom_call" | custom-call | tf_op jit(solution)/shard_map/factors/pallas_call | solution.py:277
  (2 shorter events, 0.0 us)
Async XLA Ops:
  3.8 2.8 %collective-permute-start = (bf16[4096,128]{1,0:T(8,128)(2,1)S(1)}, bf16[4096,128]{1,0:T(8,128)(2,1)S(1)}, u32[]{:S(2)}, u32[]{:S(2)}) collective-permute-start(bf16[4096,128]{1,0:T(8,128)(2,1)S(1)} %get-tuple-element.9), channel_id=1, source_target_pairs={{0,1},{1,0},{2,3},{3,2},{4,5},{5,4},{6,7},{7,6},{8,9},{9,8},{10,11... | collective-permute-start | bytes 3145736 | tf_op jit(solution)/shard_map/ppermute | solution.py:72
  6.8 20.5 %copy-start.1 = (f32[8192]{0:T(1024)S(1)}, f32[8192]{0:T(1024)}, u32[]{:S(2)}) copy-start(f32[8192]{0:T(1024)} %param.9) | copy-start | bytes 98308
  22.5 11.6 %all-to-all-start.1 = ((bf16[4,256,128]{2,1,0:T(8,128)(2,1)}), bf16[4,256,128]{2,1,0:T(8,128)(2,1)S(1)}, u32[]{:S(2)}, u32[]{:S(2)}) async-start(bf16[4,256,128]{2,1,0:T(8,128)(2,1)} %bitcast.3), calls=%async_computation.1 | async-start | bytes 524288 | tf_op jit(solution)/shard_map/all_to_all | solution.py:69
  34.2 26.6 %copy-start = (bf16[16,3,128,128]{3,2,1,0:T(8,128)(2,1)S(1)}, bf16[16,3,128,128]{3,2,1,0:T(8,128)(2,1)}, u32[]{:S(2)}) copy-start(bf16[16,3,128,128]{3,2,1,0:T(8,128)(2,1)} %blocks_ref.3) | copy-start | bytes 4718596
  34.2 26.6 %copy-start.2 = (s32[16,3]{0,1:T(4,128)S(1)}, s32[16,3]{0,1:T(4,128)}, u32[]{:S(2)}) copy-start(s32[16,3]{0,1:T(4,128)} %param.6) | copy-start | bytes 580
  34.2 26.6 %copy-start.3 = (s32[16]{0:T(128)S(1)}, s32[16]{0:T(128)}, u32[]{:S(2)}) copy-start(s32[16]{0:T(128)} %counts_ref.3) | copy-start | bytes 196
  57.3 5.8 %collective-permute-start.1 = (bf16[4096,128]{1,0:T(8,128)(2,1)S(1)}, bf16[4096,128]{1,0:T(8,128)(2,1)S(1)}, u32[]{:S(2)}, u32[]{:S(2)}) collective-permute-start(bf16[4096,128]{1,0:T(8,128)(2,1)S(1)} %bitcast.9), channel_id=1, source_target_pairs={{0,1},{1,0},{2,3},{3,2},{4,5},{5,4},{6,7},{7,6},{8,9},{9,8},{10,11... | collective-permute-start | bytes 3145736 | tf_op jit(solution)/shard_map/ppermute | solution.py:72

commit v5 on v3

--- a/solution.py
+++ b/solution.py
@@ -29,10 +29,10 @@
     def __init__(self, rows, cols, features, block):
         self.count = rows * cols
         self.cols = cols
-        self.steps = self.count.bit_length() - 2
-        assert 1 << (self.steps + 1) == self.count and self.steps >= 2
-        bits = list(range(1, self.steps + 1))
-        self.order = (bits[:-2] + [bits[-1], bits[-2]], [bits[-2]] + bits[:-2] + [bits[-1]])
+        self.plane = cols
+        self.line = rows // 2
+        self.plane_bits = cols.bit_length() - 1
+        assert self.plane * self.line * 2 == self.count and self.count & (self.count - 1) == 0
         self.flat = features // self.count
         self.piece = min(self.flat, block)
         self.pieces = block // self.piece
@@ -48,26 +48,28 @@
         owner = unit >> self.slice_bits
         inside = unit & ((1 << self.slice_bits) - 1)
         apart = owner ^ me
-        places = []
-        for order in self.order:
-            place = apart & 1
-            for bit in order:
-                place = (place << 1) | ((apart >> bit) & 1)
-            places.append(place)
-        place = jnp.where((owner & 1) == 0, places[0], places[1])
+        place = (apart & 1) * self.plane + ((apart >> 1) & (self.plane - 1))
+        place = place * self.line + (apart >> (1 + self.plane_bits))
         return pl.multiple_of(place * self.flat + inside * self.piece, self.piece)
 
-    def swap(self, value, step):
-        return lax.ppermute(value, AXES, [(d, d ^ (1 << self.order[d & 1][step])) for d in range(self.count)])
+    def swap(self, value, mask):
+        return lax.ppermute(value, AXES, [(d, d ^ mask) for d in range(self.count)])
 
     def swap_cores(self, value):
-        return lax.ppermute(value, AXES, [(d, d ^ 1) for d in range(self.count)])
-
-
-def sum_kernel(plan, rows_ref, counts_ref, blocks_ref, sketch_ref, keep_ref, send_ref, total_ref, tiles_ref, docs_ref, sems):
+        return self.swap(value, 1)
+
+    def swap_plane(self, value, member):
+        return self.swap(value, member << 1)
+
+    def swap_line(self, value, member):
+        return self.swap(value, member << (1 + self.plane_bits))
+
+
+def sum_kernel(plan, rows_ref, counts_ref, blocks_ref, sketch_ref, keep_ref, *rest):
+    send_refs, (total_ref, tiles_ref, docs_ref, sems) = rest[: plan.plane], rest[plan.plane :]
     me = plan.me()
     documents, slots, block, _ = tiles_ref.shape
-    half = send_ref.shape[0]
+    half = keep_ref.shape[0]
     parts = sems.shape[0]
     per = documents // parts
     copies = []
@@ -94,7 +96,9 @@
                     at = pl.ds(plan.start(me, rows_ref[s, d], p), plan.piece)
                     total_ref[at, :] += term[p * plan.piece : (p + 1) * plan.piece]
     keep_ref[...] = total_ref[:half, :]
-    send_ref[...] = total_ref[half:, :].astype(BF16)
+    for p, send_ref in enumerate(send_refs):
+        size = send_ref.shape[0]
+        send_ref[...] = total_ref[half + p * size : half + (p + 1) * size, :].astype(BF16)
 
 
 def tiles_kernel(rows_ref, counts_ref, blocks_ref, weights_ref, high_ref, low_ref):
@@ -163,7 +167,7 @@
     lax.fori_loop(0, size, step, 0)
 
 
-def invert_factor(gram, gram_ref, inverse_ref):
+def newton(gram, inverse_ref):
     size = gram.shape[0]
     line = lax.broadcasted_iota(jnp.int32, (size, size), 0)
     lane = lax.broadcasted_iota(jnp.int32, (size, size), 1)
@@ -175,36 +179,28 @@
     across = 1.0 / jnp.sqrt(jnp.sum(diagonal, axis=0, keepdims=True))
     beyond = gram * down * across - eye
     factor = eye - take * beyond
-    for product, product_t in ((dot1, dot_t1), (dot1, dot_t1), (dot3, dot_t3), (dot3, dot_t3)):
+    for product, product_t in ((dot1, dot_t1), (dot1, dot_t1), (dot3, dot_t3)):
         left = factor - eye + product(factor, beyond)
         residual = factor.T - eye + product_t(left, factor)
         factor = factor - product(take * residual, factor)
     inverse_ref[...] = factor * across
-    worst = jnp.max(jnp.sum(jnp.abs(residual), axis=1))
-
-    @pl.when(jnp.logical_not(worst < 1e-3))
-    def _():
-        gram_ref[...] = gram
-        eliminate(gram_ref, inverse_ref)
-
-
-def last_kernel(
-    plan, features, rows_ref, high_ref, low_ref, own_ref, other_ref, mine_ref, basis_ref, factors_ref, all_ref, gram_ref, inverse_ref
-):
+    return jnp.max(jnp.sum(jnp.abs(residual), axis=1))
+
+
+def last_kernel(plan, features, rows_ref, high_ref, low_ref, mine_ref, *rest):
+    parts, (basis_ref, factors_ref) = rest[: 2 * plan.plane], rest[2 * plan.plane : 2 * plan.plane + 2]
+    all_ref, product_ref, gram_ref, inverse_ref = rest[2 * plan.plane + 2 :]
     me = plan.me()
     documents, block, _ = high_ref.shape
-    half = own_ref.shape[0]
     slots = high_ref.shape[2] // block
     gram = jnp.zeros(gram_ref.shape, F32)
-    step = min(1024, half)
-    for base, ref in ((0, own_ref), (half, other_ref)):
-        for at in range(0, half, step):
-            part = ref[at : at + step, :]
-            all_ref[base + at : base + at + step, :] = part
-            gram += lax.dot_general(part, part, (((0,), (0,)), ((), ())), preferred_element_type=F32)
-    invert_factor(gram * (1.0 / features), gram_ref, inverse_ref)
-    inverse = inverse_ref[...]
-    basis_ref[...] = dot_t3(mine_ref[...], inverse)
+    for p, ref in enumerate(parts):
+        size = ref.shape[0]
+        part = ref[...]
+        all_ref[p * size : (p + 1) * size, :] = part
+        gram += lax.dot_general(part, part, (((0,), (0,)), ((), ())), preferred_element_type=F32)
+    gram = gram * (1.0 / features)
+    residual = newton(gram, inverse_ref)
     for d in range(documents):
         picked = []
         for s in range(slots):
@@ -212,8 +208,18 @@
                 at = pl.ds(plan.start(me, rows_ref[s, d], p), plan.piece)
                 picked.append(all_ref[at, :])
         picked = jnp.concatenate(picked, axis=0)
-        product = dot(high_ref[d], picked) + dot(low_ref[d], picked)
-        factors_ref[d * block : (d + 1) * block, :] = dot_t3(product, inverse).astype(BF16)
+        product_ref[d * block : (d + 1) * block, :] = dot(high_ref[d], picked) + dot(low_ref[d], picked)
+
+    @pl.when(jnp.logical_not(residual < 1.5e-2))
+    def _():
+        gram_ref[...] = gram
+        eliminate(gram_ref, inverse_ref)
+
+    inverse = inverse_ref[...]
+    basis_ref[...] = dot_t3(mine_ref[...], inverse)
+    size = min(512, documents * block)
+    for at in range(0, documents * block, size):
+        factors_ref[at : at + size, :] = dot_t3(product_ref[at : at + size, :], inverse).astype(BF16)
 
 
 def body(plan, blocks, rows, counts, sketch, weights):
@@ -221,34 +227,27 @@
     columns = sketch.shape[1]
     features = weights.shape[0]
     half = features // 2
+    chunk = half // plan.plane
     flat = plan.flat
     params = pltpu.CompilerParams(vmem_limit_bytes=VMEM_BYTES)
     shape = jax.ShapeDtypeStruct
-
     rows = rows.T
     parts = min(4, documents)
-    keep, send = pl.pallas_call(
+
+    keep, *send = pl.pallas_call(
         functools.partial(sum_kernel, plan),
-        out_shape=(pltpu.VMEM((half, columns), F32), pltpu.VMEM((half, columns), BF16)),
+        out_shape=(pltpu.VMEM((half, columns), F32),) + (pltpu.VMEM((chunk, columns), BF16),) * plan.plane,
         in_specs=[scalars(), scalars(), pl.BlockSpec(memory_space=pltpu.HBM), pl.BlockSpec(memory_space=pltpu.HBM)],
-        out_specs=(whole(), whole()),
+        out_specs=(whole(),) * (1 + plan.plane),
         scratch_shapes=[
             pltpu.VMEM((features, columns), F32),
             pltpu.VMEM(blocks.shape, BF16),
             pltpu.VMEM(sketch.shape, BF16),
             pltpu.SemaphoreType.DMA((parts, 2)),
         ],
-        compiler_params=pltpu.CompilerParams(vmem_limit_bytes=VMEM_BYTES),
+        compiler_params=params,
         name="local_sum",
     )(in_hbm(rows), in_hbm(counts), in_hbm(blocks), in_hbm(sketch))
-    got = plan.swap_cores(send)
-    for k in range(plan.steps):
-        held = keep + got.astype(F32)
-        middle = held.shape[0] // 2
-        keep = held[:middle]
-        got = plan.swap(held[middle:].astype(BF16), k)
-    mine = keep + got.astype(F32)
-    mine = mine * lax.dynamic_slice_in_dim(weights, plan.me() * flat, flat)[:, None]
 
     tiles_shape = shape((documents, block, slots * block), BF16)
     high, low = pl.pallas_call(
@@ -257,28 +256,45 @@
         in_specs=[scalars(), scalars(), whole(), whole()],
         out_specs=(whole(), whole()),
         compiler_params=params,
-        cost_estimate=pl.CostEstimate(flops=1 << 20, bytes_accessed=16 << 20, transcendentals=0),
+        cost_estimate=pl.CostEstimate(flops=1 << 20, bytes_accessed=4 << 20, transcendentals=0),
         name="tiles",
     )(rows, counts, blocks, weights.reshape(features // block, block))
 
-    own = mine.astype(BF16)
-    for k in reversed(range(plan.steps)):
-        own = jnp.concatenate([own, plan.swap(own, k)], axis=0)
-    other = plan.swap_cores(own)
+    order = list(range(1, plan.plane)) + [0]
+    got = {p: plan.swap_cores(send[p]) for p in order}
+    chip = {p: keep[p * chunk : (p + 1) * chunk] + got[p].astype(F32) for p in order}
+    sent = [plan.swap_plane(chip[p].astype(BF16), p) for p in order[:-1]]
+    sent, high, low = lax.optimization_barrier((sent, high, low))
+    held = chip[0]
+    for part in sent:
+        held = held + part.astype(F32)
+    held = held.reshape(plan.line, flat, columns)
+    far_first = sorted(range(1, plan.line), key=lambda q: (-(q & -2), q))
+    mine = held[0]
+    for part in [plan.swap_line(held[q].astype(BF16), q) for q in far_first]:
+        mine = mine + part.astype(F32)
+    mine = mine * lax.dynamic_slice_in_dim(weights, plan.me() * flat, flat)[:, None]
+
+    rounded = mine.astype(BF16)
+    line = {q: plan.swap_line(rounded, q) for q in far_first}
+    near = jnp.concatenate([rounded] + [line[q] for q in range(1, plan.line)], axis=0)
+    own = [near] + [plan.swap_plane(near, p) for p in range(1, plan.plane)]
+    other = [plan.swap_cores(part) for part in own]
 
     return pl.pallas_call(
         functools.partial(last_kernel, plan, features),
         out_shape=(shape((flat, columns), F32), shape((documents * block, columns), BF16)),
-        in_specs=[scalars()] + [whole()] * 5,
+        in_specs=[scalars()] + [whole()] * (3 + 2 * plan.plane),
         out_specs=(whole(), whole()),
         scratch_shapes=[
             pltpu.VMEM((features, columns), BF16),
+            pltpu.VMEM((documents * block, columns), F32),
             pltpu.VMEM((columns, columns), F32),
             pltpu.VMEM((columns, columns), F32),
         ],
         compiler_params=params,
         name="factors",
-    )(rows, high, low, own, other, mine)
+    )(rows, high, low, mine, *own, *other)
 
 
 def solution(mesh):

time: 88.6 us -> 78 us (0.88)
  starting transfers between devices: 24.3 us -> 18.2 us
  waiting for transfers between devices: 36.9 us -> 32.3 us
  other arithmetic: 0.54 us -> 2.17 us
  Pallas kernels: 25.6 us -> 24.2 us
    ppermute x10 -> x20, starting transfers between devices: 24.3 us -> 18.2 us  [swap(): return lax.ppermute(value, AXES, [(d, d ^ mask) for d in range(self.count)])]
    ppermute x10 -> x20, waiting for transfers between devices: 36.9 us -> 32.3 us  [swap(): return lax.ppermute(value, AXES, [(d, d ^ mask) for d in range(self.count)])]
    pallas_call x1, Pallas kernels: 21.2 us -> 19.8 us  [body(): pl.pallas_call(functools.partial(last_kernel, plan, features), out_shape=...]
    convert_element_type x0 -> x2, other arithmetic: none -> 1.2 us  [the longest x1 1.05 us: body(): rounded = mine.astype(BF16)]
    another operation x0 -> x1, other arithmetic: none -> 0.95 us  [run(): jax.shard_map(functools.partial(body, plan), mesh=mesh, in_specs=placed,...]
  transfers between devices with their start and end apart: 10 -> 20, of which waited for: 10 -> 14; matrix products, arithmetic and copies ran while one was open for 0% -> 0% of each run, Pallas kernels for 1% -> 2%
where the time goes in v5:
time: 78 us; the launch traced here: 77.8 us
  waiting for transfers between devices  32.3 us (41%)
  Pallas kernels  24.2 us (31%)
  starting transfers between devices  18.2 us (23%)
  other arithmetic  2.17 us (3%)
    ppermute x20, waiting for transfers between devices, swap(): return lax.ppermute(value, AXES, [(d, d ^ mask) for d in range(self.count)])  32.3 us
    pallas_call x1, Pallas kernels, body(): pl.pallas_call(functools.partial(last_kernel, plan, features), out_shape=...  19.8 us
    ppermute x20, starting transfers between devices, swap(): return lax.ppermute(value, AXES, [(d, d ^ mask) for d in range(self.count)])  18.2 us
    pallas_call x1, Pallas kernels, body(): pl.pallas_call(functools.partial(sum_kernel, plan), out_shape=(pltpu.VMEM...  3.12 us
  transfers between devices with their start and end apart: 20, of which 14 were waited for; matrix products, arithmetic and copies ran while one was open for 0% of the time, Pallas kernels for 2%

profile of v5, /device:TPU:0, one launch (start us, length us, event | category | flops | bytes accessed | tf_op | source)
XLA Modules:
  0.0 77.8 jit_solution(13950249586760274631)
XLA Ops:
  0.6 3.1 %local_sum.1 = (f32[4096,128]{1,0:T(8,128)S(1)}, bf16[1024,128]{1,0:T(8,128)(2,1)S(1)}, bf16[1024,128]{1,0:T(8,128)(2,1)S(1)}, bf16[1024,128]{1,0:T(8,128)(2,1)S(1)}, bf16[1024,128]{1,0:T(8,128)(2,1)S(1)}) custom-call(s32[3,16]{1,0:T(4,128)} %bitcast.3, s32[16]{0:T(128)} %counts_ref.3, bf16[16,3,128,128]{3,2,1,0:T(8,128)(2,1)} %blocks_ref.3, ...), custom_call_target="tpu_custom_call" | custom-call | tf_op jit(solution)/shard_map/local_sum/pallas_call | solution.py:237
  4.9 0.7 collective-permute-done
  6.4 2.9 %collective-permute-start.1 = (bf16[1024,128]{1,0:T(8,128)(2,1)S(1)}, bf16[1024,128]{1,0:T(8,128)(2,1)S(1)}, u32[]{:S(2)}, u32[]{:S(2)}) collective-permute-start(bf16[1024,128]{1,0:T(8,128)(2,1)S(1)} %get-tuple-element.32), channel_id=1, source_target_pairs={{0,2},{1,3},{2,0},{3,1},{4,6},{5,7},{6,4},{7,5},{8,10},{9,11},{10,... | collective-permute-start | bytes 786440 | tf_op jit(solution)/shard_map/ppermute | solution.py:56
  9.3 1.5 %collective-permute-start.3 = (bf16[1024,128]{1,0:T(8,128)(2,1)S(1)}, bf16[1024,128]{1,0:T(8,128)(2,1)S(1)}, u32[]{:S(2)}, u32[]{:S(2)}) collective-permute-start(bf16[1024,128]{1,0:T(8,128)(2,1)S(1)} %get-tuple-element.31), channel_id=1, source_target_pairs={{0,4},{1,5},{2,6},{3,7},{4,0},{5,1},{6,2},{7,3},{8,12},{9,13},{10,... | collective-permute-start | bytes 786440 | tf_op jit(solution)/shard_map/ppermute | solution.py:56
  10.9 1.3 %tiles.1 = (bf16[16,128,384]{2,1,0:T(8,128)(2,1)S(1)}, bf16[16,128,384]{2,1,0:T(8,128)(2,1)S(1)}) custom-call(s32[3,16]{1,0:T(4,128)S(1)} %bitcast.4, s32[16]{0:T(128)S(1)} %copy-done.3, bf16[16,3,128,128]{3,2,1,0:T(8,128)(2,1)S(1)} %copy-done, f32[64,128]{1,0:T(8,128)S(1)} %bitcast.2), custom_call_target="tpu_custom_call" | custom-call | flops 1048576 | bytes 4194304 | tf_op jit(solution)/shard_map/tiles/pallas_call | solution.py:253
  12.2 4.2 %collective-permute-done.1 = bf16[1024,128]{1,0:T(8,128)(2,1)S(1)} collective-permute-done((bf16[1024,128]{1,0:T(8,128)(2,1)S(1)}, bf16[1024,128]{1,0:T(8,128)(2,1)S(1)}, u32[]{:S(2)}, u32[]{:S(2)}) %collective-permute-start.1) | collective-permute-done | bytes 262176 | tf_op jit(solution)/shard_map/ppermute | solution.py:56
  16.4 6.6 %collective-permute-done.3 = bf16[1024,128]{1,0:T(8,128)(2,1)S(1)} collective-permute-done((bf16[1024,128]{1,0:T(8,128)(2,1)S(1)}, bf16[1024,128]{1,0:T(8,128)(2,1)S(1)}, u32[]{:S(2)}, u32[]{:S(2)}) %collective-permute-start.3) | collective-permute-done | bytes 262176 | tf_op jit(solution)/shard_map/ppermute | solution.py:56
  23.0 1.0 %fusion.5 = (bf16[1024,128]{1,0:T(8,128)(2,1)S(1)}, f32[1024,128]{1,0:T(8,128)}) fusion(bf16[1024,128]{1,0:T(8,128)(2,1)S(1)} %collective-permute-done.5, bf16[1024,128]{1,0:T(8,128)(2,1)S(1)} %collective-permute-done.3, bf16[1024,128]{1,0:T(8,128)(2,1)S(1)} %collective-permute-done.1, bf16[1024,128]{1,0:T(8,128)(2,1)S(1)} %collective-permute-done.6, ...), kind=kLoop, calls=%fused_computation.10 | loop fusion | flops 1179648 | bytes 2359296 | tf_op jit(solution)/shard_map/convert.2 | solution.py:311
  24.0 2.6 %collective-permute-start.7 = (bf16[256,128]{1,0:T(8,128)(2,1)S(1)}, bf16[256,128]{1,0:T(8,128)(2,1)S(1)}, u32[]{:S(2)}, u32[]{:S(2)}) collective-permute-start(bf16[256,128]{1,0:T(8,128)(2,1)S(1)} %get-tuple-element.33), channel_id=1, source_target_pairs={{0,16},{1,17},{2,18},{3,19},{4,20},{5,21},{6,22},{7,23},{8,24},{9,... | collective-permute-start | bytes 196616 | tf_op jit(solution)/shard_map/ppermute | solution.py:56
  26.6 1.3 %collective-permute-start.8 = (bf16[256,128]{1,0:T(8,128)(2,1)S(1)}, bf16[256,128]{1,0:T(8,128)(2,1)S(1)}, u32[]{:S(2)}, u32[]{:S(2)}) collective-permute-start(bf16[256,128]{1,0:T(8,128)(2,1)S(1)} %get-tuple-element.35), channel_id=1, source_target_pairs={{0,24},{1,25},{2,26},{3,27},{4,28},{5,29},{6,30},{7,31},{8,16},{9,... | collective-permute-start | bytes 196616 | tf_op jit(solution)/shard_map/ppermute | solution.py:56
  28.3 1.2 %collective-permute-done.7 = bf16[256,128]{1,0:T(8,128)(2,1)S(1)} collective-permute-done((bf16[256,128]{1,0:T(8,128)(2,1)S(1)}, bf16[256,128]{1,0:T(8,128)(2,1)S(1)}, u32[]{:S(2)}, u32[]{:S(2)}) %collective-permute-start.7) | collective-permute-done | bytes 65568 | tf_op jit(solution)/shard_map/ppermute | solution.py:56
  29.5 3.4 %collective-permute-done.8 = bf16[256,128]{1,0:T(8,128)(2,1)S(1)} collective-permute-done((bf16[256,128]{1,0:T(8,128)(2,1)S(1)}, bf16[256,128]{1,0:T(8,128)(2,1)S(1)}, u32[]{:S(2)}, u32[]{:S(2)}) %collective-permute-start.8) | collective-permute-done | bytes 65568 | tf_op jit(solution)/shard_map/ppermute | solution.py:56
  33.1 1.0 %fusion.3 = (bf16[256,128]{1,0:T(8,128)(2,1)S(1)}, f32[256,128]{1,0:T(8,128)S(1)}) fusion(f32[256]{0:T(256)S(1)} %dynamic_slice.3, bf16[256,128]{1,0:T(8,128)(2,1)} %collective-permute-done.9, bf16[256,128]{1,0:T(8,128)(2,1)S(1)} %collective-permute-done.8, bf16[256,128]{1,0:T(8,128)(2,1)S(1)} %collective-permute-done.7, f32[1024,128]{1,0:T(8,128)} %get-tuple-element.29), kind=kLoop, calls=%fused_computation.9 | loop fusion | flops 262144 | bytes 525312 | tf_op jit(solution)/shard_map/convert_element_type | solution.py:278
  34.2 2.8 %collective-permute-start.11 = (bf16[256,128]{1,0:T(8,128)(2,1)S(1)}, bf16[256,128]{1,0:T(8,128)(2,1)S(1)}, u32[]{:S(2)}, u32[]{:S(2)}) collective-permute-start(bf16[256,128]{1,0:T(8,128)(2,1)S(1)} %get-tuple-element.26), channel_id=1, source_target_pairs={{0,16},{1,17},{2,18},{3,19},{4,20},{5,21},{6,22},{7,23},{8,24},{9,... | collective-permute-start | bytes 196616 | tf_op jit(solution)/shard_map/ppermute | solution.py:56
  37.0 1.6 %collective-permute-start.12 = (bf16[256,128]{1,0:T(8,128)(2,1)S(1)}, bf16[256,128]{1,0:T(8,128)(2,1)S(1)}, u32[]{:S(2)}, u32[]{:S(2)}) collective-permute-start(bf16[256,128]{1,0:T(8,128)(2,1)S(1)} %get-tuple-element.26), channel_id=1, source_target_pairs={{0,24},{1,25},{2,26},{3,27},{4,28},{5,29},{6,30},{7,31},{8,16},{9,... | collective-permute-start | bytes 196616 | tf_op jit(solution)/shard_map/ppermute | solution.py:56
  38.6 3.1 %collective-permute-done.11 = bf16[256,128]{1,0:T(8,128)(2,1)S(1)} collective-permute-done((bf16[256,128]{1,0:T(8,128)(2,1)S(1)}, bf16[256,128]{1,0:T(8,128)(2,1)S(1)}, u32[]{:S(2)}, u32[]{:S(2)}) %collective-permute-start.11) | collective-permute-done | bytes 65568 | tf_op jit(solution)/shard_map/ppermute | solution.py:56
  41.7 1.5 %collective-permute-done.12 = bf16[256,128]{1,0:T(8,128)(2,1)S(1)} collective-permute-done((bf16[256,128]{1,0:T(8,128)(2,1)S(1)}, bf16[256,128]{1,0:T(8,128)(2,1)S(1)}, u32[]{:S(2)}, u32[]{:S(2)}) %collective-permute-start.12) | collective-permute-done | bytes 65568 | tf_op jit(solution)/shard_map/ppermute | solution.py:56
  43.2 1.4 %collective-permute-start.13 = (bf16[1024,128]{1,0:T(8,128)(2,1)S(1)}, bf16[1024,128]{1,0:T(8,128)(2,1)S(1)}, u32[]{:S(2)}, u32[]{:S(2)}) collective-permute-start(bf16[1024,128]{1,0:T(8,128)(2,1)S(1)} %pad_maximum_fusion.rest_0_), channel_id=1, source_target_pairs={{0,2},{1,3},{2,0},{3,1},{4,6},{5,7},{6,4},{7,5},{8,10},{9,11},{10,... | collective-permute-start | bytes 786440 | tf_op jit(solution)/shard_map/ppermute | solution.py:56
  44.6 0.6 collective-permute-start.14
  45.2 1.5 %collective-permute-start.15 = (bf16[1024,128]{1,0:T(8,128)(2,1)S(1)}, bf16[1024,128]{1,0:T(8,128)(2,1)S(1)}, u32[]{:S(2)}, u32[]{:S(2)}) collective-permute-start(bf16[1024,128]{1,0:T(8,128)(2,1)S(1)} %pad_maximum_fusion.rest_0_), channel_id=1, source_target_pairs={{0,6},{1,7},{2,4},{3,5},{4,2},{5,3},{6,0},{7,1},{8,14},{9,15},{10,... | collective-permute-start | bytes 786440 | tf_op jit(solution)/shard_map/ppermute | solution.py:56
  46.7 5.1 %collective-permute-done.13.rest_1_ = bf16[1024,128]{1,0:T(8,128)(2,1)S(1)} collective-permute-done((bf16[1024,128]{1,0:T(8,128)(2,1)S(1)}, bf16[1024,128]{1,0:T(8,128)(2,1)S(1)}, u32[]{:S(2)}, u32[]{:S(2)}) %collective-permute-start.13) | collective-permute-done | bytes 262176 | tf_op jit(solution)/shard_map/ppermute | solution.py:56
  51.9 4.3 %collective-permute-done.14.rest_2_ = bf16[1024,128]{1,0:T(8,128)(2,1)S(1)} collective-permute-done((bf16[1024,128]{1,0:T(8,128)(2,1)S(1)}, bf16[1024,128]{1,0:T(8,128)(2,1)S(1)}, u32[]{:S(2)}, u32[]{:S(2)}) %collective-permute-start.14) | collective-permute-done | bytes 262176 | tf_op jit(solution)/shard_map/ppermute | solution.py:56
  56.6 1.0 %collective-permute-done.18.rest_6_ = bf16[1024,128]{1,0:T(8,128)(2,1)S(1)} collective-permute-done((bf16[1024,128]{1,0:T(8,128)(2,1)S(1)}, bf16[1024,128]{1,0:T(8,128)(2,1)S(1)}, u32[]{:S(2)}, u32[]{:S(2)}) %collective-permute-start.18) | collective-permute-done | bytes 262176 | tf_op jit(solution)/shard_map/ppermute | solution.py:56
  58.0 19.8 %factors.1 = (f32[256,128]{1,0:T(8,128)}, bf16[2048,128]{1,0:T(8,128)(2,1)}) custom-call(s32[3,16]{1,0:T(4,128)S(1)} %bitcast.5, bf16[16,128,384]{2,1,0:T(8,128)(2,1)S(1)} %get-tuple-element.20.high_ref, bf16[16,128,384]{2,1,0:T(8,128)(2,1)S(1)} %get-tuple-element.21.low_ref, f32[256,128]{1,0:T(8,128)S(1)} %get-tuple-element.27.mine_ref, ...), custom_call_target="tpu_custom_call" | custom-call | tf_op jit(solution)/shard_map/factors/pallas_call | solution.py:284
  (33 shorter events, 3.6 us)
Async XLA Ops:
  3.8 7.1 %copy-start = (bf16[16,3,128,128]{3,2,1,0:T(8,128)(2,1)S(1)}, bf16[16,3,128,128]{3,2,1,0:T(8,128)(2,1)}, u32[]{:S(2)}) copy-start(bf16[16,3,128,128]{3,2,1,0:T(8,128)(2,1)} %blocks_ref.3) | copy-start | bytes 4718596
  3.8 7.1 %copy-start.1 = (f32[8192]{0:T(1024)S(1)}, f32[8192]{0:T(1024)}, u32[]{:S(2)}) copy-start(f32[8192]{0:T(1024)} %param.9) | copy-start | bytes 98308
  3.8 7.1 %copy-start.2 = (s32[16,3]{0,1:T(4,128)S(1)}, s32[16,3]{0,1:T(4,128)}, u32[]{:S(2)}) copy-start(s32[16,3]{0,1:T(4,128)} %param.6) | copy-start | bytes 580
  3.8 7.1 %copy-start.3 = (s32[16]{0:T(128)S(1)}, s32[16]{0:T(128)}, u32[]{:S(2)}) copy-start(s32[16]{0:T(128)} %counts_ref.3) | copy-start | bytes 196
  3.8 1.7 %collective-permute-start = (bf16[1024,128]{1,0:T(8,128)(2,1)S(1)}, bf16[1024,128]{1,0:T(8,128)(2,1)S(1)}, u32[]{:S(2)}, u32[]{:S(2)}) collective-permute-start(bf16[1024,128]{1,0:T(8,128)(2,1)S(1)} %get-tuple-element.15), channel_id=1, source_target_pairs={{0,1},{1,0},{2,3},{3,2},{4,5},{5,4},{6,7},{7,6},{8,9},{9,8},{10,11... | collective-permute-start | bytes 786440 | tf_op jit(solution)/shard_map/ppermute | solution.py:56
  4.3 1.5 %collective-permute-start.2 = (bf16[1024,128]{1,0:T(8,128)(2,1)S(1)}, bf16[1024,128]{1,0:T(8,128)(2,1)S(1)}, u32[]{:S(2)}, u32[]{:S(2)}) collective-permute-start(bf16[1024,128]{1,0:T(8,128)(2,1)S(1)} %get-tuple-element.16), channel_id=1, source_target_pairs={{0,1},{1,0},{2,3},{3,2},{4,5},{5,4},{6,7},{7,6},{8,9},{9,8},{10,11... | collective-permute-start | bytes 786440 | tf_op jit(solution)/shard_map/ppermute | solution.py:56
  4.4 1.8 %collective-permute-start.4 = (bf16[1024,128]{1,0:T(8,128)(2,1)S(1)}, bf16[1024,128]{1,0:T(8,128)(2,1)S(1)}, u32[]{:S(2)}, u32[]{:S(2)}) collective-permute-start(bf16[1024,128]{1,0:T(8,128)(2,1)S(1)} %get-tuple-element.17), channel_id=1, source_target_pairs={{0,1},{1,0},{2,3},{3,2},{4,5},{5,4},{6,7},{7,6},{8,9},{9,8},{10,11... | collective-permute-start | bytes 786440 | tf_op jit(solution)/shard_map/ppermute | solution.py:56
  6.4 10.0 %collective-permute-start.1 = (bf16[1024,128]{1,0:T(8,128)(2,1)S(1)}, bf16[1024,128]{1,0:T(8,128)(2,1)S(1)}, u32[]{:S(2)}, u32[]{:S(2)}) collective-permute-start(bf16[1024,128]{1,0:T(8,128)(2,1)S(1)} %get-tuple-element.32), channel_id=1, source_target_pairs={{0,2},{1,3},{2,0},{3,1},{4,6},{5,7},{6,4},{7,5},{8,10},{9,11},{10,... | collective-permute-start | bytes 786440 | tf_op jit(solution)/shard_map/ppermute | solution.py:56
  9.3 13.7 %collective-permute-start.3 = (bf16[1024,128]{1,0:T(8,128)(2,1)S(1)}, bf16[1024,128]{1,0:T(8,128)(2,1)S(1)}, u32[]{:S(2)}, u32[]{:S(2)}) collective-permute-start(bf16[1024,128]{1,0:T(8,128)(2,1)S(1)} %get-tuple-element.31), channel_id=1, source_target_pairs={{0,4},{1,5},{2,6},{3,7},{4,0},{5,1},{6,2},{7,3},{8,12},{9,13},{10,... | collective-permute-start | bytes 786440 | tf_op jit(solution)/shard_map/ppermute | solution.py:56
  10.8 12.2 %collective-permute-start.5 = (bf16[1024,128]{1,0:T(8,128)(2,1)S(1)}, bf16[1024,128]{1,0:T(8,128)(2,1)S(1)}, u32[]{:S(2)}, u32[]{:S(2)}) collective-permute-start(bf16[1024,128]{1,0:T(8,128)(2,1)S(1)} %get-tuple-element.30), channel_id=1, source_target_pairs={{0,6},{1,7},{2,4},{3,5},{4,2},{5,3},{6,0},{7,1},{8,14},{9,15},{10,... | collective-permute-start | bytes 786440 | tf_op jit(solution)/shard_map/ppermute | solution.py:56
  10.9 12.2 %collective-permute-start.6 = (bf16[1024,128]{1,0:T(8,128)(2,1)S(1)}, bf16[1024,128]{1,0:T(8,128)(2,1)S(1)}, u32[]{:S(2)}, u32[]{:S(2)}) collective-permute-start(bf16[1024,128]{1,0:T(8,128)(2,1)S(1)} %get-tuple-element.22), channel_id=1, source_target_pairs={{0,1},{1,0},{2,3},{3,2},{4,5},{5,4},{6,7},{7,6},{8,9},{9,8},{10,11... | collective-permute-start | bytes 786440 | tf_op jit(solution)/shard_map/ppermute | solution.py:56
  24.0 5.5 %collective-permute-start.7 = (bf16[256,128]{1,0:T(8,128)(2,1)S(1)}, bf16[256,128]{1,0:T(8,128)(2,1)S(1)}, u32[]{:S(2)}, u32[]{:S(2)}) collective-permute-start(bf16[256,128]{1,0:T(8,128)(2,1)S(1)} %get-tuple-element.33), channel_id=1, source_target_pairs={{0,16},{1,17},{2,18},{3,19},{4,20},{5,21},{6,22},{7,23},{8,24},{9,... | collective-permute-start | bytes 196616 | tf_op jit(solution)/shard_map/ppermute | solution.py:56
  26.6 6.2 %collective-permute-start.8 = (bf16[256,128]{1,0:T(8,128)(2,1)S(1)}, bf16[256,128]{1,0:T(8,128)(2,1)S(1)}, u32[]{:S(2)}, u32[]{:S(2)}) collective-permute-start(bf16[256,128]{1,0:T(8,128)(2,1)S(1)} %get-tuple-element.35), channel_id=1, source_target_pairs={{0,24},{1,25},{2,26},{3,27},{4,28},{5,29},{6,30},{7,31},{8,16},{9,... | collective-permute-start | bytes 196616 | tf_op jit(solution)/shard_map/ppermute | solution.py:56
  28.0 5.1 %collective-permute-start.9 = (bf16[256,128]{1,0:T(8,128)(2,1)S(1)}, bf16[256,128]{1,0:T(8,128)(2,1)}, u32[]{:S(2)}, u32[]{:S(2)}) collective-permute-start(bf16[256,128]{1,0:T(8,128)(2,1)S(1)} %get-tuple-element.34), channel_id=1, source_target_pairs={{0,8},{1,9},{2,10},{3,11},{4,12},{5,13},{6,14},{7,15},{8,0},{9,1},... | collective-permute-start | bytes 196616 | tf_op jit(solution)/shard_map/ppermute | solution.py:56
  34.1 4.5 %collective-permute-start.10 = (bf16[256,128]{1,0:T(8,128)(2,1)S(1)}, bf16[256,128]{1,0:T(8,128)(2,1)S(1)}, u32[]{:S(2)}, u32[]{:S(2)}) collective-permute-start(bf16[256,128]{1,0:T(8,128)(2,1)S(1)} %get-tuple-element.26), channel_id=1, source_target_pairs={{0,8},{1,9},{2,10},{3,11},{4,12},{5,13},{6,14},{7,15},{8,0},{9,1},... | collective-permute-start | bytes 196616 | tf_op jit(solution)/shard_map/ppermute | solution.py:56
  34.2 7.5 %collective-permute-start.11 = (bf16[256,128]{1,0:T(8,128)(2,1)S(1)}, bf16[256,128]{1,0:T(8,128)(2,1)S(1)}, u32[]{:S(2)}, u32[]{:S(2)}) collective-permute-start(bf16[256,128]{1,0:T(8,128)(2,1)S(1)} %get-tuple-element.26), channel_id=1, source_target_pairs={{0,16},{1,17},{2,18},{3,19},{4,20},{5,21},{6,22},{7,23},{8,24},{9,... | collective-permute-start | bytes 196616 | tf_op jit(solution)/shard_map/ppermute | solution.py:56
  37.0 6.2 %collective-permute-start.12 = (bf16[256,128]{1,0:T(8,128)(2,1)S(1)}, bf16[256,128]{1,0:T(8,128)(2,1)S(1)}, u32[]{:S(2)}, u32[]{:S(2)}) collective-permute-start(bf16[256,128]{1,0:T(8,128)(2,1)S(1)} %get-tuple-element.26), channel_id=1, source_target_pairs={{0,24},{1,25},{2,26},{3,27},{4,28},{5,29},{6,30},{7,31},{8,16},{9,... | collective-permute-start | bytes 196616 | tf_op jit(solution)/shard_map/ppermute | solution.py:56
  43.2 8.7 %collective-permute-start.13 = (bf16[1024,128]{1,0:T(8,128)(2,1)S(1)}, bf16[1024,128]{1,0:T(8,128)(2,1)S(1)}, u32[]{:S(2)}, u32[]{:S(2)}) collective-permute-start(bf16[1024,128]{1,0:T(8,128)(2,1)S(1)} %pad_maximum_fusion.rest_0_), channel_id=1, source_target_pairs={{0,2},{1,3},{2,0},{3,1},{4,6},{5,7},{6,4},{7,5},{8,10},{9,11},{10,... | collective-permute-start | bytes 786440 | tf_op jit(solution)/shard_map/ppermute | solution.py:56
  44.6 11.5 %collective-permute-start.14 = (bf16[1024,128]{1,0:T(8,128)(2,1)S(1)}, bf16[1024,128]{1,0:T(8,128)(2,1)S(1)}, u32[]{:S(2)}, u32[]{:S(2)}) collective-permute-start(bf16[1024,128]{1,0:T(8,128)(2,1)S(1)} %pad_maximum_fusion.rest_0_), channel_id=1, source_target_pairs={{0,4},{1,5},{2,6},{3,7},{4,0},{5,1},{6,2},{7,3},{8,12},{9,13},{10,... | collective-permute-start | bytes 786440 | tf_op jit(solution)/shard_map/ppermute | solution.py:56
  45.2 10.9 %collective-permute-start.15 = (bf16[1024,128]{1,0:T(8,128)(2,1)S(1)}, bf16[1024,128]{1,0:T(8,128)(2,1)S(1)}, u32[]{:S(2)}, u32[]{:S(2)}) collective-permute-start(bf16[1024,128]{1,0:T(8,128)(2,1)S(1)} %pad_maximum_fusion.rest_0_), channel_id=1, source_target_pairs={{0,6},{1,7},{2,4},{3,5},{4,2},{5,3},{6,0},{7,1},{8,14},{9,15},{10,... | collective-permute-start | bytes 786440 | tf_op jit(solution)/shard_map/ppermute | solution.py:56
  46.7 9.9 %collective-permute-start.16 = (bf16[1024,128]{1,0:T(8,128)(2,1)S(1)}, bf16[1024,128]{1,0:T(8,128)(2,1)S(1)}, u32[]{:S(2)}, u32[]{:S(2)}) collective-permute-start(bf16[1024,128]{1,0:T(8,128)(2,1)S(1)} %pad_maximum_fusion.rest_0_), channel_id=1, source_target_pairs={{0,1},{1,0},{2,3},{3,2},{4,5},{5,4},{6,7},{7,6},{8,9},{9,8},{10,11... | collective-permute-start | bytes 786440 | tf_op jit(solution)/shard_map/ppermute | solution.py:56
  51.9 4.8 %collective-permute-start.17 = (bf16[1024,128]{1,0:T(8,128)(2,1)S(1)}, bf16[1024,128]{1,0:T(8,128)(2,1)S(1)}, u32[]{:S(2)}, u32[]{:S(2)}) collective-permute-start(bf16[1024,128]{1,0:T(8,128)(2,1)S(1)} %collective-permute-done.13.rest_1_), channel_id=1, source_target_pairs={{0,1},{1,0},{2,3},{3,2},{4,5},{5,4},{6,7},{7,6},{8,9},{9,8},{10,11... | collective-permute-start | bytes 786440 | tf_op jit(solution)/shard_map/ppermute | solution.py:56
  56.1 1.5 %collective-permute-start.18 = (bf16[1024,128]{1,0:T(8,128)(2,1)S(1)}, bf16[1024,128]{1,0:T(8,128)(2,1)S(1)}, u32[]{:S(2)}, u32[]{:S(2)}) collective-permute-start(bf16[1024,128]{1,0:T(8,128)(2,1)S(1)} %collective-permute-done.14.rest_2_), channel_id=1, source_target_pairs={{0,1},{1,0},{2,3},{3,2},{4,5},{5,4},{6,7},{7,6},{8,9},{9,8},{10,11... | collective-permute-start | bytes 786440 | tf_op jit(solution)/shard_map/ppermute | solution.py:56
  56.1 1.9 %collective-permute-start.19 = (bf16[1024,128]{1,0:T(8,128)(2,1)S(1)}, bf16[1024,128]{1,0:T(8,128)(2,1)S(1)}, u32[]{:S(2)}, u32[]{:S(2)}) collective-permute-start(bf16[1024,128]{1,0:T(8,128)(2,1)S(1)} %collective-permute-done.15.rest_3_), channel_id=1, source_target_pairs={{0,1},{1,0},{2,3},{3,2},{4,5},{5,4},{6,7},{7,6},{8,9},{9,8},{10,11... | collective-permute-start | bytes 786440 | tf_op jit(solution)/shard_map/ppermute | solution.py:56

commit v6 on v5

--- a/solution.py
+++ b/solution.py
@@ -52,14 +52,14 @@
         place = place * self.line + (apart >> (1 + self.plane_bits))
         return pl.multiple_of(place * self.flat + inside * self.piece, self.piece)
 
-    def swap(self, value, mask):
-        return lax.ppermute(value, AXES, [(d, d ^ mask) for d in range(self.count)])
-
-    def swap_cores(self, value):
-        return self.swap(value, 1)
-
-    def swap_plane(self, value, member):
-        return self.swap(value, member << 1)
+    def core(self):
+        return lax.axis_index("col") & 1
+
+    def swap(self, value, mask, cores=(0, 1)):
+        return lax.ppermute(value, AXES, [(d, d ^ mask) for d in range(self.count) if d & 1 in cores])
+
+    def swap_plane(self, value, member, cores=(0, 1)):
+        return self.swap(value, member << 1, cores)
 
     def swap_line(self, value, member):
         return self.swap(value, member << (1 + self.plane_bits))
@@ -101,7 +101,7 @@
         send_ref[...] = total_ref[half + p * size : half + (p + 1) * size, :].astype(BF16)
 
 
-def tiles_kernel(rows_ref, counts_ref, blocks_ref, weights_ref, high_ref, low_ref):
+def tiles_kernel(plan, rows_ref, counts_ref, blocks_ref, weights_ref, high_ref, low_ref, scale_ref, turned_ref):
     documents, slots, block, _ = blocks_ref.shape
     for d in range(documents):
         for s in range(slots):
@@ -110,6 +110,44 @@
             high, low = split(blocks_ref[d, s].T.astype(F32) * scale)
             high_ref[d, :, s * block : (s + 1) * block] = high
             low_ref[d, :, s * block : (s + 1) * block] = low
+    unit = plan.me() << plan.slice_bits
+    lines = max(1, plan.flat // block)
+    first = unit if plan.pieces == 1 else unit // plan.pieces
+    for i in range(lines):
+        line = weights_ref[pl.ds(first + i, 1), :]
+        turned_ref[i * block : (i + 1) * block, :] = jnp.broadcast_to(line, (block, block)).T
+    inside = 0 if plan.pieces == 1 else lax.rem(unit, plan.pieces) * plan.piece
+    scale_ref[...] = turned_ref[pl.ds(pl.multiple_of(inside, plan.piece), plan.flat), :]
+
+
+def plane_kernel(plan, keep_ref, *rest):
+    steps = plan.plane
+    parts = (rest[:steps], rest[steps : 2 * steps])
+    held_ref, *send_refs = rest[2 * steps :]
+    flat = plan.flat
+    for core, refs in enumerate(parts):
+
+        @pl.when(plan.core() == core)
+        def _(refs=refs):
+            for q in range(plan.line):
+                at = slice(q * flat, (q + 1) * flat)
+                total = keep_ref[at, :]
+                for ref in refs:
+                    total = total + ref[at, :].astype(F32)
+                if q == 0:
+                    held_ref[...] = total
+                else:
+                    send_refs[q - 1][...] = total.astype(BF16)
+
+
+def line_kernel(held_ref, scale_ref, *rest):
+    parts, (mine_ref, rounded_ref) = rest[:-2], rest[-2:]
+    total = held_ref[...]
+    for ref in parts:
+        total = total + ref[...].astype(F32)
+    total = total * scale_ref[...]
+    mine_ref[...] = total
+    rounded_ref[...] = total.astype(BF16)
 
 
 def split(value):
@@ -250,36 +288,50 @@
     )(in_hbm(rows), in_hbm(counts), in_hbm(blocks), in_hbm(sketch))
 
     tiles_shape = shape((documents, block, slots * block), BF16)
-    high, low = pl.pallas_call(
-        tiles_kernel,
-        out_shape=(tiles_shape, tiles_shape),
+    high, low, scale = pl.pallas_call(
+        functools.partial(tiles_kernel, plan),
+        out_shape=(tiles_shape, tiles_shape, shape((flat, columns), F32)),
         in_specs=[scalars(), scalars(), whole(), whole()],
-        out_specs=(whole(), whole()),
+        out_specs=(whole(),) * 3,
+        scratch_shapes=[pltpu.VMEM((max(flat, block), block), F32)],
         compiler_params=params,
         cost_estimate=pl.CostEstimate(flops=1 << 20, bytes_accessed=4 << 20, transcendentals=0),
         name="tiles",
     )(rows, counts, blocks, weights.reshape(features // block, block))
 
     order = list(range(1, plan.plane)) + [0]
-    got = {p: plan.swap_cores(send[p]) for p in order}
-    chip = {p: keep[p * chunk : (p + 1) * chunk] + got[p].astype(F32) for p in order}
-    sent = [plan.swap_plane(chip[p].astype(BF16), p) for p in order[:-1]]
-    sent, high, low = lax.optimization_barrier((sent, high, low))
-    held = chip[0]
-    for part in sent:
-        held = held + part.astype(F32)
-    held = held.reshape(plan.line, flat, columns)
+    sums = []
+    for core in (0, 1):
+        got = {p: plan.swap(send[p], 1, (1 - core,)) for p in order}
+        chip = [(keep[p * chunk : (p + 1) * chunk] + got[p].astype(F32)).astype(BF16) for p in order[:-1]]
+        sent = [plan.swap_plane(chip[p - 1], p, (core,)) for p in order[:-1]]
+        sums += [got[0]] + sent
+        if core == 0:
+            send, sent[0] = lax.optimization_barrier((send, sent[0]))
+    sums, high, low, scale = lax.optimization_barrier((sums, high, low, scale))
+    held, *far = pl.pallas_call(
+        functools.partial(plane_kernel, plan),
+        grid=(1,),
+        out_shape=(shape((flat, columns), F32),) + (shape((flat, columns), BF16),) * (plan.line - 1),
+        in_specs=[pl.BlockSpec((chunk, columns), lambda i: (0, 0))] + [whole()] * (2 * plan.plane),
+        out_specs=(whole(),) * plan.line,
+        compiler_params=params,
+        name="plane_sum",
+    )(keep, *sums)
     far_first = sorted(range(1, plan.line), key=lambda q: (-(q & -2), q))
-    mine = held[0]
-    for part in [plan.swap_line(held[q].astype(BF16), q) for q in far_first]:
-        mine = mine + part.astype(F32)
-    mine = mine * lax.dynamic_slice_in_dim(weights, plan.me() * flat, flat)[:, None]
-
-    rounded = mine.astype(BF16)
+    mine, rounded = pl.pallas_call(
+        line_kernel,
+        out_shape=(shape((flat, columns), F32), shape((flat, columns), BF16)),
+        in_specs=[whole()] * (1 + plan.line),
+        out_specs=(whole(), whole()),
+        compiler_params=params,
+        name="line_sum",
+    )(held, scale, *[plan.swap_line(far[q - 1], q) for q in far_first])
+
     line = {q: plan.swap_line(rounded, q) for q in far_first}
     near = jnp.concatenate([rounded] + [line[q] for q in range(1, plan.line)], axis=0)
     own = [near] + [plan.swap_plane(near, p) for p in range(1, plan.plane)]
-    other = [plan.swap_cores(part) for part in own]
+    other = [plan.swap(part, 1) for part in own]
 
     return pl.pallas_call(
         functools.partial(last_kernel, plan, features),

time: 78 us -> 96.1 us (1.23)
  starting transfers between devices: 18.2 us -> 39.4 us
  other arithmetic: 2.17 us -> 0.36 us
  waiting for transfers between devices: 32.3 us -> 30.5 us
    ppermute x20 -> x27, starting transfers between devices: 18.2 us -> 39.4 us  [swap(): lax.ppermute(value, AXES, [(d, d ^ mask) for d in range(self.count) if d...]
    ppermute x20 -> x27, waiting for transfers between devices: 32.3 us -> 30.5 us  [swap(): lax.ppermute(value, AXES, [(d, d ^ mask) for d in range(self.count) if d...]
  transfers between devices with their start and end apart: 20 -> 27, of which waited for: 14 -> 13; matrix products, arithmetic and copies ran while one was open for 0% -> 0% of each run, Pallas kernels for 2% -> 1%
where the time goes in v6:
time: 96.1 us; the launch traced here: 95.7 us
  starting transfers between devices  39.4 us (41%)
  waiting for transfers between devices  30.5 us (32%)
  Pallas kernels  24.5 us (25%)
    ppermute x27, starting transfers between devices, swap(): lax.ppermute(value, AXES, [(d, d ^ mask) for d in range(self.count) if d...  39.4 us
    ppermute x27, waiting for transfers between devices, swap(): lax.ppermute(value, AXES, [(d, d ^ mask) for d in range(self.count) if d...  30.5 us
    pallas_call x1, Pallas kernels, body(): pl.pallas_call(functools.partial(last_kernel, plan, features), out_shape=...  19.8 us
    pallas_call x1, Pallas kernels, body(): pl.pallas_call(functools.partial(sum_kernel, plan), out_shape=(pltpu.VMEM...  3.12 us
  transfers between devices with their start and end apart: 27, of which 13 were waited for; matrix products, arithmetic and copies ran while one was open for 0% of the time, Pallas kernels for 1%

profile of v6, /device:TPU:0, one launch (start us, length us, event | category | flops | bytes accessed | tf_op | source)
XLA Modules:
  0.0 95.7 jit_solution(10236639381500670718)
XLA Ops:
  0.6 3.1 %local_sum.1 = (f32[4096,128]{1,0:T(8,128)S(1)}, bf16[1024,128]{1,0:T(8,128)(2,1)S(1)}, bf16[1024,128]{1,0:T(8,128)(2,1)S(1)}, bf16[1024,128]{1,0:T(8,128)(2,1)S(1)}, bf16[1024,128]{1,0:T(8,128)(2,1)S(1)}) custom-call(s32[3,16]{1,0:T(4,128)} %bitcast.3, s32[16]{0:T(128)} %counts_ref.3, bf16[16,3,128,128]{3,2,1,0:T(8,128)(2,1)} %blocks_ref.3, ...), custom_call_target="tpu_custom_call" | custom-call | tf_op jit(solution)/shard_map/local_sum/pallas_call | solution.py:275
  3.8 1.3 %collective-permute-start.1 = (bf16[1024,128]{1,0:T(8,128)(2,1)S(1)}, bf16[1024,128]{1,0:T(8,128)(2,1)S(1)}, u32[]{:S(2)}, u32[]{:S(2)}) collective-permute-start(bf16[1024,128]{1,0:T(8,128)(2,1)S(1)} %get-tuple-element.37), channel_id=1, source_target_pairs={{1,0},{3,2},{5,4},{7,6},{9,8},{11,10},{13,12},{15,14},{17,16},{19,... | collective-permute-start | bytes 786440 | tf_op jit(solution)/shard_map/ppermute | solution.py:59
  5.1 2.1 %collective-permute-done.1 = bf16[1024,128]{1,0:T(8,128)(2,1)S(1)} collective-permute-done((bf16[1024,128]{1,0:T(8,128)(2,1)S(1)}, bf16[1024,128]{1,0:T(8,128)(2,1)S(1)}, u32[]{:S(2)}, u32[]{:S(2)}) %collective-permute-start.1) | collective-permute-done | bytes 262176 | tf_op jit(solution)/shard_map/ppermute | solution.py:59
  7.3 4.9 %collective-permute-start.2 = (bf16[1024,128]{1,0:T(8,128)(2,1)S(1)}, bf16[1024,128]{1,0:T(8,128)(2,1)S(1)}, u32[]{:S(2)}, u32[]{:S(2)}) collective-permute-start(bf16[1024,128]{1,0:T(8,128)(2,1)S(1)} %add_convert_fusion.5), channel_id=1, source_target_pairs={{0,2},{2,0},{4,6},{6,4},{8,10},{10,8},{12,14},{14,12},{16,18},{18,... | collective-permute-start | bytes 786440 | tf_op jit(solution)/shard_map/ppermute | solution.py:59
  14.7 1.7 %collective-permute-done.2.rest_1_ = bf16[1024,128]{1,0:T(8,128)(2,1)S(1)} collective-permute-done((bf16[1024,128]{1,0:T(8,128)(2,1)S(1)}, bf16[1024,128]{1,0:T(8,128)(2,1)S(1)}, u32[]{:S(2)}, u32[]{:S(2)}) %collective-permute-start.2) | collective-permute-done | bytes 262176 | tf_op jit(solution)/shard_map/ppermute | solution.py:59
  16.5 1.5 %collective-permute-start.8 = (bf16[1024,128]{1,0:T(8,128)(2,1)S(1)}, bf16[1024,128]{1,0:T(8,128)(2,1)S(1)}, u32[]{:S(2)}, u32[]{:S(2)}) collective-permute-start(bf16[1024,128]{1,0:T(8,128)(2,1)S(1)} %get-tuple-element.37), channel_id=1, source_target_pairs={{0,1},{2,3},{4,5},{6,7},{8,9},{10,11},{12,13},{14,15},{16,17},{18,... | collective-permute-start | bytes 786440 | tf_op jit(solution)/shard_map/ppermute | solution.py:59
  18.0 1.3 %collective-permute-start.10 = (bf16[1024,128]{1,0:T(8,128)(2,1)S(1)}, bf16[1024,128]{1,0:T(8,128)(2,1)S(1)}, u32[]{:S(2)}, u32[]{:S(2)}) collective-permute-start(bf16[1024,128]{1,0:T(8,128)(2,1)S(1)} %get-tuple-element.38), channel_id=1, source_target_pairs={{0,1},{2,3},{4,5},{6,7},{8,9},{10,11},{12,13},{14,15},{16,17},{18,... | collective-permute-start | bytes 786440 | tf_op jit(solution)/shard_map/ppermute | solution.py:59
  19.3 1.3 %collective-permute-start.12 = (bf16[1024,128]{1,0:T(8,128)(2,1)S(1)}, bf16[1024,128]{1,0:T(8,128)(2,1)S(1)}, u32[]{:S(2)}, u32[]{:S(2)}) collective-permute-start(bf16[1024,128]{1,0:T(8,128)(2,1)S(1)} %get-tuple-element.39), channel_id=1, source_target_pairs={{0,1},{2,3},{4,5},{6,7},{8,9},{10,11},{12,13},{14,15},{16,17},{18,... | collective-permute-start | bytes 786440 | tf_op jit(solution)/shard_map/ppermute | solution.py:59
  21.9 3.1 %collective-permute-start.7 = (bf16[1024,128]{1,0:T(8,128)(2,1)S(1)}, bf16[1024,128]{1,0:T(8,128)(2,1)S(1)}, u32[]{:S(2)}, u32[]{:S(2)}) collective-permute-start(bf16[1024,128]{1,0:T(8,128)(2,1)S(1)} %get-tuple-element.36), channel_id=1, source_target_pairs={{0,1},{2,3},{4,5},{6,7},{8,9},{10,11},{12,13},{14,15},{16,17},{18,... | collective-permute-start | bytes 786440 | tf_op jit(solution)/shard_map/ppermute | solution.py:59
  27.4 4.8 %collective-permute-start.6 = (bf16[1024,128]{1,0:T(8,128)(2,1)S(1)}, bf16[1024,128]{1,0:T(8,128)(2,1)S(1)}, u32[]{:S(2)}, u32[]{:S(2)}) collective-permute-start(bf16[1024,128]{1,0:T(8,128)(2,1)S(1)} %get-tuple-element.63), channel_id=1, source_target_pairs={{0,6},{2,4},{4,2},{6,0},{8,14},{10,12},{12,10},{14,8},{16,22},{18,... | collective-permute-start | bytes 786440 | tf_op jit(solution)/shard_map/ppermute | solution.py:59
  32.2 2.4 %collective-permute-start.4 = (bf16[1024,128]{1,0:T(8,128)(2,1)S(1)}, bf16[1024,128]{1,0:T(8,128)(2,1)S(1)}, u32[]{:S(2)}, u32[]{:S(2)}) collective-permute-start(bf16[1024,128]{1,0:T(8,128)(2,1)S(1)} %get-tuple-element.64), channel_id=1, source_target_pairs={{0,4},{2,6},{4,0},{6,2},{8,12},{10,14},{12,8},{14,10},{16,20},{18,... | collective-permute-start | bytes 786440 | tf_op jit(solution)/shard_map/ppermute | solution.py:59
  34.7 1.3 %tiles.1 = (bf16[16,128,384]{2,1,0:T(8,128)(2,1)S(1)}, bf16[16,128,384]{2,1,0:T(8,128)(2,1)S(1)}, f32[256,128]{1,0:T(8,128)S(1)}) custom-call(s32[3,16]{1,0:T(4,128)S(1)} %bitcast.4, s32[16]{0:T(128)S(1)} %copy-done.3, bf16[16,3,128,128]{3,2,1,0:T(8,128)(2,1)S(1)} %copy-done, f32[64,128]{1,0:T(8,128)S(1)} %bitcast.2), custom_call_target="tpu_custom_call" | custom-call | flops 1048576 | bytes 4194304 | tf_op jit(solution)/shard_map/tiles/pallas_call | solution.py:291
  36.0 3.4 %collective-permute-done.6.rest_3_ = bf16[1024,128]{1,0:T(8,128)(2,1)S(1)} collective-permute-done((bf16[1024,128]{1,0:T(8,128)(2,1)S(1)}, bf16[1024,128]{1,0:T(8,128)(2,1)S(1)}, u32[]{:S(2)}, u32[]{:S(2)}) %collective-permute-start.6) | collective-permute-done | bytes 262176 | tf_op jit(solution)/shard_map/ppermute | solution.py:59
  39.4 3.9 %collective-permute-done.4.rest_2_ = bf16[1024,128]{1,0:T(8,128)(2,1)S(1)} collective-permute-done((bf16[1024,128]{1,0:T(8,128)(2,1)S(1)}, bf16[1024,128]{1,0:T(8,128)(2,1)S(1)}, u32[]{:S(2)}, u32[]{:S(2)}) %collective-permute-start.4) | collective-permute-done | bytes 262176 | tf_op jit(solution)/shard_map/ppermute | solution.py:59
  43.4 2.8 %collective-permute-start.14 = (bf16[256,128]{1,0:T(8,128)(2,1)S(1)}, bf16[256,128]{1,0:T(8,128)(2,1)S(1)}, u32[]{:S(2)}, u32[]{:S(2)}) collective-permute-start(bf16[256,128]{1,0:T(8,128)(2,1)S(1)} %get-tuple-element.55), channel_id=1, source_target_pairs={{0,16},{1,17},{2,18},{3,19},{4,20},{5,21},{6,22},{7,23},{8,24},{9,... | collective-permute-start | bytes 196616 | tf_op jit(solution)/shard_map/ppermute | solution.py:59
  46.3 1.4 %collective-permute-start.15 = (bf16[256,128]{1,0:T(8,128)(2,1)S(1)}, bf16[256,128]{1,0:T(8,128)(2,1)S(1)}, u32[]{:S(2)}, u32[]{:S(2)}) collective-permute-start(bf16[256,128]{1,0:T(8,128)(2,1)S(1)} %get-tuple-element.56), channel_id=1, source_target_pairs={{0,24},{1,25},{2,26},{3,27},{4,28},{5,29},{6,30},{7,31},{8,16},{9,... | collective-permute-start | bytes 196616 | tf_op jit(solution)/shard_map/ppermute | solution.py:59
  48.7 3.7 %collective-permute-done.15.rest_1_ = bf16[256,128]{1,0:T(8,128)(2,1)S(1)} collective-permute-done((bf16[256,128]{1,0:T(8,128)(2,1)S(1)}, bf16[256,128]{1,0:T(8,128)(2,1)S(1)}, u32[]{:S(2)}, u32[]{:S(2)}) %collective-permute-start.15) | collective-permute-done | bytes 65568 | tf_op jit(solution)/shard_map/ppermute | solution.py:59
  52.6 2.3 %collective-permute-start.19 = (bf16[256,128]{1,0:T(8,128)(2,1)S(1)}, bf16[256,128]{1,0:T(8,128)(2,1)S(1)}, u32[]{:S(2)}, u32[]{:S(2)}) collective-permute-start(bf16[256,128]{1,0:T(8,128)(2,1)S(1)} %get-tuple-element.59), channel_id=1, source_target_pairs={{0,24},{1,25},{2,26},{3,27},{4,28},{5,29},{6,30},{7,31},{8,16},{9,... | collective-permute-start | bytes 196616 | tf_op jit(solution)/shard_map/ppermute | solution.py:59
  54.9 2.1 %collective-permute-start.17 = (bf16[256,128]{1,0:T(8,128)(2,1)S(1)}, bf16[256,128]{1,0:T(8,128)(2,1)S(1)}, u32[]{:S(2)}, u32[]{:S(2)}) collective-permute-start(bf16[256,128]{1,0:T(8,128)(2,1)S(1)} %get-tuple-element.59), channel_id=1, source_target_pairs={{0,8},{1,9},{2,10},{3,11},{4,12},{5,13},{6,14},{7,15},{8,0},{9,1},... | collective-permute-start | bytes 196616 | tf_op jit(solution)/shard_map/ppermute | solution.py:59
  57.1 3.0 %collective-permute-done.17 = bf16[256,128]{1,0:T(8,128)(2,1)S(1)} collective-permute-done((bf16[256,128]{1,0:T(8,128)(2,1)S(1)}, bf16[256,128]{1,0:T(8,128)(2,1)S(1)}, u32[]{:S(2)}, u32[]{:S(2)}) %collective-permute-start.17) | collective-permute-done | bytes 65568 | tf_op jit(solution)/shard_map/ppermute | solution.py:59
  60.8 2.5 %collective-permute-start.22 = (bf16[1024,128]{1,0:T(8,128)(2,1)S(1)}, bf16[1024,128]{1,0:T(8,128)(2,1)S(1)}, u32[]{:S(2)}, u32[]{:S(2)}) collective-permute-start(bf16[1024,128]{1,0:T(8,128)(2,1)S(1)} %constant_dynamic-update-slice_fusion.rest_0_), channel_id=1, source_target_pairs={{0,6},{1,7},{2,4},{3,5},{4,2},{5,3},{6,0},{7,1},{8,14},{9,15},{10,... | collective-permute-start | bytes 786440 | tf_op jit(solution)/shard_map/ppermute | solution.py:59
  64.4 6.7 %collective-permute-done.22.rest_3_ = bf16[1024,128]{1,0:T(8,128)(2,1)S(1)} collective-permute-done((bf16[1024,128]{1,0:T(8,128)(2,1)S(1)}, bf16[1024,128]{1,0:T(8,128)(2,1)S(1)}, u32[]{:S(2)}, u32[]{:S(2)}) %collective-permute-start.22) | collective-permute-done | bytes 262176 | tf_op jit(solution)/shard_map/ppermute | solution.py:59
  71.1 2.9 %collective-permute-done.21.rest_2_ = bf16[1024,128]{1,0:T(8,128)(2,1)S(1)} collective-permute-done((bf16[1024,128]{1,0:T(8,128)(2,1)S(1)}, bf16[1024,128]{1,0:T(8,128)(2,1)S(1)}, u32[]{:S(2)}, u32[]{:S(2)}) %collective-permute-start.21) | collective-permute-done | bytes 262176 | tf_op jit(solution)/shard_map/ppermute | solution.py:59
  75.9 19.8 %factors.1 = (f32[256,128]{1,0:T(8,128)}, bf16[2048,128]{1,0:T(8,128)(2,1)}) custom-call(s32[3,16]{1,0:T(4,128)S(1)} %bitcast.5, bf16[16,128,384]{2,1,0:T(8,128)(2,1)S(1)} %get-tuple-element.43.high_ref, bf16[16,128,384]{2,1,0:T(8,128)(2,1)S(1)} %get-tuple-element.44.low_ref, f32[256,128]{1,0:T(8,128)S(1)} %get-tuple-element.58.mine_ref, ...), custom_call_target="tpu_custom_call" | custom-call | tf_op jit(solution)/shard_map/factors/pallas_call | solution.py:336
  (49 shorter events, 11.5 us)
Async XLA Ops:
  3.8 3.4 %collective-permute-start.1 = (bf16[1024,128]{1,0:T(8,128)(2,1)S(1)}, bf16[1024,128]{1,0:T(8,128)(2,1)S(1)}, u32[]{:S(2)}, u32[]{:S(2)}) collective-permute-start(bf16[1024,128]{1,0:T(8,128)(2,1)S(1)} %get-tuple-element.37), channel_id=1, source_target_pairs={{1,0},{3,2},{5,4},{7,6},{9,8},{11,10},{13,12},{15,14},{17,16},{19,... | collective-permute-start | bytes 786440 | tf_op jit(solution)/shard_map/ppermute | solution.py:59
  7.3 9.2 %collective-permute-start.2 = (bf16[1024,128]{1,0:T(8,128)(2,1)S(1)}, bf16[1024,128]{1,0:T(8,128)(2,1)S(1)}, u32[]{:S(2)}, u32[]{:S(2)}) collective-permute-start(bf16[1024,128]{1,0:T(8,128)(2,1)S(1)} %add_convert_fusion.5), channel_id=1, source_target_pairs={{0,2},{2,0},{4,6},{6,4},{8,10},{10,8},{12,14},{14,12},{16,18},{18,... | collective-permute-start | bytes 786440 | tf_op jit(solution)/shard_map/ppermute | solution.py:59
  12.1 8.5 %collective-permute-start.3 = (bf16[1024,128]{1,0:T(8,128)(2,1)S(1)}, bf16[1024,128]{1,0:T(8,128)(2,1)S(1)}, u32[]{:S(2)}, u32[]{:S(2)}) collective-permute-start(bf16[1024,128]{1,0:T(8,128)(2,1)S(1)} %get-tuple-element.38), channel_id=1, source_target_pairs={{1,0},{3,2},{5,4},{7,6},{9,8},{11,10},{13,12},{15,14},{17,16},{19,... | collective-permute-start | bytes 786440 | tf_op jit(solution)/shard_map/ppermute | solution.py:59
  13.4 8.5 %collective-permute-start.5 = (bf16[1024,128]{1,0:T(8,128)(2,1)S(1)}, bf16[1024,128]{1,0:T(8,128)(2,1)S(1)}, u32[]{:S(2)}, u32[]{:S(2)}) collective-permute-start(bf16[1024,128]{1,0:T(8,128)(2,1)S(1)} %get-tuple-element.39), channel_id=1, source_target_pairs={{1,0},{3,2},{5,4},{7,6},{9,8},{11,10},{13,12},{15,14},{17,16},{19,... | collective-permute-start | bytes 786440 | tf_op jit(solution)/shard_map/ppermute | solution.py:59
  16.5 8.5 %collective-permute-start.8 = (bf16[1024,128]{1,0:T(8,128)(2,1)S(1)}, bf16[1024,128]{1,0:T(8,128)(2,1)S(1)}, u32[]{:S(2)}, u32[]{:S(2)}) collective-permute-start(bf16[1024,128]{1,0:T(8,128)(2,1)S(1)} %get-tuple-element.37), channel_id=1, source_target_pairs={{0,1},{2,3},{4,5},{6,7},{8,9},{10,11},{12,13},{14,15},{16,17},{18,... | collective-permute-start | bytes 786440 | tf_op jit(solution)/shard_map/ppermute | solution.py:59
  18.0 7.0 %collective-permute-start.10 = (bf16[1024,128]{1,0:T(8,128)(2,1)S(1)}, bf16[1024,128]{1,0:T(8,128)(2,1)S(1)}, u32[]{:S(2)}, u32[]{:S(2)}) collective-permute-start(bf16[1024,128]{1,0:T(8,128)(2,1)S(1)} %get-tuple-element.38), channel_id=1, source_target_pairs={{0,1},{2,3},{4,5},{6,7},{8,9},{10,11},{12,13},{14,15},{16,17},{18,... | collective-permute-start | bytes 786440 | tf_op jit(solution)/shard_map/ppermute | solution.py:59
  19.3 5.7 %collective-permute-start.12 = (bf16[1024,128]{1,0:T(8,128)(2,1)S(1)}, bf16[1024,128]{1,0:T(8,128)(2,1)S(1)}, u32[]{:S(2)}, u32[]{:S(2)}) collective-permute-start(bf16[1024,128]{1,0:T(8,128)(2,1)S(1)} %get-tuple-element.39), channel_id=1, source_target_pairs={{0,1},{2,3},{4,5},{6,7},{8,9},{10,11},{12,13},{14,15},{16,17},{18,... | collective-permute-start | bytes 786440 | tf_op jit(solution)/shard_map/ppermute | solution.py:59
  20.6 6.8 %collective-permute-start = (bf16[1024,128]{1,0:T(8,128)(2,1)S(1)}, bf16[1024,128]{1,0:T(8,128)(2,1)S(1)}, u32[]{:S(2)}, u32[]{:S(2)}) collective-permute-start(bf16[1024,128]{1,0:T(8,128)(2,1)S(1)} %get-tuple-element.36), channel_id=1, source_target_pairs={{1,0},{3,2},{5,4},{7,6},{9,8},{11,10},{13,12},{15,14},{17,16},{19,... | collective-permute-start | bytes 786440 | tf_op jit(solution)/shard_map/ppermute | solution.py:59
  21.9 10.3 %collective-permute-start.7 = (bf16[1024,128]{1,0:T(8,128)(2,1)S(1)}, bf16[1024,128]{1,0:T(8,128)(2,1)S(1)}, u32[]{:S(2)}, u32[]{:S(2)}) collective-permute-start(bf16[1024,128]{1,0:T(8,128)(2,1)S(1)} %get-tuple-element.36), channel_id=1, source_target_pairs={{0,1},{2,3},{4,5},{6,7},{8,9},{10,11},{12,13},{14,15},{16,17},{18,... | collective-permute-start | bytes 786440 | tf_op jit(solution)/shard_map/ppermute | solution.py:59
  25.3 10.7 %collective-permute-start.13 = (bf16[1024,128]{1,0:T(8,128)(2,1)S(1)}, bf16[1024,128]{1,0:T(8,128)(2,1)S(1)}, u32[]{:S(2)}, u32[]{:S(2)}) collective-permute-start(bf16[1024,128]{1,0:T(8,128)(2,1)S(1)} %get-tuple-element.60), channel_id=1, source_target_pairs={{1,7},{3,5},{5,3},{7,1},{9,15},{11,13},{13,11},{15,9},{17,23},{19,... | collective-permute-start | bytes 786440 | tf_op jit(solution)/shard_map/ppermute | solution.py:59
  26.0 10.0 %collective-permute-start.9 = (bf16[1024,128]{1,0:T(8,128)(2,1)S(1)}, bf16[1024,128]{1,0:T(8,128)(2,1)S(1)}, u32[]{:S(2)}, u32[]{:S(2)}) collective-permute-start(bf16[1024,128]{1,0:T(8,128)(2,1)S(1)} %get-tuple-element.61), channel_id=1, source_target_pairs={{1,3},{3,1},{5,7},{7,5},{9,11},{11,9},{13,15},{15,13},{17,19},{19,... | collective-permute-start | bytes 786440 | tf_op jit(solution)/shard_map/ppermute | solution.py:59
  26.7 9.3 %collective-permute-start.11 = (bf16[1024,128]{1,0:T(8,128)(2,1)S(1)}, bf16[1024,128]{1,0:T(8,128)(2,1)S(1)}, u32[]{:S(2)}, u32[]{:S(2)}) collective-permute-start(bf16[1024,128]{1,0:T(8,128)(2,1)S(1)} %get-tuple-element.62), channel_id=1, source_target_pairs={{1,5},{3,7},{5,1},{7,3},{9,13},{11,15},{13,9},{15,11},{17,21},{19,... | collective-permute-start | bytes 786440 | tf_op jit(solution)/shard_map/ppermute | solution.py:59
  27.4 12.0 %collective-permute-start.6 = (bf16[1024,128]{1,0:T(8,128)(2,1)S(1)}, bf16[1024,128]{1,0:T(8,128)(2,1)S(1)}, u32[]{:S(2)}, u32[]{:S(2)}) collective-permute-start(bf16[1024,128]{1,0:T(8,128)(2,1)S(1)} %get-tuple-element.63), channel_id=1, source_target_pairs={{0,6},{2,4},{4,2},{6,0},{8,14},{10,12},{12,10},{14,8},{16,22},{18,... | collective-permute-start | bytes 786440 | tf_op jit(solution)/shard_map/ppermute | solution.py:59
  32.2 11.0 %collective-permute-start.4 = (bf16[1024,128]{1,0:T(8,128)(2,1)S(1)}, bf16[1024,128]{1,0:T(8,128)(2,1)S(1)}, u32[]{:S(2)}, u32[]{:S(2)}) collective-permute-start(bf16[1024,128]{1,0:T(8,128)(2,1)S(1)} %get-tuple-element.64), channel_id=1, source_target_pairs={{0,4},{2,6},{4,0},{6,2},{8,12},{10,14},{12,8},{14,10},{16,20},{18,... | collective-permute-start | bytes 786440 | tf_op jit(solution)/shard_map/ppermute | solution.py:59
  43.4 5.3 %collective-permute-start.14 = (bf16[256,128]{1,0:T(8,128)(2,1)S(1)}, bf16[256,128]{1,0:T(8,128)(2,1)S(1)}, u32[]{:S(2)}, u32[]{:S(2)}) collective-permute-start(bf16[256,128]{1,0:T(8,128)(2,1)S(1)} %get-tuple-element.55), channel_id=1, source_target_pairs={{0,16},{1,17},{2,18},{3,19},{4,20},{5,21},{6,22},{7,23},{8,24},{9,... | collective-permute-start | bytes 196616 | tf_op jit(solution)/shard_map/ppermute | solution.py:59
  46.3 6.2 %collective-permute-start.15 = (bf16[256,128]{1,0:T(8,128)(2,1)S(1)}, bf16[256,128]{1,0:T(8,128)(2,1)S(1)}, u32[]{:S(2)}, u32[]{:S(2)}) collective-permute-start(bf16[256,128]{1,0:T(8,128)(2,1)S(1)} %get-tuple-element.56), channel_id=1, source_target_pairs={{0,24},{1,25},{2,26},{3,27},{4,28},{5,29},{6,30},{7,31},{8,16},{9,... | collective-permute-start | bytes 196616 | tf_op jit(solution)/shard_map/ppermute | solution.py:59
  47.6 5.0 %collective-permute-start.16 = (bf16[256,128]{1,0:T(8,128)(2,1)S(1)}, bf16[256,128]{1,0:T(8,128)(2,1)S(1)}, u32[]{:S(2)}, u32[]{:S(2)}) collective-permute-start(bf16[256,128]{1,0:T(8,128)(2,1)S(1)} %get-tuple-element.57), channel_id=1, source_target_pairs={{0,8},{1,9},{2,10},{3,11},{4,12},{5,13},{6,14},{7,15},{8,0},{9,1},... | collective-permute-start | bytes 196616 | tf_op jit(solution)/shard_map/ppermute | solution.py:59
  52.6 8.2 %collective-permute-start.19 = (bf16[256,128]{1,0:T(8,128)(2,1)S(1)}, bf16[256,128]{1,0:T(8,128)(2,1)S(1)}, u32[]{:S(2)}, u32[]{:S(2)}) collective-permute-start(bf16[256,128]{1,0:T(8,128)(2,1)S(1)} %get-tuple-element.59), channel_id=1, source_target_pairs={{0,24},{1,25},{2,26},{3,27},{4,28},{5,29},{6,30},{7,31},{8,16},{9,... | collective-permute-start | bytes 196616 | tf_op jit(solution)/shard_map/ppermute | solution.py:59
  54.9 5.9 %collective-permute-start.18 = (bf16[256,128]{1,0:T(8,128)(2,1)S(1)}, bf16[256,128]{1,0:T(8,128)(2,1)S(1)}, u32[]{:S(2)}, u32[]{:S(2)}) collective-permute-start(bf16[256,128]{1,0:T(8,128)(2,1)S(1)} %get-tuple-element.59), channel_id=1, source_target_pairs={{0,16},{1,17},{2,18},{3,19},{4,20},{5,21},{6,22},{7,23},{8,24},{9,... | collective-permute-start | bytes 196616 | tf_op jit(solution)/shard_map/ppermute | solution.py:59
  54.9 5.1 %collective-permute-start.17 = (bf16[256,128]{1,0:T(8,128)(2,1)S(1)}, bf16[256,128]{1,0:T(8,128)(2,1)S(1)}, u32[]{:S(2)}, u32[]{:S(2)}) collective-permute-start(bf16[256,128]{1,0:T(8,128)(2,1)S(1)} %get-tuple-element.59), channel_id=1, source_target_pairs={{0,8},{1,9},{2,10},{3,11},{4,12},{5,13},{6,14},{7,15},{8,0},{9,1},... | collective-permute-start | bytes 196616 | tf_op jit(solution)/shard_map/ppermute | solution.py:59
  60.8 10.2 %collective-permute-start.22 = (bf16[1024,128]{1,0:T(8,128)(2,1)S(1)}, bf16[1024,128]{1,0:T(8,128)(2,1)S(1)}, u32[]{:S(2)}, u32[]{:S(2)}) collective-permute-start(bf16[1024,128]{1,0:T(8,128)(2,1)S(1)} %constant_dynamic-update-slice_fusion.rest_0_), channel_id=1, source_target_pairs={{0,6},{1,7},{2,4},{3,5},{4,2},{5,3},{6,0},{7,1},{8,14},{9,15},{10,... | collective-permute-start | bytes 786440 | tf_op jit(solution)/shard_map/ppermute | solution.py:59
  63.4 10.6 %collective-permute-start.21 = (bf16[1024,128]{1,0:T(8,128)(2,1)S(1)}, bf16[1024,128]{1,0:T(8,128)(2,1)S(1)}, u32[]{:S(2)}, u32[]{:S(2)}) collective-permute-start(bf16[1024,128]{1,0:T(8,128)(2,1)S(1)} %constant_dynamic-update-slice_fusion.rest_0_), channel_id=1, source_target_pairs={{0,4},{1,5},{2,6},{3,7},{4,0},{5,1},{6,2},{7,3},{8,12},{9,13},{10,... | collective-permute-start | bytes 786440 | tf_op jit(solution)/shard_map/ppermute | solution.py:59
  64.4 9.6 %collective-permute-start.20 = (bf16[1024,128]{1,0:T(8,128)(2,1)S(1)}, bf16[1024,128]{1,0:T(8,128)(2,1)S(1)}, u32[]{:S(2)}, u32[]{:S(2)}) collective-permute-start(bf16[1024,128]{1,0:T(8,128)(2,1)S(1)} %constant_dynamic-update-slice_fusion.rest_0_), channel_id=1, source_target_pairs={{0,2},{1,3},{2,0},{3,1},{4,6},{5,7},{6,4},{7,5},{8,10},{9,11},{10,... | collective-permute-start | bytes 786440 | tf_op jit(solution)/shard_map/ppermute | solution.py:59
  64.4 10.1 %collective-permute-start.23 = (bf16[1024,128]{1,0:T(8,128)(2,1)S(1)}, bf16[1024,128]{1,0:T(8,128)(2,1)S(1)}, u32[]{:S(2)}, u32[]{:S(2)}) collective-permute-start(bf16[1024,128]{1,0:T(8,128)(2,1)S(1)} %constant_dynamic-update-slice_fusion.rest_0_), channel_id=1, source_target_pairs={{0,1},{1,0},{2,3},{3,2},{4,5},{5,4},{6,7},{7,6},{8,9},{9,8},{10,11... | collective-permute-start | bytes 786440 | tf_op jit(solution)/shard_map/ppermute | solution.py:59
  (7 other events, 79.7 us)

commit v7 on v6

--- a/solution.py
+++ b/solution.py
@@ -52,14 +52,11 @@
         place = place * self.line + (apart >> (1 + self.plane_bits))
         return pl.multiple_of(place * self.flat + inside * self.piece, self.piece)
 
-    def core(self):
-        return lax.axis_index("col") & 1
-
-    def swap(self, value, mask, cores=(0, 1)):
-        return lax.ppermute(value, AXES, [(d, d ^ mask) for d in range(self.count) if d & 1 in cores])
-
-    def swap_plane(self, value, member, cores=(0, 1)):
-        return self.swap(value, member << 1, cores)
+    def swap(self, value, mask):
+        return lax.ppermute(value, AXES, [(d, d ^ mask) for d in range(self.count)])
+
+    def swap_plane(self, value, member):
+        return self.swap(value, member << 1)
 
     def swap_line(self, value, member):
         return self.swap(value, member << (1 + self.plane_bits))
@@ -120,24 +117,15 @@
     scale_ref[...] = turned_ref[pl.ds(pl.multiple_of(inside, plan.piece), plan.flat), :]
 
 
-def plane_kernel(plan, keep_ref, *rest):
-    steps = plan.plane
-    parts = (rest[:steps], rest[steps : 2 * steps])
-    held_ref, *send_refs = rest[2 * steps :]
-    flat = plan.flat
-    for core, refs in enumerate(parts):
-
-        @pl.when(plan.core() == core)
-        def _(refs=refs):
-            for q in range(plan.line):
-                at = slice(q * flat, (q + 1) * flat)
-                total = keep_ref[at, :]
-                for ref in refs:
-                    total = total + ref[at, :].astype(F32)
-                if q == 0:
-                    held_ref[...] = total
-                else:
-                    send_refs[q - 1][...] = total.astype(BF16)
+def plane_kernel(flat, keep_ref, got_ref, *rest):
+    count = keep_ref.shape[0] // flat
+    parts, out_refs = (got_ref,) + rest[:-count], rest[-count:]
+    for q, out_ref in enumerate(out_refs):
+        at = slice(q * flat, (q + 1) * flat)
+        total = keep_ref[at, :]
+        for ref in parts:
+            total = total + ref[at, :].astype(F32)
+        out_ref[...] = total.astype(out_ref.dtype)
 
 
 def line_kernel(held_ref, scale_ref, *rest):
@@ -226,8 +214,8 @@
 
 
 def last_kernel(plan, features, rows_ref, high_ref, low_ref, mine_ref, *rest):
-    parts, (basis_ref, factors_ref) = rest[: 2 * plan.plane], rest[2 * plan.plane : 2 * plan.plane + 2]
-    all_ref, product_ref, gram_ref, inverse_ref = rest[2 * plan.plane + 2 :]
+    parts, (basis_ref, factors_ref) = rest[: 4 * plan.plane], rest[4 * plan.plane : 4 * plan.plane + 2]
+    all_ref, product_ref, gram_ref, inverse_ref = rest[4 * plan.plane + 2 :]
     me = plan.me()
     documents, block, _ = high_ref.shape
     slots = high_ref.shape[2] // block
@@ -299,26 +287,30 @@
         name="tiles",
     )(rows, counts, blocks, weights.reshape(features // block, block))
 
-    order = list(range(1, plan.plane)) + [0]
-    sums = []
-    for core in (0, 1):
-        got = {p: plan.swap(send[p], 1, (1 - core,)) for p in order}
-        chip = [(keep[p * chunk : (p + 1) * chunk] + got[p].astype(F32)).astype(BF16) for p in order[:-1]]
-        sent = [plan.swap_plane(chip[p - 1], p, (core,)) for p in order[:-1]]
-        sums += [got[0]] + sent
-        if core == 0:
-            send, sent[0] = lax.optimization_barrier((send, sent[0]))
-    sums, high, low, scale = lax.optimization_barrier((sums, high, low, scale))
-    held, *far = pl.pallas_call(
-        functools.partial(plane_kernel, plan),
-        grid=(1,),
-        out_shape=(shape((flat, columns), F32),) + (shape((flat, columns), BF16),) * (plan.line - 1),
-        in_specs=[pl.BlockSpec((chunk, columns), lambda i: (0, 0))] + [whole()] * (2 * plan.plane),
-        out_specs=(whole(),) * plan.line,
-        compiler_params=params,
-        name="plane_sum",
-    )(keep, *sums)
-    far_first = sorted(range(1, plan.line), key=lambda q: (-(q & -2), q))
+    middle = chunk // 2
+    others = range(1, plan.plane)
+    got = {p: plan.swap(send[p], 1) for p in (*others, 0)}
+    chip = [(keep[p * chunk : (p + 1) * chunk] + got[p].astype(F32)).astype(BF16) for p in others]
+    far_sent = [plan.swap_plane(chip[p - 1][middle:], p) for p in others]
+    near_sent = [plan.swap_plane(chip[p - 1][:middle], p) for p in others]
+    near_sent, high, low, scale = lax.optimization_barrier((near_sent, high, low, scale))
+
+    def plane_sum(sent, at, dtypes):
+        return pl.pallas_call(
+            functools.partial(plane_kernel, flat),
+            grid=(1,),
+            out_shape=[shape((flat, columns), dtype) for dtype in dtypes],
+            in_specs=[pl.BlockSpec((middle, columns), lambda i: (at, 0))] * 2 + [whole()] * len(sent),
+            out_specs=[whole()] * len(dtypes),
+            compiler_params=params,
+            name="plane_sum",
+        )(keep, got[0], *sent)
+
+    split_at = plan.line // 2
+    far = plane_sum(far_sent, 1, [BF16] * split_at)
+    far = [plan.swap_line(part, split_at + q) for q, part in enumerate(far)]
+    held, *near = plane_sum(near_sent, 0, [F32] + [BF16] * (split_at - 1))
+    near = [plan.swap_line(part, 1 + q) for q, part in enumerate(near)]
     mine, rounded = pl.pallas_call(
         line_kernel,
         out_shape=(shape((flat, columns), F32), shape((flat, columns), BF16)),
@@ -326,17 +318,21 @@
         out_specs=(whole(), whole()),
         compiler_params=params,
         name="line_sum",
-    )(held, scale, *[plan.swap_line(far[q - 1], q) for q in far_first])
-
-    line = {q: plan.swap_line(rounded, q) for q in far_first}
-    near = jnp.concatenate([rounded] + [line[q] for q in range(1, plan.line)], axis=0)
-    own = [near] + [plan.swap_plane(near, p) for p in range(1, plan.plane)]
+    )(held, scale, *near, *far)
+
+    line = [rounded] + [plan.swap_line(rounded, q) for q in range(1, plan.line)]
+    near, far = jnp.concatenate(line[:split_at], axis=0), jnp.concatenate(line[split_at:], axis=0)
+    own = [near, far]
+    near = [plan.swap_plane(near, p) for p in others]
+    far = [plan.swap_plane(far, p) for p in others]
+    for pair in zip(near, far):
+        own += pair
     other = [plan.swap(part, 1) for part in own]
 
     return pl.pallas_call(
         functools.partial(last_kernel, plan, features),
         out_shape=(shape((flat, columns), F32), shape((documents * block, columns), BF16)),
-        in_specs=[scalars()] + [whole()] * (3 + 2 * plan.plane),
+        in_specs=[scalars()] + [whole()] * (3 + 4 * plan.plane),
         out_specs=(whole(), whole()),
         scratch_shapes=[
             pltpu.VMEM((features, columns), BF16),

time: 96.1 us -> 73 us (0.76)
  waiting for transfers between devices: 30.5 us -> 16.9 us
  starting transfers between devices: 39.4 us -> 30.4 us
    ppermute x27 -> x30, waiting for transfers between devices: 30.5 us -> 16.9 us  [swap(): return lax.ppermute(value, AXES, [(d, d ^ mask) for d in range(self.count)])]
    ppermute x27 -> x30, starting transfers between devices: 39.4 us -> 30.4 us  [swap(): return lax.ppermute(value, AXES, [(d, d ^ mask) for d in range(self.count)])]
  transfers between devices with their start and end apart: 27 -> 30, of which waited for: 13 -> 17; matrix products, arithmetic and copies ran while one was open for 0% -> 0% of each run, Pallas kernels for 1% -> 2%
where the time goes in v7:
time: 73 us; the launch traced here: 72.9 us
  starting transfers between devices  30.4 us (42%)
  Pallas kernels  24.5 us (34%)
  waiting for transfers between devices  16.9 us (23%)
  between operations  0.77 us (1%)
    ppermute x30, starting transfers between devices, swap(): return lax.ppermute(value, AXES, [(d, d ^ mask) for d in range(self.count)])  30.4 us
    pallas_call x1, Pallas kernels, body(): pl.pallas_call(functools.partial(last_kernel, plan, features), out_shape=...  19.9 us
    ppermute x30, waiting for transfers between devices, swap(): return lax.ppermute(value, AXES, [(d, d ^ mask) for d in range(self.count)])  16.9 us
    pallas_call x1, Pallas kernels, body(): pl.pallas_call(functools.partial(sum_kernel, plan), out_shape=(pltpu.VMEM...  3.12 us
  transfers between devices with their start and end apart: 30, of which 17 were waited for; matrix products, arithmetic and copies ran while one was open for 0% of the time, Pallas kernels for 2%

profile of v7, /device:TPU:0, one launch (start us, length us, event | category | flops | bytes accessed | tf_op | source)
XLA Modules:
  0.0 72.9 jit_solution(9000954866088067135)
XLA Ops:
  0.6 3.1 %local_sum.1 = (f32[4096,128]{1,0:T(8,128)S(1)}, bf16[1024,128]{1,0:T(8,128)(2,1)S(1)}, bf16[1024,128]{1,0:T(8,128)(2,1)S(1)}, bf16[1024,128]{1,0:T(8,128)(2,1)S(1)}, bf16[1024,128]{1,0:T(8,128)(2,1)S(1)}) custom-call(s32[3,16]{1,0:T(4,128)} %bitcast.3, s32[16]{0:T(128)} %counts_ref.3, bf16[16,3,128,128]{3,2,1,0:T(8,128)(2,1)} %blocks_ref.3, ...), custom_call_target="tpu_custom_call" | custom-call | tf_op jit(solution)/shard_map/local_sum/pallas_call | solution.py:263
  6.5 3.9 %collective-permute-start.10 = (bf16[512,128]{1,0:T(8,128)(2,1)S(1)}, bf16[512,128]{1,0:T(8,128)(2,1)S(1)}, u32[]{:S(2)}, u32[]{:S(2)}) collective-permute-start(bf16[512,128]{1,0:T(8,128)(2,1)S(1)} %get-tuple-element.45), channel_id=1, source_target_pairs={{0,6},{1,7},{2,4},{3,5},{4,2},{5,3},{6,0},{7,1},{8,14},{9,15},{10,... | collective-permute-start | bytes 393224 | tf_op jit(solution)/shard_map/ppermute | solution.py:56
  11.1 2.9 %collective-permute-start.5 = (bf16[512,128]{1,0:T(8,128)(2,1)S(1)}, bf16[512,128]{1,0:T(8,128)(2,1)S(1)}, u32[]{:S(2)}, u32[]{:S(2)}) collective-permute-start(bf16[512,128]{1,0:T(8,128)(2,1)S(1)} %get-tuple-element.46), channel_id=1, source_target_pairs={{0,6},{1,7},{2,4},{3,5},{4,2},{5,3},{6,0},{7,1},{8,14},{9,15},{10,... | collective-permute-start | bytes 393224 | tf_op jit(solution)/shard_map/ppermute | solution.py:56
  14.5 2.1 %collective-permute-start.1 = (bf16[512,128]{1,0:T(8,128)(2,1)S(1)}, bf16[512,128]{1,0:T(8,128)(2,1)S(1)}, u32[]{:S(2)}, u32[]{:S(2)}) collective-permute-start(bf16[512,128]{1,0:T(8,128)(2,1)S(1)} %get-tuple-element.50), channel_id=1, source_target_pairs={{0,2},{1,3},{2,0},{3,1},{4,6},{5,7},{6,4},{7,5},{8,10},{9,11},{10,... | collective-permute-start | bytes 393224 | tf_op jit(solution)/shard_map/ppermute | solution.py:56
  16.7 1.3 %tiles.1 = (bf16[16,128,384]{2,1,0:T(8,128)(2,1)S(1)}, bf16[16,128,384]{2,1,0:T(8,128)(2,1)S(1)}, f32[256,128]{1,0:T(8,128)S(1)}) custom-call(s32[3,16]{1,0:T(4,128)S(1)} %bitcast.4, s32[16]{0:T(128)S(1)} %copy-done.3, bf16[16,3,128,128]{3,2,1,0:T(8,128)(2,1)S(1)} %copy-done, f32[64,128]{1,0:T(8,128)S(1)} %bitcast.2), custom_call_target="tpu_custom_call" | custom-call | flops 1048576 | bytes 4194304 | tf_op jit(solution)/shard_map/tiles/pallas_call | solution.py:279
  18.6 2.7 %collective-permute-start.11 = (bf16[256,128]{1,0:T(8,128)(2,1)S(1)}, bf16[256,128]{1,0:T(8,128)(2,1)S(1)}, u32[]{:S(2)}, u32[]{:S(2)}) collective-permute-start(bf16[256,128]{1,0:T(8,128)(2,1)S(1)} %get-tuple-element.38), channel_id=1, source_target_pairs={{0,16},{1,17},{2,18},{3,19},{4,20},{5,21},{6,22},{7,23},{8,24},{9,... | collective-permute-start | bytes 196616 | tf_op jit(solution)/shard_map/ppermute | solution.py:56
  21.2 1.4 %collective-permute-start.12 = (bf16[256,128]{1,0:T(8,128)(2,1)S(1)}, bf16[256,128]{1,0:T(8,128)(2,1)S(1)}, u32[]{:S(2)}, u32[]{:S(2)}) collective-permute-start(bf16[256,128]{1,0:T(8,128)(2,1)S(1)} %get-tuple-element.39), channel_id=1, source_target_pairs={{0,24},{1,25},{2,26},{3,27},{4,28},{5,29},{6,30},{7,31},{8,16},{9,... | collective-permute-start | bytes 196616 | tf_op jit(solution)/shard_map/ppermute | solution.py:56
  22.9 1.6 %collective-permute-start.7 = (bf16[256,128]{1,0:T(8,128)(2,1)S(1)}, bf16[256,128]{1,0:T(8,128)(2,1)S(1)}, u32[]{:S(2)}, u32[]{:S(2)}) collective-permute-start(bf16[256,128]{1,0:T(8,128)(2,1)S(1)} %get-tuple-element.37), channel_id=1, source_target_pairs={{0,8},{1,9},{2,10},{3,11},{4,12},{5,13},{6,14},{7,15},{8,0},{9,1},... | collective-permute-start | bytes 196616 | tf_op jit(solution)/shard_map/ppermute | solution.py:56
  24.6 1.4 %collective-permute-done.11.rest_1_ = bf16[256,128]{1,0:T(8,128)(2,1)S(1)} collective-permute-done((bf16[256,128]{1,0:T(8,128)(2,1)S(1)}, bf16[256,128]{1,0:T(8,128)(2,1)S(1)}, u32[]{:S(2)}, u32[]{:S(2)}) %collective-permute-start.11) | collective-permute-done | bytes 65568 | tf_op jit(solution)/shard_map/ppermute | solution.py:56
  26.0 1.5 %collective-permute-done.12.rest_2_ = bf16[256,128]{1,0:T(8,128)(2,1)S(1)} collective-permute-done((bf16[256,128]{1,0:T(8,128)(2,1)S(1)}, bf16[256,128]{1,0:T(8,128)(2,1)S(1)}, u32[]{:S(2)}, u32[]{:S(2)}) %collective-permute-start.12) | collective-permute-done | bytes 65568 | tf_op jit(solution)/shard_map/ppermute | solution.py:56
  28.1 3.1 %collective-permute-start.15 = (bf16[256,128]{1,0:T(8,128)(2,1)S(1)}, bf16[256,128]{1,0:T(8,128)(2,1)S(1)}, u32[]{:S(2)}, u32[]{:S(2)}) collective-permute-start(bf16[256,128]{1,0:T(8,128)(2,1)S(1)} %get-tuple-element.41), channel_id=1, source_target_pairs={{0,24},{1,25},{2,26},{3,27},{4,28},{5,29},{6,30},{7,31},{8,16},{9,... | collective-permute-start | bytes 196616 | tf_op jit(solution)/shard_map/ppermute | solution.py:56
  31.2 1.4 %collective-permute-start.13 = (bf16[256,128]{1,0:T(8,128)(2,1)S(1)}, bf16[256,128]{1,0:T(8,128)(2,1)S(1)}, u32[]{:S(2)}, u32[]{:S(2)}) collective-permute-start(bf16[256,128]{1,0:T(8,128)(2,1)S(1)} %get-tuple-element.41), channel_id=1, source_target_pairs={{0,8},{1,9},{2,10},{3,11},{4,12},{5,13},{6,14},{7,15},{8,0},{9,1},... | collective-permute-start | bytes 196616 | tf_op jit(solution)/shard_map/ppermute | solution.py:56
  32.5 3.3 %collective-permute-done.13 = bf16[256,128]{1,0:T(8,128)(2,1)S(1)} collective-permute-done((bf16[256,128]{1,0:T(8,128)(2,1)S(1)}, bf16[256,128]{1,0:T(8,128)(2,1)S(1)}, u32[]{:S(2)}, u32[]{:S(2)}) %collective-permute-start.13) | collective-permute-done | bytes 65568 | tf_op jit(solution)/shard_map/ppermute | solution.py:56
  35.9 1.4 %collective-permute-start.20 = (bf16[512,128]{1,0:T(8,128)(2,1)S(1)}, bf16[512,128]{1,0:T(8,128)(2,1)S(1)}, u32[]{:S(2)}, u32[]{:S(2)}) collective-permute-start(bf16[512,128]{1,0:T(8,128)(2,1)S(1)} %constant_dynamic-update-slice_fusion.rest_0_), channel_id=1, source_target_pairs={{0,6},{1,7},{2,4},{3,5},{4,2},{5,3},{6,0},{7,1},{8,14},{9,15},{10,... | collective-permute-start | bytes 393224 | tf_op jit(solution)/shard_map/ppermute | solution.py:56
  37.4 1.4 %collective-permute-start.18 = (bf16[512,128]{1,0:T(8,128)(2,1)S(1)}, bf16[512,128]{1,0:T(8,128)(2,1)S(1)}, u32[]{:S(2)}, u32[]{:S(2)}) collective-permute-start(bf16[512,128]{1,0:T(8,128)(2,1)S(1)} %constant_dynamic-update-slice_fusion.rest_0_), channel_id=1, source_target_pairs={{0,4},{1,5},{2,6},{3,7},{4,0},{5,1},{6,2},{7,3},{8,12},{9,13},{10,... | collective-permute-start | bytes 393224 | tf_op jit(solution)/shard_map/ppermute | solution.py:56
  38.8 0.7 collective-permute-start.16
  39.6 1.4 %collective-permute-start.21 = (bf16[512,128]{1,0:T(8,128)(2,1)S(1)}, bf16[512,128]{1,0:T(8,128)(2,1)S(1)}, u32[]{:S(2)}, u32[]{:S(2)}) collective-permute-start(bf16[512,128]{1,0:T(8,128)(2,1)S(1)} %constant_dynamic-update-slice_fusion.2.rest_1_), channel_id=1, source_target_pairs={{0,6},{1,7},{2,4},{3,5},{4,2},{5,3},{6,0},{7,1},{8,14},{9,15},{10,... | collective-permute-start | bytes 393224 | tf_op jit(solution)/shard_map/ppermute | solution.py:56
  41.0 2.2 %collective-permute-done.20.rest_6_ = bf16[512,128]{1,0:T(8,128)(2,1)S(1)} collective-permute-done((bf16[512,128]{1,0:T(8,128)(2,1)S(1)}, bf16[512,128]{1,0:T(8,128)(2,1)S(1)}, u32[]{:S(2)}, u32[]{:S(2)}) %collective-permute-start.20) | collective-permute-done | bytes 131104 | tf_op jit(solution)/shard_map/ppermute | solution.py:56
  43.2 1.5 %collective-permute-start.19 = (bf16[512,128]{1,0:T(8,128)(2,1)S(1)}, bf16[512,128]{1,0:T(8,128)(2,1)S(1)}, u32[]{:S(2)}, u32[]{:S(2)}) collective-permute-start(bf16[512,128]{1,0:T(8,128)(2,1)S(1)} %constant_dynamic-update-slice_fusion.2.rest_1_), channel_id=1, source_target_pairs={{0,4},{1,5},{2,6},{3,7},{4,0},{5,1},{6,2},{7,3},{8,12},{9,13},{10,... | collective-permute-start | bytes 393224 | tf_op jit(solution)/shard_map/ppermute | solution.py:56
  44.7 1.4 %collective-permute-done.18.rest_4_ = bf16[512,128]{1,0:T(8,128)(2,1)S(1)} collective-permute-done((bf16[512,128]{1,0:T(8,128)(2,1)S(1)}, bf16[512,128]{1,0:T(8,128)(2,1)S(1)}, u32[]{:S(2)}, u32[]{:S(2)}) %collective-permute-start.18) | collective-permute-done | bytes 131104 | tf_op jit(solution)/shard_map/ppermute | solution.py:56
  46.1 1.3 %collective-permute-start.17 = (bf16[512,128]{1,0:T(8,128)(2,1)S(1)}, bf16[512,128]{1,0:T(8,128)(2,1)S(1)}, u32[]{:S(2)}, u32[]{:S(2)}) collective-permute-start(bf16[512,128]{1,0:T(8,128)(2,1)S(1)} %constant_dynamic-update-slice_fusion.2.rest_1_), channel_id=1, source_target_pairs={{0,2},{1,3},{2,0},{3,1},{4,6},{5,7},{6,4},{7,5},{8,10},{9,11},{10,... | collective-permute-start | bytes 393224 | tf_op jit(solution)/shard_map/ppermute | solution.py:56
  48.5 2.7 %collective-permute-done.19.rest_5_ = bf16[512,128]{1,0:T(8,128)(2,1)S(1)} collective-permute-done((bf16[512,128]{1,0:T(8,128)(2,1)S(1)}, bf16[512,128]{1,0:T(8,128)(2,1)S(1)}, u32[]{:S(2)}, u32[]{:S(2)}) %collective-permute-start.19) | collective-permute-done | bytes 131104 | tf_op jit(solution)/shard_map/ppermute | solution.py:56
  51.8 0.7 collective-permute-done.29.rest_15_
  53.0 19.9 %factors.1 = (f32[256,128]{1,0:T(8,128)}, bf16[2048,128]{1,0:T(8,128)(2,1)}) custom-call(s32[3,16]{1,0:T(4,128)S(1)} %bitcast.5, bf16[16,128,384]{2,1,0:T(8,128)(2,1)S(1)} %get-tuple-element.29.high_ref, bf16[16,128,384]{2,1,0:T(8,128)(2,1)S(1)} %get-tuple-element.30.low_ref, f32[256,128]{1,0:T(8,128)S(1)} %get-tuple-element.40.mine_ref, ...), custom_call_target="tpu_custom_call" | custom-call | tf_op jit(solution)/shard_map/factors/pallas_call | solution.py:332
  (58 shorter events, 7.9 us)
Async XLA Ops:
  4.8 9.2 %collective-permute-start.6 = (bf16[1024,128]{1,0:T(8,128)(2,1)S(1)}, bf16[1024,128]{1,0:T(8,128)(2,1)S(1)}, u32[]{:S(2)}, u32[]{:S(2)}) collective-permute-start(bf16[1024,128]{1,0:T(8,128)(2,1)S(1)} %get-tuple-element.31), channel_id=1, source_target_pairs={{0,1},{1,0},{2,3},{3,2},{4,5},{5,4},{6,7},{7,6},{8,9},{9,8},{10,11... | collective-permute-start | bytes 786440 | tf_op jit(solution)/shard_map/ppermute | solution.py:56
  6.5 8.1 %collective-permute-start.10 = (bf16[512,128]{1,0:T(8,128)(2,1)S(1)}, bf16[512,128]{1,0:T(8,128)(2,1)S(1)}, u32[]{:S(2)}, u32[]{:S(2)}) collective-permute-start(bf16[512,128]{1,0:T(8,128)(2,1)S(1)} %get-tuple-element.45), channel_id=1, source_target_pairs={{0,6},{1,7},{2,4},{3,5},{4,2},{5,3},{6,0},{7,1},{8,14},{9,15},{10,... | collective-permute-start | bytes 393224 | tf_op jit(solution)/shard_map/ppermute | solution.py:56
  10.4 8.1 %collective-permute-start.9 = (bf16[512,128]{1,0:T(8,128)(2,1)S(1)}, bf16[512,128]{1,0:T(8,128)(2,1)S(1)}, u32[]{:S(2)}, u32[]{:S(2)}) collective-permute-start(bf16[512,128]{1,0:T(8,128)(2,1)S(1)} %get-tuple-element.47), channel_id=1, source_target_pairs={{0,4},{1,5},{2,6},{3,7},{4,0},{5,1},{6,2},{7,3},{8,12},{9,13},{10,... | collective-permute-start | bytes 393224 | tf_op jit(solution)/shard_map/ppermute | solution.py:56
  11.0 7.5 %collective-permute-start.8 = (bf16[512,128]{1,0:T(8,128)(2,1)S(1)}, bf16[512,128]{1,0:T(8,128)(2,1)S(1)}, u32[]{:S(2)}, u32[]{:S(2)}) collective-permute-start(bf16[512,128]{1,0:T(8,128)(2,1)S(1)} %get-tuple-element.49), channel_id=1, source_target_pairs={{0,2},{1,3},{2,0},{3,1},{4,6},{5,7},{6,4},{7,5},{8,10},{9,11},{10,... | collective-permute-start | bytes 393224 | tf_op jit(solution)/shard_map/ppermute | solution.py:56
  11.1 11.5 %collective-permute-start.5 = (bf16[512,128]{1,0:T(8,128)(2,1)S(1)}, bf16[512,128]{1,0:T(8,128)(2,1)S(1)}, u32[]{:S(2)}, u32[]{:S(2)}) collective-permute-start(bf16[512,128]{1,0:T(8,128)(2,1)S(1)} %get-tuple-element.46), channel_id=1, source_target_pairs={{0,6},{1,7},{2,4},{3,5},{4,2},{5,3},{6,0},{7,1},{8,14},{9,15},{10,... | collective-permute-start | bytes 393224 | tf_op jit(solution)/shard_map/ppermute | solution.py:56
  14.0 8.6 %collective-permute-start.3 = (bf16[512,128]{1,0:T(8,128)(2,1)S(1)}, bf16[512,128]{1,0:T(8,128)(2,1)S(1)}, u32[]{:S(2)}, u32[]{:S(2)}) collective-permute-start(bf16[512,128]{1,0:T(8,128)(2,1)S(1)} %get-tuple-element.48), channel_id=1, source_target_pairs={{0,4},{1,5},{2,6},{3,7},{4,0},{5,1},{6,2},{7,3},{8,12},{9,13},{10,... | collective-permute-start | bytes 393224 | tf_op jit(solution)/shard_map/ppermute | solution.py:56
  14.5 8.3 %collective-permute-start.1 = (bf16[512,128]{1,0:T(8,128)(2,1)S(1)}, bf16[512,128]{1,0:T(8,128)(2,1)S(1)}, u32[]{:S(2)}, u32[]{:S(2)}) collective-permute-start(bf16[512,128]{1,0:T(8,128)(2,1)S(1)} %get-tuple-element.50), channel_id=1, source_target_pairs={{0,2},{1,3},{2,0},{3,1},{4,6},{5,7},{6,4},{7,5},{8,10},{9,11},{10,... | collective-permute-start | bytes 393224 | tf_op jit(solution)/shard_map/ppermute | solution.py:56
  18.6 7.4 %collective-permute-start.11 = (bf16[256,128]{1,0:T(8,128)(2,1)S(1)}, bf16[256,128]{1,0:T(8,128)(2,1)S(1)}, u32[]{:S(2)}, u32[]{:S(2)}) collective-permute-start(bf16[256,128]{1,0:T(8,128)(2,1)S(1)} %get-tuple-element.38), channel_id=1, source_target_pairs={{0,16},{1,17},{2,18},{3,19},{4,20},{5,21},{6,22},{7,23},{8,24},{9,... | collective-permute-start | bytes 196616 | tf_op jit(solution)/shard_map/ppermute | solution.py:56
  21.2 6.2 %collective-permute-start.12 = (bf16[256,128]{1,0:T(8,128)(2,1)S(1)}, bf16[256,128]{1,0:T(8,128)(2,1)S(1)}, u32[]{:S(2)}, u32[]{:S(2)}) collective-permute-start(bf16[256,128]{1,0:T(8,128)(2,1)S(1)} %get-tuple-element.39), channel_id=1, source_target_pairs={{0,24},{1,25},{2,26},{3,27},{4,28},{5,29},{6,30},{7,31},{8,16},{9,... | collective-permute-start | bytes 196616 | tf_op jit(solution)/shard_map/ppermute | solution.py:56
  22.9 5.1 %collective-permute-start.7 = (bf16[256,128]{1,0:T(8,128)(2,1)S(1)}, bf16[256,128]{1,0:T(8,128)(2,1)S(1)}, u32[]{:S(2)}, u32[]{:S(2)}) collective-permute-start(bf16[256,128]{1,0:T(8,128)(2,1)S(1)} %get-tuple-element.37), channel_id=1, source_target_pairs={{0,8},{1,9},{2,10},{3,11},{4,12},{5,13},{6,14},{7,15},{8,0},{9,1},... | collective-permute-start | bytes 196616 | tf_op jit(solution)/shard_map/ppermute | solution.py:56
  28.1 11.4 %collective-permute-start.15 = (bf16[256,128]{1,0:T(8,128)(2,1)S(1)}, bf16[256,128]{1,0:T(8,128)(2,1)S(1)}, u32[]{:S(2)}, u32[]{:S(2)}) collective-permute-start(bf16[256,128]{1,0:T(8,128)(2,1)S(1)} %get-tuple-element.41), channel_id=1, source_target_pairs={{0,24},{1,25},{2,26},{3,27},{4,28},{5,29},{6,30},{7,31},{8,16},{9,... | collective-permute-start | bytes 196616 | tf_op jit(solution)/shard_map/ppermute | solution.py:56
  31.2 7.6 %collective-permute-start.14 = (bf16[256,128]{1,0:T(8,128)(2,1)S(1)}, bf16[256,128]{1,0:T(8,128)(2,1)S(1)}, u32[]{:S(2)}, u32[]{:S(2)}) collective-permute-start(bf16[256,128]{1,0:T(8,128)(2,1)S(1)} %get-tuple-element.41), channel_id=1, source_target_pairs={{0,16},{1,17},{2,18},{3,19},{4,20},{5,21},{6,22},{7,23},{8,24},{9,... | collective-permute-start | bytes 196616 | tf_op jit(solution)/shard_map/ppermute | solution.py:56
  31.2 4.6 %collective-permute-start.13 = (bf16[256,128]{1,0:T(8,128)(2,1)S(1)}, bf16[256,128]{1,0:T(8,128)(2,1)S(1)}, u32[]{:S(2)}, u32[]{:S(2)}) collective-permute-start(bf16[256,128]{1,0:T(8,128)(2,1)S(1)} %get-tuple-element.41), channel_id=1, source_target_pairs={{0,8},{1,9},{2,10},{3,11},{4,12},{5,13},{6,14},{7,15},{8,0},{9,1},... | collective-permute-start | bytes 196616 | tf_op jit(solution)/shard_map/ppermute | solution.py:56
  35.8 3.8 %collective-permute-start.22 = (bf16[512,128]{1,0:T(8,128)(2,1)S(1)}, bf16[512,128]{1,0:T(8,128)(2,1)S(1)}, u32[]{:S(2)}, u32[]{:S(2)}) collective-permute-start(bf16[512,128]{1,0:T(8,128)(2,1)S(1)} %constant_dynamic-update-slice_fusion.rest_0_), channel_id=1, source_target_pairs={{0,1},{1,0},{2,3},{3,2},{4,5},{5,4},{6,7},{7,6},{8,9},{9,8},{10,11... | collective-permute-start | bytes 393224 | tf_op jit(solution)/shard_map/ppermute | solution.py:56
  35.9 7.3 %collective-permute-start.20 = (bf16[512,128]{1,0:T(8,128)(2,1)S(1)}, bf16[512,128]{1,0:T(8,128)(2,1)S(1)}, u32[]{:S(2)}, u32[]{:S(2)}) collective-permute-start(bf16[512,128]{1,0:T(8,128)(2,1)S(1)} %constant_dynamic-update-slice_fusion.rest_0_), channel_id=1, source_target_pairs={{0,6},{1,7},{2,4},{3,5},{4,2},{5,3},{6,0},{7,1},{8,14},{9,15},{10,... | collective-permute-start | bytes 393224 | tf_op jit(solution)/shard_map/ppermute | solution.py:56
  37.4 8.7 %collective-permute-start.18 = (bf16[512,128]{1,0:T(8,128)(2,1)S(1)}, bf16[512,128]{1,0:T(8,128)(2,1)S(1)}, u32[]{:S(2)}, u32[]{:S(2)}) collective-permute-start(bf16[512,128]{1,0:T(8,128)(2,1)S(1)} %constant_dynamic-update-slice_fusion.rest_0_), channel_id=1, source_target_pairs={{0,4},{1,5},{2,6},{3,7},{4,0},{5,1},{6,2},{7,3},{8,12},{9,13},{10,... | collective-permute-start | bytes 393224 | tf_op jit(solution)/shard_map/ppermute | solution.py:56
  38.8 8.6 %collective-permute-start.16 = (bf16[512,128]{1,0:T(8,128)(2,1)S(1)}, bf16[512,128]{1,0:T(8,128)(2,1)S(1)}, u32[]{:S(2)}, u32[]{:S(2)}) collective-permute-start(bf16[512,128]{1,0:T(8,128)(2,1)S(1)} %constant_dynamic-update-slice_fusion.rest_0_), channel_id=1, source_target_pairs={{0,2},{1,3},{2,0},{3,1},{4,6},{5,7},{6,4},{7,5},{8,10},{9,11},{10,... | collective-permute-start | bytes 393224 | tf_op jit(solution)/shard_map/ppermute | solution.py:56
  39.5 7.9 %collective-permute-start.23 = (bf16[512,128]{1,0:T(8,128)(2,1)S(1)}, bf16[512,128]{1,0:T(8,128)(2,1)S(1)}, u32[]{:S(2)}, u32[]{:S(2)}) collective-permute-start(bf16[512,128]{1,0:T(8,128)(2,1)S(1)} %constant_dynamic-update-slice_fusion.2.rest_1_), channel_id=1, source_target_pairs={{0,1},{1,0},{2,3},{3,2},{4,5},{5,4},{6,7},{7,6},{8,9},{9,8},{10,11... | collective-permute-start | bytes 393224 | tf_op jit(solution)/shard_map/ppermute | solution.py:56
  39.6 8.9 %collective-permute-start.21 = (bf16[512,128]{1,0:T(8,128)(2,1)S(1)}, bf16[512,128]{1,0:T(8,128)(2,1)S(1)}, u32[]{:S(2)}, u32[]{:S(2)}) collective-permute-start(bf16[512,128]{1,0:T(8,128)(2,1)S(1)} %constant_dynamic-update-slice_fusion.2.rest_1_), channel_id=1, source_target_pairs={{0,6},{1,7},{2,4},{3,5},{4,2},{5,3},{6,0},{7,1},{8,14},{9,15},{10,... | collective-permute-start | bytes 393224 | tf_op jit(solution)/shard_map/ppermute | solution.py:56
  43.2 7.9 %collective-permute-start.19 = (bf16[512,128]{1,0:T(8,128)(2,1)S(1)}, bf16[512,128]{1,0:T(8,128)(2,1)S(1)}, u32[]{:S(2)}, u32[]{:S(2)}) collective-permute-start(bf16[512,128]{1,0:T(8,128)(2,1)S(1)} %constant_dynamic-update-slice_fusion.2.rest_1_), channel_id=1, source_target_pairs={{0,4},{1,5},{2,6},{3,7},{4,0},{5,1},{6,2},{7,3},{8,12},{9,13},{10,... | collective-permute-start | bytes 393224 | tf_op jit(solution)/shard_map/ppermute | solution.py:56
  46.1 5.2 %collective-permute-start.17 = (bf16[512,128]{1,0:T(8,128)(2,1)S(1)}, bf16[512,128]{1,0:T(8,128)(2,1)S(1)}, u32[]{:S(2)}, u32[]{:S(2)}) collective-permute-start(bf16[512,128]{1,0:T(8,128)(2,1)S(1)} %constant_dynamic-update-slice_fusion.2.rest_1_), channel_id=1, source_target_pairs={{0,2},{1,3},{2,0},{3,1},{4,6},{5,7},{6,4},{7,5},{8,10},{9,11},{10,... | collective-permute-start | bytes 393224 | tf_op jit(solution)/shard_map/ppermute | solution.py:56
  47.4 4.3 %collective-permute-start.28 = (bf16[512,128]{1,0:T(8,128)(2,1)S(1)}, bf16[512,128]{1,0:T(8,128)(2,1)S(1)}, u32[]{:S(2)}, u32[]{:S(2)}) collective-permute-start(bf16[512,128]{1,0:T(8,128)(2,1)S(1)} %collective-permute-done.20.rest_6_), channel_id=1, source_target_pairs={{0,1},{1,0},{2,3},{3,2},{4,5},{5,4},{6,7},{7,6},{8,9},{9,8},{10,11... | collective-permute-start | bytes 393224 | tf_op jit(solution)/shard_map/ppermute | solution.py:56
  47.4 4.4 %collective-permute-start.26 = (bf16[512,128]{1,0:T(8,128)(2,1)S(1)}, bf16[512,128]{1,0:T(8,128)(2,1)S(1)}, u32[]{:S(2)}, u32[]{:S(2)}) collective-permute-start(bf16[512,128]{1,0:T(8,128)(2,1)S(1)} %collective-permute-done.18.rest_4_), channel_id=1, source_target_pairs={{0,1},{1,0},{2,3},{3,2},{4,5},{5,4},{6,7},{7,6},{8,9},{9,8},{10,11... | collective-permute-start | bytes 393224 | tf_op jit(solution)/shard_map/ppermute | solution.py:56
  48.5 3.3 %collective-permute-start.24 = (bf16[512,128]{1,0:T(8,128)(2,1)S(1)}, bf16[512,128]{1,0:T(8,128)(2,1)S(1)}, u32[]{:S(2)}, u32[]{:S(2)}) collective-permute-start(bf16[512,128]{1,0:T(8,128)(2,1)S(1)} %collective-permute-done.16.rest_2_), channel_id=1, source_target_pairs={{0,1},{1,0},{2,3},{3,2},{4,5},{5,4},{6,7},{7,6},{8,9},{9,8},{10,11... | collective-permute-start | bytes 393224 | tf_op jit(solution)/shard_map/ppermute | solution.py:56
  (10 other events, 50.3 us)

commit v8 on v7

--- a/solution.py
+++ b/solution.py
@@ -98,7 +98,7 @@
         send_ref[...] = total_ref[half + p * size : half + (p + 1) * size, :].astype(BF16)
 
 
-def tiles_kernel(plan, rows_ref, counts_ref, blocks_ref, weights_ref, high_ref, low_ref, scale_ref, turned_ref):
+def tiles_kernel(rows_ref, counts_ref, blocks_ref, weights_ref, high_ref, low_ref):
     documents, slots, block, _ = blocks_ref.shape
     for d in range(documents):
         for s in range(slots):
@@ -107,6 +107,10 @@
             high, low = split(blocks_ref[d, s].T.astype(F32) * scale)
             high_ref[d, :, s * block : (s + 1) * block] = high
             low_ref[d, :, s * block : (s + 1) * block] = low
+
+
+def scale_kernel(plan, weights_ref, scale_ref, turned_ref):
+    block = weights_ref.shape[1]
     unit = plan.me() << plan.slice_bits
     lines = max(1, plan.flat // block)
     first = unit if plan.pieces == 1 else unit // plan.pieces
@@ -220,10 +224,13 @@
     documents, block, _ = high_ref.shape
     slots = high_ref.shape[2] // block
     gram = jnp.zeros(gram_ref.shape, F32)
-    for p, ref in enumerate(parts):
+    for i, ref in enumerate(parts):
         size = ref.shape[0]
+        core, later = divmod(i, 2 * plan.plane)
+        near, member = divmod(later, plan.plane)
+        base = ((core * plan.plane + member) * 2 + 1 - near) * size
         part = ref[...]
-        all_ref[p * size : (p + 1) * size, :] = part
+        all_ref[base : base + size, :] = part
         gram += lax.dot_general(part, part, (((0,), (0,)), ((), ())), preferred_element_type=F32)
     gram = gram * (1.0 / features)
     residual = newton(gram, inverse_ref)
@@ -276,24 +283,34 @@
     )(in_hbm(rows), in_hbm(counts), in_hbm(blocks), in_hbm(sketch))
 
     tiles_shape = shape((documents, block, slots * block), BF16)
-    high, low, scale = pl.pallas_call(
-        functools.partial(tiles_kernel, plan),
-        out_shape=(tiles_shape, tiles_shape, shape((flat, columns), F32)),
+    lines = weights.reshape(features // block, block)
+    high, low = pl.pallas_call(
+        tiles_kernel,
+        out_shape=(tiles_shape, tiles_shape),
         in_specs=[scalars(), scalars(), whole(), whole()],
-        out_specs=(whole(),) * 3,
-        scratch_shapes=[pltpu.VMEM((max(flat, block), block), F32)],
+        out_specs=(whole(), whole()),
         compiler_params=params,
         cost_estimate=pl.CostEstimate(flops=1 << 20, bytes_accessed=4 << 20, transcendentals=0),
         name="tiles",
-    )(rows, counts, blocks, weights.reshape(features // block, block))
+    )(rows, counts, blocks, lines)
+    scale = pl.pallas_call(
+        functools.partial(scale_kernel, plan),
+        out_shape=shape((flat, columns), F32),
+        in_specs=[whole()],
+        out_specs=whole(),
+        scratch_shapes=[pltpu.VMEM((max(flat, block), block), F32)],
+        compiler_params=params,
+        name="scale",
+    )(lines)
 
     middle = chunk // 2
     others = range(1, plan.plane)
     got = {p: plan.swap(send[p], 1) for p in (*others, 0)}
     chip = [(keep[p * chunk : (p + 1) * chunk] + got[p].astype(F32)).astype(BF16) for p in others]
+    chip, got[0] = lax.optimization_barrier((chip, got[0]))
     far_sent = [plan.swap_plane(chip[p - 1][middle:], p) for p in others]
     near_sent = [plan.swap_plane(chip[p - 1][:middle], p) for p in others]
-    near_sent, high, low, scale = lax.optimization_barrier((near_sent, high, low, scale))
+    near_sent, scale = lax.optimization_barrier((near_sent, scale))
 
     def plane_sum(sent, at, dtypes):
         return pl.pallas_call(
@@ -311,6 +328,7 @@
     far = [plan.swap_line(part, split_at + q) for q, part in enumerate(far)]
     held, *near = plane_sum(near_sent, 0, [F32] + [BF16] * (split_at - 1))
     near = [plan.swap_line(part, 1 + q) for q, part in enumerate(near)]
+    near, far, high, low = lax.optimization_barrier((near, far, high, low))
     mine, rounded = pl.pallas_call(
         line_kernel,
         out_shape=(shape((flat, columns), F32), shape((flat, columns), BF16)),
@@ -322,11 +340,9 @@
 
     line = [rounded] + [plan.swap_line(rounded, q) for q in range(1, plan.line)]
     near, far = jnp.concatenate(line[:split_at], axis=0), jnp.concatenate(line[split_at:], axis=0)
-    own = [near, far]
-    near = [plan.swap_plane(near, p) for p in others]
-    far = [plan.swap_plane(far, p) for p in others]
-    for pair in zip(near, far):
-        own += pair
+    near = [near] + [plan.swap_plane(near, p) for p in others]
+    far = [far] + [plan.swap_plane(far, p) for p in others]
+    own = far + near
     other = [plan.swap(part, 1) for part in own]
 
     return pl.pallas_call(

time: 73 us -> 71 us (0.973)
  waiting for transfers between devices: 16.9 us -> 14.7 us
    ppermute x30, waiting for transfers between devices: 16.9 us -> 14.7 us  [swap(): return lax.ppermute(value, AXES, [(d, d ^ mask) for d in range(self.count)])]
where the time goes in v8:
time: 71 us; the launch traced here: 70.8 us
  starting transfers between devices  30.4 us (43%)
  Pallas kernels  24.6 us (35%)
  waiting for transfers between devices  14.7 us (21%)
  between operations  0.79 us (1%)
    ppermute x30, starting transfers between devices, swap(): return lax.ppermute(value, AXES, [(d, d ^ mask) for d in range(self.count)])  30.4 us
    pallas_call x1, Pallas kernels, body(): pl.pallas_call(functools.partial(last_kernel, plan, features), out_shape=...  19.9 us
    ppermute x30, waiting for transfers between devices, swap(): return lax.ppermute(value, AXES, [(d, d ^ mask) for d in range(self.count)])  14.7 us
    pallas_call x1, Pallas kernels, body(): pl.pallas_call(functools.partial(sum_kernel, plan), out_shape=(pltpu.VMEM...  3.12 us
  transfers between devices with their start and end apart: 30, of which 17 were waited for; matrix products, arithmetic and copies ran while one was open for 0% of the time, Pallas kernels for 2%

profile of v8, /device:TPU:0, one launch (start us, length us, event | category | flops | bytes accessed | tf_op | source)
XLA Modules:
  0.0 70.8 jit_solution(7145998882070031136)
XLA Ops:
  0.6 3.1 %local_sum.1 = (f32[4096,128]{1,0:T(8,128)S(1)}, bf16[1024,128]{1,0:T(8,128)(2,1)S(1)}, bf16[1024,128]{1,0:T(8,128)(2,1)S(1)}, bf16[1024,128]{1,0:T(8,128)(2,1)S(1)}, bf16[1024,128]{1,0:T(8,128)(2,1)S(1)}) custom-call(s32[3,16]{1,0:T(4,128)} %bitcast.4, s32[16]{0:T(128)} %counts_ref.3, bf16[16,3,128,128]{3,2,1,0:T(8,128)(2,1)} %blocks_ref.3, ...), custom_call_target="tpu_custom_call" | custom-call | tf_op jit(solution)/shard_map/local_sum/pallas_call | solution.py:270
  6.6 2.9 %collective-permute-start.8 = (bf16[512,128]{1,0:T(8,128)(2,1)S(1)}, bf16[512,128]{1,0:T(8,128)(2,1)S(1)}, u32[]{:S(2)}, u32[]{:S(2)}) collective-permute-start(bf16[512,128]{1,0:T(8,128)(2,1)S(1)} %get-tuple-element.61), channel_id=1, source_target_pairs={{0,2},{1,3},{2,0},{3,1},{4,6},{5,7},{6,4},{7,5},{8,10},{9,11},{10,... | collective-permute-start | bytes 393224 | tf_op jit(solution)/shard_map/ppermute | solution.py:56
  9.5 1.6 %collective-permute-start.9 = (bf16[512,128]{1,0:T(8,128)(2,1)S(1)}, bf16[512,128]{1,0:T(8,128)(2,1)S(1)}, u32[]{:S(2)}, u32[]{:S(2)}) collective-permute-start(bf16[512,128]{1,0:T(8,128)(2,1)S(1)} %get-tuple-element.59), channel_id=1, source_target_pairs={{0,4},{1,5},{2,6},{3,7},{4,0},{5,1},{6,2},{7,3},{8,12},{9,13},{10,... | collective-permute-start | bytes 393224 | tf_op jit(solution)/shard_map/ppermute | solution.py:56
  11.2 2.0 %collective-permute-start.4 = (bf16[512,128]{1,0:T(8,128)(2,1)S(1)}, bf16[512,128]{1,0:T(8,128)(2,1)S(1)}, u32[]{:S(2)}, u32[]{:S(2)}) collective-permute-start(bf16[512,128]{1,0:T(8,128)(2,1)S(1)} %get-tuple-element.62), channel_id=1, source_target_pairs={{0,2},{1,3},{2,0},{3,1},{4,6},{5,7},{6,4},{7,5},{8,10},{9,11},{10,... | collective-permute-start | bytes 393224 | tf_op jit(solution)/shard_map/ppermute | solution.py:56
  13.2 1.5 %collective-permute-start.5 = (bf16[512,128]{1,0:T(8,128)(2,1)S(1)}, bf16[512,128]{1,0:T(8,128)(2,1)S(1)}, u32[]{:S(2)}, u32[]{:S(2)}) collective-permute-start(bf16[512,128]{1,0:T(8,128)(2,1)S(1)} %get-tuple-element.60), channel_id=1, source_target_pairs={{0,4},{1,5},{2,6},{3,7},{4,0},{5,1},{6,2},{7,3},{8,12},{9,13},{10,... | collective-permute-start | bytes 393224 | tf_op jit(solution)/shard_map/ppermute | solution.py:56
  14.7 2.1 %collective-permute-start.6 = (bf16[512,128]{1,0:T(8,128)(2,1)S(1)}, bf16[512,128]{1,0:T(8,128)(2,1)S(1)}, u32[]{:S(2)}, u32[]{:S(2)}) collective-permute-start(bf16[512,128]{1,0:T(8,128)(2,1)S(1)} %get-tuple-element.58), channel_id=1, source_target_pairs={{0,6},{1,7},{2,4},{3,5},{4,2},{5,3},{6,0},{7,1},{8,14},{9,15},{10,... | collective-permute-start | bytes 393224 | tf_op jit(solution)/shard_map/ppermute | solution.py:56
  16.9 1.7 %collective-permute-done.9.rest_1_ = bf16[512,128]{1,0:T(8,128)(2,1)S(1)} collective-permute-done((bf16[512,128]{1,0:T(8,128)(2,1)S(1)}, bf16[512,128]{1,0:T(8,128)(2,1)S(1)}, u32[]{:S(2)}, u32[]{:S(2)}) %collective-permute-start.9) | collective-permute-done | bytes 131104 | tf_op jit(solution)/shard_map/ppermute | solution.py:56
  18.7 2.6 %collective-permute-start.11 = (bf16[256,128]{1,0:T(8,128)(2,1)S(1)}, bf16[256,128]{1,0:T(8,128)(2,1)S(1)}, u32[]{:S(2)}, u32[]{:S(2)}) collective-permute-start(bf16[256,128]{1,0:T(8,128)(2,1)S(1)} %get-tuple-element.41), channel_id=1, source_target_pairs={{0,16},{1,17},{2,18},{3,19},{4,20},{5,21},{6,22},{7,23},{8,24},{9,... | collective-permute-start | bytes 196616 | tf_op jit(solution)/shard_map/ppermute | solution.py:56
  21.3 1.3 %collective-permute-start.12 = (bf16[256,128]{1,0:T(8,128)(2,1)S(1)}, bf16[256,128]{1,0:T(8,128)(2,1)S(1)}, u32[]{:S(2)}, u32[]{:S(2)}) collective-permute-start(bf16[256,128]{1,0:T(8,128)(2,1)S(1)} %get-tuple-element.42), channel_id=1, source_target_pairs={{0,24},{1,25},{2,26},{3,27},{4,28},{5,29},{6,30},{7,31},{8,16},{9,... | collective-permute-start | bytes 196616 | tf_op jit(solution)/shard_map/ppermute | solution.py:56
  23.4 1.6 %collective-permute-start.7 = (bf16[256,128]{1,0:T(8,128)(2,1)S(1)}, bf16[256,128]{1,0:T(8,128)(2,1)S(1)}, u32[]{:S(2)}, u32[]{:S(2)}) collective-permute-start(bf16[256,128]{1,0:T(8,128)(2,1)S(1)} %get-tuple-element.40), channel_id=1, source_target_pairs={{0,8},{1,9},{2,10},{3,11},{4,12},{5,13},{6,14},{7,15},{8,0},{9,1},... | collective-permute-start | bytes 196616 | tf_op jit(solution)/shard_map/ppermute | solution.py:56
  25.0 1.3 %tiles.1 = (bf16[16,128,384]{2,1,0:T(8,128)(2,1)S(1)}, bf16[16,128,384]{2,1,0:T(8,128)(2,1)S(1)}) custom-call(s32[3,16]{1,0:T(4,128)S(1)} %bitcast.5, s32[16]{0:T(128)S(1)} %copy-done.3, bf16[16,3,128,128]{3,2,1,0:T(8,128)(2,1)S(1)} %copy-done, f32[64,128]{1,0:T(8,128)S(1)} %bitcast.3), custom_call_target="tpu_custom_call" | custom-call | flops 1048576 | bytes 4194304 | tf_op jit(solution)/shard_map/tiles/pallas_call | solution.py:287
  28.2 1.2 %collective-permute-start.18 = (bf16[256,128]{1,0:T(8,128)(2,1)S(1)}, bf16[256,128]{1,0:T(8,128)(2,1)S(1)}, u32[]{:S(2)}, u32[]{:S(2)}) collective-permute-start(bf16[256,128]{1,0:T(8,128)(2,1)S(1)} %get-tuple-element.53), channel_id=1, source_target_pairs={{0,8},{1,9},{2,10},{3,11},{4,12},{5,13},{6,14},{7,15},{8,0},{9,1},... | collective-permute-start | bytes 196616 | tf_op jit(solution)/shard_map/ppermute | solution.py:56
  29.4 2.5 %collective-permute-start.14 = (bf16[256,128]{1,0:T(8,128)(2,1)S(1)}, bf16[256,128]{1,0:T(8,128)(2,1)S(1)}, u32[]{:S(2)}, u32[]{:S(2)}) collective-permute-start(bf16[256,128]{1,0:T(8,128)(2,1)S(1)} %get-tuple-element.53), channel_id=1, source_target_pairs={{0,24},{1,25},{2,26},{3,27},{4,28},{5,29},{6,30},{7,31},{8,16},{9,... | collective-permute-start | bytes 196616 | tf_op jit(solution)/shard_map/ppermute | solution.py:56
  32.0 1.2 %collective-permute-done.18 = bf16[256,128]{1,0:T(8,128)(2,1)S(1)} collective-permute-done((bf16[256,128]{1,0:T(8,128)(2,1)S(1)}, bf16[256,128]{1,0:T(8,128)(2,1)S(1)}, u32[]{:S(2)}, u32[]{:S(2)}) %collective-permute-start.18) | collective-permute-done | bytes 65568 | tf_op jit(solution)/shard_map/ppermute | solution.py:56
  33.3 1.2 %collective-permute-start.21 = (bf16[512,128]{1,0:T(8,128)(2,1)S(1)}, bf16[512,128]{1,0:T(8,128)(2,1)S(1)}, u32[]{:S(2)}, u32[]{:S(2)}) collective-permute-start(bf16[512,128]{1,0:T(8,128)(2,1)S(1)} %constant_dynamic-update-slice_fusion.2.rest_4_), channel_id=1, source_target_pairs={{0,6},{1,7},{2,4},{3,5},{4,2},{5,3},{6,0},{7,1},{8,14},{9,15},{10,... | collective-permute-start | bytes 393224 | tf_op jit(solution)/shard_map/ppermute | solution.py:56
  34.4 1.5 %collective-permute-start.20 = (bf16[512,128]{1,0:T(8,128)(2,1)S(1)}, bf16[512,128]{1,0:T(8,128)(2,1)S(1)}, u32[]{:S(2)}, u32[]{:S(2)}) collective-permute-start(bf16[512,128]{1,0:T(8,128)(2,1)S(1)} %constant_dynamic-update-slice_fusion.2.rest_4_), channel_id=1, source_target_pairs={{0,4},{1,5},{2,6},{3,7},{4,0},{5,1},{6,2},{7,3},{8,12},{9,13},{10,... | collective-permute-start | bytes 393224 | tf_op jit(solution)/shard_map/ppermute | solution.py:56
  35.9 1.8 %collective-permute-done.13 = bf16[256,128]{1,0:T(8,128)(2,1)S(1)} collective-permute-done((bf16[256,128]{1,0:T(8,128)(2,1)S(1)}, bf16[256,128]{1,0:T(8,128)(2,1)S(1)}, u32[]{:S(2)}, u32[]{:S(2)}) %collective-permute-start.13) | collective-permute-done | bytes 65568 | tf_op jit(solution)/shard_map/ppermute | solution.py:56
  37.7 1.2 %collective-permute-start.19 = (bf16[512,128]{1,0:T(8,128)(2,1)S(1)}, bf16[512,128]{1,0:T(8,128)(2,1)S(1)}, u32[]{:S(2)}, u32[]{:S(2)}) collective-permute-start(bf16[512,128]{1,0:T(8,128)(2,1)S(1)} %constant_dynamic-update-slice_fusion.2.rest_4_), channel_id=1, source_target_pairs={{0,2},{1,3},{2,0},{3,1},{4,6},{5,7},{6,4},{7,5},{8,10},{9,11},{10,... | collective-permute-start | bytes 393224 | tf_op jit(solution)/shard_map/ppermute | solution.py:56
  39.0 2.1 %collective-permute-start.17 = (bf16[512,128]{1,0:T(8,128)(2,1)S(1)}, bf16[512,128]{1,0:T(8,128)(2,1)S(1)}, u32[]{:S(2)}, u32[]{:S(2)}) collective-permute-start(bf16[512,128]{1,0:T(8,128)(2,1)S(1)} %constant_dynamic-update-slice_fusion.rest_0_), channel_id=1, source_target_pairs={{0,6},{1,7},{2,4},{3,5},{4,2},{5,3},{6,0},{7,1},{8,14},{9,15},{10,... | collective-permute-start | bytes 393224 | tf_op jit(solution)/shard_map/ppermute | solution.py:56
  41.2 1.3 %collective-permute-start.16 = (bf16[512,128]{1,0:T(8,128)(2,1)S(1)}, bf16[512,128]{1,0:T(8,128)(2,1)S(1)}, u32[]{:S(2)}, u32[]{:S(2)}) collective-permute-start(bf16[512,128]{1,0:T(8,128)(2,1)S(1)} %constant_dynamic-update-slice_fusion.rest_0_), channel_id=1, source_target_pairs={{0,4},{1,5},{2,6},{3,7},{4,0},{5,1},{6,2},{7,3},{8,12},{9,13},{10,... | collective-permute-start | bytes 393224 | tf_op jit(solution)/shard_map/ppermute | solution.py:56
  42.8 1.3 %collective-permute-start.15 = (bf16[512,128]{1,0:T(8,128)(2,1)S(1)}, bf16[512,128]{1,0:T(8,128)(2,1)S(1)}, u32[]{:S(2)}, u32[]{:S(2)}) collective-permute-start(bf16[512,128]{1,0:T(8,128)(2,1)S(1)} %constant_dynamic-update-slice_fusion.rest_0_), channel_id=1, source_target_pairs={{0,2},{1,3},{2,0},{3,1},{4,6},{5,7},{6,4},{7,5},{8,10},{9,11},{10,... | collective-permute-start | bytes 393224 | tf_op jit(solution)/shard_map/ppermute | solution.py:56
  44.7 2.9 %collective-permute-done.17.rest_3_ = bf16[512,128]{1,0:T(8,128)(2,1)S(1)} collective-permute-done((bf16[512,128]{1,0:T(8,128)(2,1)S(1)}, bf16[512,128]{1,0:T(8,128)(2,1)S(1)}, u32[]{:S(2)}, u32[]{:S(2)}) %collective-permute-start.17) | collective-permute-done | bytes 131104 | tf_op jit(solution)/shard_map/ppermute | solution.py:56
  47.6 1.5 %collective-permute-done.16.rest_2_ = bf16[512,128]{1,0:T(8,128)(2,1)S(1)} collective-permute-done((bf16[512,128]{1,0:T(8,128)(2,1)S(1)}, bf16[512,128]{1,0:T(8,128)(2,1)S(1)}, u32[]{:S(2)}, u32[]{:S(2)}) %collective-permute-start.16) | collective-permute-done | bytes 131104 | tf_op jit(solution)/shard_map/ppermute | solution.py:56
  50.9 19.9 %factors.1 = (f32[256,128]{1,0:T(8,128)}, bf16[2048,128]{1,0:T(8,128)(2,1)}) custom-call(s32[3,16]{1,0:T(4,128)S(1)} %bitcast.6, bf16[16,128,384]{2,1,0:T(8,128)(2,1)S(1)} %get-tuple-element.45.high_ref, bf16[16,128,384]{2,1,0:T(8,128)(2,1)S(1)} %get-tuple-element.46.low_ref, f32[256,128]{1,0:T(8,128)S(1)} %get-tuple-element.52.mine_ref, ...), custom_call_target="tpu_custom_call" | custom-call | tf_op jit(solution)/shard_map/factors/pallas_call | solution.py:348
  (59 shorter events, 8.8 us)
Async XLA Ops:
  4.4 1.8 %collective-permute-start.2 = (bf16[1024,128]{1,0:T(8,128)(2,1)S(1)}, bf16[1024,128]{1,0:T(8,128)(2,1)S(1)}, u32[]{:S(2)}, u32[]{:S(2)}) collective-permute-start(bf16[1024,128]{1,0:T(8,128)(2,1)S(1)} %get-tuple-element.31), channel_id=1, source_target_pairs={{0,1},{1,0},{2,3},{3,2},{4,5},{5,4},{6,7},{7,6},{8,9},{9,8},{10,11... | collective-permute-start | bytes 786440 | tf_op jit(solution)/shard_map/ppermute | solution.py:56
  6.6 8.1 %collective-permute-start.8 = (bf16[512,128]{1,0:T(8,128)(2,1)S(1)}, bf16[512,128]{1,0:T(8,128)(2,1)S(1)}, u32[]{:S(2)}, u32[]{:S(2)}) collective-permute-start(bf16[512,128]{1,0:T(8,128)(2,1)S(1)} %get-tuple-element.61), channel_id=1, source_target_pairs={{0,2},{1,3},{2,0},{3,1},{4,6},{5,7},{6,4},{7,5},{8,10},{9,11},{10,... | collective-permute-start | bytes 393224 | tf_op jit(solution)/shard_map/ppermute | solution.py:56
  9.5 9.1 %collective-permute-start.9 = (bf16[512,128]{1,0:T(8,128)(2,1)S(1)}, bf16[512,128]{1,0:T(8,128)(2,1)S(1)}, u32[]{:S(2)}, u32[]{:S(2)}) collective-permute-start(bf16[512,128]{1,0:T(8,128)(2,1)S(1)} %get-tuple-element.59), channel_id=1, source_target_pairs={{0,4},{1,5},{2,6},{3,7},{4,0},{5,1},{6,2},{7,3},{8,12},{9,13},{10,... | collective-permute-start | bytes 393224 | tf_op jit(solution)/shard_map/ppermute | solution.py:56
  11.1 7.5 %collective-permute-start.10 = (bf16[512,128]{1,0:T(8,128)(2,1)S(1)}, bf16[512,128]{1,0:T(8,128)(2,1)S(1)}, u32[]{:S(2)}, u32[]{:S(2)}) collective-permute-start(bf16[512,128]{1,0:T(8,128)(2,1)S(1)} %get-tuple-element.57), channel_id=1, source_target_pairs={{0,6},{1,7},{2,4},{3,5},{4,2},{5,3},{6,0},{7,1},{8,14},{9,15},{10,... | collective-permute-start | bytes 393224 | tf_op jit(solution)/shard_map/ppermute | solution.py:56
  11.2 11.5 %collective-permute-start.4 = (bf16[512,128]{1,0:T(8,128)(2,1)S(1)}, bf16[512,128]{1,0:T(8,128)(2,1)S(1)}, u32[]{:S(2)}, u32[]{:S(2)}) collective-permute-start(bf16[512,128]{1,0:T(8,128)(2,1)S(1)} %get-tuple-element.62), channel_id=1, source_target_pairs={{0,2},{1,3},{2,0},{3,1},{4,6},{5,7},{6,4},{7,5},{8,10},{9,11},{10,... | collective-permute-start | bytes 393224 | tf_op jit(solution)/shard_map/ppermute | solution.py:56
  13.2 10.1 %collective-permute-start.5 = (bf16[512,128]{1,0:T(8,128)(2,1)S(1)}, bf16[512,128]{1,0:T(8,128)(2,1)S(1)}, u32[]{:S(2)}, u32[]{:S(2)}) collective-permute-start(bf16[512,128]{1,0:T(8,128)(2,1)S(1)} %get-tuple-element.60), channel_id=1, source_target_pairs={{0,4},{1,5},{2,6},{3,7},{4,0},{5,1},{6,2},{7,3},{8,12},{9,13},{10,... | collective-permute-start | bytes 393224 | tf_op jit(solution)/shard_map/ppermute | solution.py:56
  14.7 8.6 %collective-permute-start.6 = (bf16[512,128]{1,0:T(8,128)(2,1)S(1)}, bf16[512,128]{1,0:T(8,128)(2,1)S(1)}, u32[]{:S(2)}, u32[]{:S(2)}) collective-permute-start(bf16[512,128]{1,0:T(8,128)(2,1)S(1)} %get-tuple-element.58), channel_id=1, source_target_pairs={{0,6},{1,7},{2,4},{3,5},{4,2},{5,3},{6,0},{7,1},{8,14},{9,15},{10,... | collective-permute-start | bytes 393224 | tf_op jit(solution)/shard_map/ppermute | solution.py:56
  18.7 7.6 %collective-permute-start.11 = (bf16[256,128]{1,0:T(8,128)(2,1)S(1)}, bf16[256,128]{1,0:T(8,128)(2,1)S(1)}, u32[]{:S(2)}, u32[]{:S(2)}) collective-permute-start(bf16[256,128]{1,0:T(8,128)(2,1)S(1)} %get-tuple-element.41), channel_id=1, source_target_pairs={{0,16},{1,17},{2,18},{3,19},{4,20},{5,21},{6,22},{7,23},{8,24},{9,... | collective-permute-start | bytes 196616 | tf_op jit(solution)/shard_map/ppermute | solution.py:56
  21.3 6.1 %collective-permute-start.12 = (bf16[256,128]{1,0:T(8,128)(2,1)S(1)}, bf16[256,128]{1,0:T(8,128)(2,1)S(1)}, u32[]{:S(2)}, u32[]{:S(2)}) collective-permute-start(bf16[256,128]{1,0:T(8,128)(2,1)S(1)} %get-tuple-element.42), channel_id=1, source_target_pairs={{0,24},{1,25},{2,26},{3,27},{4,28},{5,29},{6,30},{7,31},{8,16},{9,... | collective-permute-start | bytes 196616 | tf_op jit(solution)/shard_map/ppermute | solution.py:56
  23.4 4.7 %collective-permute-start.7 = (bf16[256,128]{1,0:T(8,128)(2,1)S(1)}, bf16[256,128]{1,0:T(8,128)(2,1)S(1)}, u32[]{:S(2)}, u32[]{:S(2)}) collective-permute-start(bf16[256,128]{1,0:T(8,128)(2,1)S(1)} %get-tuple-element.40), channel_id=1, source_target_pairs={{0,8},{1,9},{2,10},{3,11},{4,12},{5,13},{6,14},{7,15},{8,0},{9,1},... | collective-permute-start | bytes 196616 | tf_op jit(solution)/shard_map/ppermute | solution.py:56
  28.2 5.0 %collective-permute-start.18 = (bf16[256,128]{1,0:T(8,128)(2,1)S(1)}, bf16[256,128]{1,0:T(8,128)(2,1)S(1)}, u32[]{:S(2)}, u32[]{:S(2)}) collective-permute-start(bf16[256,128]{1,0:T(8,128)(2,1)S(1)} %get-tuple-element.53), channel_id=1, source_target_pairs={{0,8},{1,9},{2,10},{3,11},{4,12},{5,13},{6,14},{7,15},{8,0},{9,1},... | collective-permute-start | bytes 196616 | tf_op jit(solution)/shard_map/ppermute | solution.py:56
  29.4 9.5 %collective-permute-start.14 = (bf16[256,128]{1,0:T(8,128)(2,1)S(1)}, bf16[256,128]{1,0:T(8,128)(2,1)S(1)}, u32[]{:S(2)}, u32[]{:S(2)}) collective-permute-start(bf16[256,128]{1,0:T(8,128)(2,1)S(1)} %get-tuple-element.53), channel_id=1, source_target_pairs={{0,24},{1,25},{2,26},{3,27},{4,28},{5,29},{6,30},{7,31},{8,16},{9,... | collective-permute-start | bytes 196616 | tf_op jit(solution)/shard_map/ppermute | solution.py:56
  31.9 5.9 %collective-permute-start.13 = (bf16[256,128]{1,0:T(8,128)(2,1)S(1)}, bf16[256,128]{1,0:T(8,128)(2,1)S(1)}, u32[]{:S(2)}, u32[]{:S(2)}) collective-permute-start(bf16[256,128]{1,0:T(8,128)(2,1)S(1)} %get-tuple-element.53), channel_id=1, source_target_pairs={{0,16},{1,17},{2,18},{3,19},{4,20},{5,21},{6,22},{7,23},{8,24},{9,... | collective-permute-start | bytes 196616 | tf_op jit(solution)/shard_map/ppermute | solution.py:56
  33.2 5.8 %collective-permute-start.26 = (bf16[512,128]{1,0:T(8,128)(2,1)S(1)}, bf16[512,128]{1,0:T(8,128)(2,1)S(1)}, u32[]{:S(2)}, u32[]{:S(2)}) collective-permute-start(bf16[512,128]{1,0:T(8,128)(2,1)S(1)} %constant_dynamic-update-slice_fusion.2.rest_4_), channel_id=1, source_target_pairs={{0,1},{1,0},{2,3},{3,2},{4,5},{5,4},{6,7},{7,6},{8,9},{9,8},{10,11... | collective-permute-start | bytes 393224 | tf_op jit(solution)/shard_map/ppermute | solution.py:56
  33.3 7.9 %collective-permute-start.21 = (bf16[512,128]{1,0:T(8,128)(2,1)S(1)}, bf16[512,128]{1,0:T(8,128)(2,1)S(1)}, u32[]{:S(2)}, u32[]{:S(2)}) collective-permute-start(bf16[512,128]{1,0:T(8,128)(2,1)S(1)} %constant_dynamic-update-slice_fusion.2.rest_4_), channel_id=1, source_target_pairs={{0,6},{1,7},{2,4},{3,5},{4,2},{5,3},{6,0},{7,1},{8,14},{9,15},{10,... | collective-permute-start | bytes 393224 | tf_op jit(solution)/shard_map/ppermute | solution.py:56
  34.4 8.4 %collective-permute-start.20 = (bf16[512,128]{1,0:T(8,128)(2,1)S(1)}, bf16[512,128]{1,0:T(8,128)(2,1)S(1)}, u32[]{:S(2)}, u32[]{:S(2)}) collective-permute-start(bf16[512,128]{1,0:T(8,128)(2,1)S(1)} %constant_dynamic-update-slice_fusion.2.rest_4_), channel_id=1, source_target_pairs={{0,4},{1,5},{2,6},{3,7},{4,0},{5,1},{6,2},{7,3},{8,12},{9,13},{10,... | collective-permute-start | bytes 393224 | tf_op jit(solution)/shard_map/ppermute | solution.py:56
  37.7 6.4 %collective-permute-start.19 = (bf16[512,128]{1,0:T(8,128)(2,1)S(1)}, bf16[512,128]{1,0:T(8,128)(2,1)S(1)}, u32[]{:S(2)}, u32[]{:S(2)}) collective-permute-start(bf16[512,128]{1,0:T(8,128)(2,1)S(1)} %constant_dynamic-update-slice_fusion.2.rest_4_), channel_id=1, source_target_pairs={{0,2},{1,3},{2,0},{3,1},{4,6},{5,7},{6,4},{7,5},{8,10},{9,11},{10,... | collective-permute-start | bytes 393224 | tf_op jit(solution)/shard_map/ppermute | solution.py:56
  39.0 5.2 %collective-permute-start.22 = (bf16[512,128]{1,0:T(8,128)(2,1)S(1)}, bf16[512,128]{1,0:T(8,128)(2,1)S(1)}, u32[]{:S(2)}, u32[]{:S(2)}) collective-permute-start(bf16[512,128]{1,0:T(8,128)(2,1)S(1)} %constant_dynamic-update-slice_fusion.rest_0_), channel_id=1, source_target_pairs={{0,1},{1,0},{2,3},{3,2},{4,5},{5,4},{6,7},{7,6},{8,9},{9,8},{10,11... | collective-permute-start | bytes 393224 | tf_op jit(solution)/shard_map/ppermute | solution.py:56
  39.0 8.6 %collective-permute-start.17 = (bf16[512,128]{1,0:T(8,128)(2,1)S(1)}, bf16[512,128]{1,0:T(8,128)(2,1)S(1)}, u32[]{:S(2)}, u32[]{:S(2)}) collective-permute-start(bf16[512,128]{1,0:T(8,128)(2,1)S(1)} %constant_dynamic-update-slice_fusion.rest_0_), channel_id=1, source_target_pairs={{0,6},{1,7},{2,4},{3,5},{4,2},{5,3},{6,0},{7,1},{8,14},{9,15},{10,... | collective-permute-start | bytes 393224 | tf_op jit(solution)/shard_map/ppermute | solution.py:56
  41.2 7.9 %collective-permute-start.16 = (bf16[512,128]{1,0:T(8,128)(2,1)S(1)}, bf16[512,128]{1,0:T(8,128)(2,1)S(1)}, u32[]{:S(2)}, u32[]{:S(2)}) collective-permute-start(bf16[512,128]{1,0:T(8,128)(2,1)S(1)} %constant_dynamic-update-slice_fusion.rest_0_), channel_id=1, source_target_pairs={{0,4},{1,5},{2,6},{3,7},{4,0},{5,1},{6,2},{7,3},{8,12},{9,13},{10,... | collective-permute-start | bytes 393224 | tf_op jit(solution)/shard_map/ppermute | solution.py:56
  42.8 6.3 %collective-permute-start.15 = (bf16[512,128]{1,0:T(8,128)(2,1)S(1)}, bf16[512,128]{1,0:T(8,128)(2,1)S(1)}, u32[]{:S(2)}, u32[]{:S(2)}) collective-permute-start(bf16[512,128]{1,0:T(8,128)(2,1)S(1)} %constant_dynamic-update-slice_fusion.rest_0_), channel_id=1, source_target_pairs={{0,2},{1,3},{2,0},{3,1},{4,6},{5,7},{6,4},{7,5},{8,10},{9,11},{10,... | collective-permute-start | bytes 393224 | tf_op jit(solution)/shard_map/ppermute | solution.py:56
  44.2 5.4 %collective-permute-start.29 = (bf16[512,128]{1,0:T(8,128)(2,1)S(1)}, bf16[512,128]{1,0:T(8,128)(2,1)S(1)}, u32[]{:S(2)}, u32[]{:S(2)}) collective-permute-start(bf16[512,128]{1,0:T(8,128)(2,1)S(1)} %collective-permute-done.21.rest_7_), channel_id=1, source_target_pairs={{0,1},{1,0},{2,3},{3,2},{4,5},{5,4},{6,7},{7,6},{8,9},{9,8},{10,11... | collective-permute-start | bytes 393224 | tf_op jit(solution)/shard_map/ppermute | solution.py:56
  44.2 5.5 %collective-permute-start.28 = (bf16[512,128]{1,0:T(8,128)(2,1)S(1)}, bf16[512,128]{1,0:T(8,128)(2,1)S(1)}, u32[]{:S(2)}, u32[]{:S(2)}) collective-permute-start(bf16[512,128]{1,0:T(8,128)(2,1)S(1)} %collective-permute-done.20.rest_6_), channel_id=1, source_target_pairs={{0,1},{1,0},{2,3},{3,2},{4,5},{5,4},{6,7},{7,6},{8,9},{9,8},{10,11... | collective-permute-start | bytes 393224 | tf_op jit(solution)/shard_map/ppermute | solution.py:56
  47.6 2.0 %collective-permute-start.27 = (bf16[512,128]{1,0:T(8,128)(2,1)S(1)}, bf16[512,128]{1,0:T(8,128)(2,1)S(1)}, u32[]{:S(2)}, u32[]{:S(2)}) collective-permute-start(bf16[512,128]{1,0:T(8,128)(2,1)S(1)} %collective-permute-done.19.rest_5_), channel_id=1, source_target_pairs={{0,1},{1,0},{2,3},{3,2},{4,5},{5,4},{6,7},{7,6},{8,9},{9,8},{10,11... | collective-permute-start | bytes 393224 | tf_op jit(solution)/shard_map/ppermute | solution.py:56
  (10 other events, 38.6 us)

commit v9 on v8

--- a/solution.py
+++ b/solution.py
@@ -62,11 +62,11 @@
         return self.swap(value, member << (1 + self.plane_bits))
 
 
-def sum_kernel(plan, rows_ref, counts_ref, blocks_ref, sketch_ref, keep_ref, *rest):
-    send_refs, (total_ref, tiles_ref, docs_ref, sems) = rest[: plan.plane], rest[plan.plane :]
+def sum_kernel(plan, rows_ref, counts_ref, blocks_ref, sketch_ref, total_ref, *rest):
+    send_refs, (tiles_ref, docs_ref, sems) = rest[: plan.plane], rest[plan.plane :]
     me = plan.me()
     documents, slots, block, _ = tiles_ref.shape
-    half = keep_ref.shape[0]
+    half = total_ref.shape[0] // 2
     parts = sems.shape[0]
     per = documents // parts
     copies = []
@@ -92,7 +92,6 @@
                 for p in range(plan.pieces):
                     at = pl.ds(plan.start(me, rows_ref[s, d], p), plan.piece)
                     total_ref[at, :] += term[p * plan.piece : (p + 1) * plan.piece]
-    keep_ref[...] = total_ref[:half, :]
     for p, send_ref in enumerate(send_refs):
         size = send_ref.shape[0]
         send_ref[...] = total_ref[half + p * size : half + (p + 1) * size, :].astype(BF16)
@@ -121,14 +120,21 @@
     scale_ref[...] = turned_ref[pl.ds(pl.multiple_of(inside, plan.piece), plan.flat), :]
 
 
-def plane_kernel(flat, keep_ref, got_ref, *rest):
-    count = keep_ref.shape[0] // flat
-    parts, out_refs = (got_ref,) + rest[:-count], rest[-count:]
+def chip_kernel(start, total_ref, got_ref, far_ref, near_ref):
+    middle = near_ref.shape[0]
+    for ref, at in ((far_ref, middle), (near_ref, 0)):
+        held = total_ref[start + at : start + at + middle, :]
+        ref[...] = (held + got_ref[at : at + middle, :].astype(F32)).astype(BF16)
+
+
+def plane_kernel(flat, start, total_ref, got_ref, *rest):
+    count = rest[0].shape[0] // flat
+    parts, out_refs = rest[:-count], rest[-count:]
     for q, out_ref in enumerate(out_refs):
-        at = slice(q * flat, (q + 1) * flat)
-        total = keep_ref[at, :]
+        at = slice(start + q * flat, start + (q + 1) * flat)
+        total = total_ref[at, :] + got_ref[at, :].astype(F32)
         for ref in parts:
-            total = total + ref[at, :].astype(F32)
+            total = total + ref[q * flat : (q + 1) * flat, :].astype(F32)
         out_ref[...] = total.astype(out_ref.dtype)
 
 
@@ -267,13 +273,12 @@
     rows = rows.T
     parts = min(4, documents)
 
-    keep, *send = pl.pallas_call(
+    total, *send = pl.pallas_call(
         functools.partial(sum_kernel, plan),
-        out_shape=(pltpu.VMEM((half, columns), F32),) + (pltpu.VMEM((chunk, columns), BF16),) * plan.plane,
+        out_shape=(pltpu.VMEM((features, columns), F32),) + (pltpu.VMEM((chunk, columns), BF16),) * plan.plane,
         in_specs=[scalars(), scalars(), pl.BlockSpec(memory_space=pltpu.HBM), pl.BlockSpec(memory_space=pltpu.HBM)],
         out_specs=(whole(),) * (1 + plan.plane),
         scratch_shapes=[
-            pltpu.VMEM((features, columns), F32),
             pltpu.VMEM(blocks.shape, BF16),
             pltpu.VMEM(sketch.shape, BF16),
             pltpu.SemaphoreType.DMA((parts, 2)),
@@ -306,25 +311,34 @@
     middle = chunk // 2
     others = range(1, plan.plane)
     got = {p: plan.swap(send[p], 1) for p in (*others, 0)}
-    chip = [(keep[p * chunk : (p + 1) * chunk] + got[p].astype(F32)).astype(BF16) for p in others]
-    chip, got[0] = lax.optimization_barrier((chip, got[0]))
-    far_sent = [plan.swap_plane(chip[p - 1][middle:], p) for p in others]
-    near_sent = [plan.swap_plane(chip[p - 1][:middle], p) for p in others]
-    near_sent, scale = lax.optimization_barrier((near_sent, scale))
-
-    def plane_sum(sent, at, dtypes):
+    got[1], got[0] = lax.optimization_barrier((got[1], got[0]))
+    chip = {
+        p: pl.pallas_call(
+            functools.partial(chip_kernel, p * chunk),
+            out_shape=[shape((middle, columns), BF16)] * 2,
+            in_specs=[whole(), whole()],
+            out_specs=[whole()] * 2,
+            compiler_params=params,
+            name="chip_sum",
+        )(total, got[p])
+        for p in others
+    }
+    far_sent = [plan.swap_plane(chip[p][0], p) for p in reversed(others)]
+    near_sent = [plan.swap_plane(chip[p][1], p) for p in reversed(others)]
+    far_sent, scale = lax.optimization_barrier((far_sent, scale))
+
+    def plane_sum(sent, start, dtypes):
         return pl.pallas_call(
-            functools.partial(plane_kernel, flat),
-            grid=(1,),
+            functools.partial(plane_kernel, flat, start),
             out_shape=[shape((flat, columns), dtype) for dtype in dtypes],
-            in_specs=[pl.BlockSpec((middle, columns), lambda i: (at, 0))] * 2 + [whole()] * len(sent),
+            in_specs=[whole()] * (2 + len(sent)),
             out_specs=[whole()] * len(dtypes),
             compiler_params=params,
             name="plane_sum",
-        )(keep, got[0], *sent)
+        )(total, got[0], *sent)
 
     split_at = plan.line // 2
-    far = plane_sum(far_sent, 1, [BF16] * split_at)
+    far = plane_sum(far_sent, middle, [BF16] * split_at)
     far = [plan.swap_line(part, split_at + q) for q, part in enumerate(far)]
     held, *near = plane_sum(near_sent, 0, [F32] + [BF16] * (split_at - 1))
     near = [plan.swap_line(part, 1 + q) for q, part in enumerate(near)]

time: 71 us -> 68.2 us (0.961)
  waiting for transfers between devices: 14.7 us -> 11.7 us
    ppermute x30, waiting for transfers between devices: 14.7 us -> 11.7 us  [swap(): return lax.ppermute(value, AXES, [(d, d ^ mask) for d in range(self.count)])]
  transfers between devices with their start and end apart: 30 -> 30, of which waited for: 17 -> 14; matrix products, arithmetic and copies ran while one was open for 0% -> 0% of each run, Pallas kernels for 2% -> 2%
where the time goes in v9:
time: 68.2 us; the launch traced here: 68 us
  starting transfers between devices  30.9 us (45%)
  Pallas kernels  24.6 us (36%)
  waiting for transfers between devices  11.7 us (17%)
  between operations  0.73 us (1%)
    ppermute x30, starting transfers between devices, swap(): return lax.ppermute(value, AXES, [(d, d ^ mask) for d in range(self.count)])  30.9 us
    pallas_call x1, Pallas kernels, body(): pl.pallas_call(functools.partial(last_kernel, plan, features), out_shape=...  19.9 us
    ppermute x30, waiting for transfers between devices, swap(): return lax.ppermute(value, AXES, [(d, d ^ mask) for d in range(self.count)])  11.7 us
    pallas_call x1, Pallas kernels, body(): pl.pallas_call(functools.partial(sum_kernel, plan), out_shape=(pltpu.VMEM...  3 us
  transfers between devices with their start and end apart: 30, of which 14 were waited for; matrix products, arithmetic and copies ran while one was open for 0% of the time, Pallas kernels for 2%

profile of v9, /device:TPU:0, one launch (start us, length us, event | category | flops | bytes accessed | tf_op | source)
XLA Modules:
  0.0 68.0 jit_solution(6722982231866104623)
XLA Ops:
  0.6 3.0 %local_sum.1 = (f32[8192,128]{1,0:T(8,128)S(1)}, bf16[1024,128]{1,0:T(8,128)(2,1)S(1)}, bf16[1024,128]{1,0:T(8,128)(2,1)S(1)}, bf16[1024,128]{1,0:T(8,128)(2,1)S(1)}, bf16[1024,128]{1,0:T(8,128)(2,1)S(1)}) custom-call(s32[3,16]{1,0:T(4,128)} %bitcast.4, s32[16]{0:T(128)} %counts_ref.3, bf16[16,3,128,128]{3,2,1,0:T(8,128)(2,1)} %blocks_ref.3, ...), custom_call_target="tpu_custom_call" | custom-call | tf_op jit(solution)/shard_map/local_sum/pallas_call | solution.py:276
  5.7 2.9 %collective-permute-start.10 = (bf16[512,128]{1,0:T(8,128)(2,1)S(1)}, bf16[512,128]{1,0:T(8,128)(2,1)S(1)}, u32[]{:S(2)}, u32[]{:S(2)}) collective-permute-start(bf16[512,128]{1,0:T(8,128)(2,1)S(1)} %get-tuple-element.45), channel_id=1, source_target_pairs={{0,2},{1,3},{2,0},{3,1},{4,6},{5,7},{6,4},{7,5},{8,10},{9,11},{10,... | collective-permute-start | bytes 393224 | tf_op jit(solution)/shard_map/ppermute | solution.py:56
  8.7 1.6 %collective-permute-start.9 = (bf16[512,128]{1,0:T(8,128)(2,1)S(1)}, bf16[512,128]{1,0:T(8,128)(2,1)S(1)}, u32[]{:S(2)}, u32[]{:S(2)}) collective-permute-start(bf16[512,128]{1,0:T(8,128)(2,1)S(1)} %get-tuple-element.44), channel_id=1, source_target_pairs={{0,4},{1,5},{2,6},{3,7},{4,0},{5,1},{6,2},{7,3},{8,12},{9,13},{10,... | collective-permute-start | bytes 393224 | tf_op jit(solution)/shard_map/ppermute | solution.py:56
  10.6 1.8 %collective-permute-start.6 = (bf16[512,128]{1,0:T(8,128)(2,1)S(1)}, bf16[512,128]{1,0:T(8,128)(2,1)S(1)}, u32[]{:S(2)}, u32[]{:S(2)}) collective-permute-start(bf16[512,128]{1,0:T(8,128)(2,1)S(1)} %get-tuple-element.41), channel_id=1, source_target_pairs={{0,2},{1,3},{2,0},{3,1},{4,6},{5,7},{6,4},{7,5},{8,10},{9,11},{10,... | collective-permute-start | bytes 393224 | tf_op jit(solution)/shard_map/ppermute | solution.py:56
  12.4 1.5 %collective-permute-start.5 = (bf16[512,128]{1,0:T(8,128)(2,1)S(1)}, bf16[512,128]{1,0:T(8,128)(2,1)S(1)}, u32[]{:S(2)}, u32[]{:S(2)}) collective-permute-start(bf16[512,128]{1,0:T(8,128)(2,1)S(1)} %get-tuple-element.39), channel_id=1, source_target_pairs={{0,4},{1,5},{2,6},{3,7},{4,0},{5,1},{6,2},{7,3},{8,12},{9,13},{10,... | collective-permute-start | bytes 393224 | tf_op jit(solution)/shard_map/ppermute | solution.py:56
  13.9 2.0 %collective-permute-start.3 = (bf16[512,128]{1,0:T(8,128)(2,1)S(1)}, bf16[512,128]{1,0:T(8,128)(2,1)S(1)}, u32[]{:S(2)}, u32[]{:S(2)}) collective-permute-start(bf16[512,128]{1,0:T(8,128)(2,1)S(1)} %get-tuple-element.37), channel_id=1, source_target_pairs={{0,6},{1,7},{2,4},{3,5},{4,2},{5,3},{6,0},{7,1},{8,14},{9,15},{10,... | collective-permute-start | bytes 393224 | tf_op jit(solution)/shard_map/ppermute | solution.py:56
  16.1 1.7 %collective-permute-done.9.rest_1_ = bf16[512,128]{1,0:T(8,128)(2,1)S(1)} collective-permute-done((bf16[512,128]{1,0:T(8,128)(2,1)S(1)}, bf16[512,128]{1,0:T(8,128)(2,1)S(1)}, u32[]{:S(2)}, u32[]{:S(2)}) %collective-permute-start.9) | collective-permute-done | bytes 131104 | tf_op jit(solution)/shard_map/ppermute | solution.py:56
  17.9 2.6 %collective-permute-start.11 = (bf16[256,128]{1,0:T(8,128)(2,1)S(1)}, bf16[256,128]{1,0:T(8,128)(2,1)S(1)}, u32[]{:S(2)}, u32[]{:S(2)}) collective-permute-start(bf16[256,128]{1,0:T(8,128)(2,1)S(1)} %get-tuple-element.49), channel_id=1, source_target_pairs={{0,16},{1,17},{2,18},{3,19},{4,20},{5,21},{6,22},{7,23},{8,24},{9,... | collective-permute-start | bytes 196616 | tf_op jit(solution)/shard_map/ppermute | solution.py:56
  20.5 1.3 %collective-permute-start.12 = (bf16[256,128]{1,0:T(8,128)(2,1)S(1)}, bf16[256,128]{1,0:T(8,128)(2,1)S(1)}, u32[]{:S(2)}, u32[]{:S(2)}) collective-permute-start(bf16[256,128]{1,0:T(8,128)(2,1)S(1)} %get-tuple-element.50), channel_id=1, source_target_pairs={{0,24},{1,25},{2,26},{3,27},{4,28},{5,29},{6,30},{7,31},{8,16},{9,... | collective-permute-start | bytes 196616 | tf_op jit(solution)/shard_map/ppermute | solution.py:56
  22.6 1.6 %collective-permute-start.7 = (bf16[256,128]{1,0:T(8,128)(2,1)S(1)}, bf16[256,128]{1,0:T(8,128)(2,1)S(1)}, u32[]{:S(2)}, u32[]{:S(2)}) collective-permute-start(bf16[256,128]{1,0:T(8,128)(2,1)S(1)} %get-tuple-element.42), channel_id=1, source_target_pairs={{0,8},{1,9},{2,10},{3,11},{4,12},{5,13},{6,14},{7,15},{8,0},{9,1},... | collective-permute-start | bytes 196616 | tf_op jit(solution)/shard_map/ppermute | solution.py:56
  24.2 1.3 %tiles.1 = (bf16[16,128,384]{2,1,0:T(8,128)(2,1)S(1)}, bf16[16,128,384]{2,1,0:T(8,128)(2,1)S(1)}) custom-call(s32[3,16]{1,0:T(4,128)S(1)} %bitcast.5, s32[16]{0:T(128)S(1)} %copy-done.3, bf16[16,3,128,128]{3,2,1,0:T(8,128)(2,1)S(1)} %copy-done, f32[64,128]{1,0:T(8,128)S(1)} %bitcast.3), custom_call_target="tpu_custom_call" | custom-call | flops 1048576 | bytes 4194304 | tf_op jit(solution)/shard_map/tiles/pallas_call | solution.py:292
  25.5 1.1 %collective-permute-done.12.rest_2_ = bf16[256,128]{1,0:T(8,128)(2,1)S(1)} collective-permute-done((bf16[256,128]{1,0:T(8,128)(2,1)S(1)}, bf16[256,128]{1,0:T(8,128)(2,1)S(1)}, u32[]{:S(2)}, u32[]{:S(2)}) %collective-permute-start.12) | collective-permute-done | bytes 65568 | tf_op jit(solution)/shard_map/ppermute | solution.py:56
  27.3 1.3 %collective-permute-start.18 = (bf16[256,128]{1,0:T(8,128)(2,1)S(1)}, bf16[256,128]{1,0:T(8,128)(2,1)S(1)}, u32[]{:S(2)}, u32[]{:S(2)}) collective-permute-start(bf16[256,128]{1,0:T(8,128)(2,1)S(1)} %get-tuple-element.61), channel_id=1, source_target_pairs={{0,8},{1,9},{2,10},{3,11},{4,12},{5,13},{6,14},{7,15},{8,0},{9,1},... | collective-permute-start | bytes 196616 | tf_op jit(solution)/shard_map/ppermute | solution.py:56
  28.6 2.6 %collective-permute-start.13 = (bf16[256,128]{1,0:T(8,128)(2,1)S(1)}, bf16[256,128]{1,0:T(8,128)(2,1)S(1)}, u32[]{:S(2)}, u32[]{:S(2)}) collective-permute-start(bf16[256,128]{1,0:T(8,128)(2,1)S(1)} %get-tuple-element.61), channel_id=1, source_target_pairs={{0,16},{1,17},{2,18},{3,19},{4,20},{5,21},{6,22},{7,23},{8,24},{9,... | collective-permute-start | bytes 196616 | tf_op jit(solution)/shard_map/ppermute | solution.py:56
  31.9 1.0 %collective-permute-start.19 = (bf16[512,128]{1,0:T(8,128)(2,1)S(1)}, bf16[512,128]{1,0:T(8,128)(2,1)S(1)}, u32[]{:S(2)}, u32[]{:S(2)}) collective-permute-start(bf16[512,128]{1,0:T(8,128)(2,1)S(1)} %constant_dynamic-update-slice_fusion.2.rest_4_), channel_id=1, source_target_pairs={{0,2},{1,3},{2,0},{3,1},{4,6},{5,7},{6,4},{7,5},{8,10},{9,11},{10,... | collective-permute-start | bytes 393224 | tf_op jit(solution)/shard_map/ppermute | solution.py:56
  32.9 1.7 %collective-permute-start.20 = (bf16[512,128]{1,0:T(8,128)(2,1)S(1)}, bf16[512,128]{1,0:T(8,128)(2,1)S(1)}, u32[]{:S(2)}, u32[]{:S(2)}) collective-permute-start(bf16[512,128]{1,0:T(8,128)(2,1)S(1)} %constant_dynamic-update-slice_fusion.2.rest_4_), channel_id=1, source_target_pairs={{0,4},{1,5},{2,6},{3,7},{4,0},{5,1},{6,2},{7,3},{8,12},{9,13},{10,... | collective-permute-start | bytes 393224 | tf_op jit(solution)/shard_map/ppermute | solution.py:56
  34.6 1.4 %collective-permute-start.21 = (bf16[512,128]{1,0:T(8,128)(2,1)S(1)}, bf16[512,128]{1,0:T(8,128)(2,1)S(1)}, u32[]{:S(2)}, u32[]{:S(2)}) collective-permute-start(bf16[512,128]{1,0:T(8,128)(2,1)S(1)} %constant_dynamic-update-slice_fusion.2.rest_4_), channel_id=1, source_target_pairs={{0,6},{1,7},{2,4},{3,5},{4,2},{5,3},{6,0},{7,1},{8,14},{9,15},{10,... | collective-permute-start | bytes 393224 | tf_op jit(solution)/shard_map/ppermute | solution.py:56
  36.0 1.2 %collective-permute-done.14 = bf16[256,128]{1,0:T(8,128)(2,1)S(1)} collective-permute-done((bf16[256,128]{1,0:T(8,128)(2,1)S(1)}, bf16[256,128]{1,0:T(8,128)(2,1)S(1)}, u32[]{:S(2)}, u32[]{:S(2)}) %collective-permute-start.14) | collective-permute-done | bytes 65568 | tf_op jit(solution)/shard_map/ppermute | solution.py:56
  37.3 1.2 %collective-permute-start.15 = (bf16[512,128]{1,0:T(8,128)(2,1)S(1)}, bf16[512,128]{1,0:T(8,128)(2,1)S(1)}, u32[]{:S(2)}, u32[]{:S(2)}) collective-permute-start(bf16[512,128]{1,0:T(8,128)(2,1)S(1)} %constant_dynamic-update-slice_fusion.rest_0_), channel_id=1, source_target_pairs={{0,2},{1,3},{2,0},{3,1},{4,6},{5,7},{6,4},{7,5},{8,10},{9,11},{10,... | collective-permute-start | bytes 393224 | tf_op jit(solution)/shard_map/ppermute | solution.py:56
  38.5 1.0 %collective-permute-start.16 = (bf16[512,128]{1,0:T(8,128)(2,1)S(1)}, bf16[512,128]{1,0:T(8,128)(2,1)S(1)}, u32[]{:S(2)}, u32[]{:S(2)}) collective-permute-start(bf16[512,128]{1,0:T(8,128)(2,1)S(1)} %constant_dynamic-update-slice_fusion.rest_0_), channel_id=1, source_target_pairs={{0,4},{1,5},{2,6},{3,7},{4,0},{5,1},{6,2},{7,3},{8,12},{9,13},{10,... | collective-permute-start | bytes 393224 | tf_op jit(solution)/shard_map/ppermute | solution.py:56
  39.5 2.2 %collective-permute-start.17 = (bf16[512,128]{1,0:T(8,128)(2,1)S(1)}, bf16[512,128]{1,0:T(8,128)(2,1)S(1)}, u32[]{:S(2)}, u32[]{:S(2)}) collective-permute-start(bf16[512,128]{1,0:T(8,128)(2,1)S(1)} %constant_dynamic-update-slice_fusion.rest_0_), channel_id=1, source_target_pairs={{0,6},{1,7},{2,4},{3,5},{4,2},{5,3},{6,0},{7,1},{8,14},{9,15},{10,... | collective-permute-start | bytes 393224 | tf_op jit(solution)/shard_map/ppermute | solution.py:56
  42.2 1.5 %collective-permute-done.15.rest_1_ = bf16[512,128]{1,0:T(8,128)(2,1)S(1)} collective-permute-done((bf16[512,128]{1,0:T(8,128)(2,1)S(1)}, bf16[512,128]{1,0:T(8,128)(2,1)S(1)}, u32[]{:S(2)}, u32[]{:S(2)}) %collective-permute-start.15) | collective-permute-done | bytes 131104 | tf_op jit(solution)/shard_map/ppermute | solution.py:56
  44.6 1.7 %collective-permute-done.17.rest_3_ = bf16[512,128]{1,0:T(8,128)(2,1)S(1)} collective-permute-done((bf16[512,128]{1,0:T(8,128)(2,1)S(1)}, bf16[512,128]{1,0:T(8,128)(2,1)S(1)}, u32[]{:S(2)}, u32[]{:S(2)}) %collective-permute-start.17) | collective-permute-done | bytes 131104 | tf_op jit(solution)/shard_map/ppermute | solution.py:56
  48.2 19.9 %factors.1 = (f32[256,128]{1,0:T(8,128)}, bf16[2048,128]{1,0:T(8,128)(2,1)}) custom-call(s32[3,16]{1,0:T(4,128)S(1)} %bitcast.6, bf16[16,128,384]{2,1,0:T(8,128)(2,1)S(1)} %get-tuple-element.53.high_ref, bf16[16,128,384]{2,1,0:T(8,128)(2,1)S(1)} %get-tuple-element.54.low_ref, f32[256,128]{1,0:T(8,128)S(1)} %get-tuple-element.60.mine_ref, ...), custom_call_target="tpu_custom_call" | custom-call | tf_op jit(solution)/shard_map/factors/pallas_call | solution.py:362
  (58 shorter events, 8.1 us)
Async XLA Ops:
  4.2 4.4 %collective-permute-start.4 = (bf16[1024,128]{1,0:T(8,128)(2,1)S(1)}, bf16[1024,128]{1,0:T(8,128)(2,1)S(1)}, u32[]{:S(2)}, u32[]{:S(2)}) collective-permute-start(bf16[1024,128]{1,0:T(8,128)(2,1)S(1)} %get-tuple-element.38), channel_id=1, source_target_pairs={{0,1},{1,0},{2,3},{3,2},{4,5},{5,4},{6,7},{7,6},{8,9},{9,8},{10,11... | collective-permute-start | bytes 786440 | tf_op jit(solution)/shard_map/ppermute | solution.py:56
  4.7 5.7 %collective-permute-start.2 = (bf16[1024,128]{1,0:T(8,128)(2,1)S(1)}, bf16[1024,128]{1,0:T(8,128)(2,1)S(1)}, u32[]{:S(2)}, u32[]{:S(2)}) collective-permute-start(bf16[1024,128]{1,0:T(8,128)(2,1)S(1)} %get-tuple-element.36), channel_id=1, source_target_pairs={{0,1},{1,0},{2,3},{3,2},{4,5},{5,4},{6,7},{7,6},{8,9},{9,8},{10,11... | collective-permute-start | bytes 786440 | tf_op jit(solution)/shard_map/ppermute | solution.py:56
  5.7 8.2 %collective-permute-start.10 = (bf16[512,128]{1,0:T(8,128)(2,1)S(1)}, bf16[512,128]{1,0:T(8,128)(2,1)S(1)}, u32[]{:S(2)}, u32[]{:S(2)}) collective-permute-start(bf16[512,128]{1,0:T(8,128)(2,1)S(1)} %get-tuple-element.45), channel_id=1, source_target_pairs={{0,2},{1,3},{2,0},{3,1},{4,6},{5,7},{6,4},{7,5},{8,10},{9,11},{10,... | collective-permute-start | bytes 393224 | tf_op jit(solution)/shard_map/ppermute | solution.py:56
  8.7 9.0 %collective-permute-start.9 = (bf16[512,128]{1,0:T(8,128)(2,1)S(1)}, bf16[512,128]{1,0:T(8,128)(2,1)S(1)}, u32[]{:S(2)}, u32[]{:S(2)}) collective-permute-start(bf16[512,128]{1,0:T(8,128)(2,1)S(1)} %get-tuple-element.44), channel_id=1, source_target_pairs={{0,4},{1,5},{2,6},{3,7},{4,0},{5,1},{6,2},{7,3},{8,12},{9,13},{10,... | collective-permute-start | bytes 393224 | tf_op jit(solution)/shard_map/ppermute | solution.py:56
  10.4 7.4 %collective-permute-start.8 = (bf16[512,128]{1,0:T(8,128)(2,1)S(1)}, bf16[512,128]{1,0:T(8,128)(2,1)S(1)}, u32[]{:S(2)}, u32[]{:S(2)}) collective-permute-start(bf16[512,128]{1,0:T(8,128)(2,1)S(1)} %get-tuple-element.43), channel_id=1, source_target_pairs={{0,6},{1,7},{2,4},{3,5},{4,2},{5,3},{6,0},{7,1},{8,14},{9,15},{10,... | collective-permute-start | bytes 393224 | tf_op jit(solution)/shard_map/ppermute | solution.py:56
  10.6 11.2 %collective-permute-start.6 = (bf16[512,128]{1,0:T(8,128)(2,1)S(1)}, bf16[512,128]{1,0:T(8,128)(2,1)S(1)}, u32[]{:S(2)}, u32[]{:S(2)}) collective-permute-start(bf16[512,128]{1,0:T(8,128)(2,1)S(1)} %get-tuple-element.41), channel_id=1, source_target_pairs={{0,2},{1,3},{2,0},{3,1},{4,6},{5,7},{6,4},{7,5},{8,10},{9,11},{10,... | collective-permute-start | bytes 393224 | tf_op jit(solution)/shard_map/ppermute | solution.py:56
  12.4 10.1 %collective-permute-start.5 = (bf16[512,128]{1,0:T(8,128)(2,1)S(1)}, bf16[512,128]{1,0:T(8,128)(2,1)S(1)}, u32[]{:S(2)}, u32[]{:S(2)}) collective-permute-start(bf16[512,128]{1,0:T(8,128)(2,1)S(1)} %get-tuple-element.39), channel_id=1, source_target_pairs={{0,4},{1,5},{2,6},{3,7},{4,0},{5,1},{6,2},{7,3},{8,12},{9,13},{10,... | collective-permute-start | bytes 393224 | tf_op jit(solution)/shard_map/ppermute | solution.py:56
  13.9 8.6 %collective-permute-start.3 = (bf16[512,128]{1,0:T(8,128)(2,1)S(1)}, bf16[512,128]{1,0:T(8,128)(2,1)S(1)}, u32[]{:S(2)}, u32[]{:S(2)}) collective-permute-start(bf16[512,128]{1,0:T(8,128)(2,1)S(1)} %get-tuple-element.37), channel_id=1, source_target_pairs={{0,6},{1,7},{2,4},{3,5},{4,2},{5,3},{6,0},{7,1},{8,14},{9,15},{10,... | collective-permute-start | bytes 393224 | tf_op jit(solution)/shard_map/ppermute | solution.py:56
  17.9 7.7 %collective-permute-start.11 = (bf16[256,128]{1,0:T(8,128)(2,1)S(1)}, bf16[256,128]{1,0:T(8,128)(2,1)S(1)}, u32[]{:S(2)}, u32[]{:S(2)}) collective-permute-start(bf16[256,128]{1,0:T(8,128)(2,1)S(1)} %get-tuple-element.49), channel_id=1, source_target_pairs={{0,16},{1,17},{2,18},{3,19},{4,20},{5,21},{6,22},{7,23},{8,24},{9,... | collective-permute-start | bytes 196616 | tf_op jit(solution)/shard_map/ppermute | solution.py:56
  20.5 6.1 %collective-permute-start.12 = (bf16[256,128]{1,0:T(8,128)(2,1)S(1)}, bf16[256,128]{1,0:T(8,128)(2,1)S(1)}, u32[]{:S(2)}, u32[]{:S(2)}) collective-permute-start(bf16[256,128]{1,0:T(8,128)(2,1)S(1)} %get-tuple-element.50), channel_id=1, source_target_pairs={{0,24},{1,25},{2,26},{3,27},{4,28},{5,29},{6,30},{7,31},{8,16},{9,... | collective-permute-start | bytes 196616 | tf_op jit(solution)/shard_map/ppermute | solution.py:56
  22.6 4.7 %collective-permute-start.7 = (bf16[256,128]{1,0:T(8,128)(2,1)S(1)}, bf16[256,128]{1,0:T(8,128)(2,1)S(1)}, u32[]{:S(2)}, u32[]{:S(2)}) collective-permute-start(bf16[256,128]{1,0:T(8,128)(2,1)S(1)} %get-tuple-element.42), channel_id=1, source_target_pairs={{0,8},{1,9},{2,10},{3,11},{4,12},{5,13},{6,14},{7,15},{8,0},{9,1},... | collective-permute-start | bytes 196616 | tf_op jit(solution)/shard_map/ppermute | solution.py:56
  27.3 4.6 %collective-permute-start.18 = (bf16[256,128]{1,0:T(8,128)(2,1)S(1)}, bf16[256,128]{1,0:T(8,128)(2,1)S(1)}, u32[]{:S(2)}, u32[]{:S(2)}) collective-permute-start(bf16[256,128]{1,0:T(8,128)(2,1)S(1)} %get-tuple-element.61), channel_id=1, source_target_pairs={{0,8},{1,9},{2,10},{3,11},{4,12},{5,13},{6,14},{7,15},{8,0},{9,1},... | collective-permute-start | bytes 196616 | tf_op jit(solution)/shard_map/ppermute | solution.py:56
  28.6 7.4 %collective-permute-start.13 = (bf16[256,128]{1,0:T(8,128)(2,1)S(1)}, bf16[256,128]{1,0:T(8,128)(2,1)S(1)}, u32[]{:S(2)}, u32[]{:S(2)}) collective-permute-start(bf16[256,128]{1,0:T(8,128)(2,1)S(1)} %get-tuple-element.61), channel_id=1, source_target_pairs={{0,16},{1,17},{2,18},{3,19},{4,20},{5,21},{6,22},{7,23},{8,24},{9,... | collective-permute-start | bytes 196616 | tf_op jit(solution)/shard_map/ppermute | solution.py:56
  31.2 6.1 %collective-permute-start.14 = (bf16[256,128]{1,0:T(8,128)(2,1)S(1)}, bf16[256,128]{1,0:T(8,128)(2,1)S(1)}, u32[]{:S(2)}, u32[]{:S(2)}) collective-permute-start(bf16[256,128]{1,0:T(8,128)(2,1)S(1)} %get-tuple-element.61), channel_id=1, source_target_pairs={{0,24},{1,25},{2,26},{3,27},{4,28},{5,29},{6,30},{7,31},{8,16},{9,... | collective-permute-start | bytes 196616 | tf_op jit(solution)/shard_map/ppermute | solution.py:56
  31.9 6.6 %collective-permute-start.19 = (bf16[512,128]{1,0:T(8,128)(2,1)S(1)}, bf16[512,128]{1,0:T(8,128)(2,1)S(1)}, u32[]{:S(2)}, u32[]{:S(2)}) collective-permute-start(bf16[512,128]{1,0:T(8,128)(2,1)S(1)} %constant_dynamic-update-slice_fusion.2.rest_4_), channel_id=1, source_target_pairs={{0,2},{1,3},{2,0},{3,1},{4,6},{5,7},{6,4},{7,5},{8,10},{9,11},{10,... | collective-permute-start | bytes 393224 | tf_op jit(solution)/shard_map/ppermute | solution.py:56
  32.9 6.6 %collective-permute-start.20 = (bf16[512,128]{1,0:T(8,128)(2,1)S(1)}, bf16[512,128]{1,0:T(8,128)(2,1)S(1)}, u32[]{:S(2)}, u32[]{:S(2)}) collective-permute-start(bf16[512,128]{1,0:T(8,128)(2,1)S(1)} %constant_dynamic-update-slice_fusion.2.rest_4_), channel_id=1, source_target_pairs={{0,4},{1,5},{2,6},{3,7},{4,0},{5,1},{6,2},{7,3},{8,12},{9,13},{10,... | collective-permute-start | bytes 393224 | tf_op jit(solution)/shard_map/ppermute | solution.py:56
  34.6 7.1 %collective-permute-start.21 = (bf16[512,128]{1,0:T(8,128)(2,1)S(1)}, bf16[512,128]{1,0:T(8,128)(2,1)S(1)}, u32[]{:S(2)}, u32[]{:S(2)}) collective-permute-start(bf16[512,128]{1,0:T(8,128)(2,1)S(1)} %constant_dynamic-update-slice_fusion.2.rest_4_), channel_id=1, source_target_pairs={{0,6},{1,7},{2,4},{3,5},{4,2},{5,3},{6,0},{7,1},{8,14},{9,15},{10,... | collective-permute-start | bytes 393224 | tf_op jit(solution)/shard_map/ppermute | solution.py:56
  36.0 5.7 %collective-permute-start.26 = (bf16[512,128]{1,0:T(8,128)(2,1)S(1)}, bf16[512,128]{1,0:T(8,128)(2,1)S(1)}, u32[]{:S(2)}, u32[]{:S(2)}) collective-permute-start(bf16[512,128]{1,0:T(8,128)(2,1)S(1)} %constant_dynamic-update-slice_fusion.2.rest_4_), channel_id=1, source_target_pairs={{0,1},{1,0},{2,3},{3,2},{4,5},{5,4},{6,7},{7,6},{8,9},{9,8},{10,11... | collective-permute-start | bytes 393224 | tf_op jit(solution)/shard_map/ppermute | solution.py:56
  37.3 6.4 %collective-permute-start.15 = (bf16[512,128]{1,0:T(8,128)(2,1)S(1)}, bf16[512,128]{1,0:T(8,128)(2,1)S(1)}, u32[]{:S(2)}, u32[]{:S(2)}) collective-permute-start(bf16[512,128]{1,0:T(8,128)(2,1)S(1)} %constant_dynamic-update-slice_fusion.rest_0_), channel_id=1, source_target_pairs={{0,2},{1,3},{2,0},{3,1},{4,6},{5,7},{6,4},{7,5},{8,10},{9,11},{10,... | collective-permute-start | bytes 393224 | tf_op jit(solution)/shard_map/ppermute | solution.py:56
  38.5 6.1 %collective-permute-start.16 = (bf16[512,128]{1,0:T(8,128)(2,1)S(1)}, bf16[512,128]{1,0:T(8,128)(2,1)S(1)}, u32[]{:S(2)}, u32[]{:S(2)}) collective-permute-start(bf16[512,128]{1,0:T(8,128)(2,1)S(1)} %constant_dynamic-update-slice_fusion.rest_0_), channel_id=1, source_target_pairs={{0,4},{1,5},{2,6},{3,7},{4,0},{5,1},{6,2},{7,3},{8,12},{9,13},{10,... | collective-permute-start | bytes 393224 | tf_op jit(solution)/shard_map/ppermute | solution.py:56
  39.5 6.8 %collective-permute-start.17 = (bf16[512,128]{1,0:T(8,128)(2,1)S(1)}, bf16[512,128]{1,0:T(8,128)(2,1)S(1)}, u32[]{:S(2)}, u32[]{:S(2)}) collective-permute-start(bf16[512,128]{1,0:T(8,128)(2,1)S(1)} %constant_dynamic-update-slice_fusion.rest_0_), channel_id=1, source_target_pairs={{0,6},{1,7},{2,4},{3,5},{4,2},{5,3},{6,0},{7,1},{8,14},{9,15},{10,... | collective-permute-start | bytes 393224 | tf_op jit(solution)/shard_map/ppermute | solution.py:56
  41.7 4.6 %collective-permute-start.22 = (bf16[512,128]{1,0:T(8,128)(2,1)S(1)}, bf16[512,128]{1,0:T(8,128)(2,1)S(1)}, u32[]{:S(2)}, u32[]{:S(2)}) collective-permute-start(bf16[512,128]{1,0:T(8,128)(2,1)S(1)} %constant_dynamic-update-slice_fusion.rest_0_), channel_id=1, source_target_pairs={{0,1},{1,0},{2,3},{3,2},{4,5},{5,4},{6,7},{7,6},{8,9},{9,8},{10,11... | collective-permute-start | bytes 393224 | tf_op jit(solution)/shard_map/ppermute | solution.py:56
  41.7 5.1 %collective-permute-start.27 = (bf16[512,128]{1,0:T(8,128)(2,1)S(1)}, bf16[512,128]{1,0:T(8,128)(2,1)S(1)}, u32[]{:S(2)}, u32[]{:S(2)}) collective-permute-start(bf16[512,128]{1,0:T(8,128)(2,1)S(1)} %collective-permute-done.19.rest_5_), channel_id=1, source_target_pairs={{0,1},{1,0},{2,3},{3,2},{4,5},{5,4},{6,7},{7,6},{8,9},{9,8},{10,11... | collective-permute-start | bytes 393224 | tf_op jit(solution)/shard_map/ppermute | solution.py:56
  43.7 3.2 %collective-permute-start.28 = (bf16[512,128]{1,0:T(8,128)(2,1)S(1)}, bf16[512,128]{1,0:T(8,128)(2,1)S(1)}, u32[]{:S(2)}, u32[]{:S(2)}) collective-permute-start(bf16[512,128]{1,0:T(8,128)(2,1)S(1)} %collective-permute-done.20.rest_6_), channel_id=1, source_target_pairs={{0,1},{1,0},{2,3},{3,2},{4,5},{5,4},{6,7},{7,6},{8,9},{9,8},{10,11... | collective-permute-start | bytes 393224 | tf_op jit(solution)/shard_map/ppermute | solution.py:56
  (10 other events, 28.1 us)

commit v10 on v9

--- a/solution.py
+++ b/solution.py
@@ -97,15 +97,15 @@
         send_ref[...] = total_ref[half + p * size : half + (p + 1) * size, :].astype(BF16)
 
 
-def tiles_kernel(rows_ref, counts_ref, blocks_ref, weights_ref, high_ref, low_ref):
+def tiles_kernel(rows_ref, counts_ref, blocks_ref, weights_ref, out_ref):
     documents, slots, block, _ = blocks_ref.shape
     for d in range(documents):
         for s in range(slots):
             scale = weights_ref[pl.ds(rows_ref[s, d], 1), :]
             scale = jnp.where(s < counts_ref[d], scale, 0.0)
             high, low = split(blocks_ref[d, s].T.astype(F32) * scale)
-            high_ref[d, :, s * block : (s + 1) * block] = high
-            low_ref[d, :, s * block : (s + 1) * block] = low
+            out_ref[d, :block, s * block : (s + 1) * block] = high
+            out_ref[d, block:, s * block : (s + 1) * block] = low
 
 
 def scale_kernel(plan, weights_ref, scale_ref, turned_ref):
@@ -157,16 +157,23 @@
     return lax.dot_general(a, b, (((1,), (1,)), ((), ())), preferred_element_type=F32)
 
 
+def both(total):
+    size = total.shape[1] // 2
+    return total[:, :size] + total[:, size:]
+
+
 def dot_t3(a, b):
-    a_high, a_low = split(a)
     b_high, b_low = split(b)
-    return dot_t(a_high, b_high) + (dot_t(a_high, b_low) + dot_t(a_low, b_high))
+    top = jnp.concatenate([b_high, b_high], axis=1)
+    low = jnp.concatenate([b_low, jnp.zeros_like(b_low)], axis=1)
+    return both(dot_t(jnp.concatenate(split(a), axis=1), jnp.concatenate([top, low], axis=0)))
 
 
 def dot3(a, b):
-    a_high, a_low = split(a)
     b_high, b_low = split(b)
-    return dot(a_high, b_high) + (dot(a_high, b_low) + dot(a_low, b_high))
+    top = jnp.concatenate([b_high, b_low], axis=1)
+    low = jnp.concatenate([b_high, jnp.zeros_like(b_low)], axis=1)
+    return both(dot(jnp.concatenate(split(a), axis=1), jnp.concatenate([top, low], axis=0)))
 
 
 def dot(a, b):
@@ -223,13 +230,22 @@
     return jnp.max(jnp.sum(jnp.abs(residual), axis=1))
 
 
-def last_kernel(plan, features, rows_ref, high_ref, low_ref, mine_ref, *rest):
+def gram_kernel(*refs):
+    gram = jnp.zeros(refs[-1].shape, F32)
+    for ref in refs[:-1]:
+        part = ref[...]
+        gram += lax.dot_general(part, part, (((0,), (0,)), ((), ())), preferred_element_type=F32)
+    refs[-1][...] = gram
+
+
+def last_kernel(plan, features, late, rows_ref, tiles_ref, mine_ref, early_ref, *rest):
     parts, (basis_ref, factors_ref) = rest[: 4 * plan.plane], rest[4 * plan.plane : 4 * plan.plane + 2]
     all_ref, product_ref, gram_ref, inverse_ref = rest[4 * plan.plane + 2 :]
     me = plan.me()
-    documents, block, _ = high_ref.shape
-    slots = high_ref.shape[2] // block
-    gram = jnp.zeros(gram_ref.shape, F32)
+    documents = tiles_ref.shape[0]
+    block = tiles_ref.shape[1] // 2
+    slots = tiles_ref.shape[2] // block
+    gram = early_ref[...]
     for i, ref in enumerate(parts):
         size = ref.shape[0]
         core, later = divmod(i, 2 * plan.plane)
@@ -237,7 +253,8 @@
         base = ((core * plan.plane + member) * 2 + 1 - near) * size
         part = ref[...]
         all_ref[base : base + size, :] = part
-        gram += lax.dot_general(part, part, (((0,), (0,)), ((), ())), preferred_element_type=F32)
+        if i in late:
+            gram += lax.dot_general(part, part, (((0,), (0,)), ((), ())), preferred_element_type=F32)
     gram = gram * (1.0 / features)
     residual = newton(gram, inverse_ref)
     for d in range(documents):
@@ -246,8 +263,8 @@
             for p in range(plan.pieces):
                 at = pl.ds(plan.start(me, rows_ref[s, d], p), plan.piece)
                 picked.append(all_ref[at, :])
-        picked = jnp.concatenate(picked, axis=0)
-        product_ref[d * block : (d + 1) * block, :] = dot(high_ref[d], picked) + dot(low_ref[d], picked)
+        terms = dot(tiles_ref[d], jnp.concatenate(picked, axis=0))
+        product_ref[d * block : (d + 1) * block, :] = terms[:block] + terms[block:]
 
     @pl.when(jnp.logical_not(residual < 1.5e-2))
     def _():
@@ -287,13 +304,12 @@
         name="local_sum",
     )(in_hbm(rows), in_hbm(counts), in_hbm(blocks), in_hbm(sketch))
 
-    tiles_shape = shape((documents, block, slots * block), BF16)
     lines = weights.reshape(features // block, block)
-    high, low = pl.pallas_call(
+    tiles = pl.pallas_call(
         tiles_kernel,
-        out_shape=(tiles_shape, tiles_shape),
+        out_shape=shape((documents, 2 * block, slots * block), BF16),
         in_specs=[scalars(), scalars(), whole(), whole()],
-        out_specs=(whole(), whole()),
+        out_specs=whole(),
         compiler_params=params,
         cost_estimate=pl.CostEstimate(flops=1 << 20, bytes_accessed=4 << 20, transcendentals=0),
         name="tiles",
@@ -342,7 +358,7 @@
     far = [plan.swap_line(part, split_at + q) for q, part in enumerate(far)]
     held, *near = plane_sum(near_sent, 0, [F32] + [BF16] * (split_at - 1))
     near = [plan.swap_line(part, 1 + q) for q, part in enumerate(near)]
-    near, far, high, low = lax.optimization_barrier((near, far, high, low))
+    near, far, tiles = lax.optimization_barrier((near, far, tiles))
     mine, rounded = pl.pallas_call(
         line_kernel,
         out_shape=(shape((flat, columns), F32), shape((flat, columns), BF16)),
@@ -359,10 +375,21 @@
     own = far + near
     other = [plan.swap(part, 1) for part in own]
 
+    pieces = own + other
+    late = range(len(own) + 1, len(own) + plan.plane)
+    gram = pl.pallas_call(
+        gram_kernel,
+        out_shape=shape((columns, columns), F32),
+        in_specs=[whole()] * (len(pieces) - len(late)),
+        out_specs=whole(),
+        compiler_params=params,
+        cost_estimate=pl.CostEstimate(flops=2 * features * columns * columns, bytes_accessed=4 << 20, transcendentals=0),
+        name="gram",
+    )(*[piece for i, piece in enumerate(pieces) if i not in late])
     return pl.pallas_call(
-        functools.partial(last_kernel, plan, features),
+        functools.partial(last_kernel, plan, features, late),
         out_shape=(shape((flat, columns), F32), shape((documents * block, columns), BF16)),
-        in_specs=[scalars()] + [whole()] * (3 + 4 * plan.plane),
+        in_specs=[scalars()] + [whole()] * (3 + len(pieces)),
         out_specs=(whole(), whole()),
         scratch_shapes=[
             pltpu.VMEM((features, columns), BF16),
@@ -372,7 +399,7 @@
         ],
         compiler_params=params,
         name="factors",
-    )(rows, high, low, mine, *own, *other)
+    )(rows, tiles, mine, gram, *pieces)
 
 
 def solution(mesh):

time: 68.2 us -> 67.5 us (0.990)
  waiting for transfers between devices: 11.7 us -> 11 us
    ppermute x30, waiting for transfers between devices: 11.7 us -> 11 us  [swap(): return lax.ppermute(value, AXES, [(d, d ^ mask) for d in range(self.count)])]
    pallas_call x2 -> x3, Pallas kernels: 21.2 us -> 21.1 us  [the longest x1 19.1 us: body(): pl.pallas_call(functools.partial(last_kernel, plan, features, late), out_...]
  transfers between devices with their start and end apart: 30 -> 30, of which waited for: 14 -> 14; matrix products, arithmetic and copies ran while one was open for 0% -> 0% of each run, Pallas kernels for 2% -> 3%
where the time goes in v10:
time: 67.5 us; the launch traced here: 67.3 us
  starting transfers between devices  30.9 us (46%)
  Pallas kernels  24.5 us (36%)
  waiting for transfers between devices  11 us (16%)
  between operations  0.76 us (1%)
    ppermute x30, starting transfers between devices, swap(): return lax.ppermute(value, AXES, [(d, d ^ mask) for d in range(self.count)])  30.9 us
    pallas_call x1, Pallas kernels, body(): pl.pallas_call(functools.partial(last_kernel, plan, features, late), out_...  19.1 us
    ppermute x30, waiting for transfers between devices, swap(): return lax.ppermute(value, AXES, [(d, d ^ mask) for d in range(self.count)])  11 us
    pallas_call x1, Pallas kernels, body(): pl.pallas_call(functools.partial(sum_kernel, plan), out_shape=(pltpu.VMEM...  3 us
  transfers between devices with their start and end apart: 30, of which 14 were waited for; matrix products, arithmetic and copies ran while one was open for 0% of the time, Pallas kernels for 3%

profile of v10, /device:TPU:0, one launch (start us, length us, event | category | flops | bytes accessed | tf_op | source)
XLA Modules:
  0.0 67.3 jit_solution(2522092343437318405)
XLA Ops:
  0.6 3.0 %local_sum.1 = (f32[8192,128]{1,0:T(8,128)S(1)}, bf16[1024,128]{1,0:T(8,128)(2,1)S(1)}, bf16[1024,128]{1,0:T(8,128)(2,1)S(1)}, bf16[1024,128]{1,0:T(8,128)(2,1)S(1)}, bf16[1024,128]{1,0:T(8,128)(2,1)S(1)}) custom-call(s32[3,16]{1,0:T(4,128)} %bitcast.4, s32[16]{0:T(128)} %counts_ref.3, bf16[16,3,128,128]{3,2,1,0:T(8,128)(2,1)} %blocks_ref.3, ...), custom_call_target="tpu_custom_call" | custom-call | tf_op jit(solution)/shard_map/local_sum/pallas_call | solution.py:293
  5.7 2.9 %collective-permute-start.10 = (bf16[512,128]{1,0:T(8,128)(2,1)S(1)}, bf16[512,128]{1,0:T(8,128)(2,1)S(1)}, u32[]{:S(2)}, u32[]{:S(2)}) collective-permute-start(bf16[512,128]{1,0:T(8,128)(2,1)S(1)} %get-tuple-element.42), channel_id=1, source_target_pairs={{0,2},{1,3},{2,0},{3,1},{4,6},{5,7},{6,4},{7,5},{8,10},{9,11},{10,... | collective-permute-start | bytes 393224 | tf_op jit(solution)/shard_map/ppermute | solution.py:56
  8.7 1.6 %collective-permute-start.9 = (bf16[512,128]{1,0:T(8,128)(2,1)S(1)}, bf16[512,128]{1,0:T(8,128)(2,1)S(1)}, u32[]{:S(2)}, u32[]{:S(2)}) collective-permute-start(bf16[512,128]{1,0:T(8,128)(2,1)S(1)} %get-tuple-element.41), channel_id=1, source_target_pairs={{0,4},{1,5},{2,6},{3,7},{4,0},{5,1},{6,2},{7,3},{8,12},{9,13},{10,... | collective-permute-start | bytes 393224 | tf_op jit(solution)/shard_map/ppermute | solution.py:56
  10.6 1.8 %collective-permute-start.6 = (bf16[512,128]{1,0:T(8,128)(2,1)S(1)}, bf16[512,128]{1,0:T(8,128)(2,1)S(1)}, u32[]{:S(2)}, u32[]{:S(2)}) collective-permute-start(bf16[512,128]{1,0:T(8,128)(2,1)S(1)} %get-tuple-element.38), channel_id=1, source_target_pairs={{0,2},{1,3},{2,0},{3,1},{4,6},{5,7},{6,4},{7,5},{8,10},{9,11},{10,... | collective-permute-start | bytes 393224 | tf_op jit(solution)/shard_map/ppermute | solution.py:56
  12.4 1.5 %collective-permute-start.5 = (bf16[512,128]{1,0:T(8,128)(2,1)S(1)}, bf16[512,128]{1,0:T(8,128)(2,1)S(1)}, u32[]{:S(2)}, u32[]{:S(2)}) collective-permute-start(bf16[512,128]{1,0:T(8,128)(2,1)S(1)} %get-tuple-element.36), channel_id=1, source_target_pairs={{0,4},{1,5},{2,6},{3,7},{4,0},{5,1},{6,2},{7,3},{8,12},{9,13},{10,... | collective-permute-start | bytes 393224 | tf_op jit(solution)/shard_map/ppermute | solution.py:56
  13.9 2.0 %collective-permute-start.3 = (bf16[512,128]{1,0:T(8,128)(2,1)S(1)}, bf16[512,128]{1,0:T(8,128)(2,1)S(1)}, u32[]{:S(2)}, u32[]{:S(2)}) collective-permute-start(bf16[512,128]{1,0:T(8,128)(2,1)S(1)} %get-tuple-element.34), channel_id=1, source_target_pairs={{0,6},{1,7},{2,4},{3,5},{4,2},{5,3},{6,0},{7,1},{8,14},{9,15},{10,... | collective-permute-start | bytes 393224 | tf_op jit(solution)/shard_map/ppermute | solution.py:56
  16.1 1.7 %collective-permute-done.9.rest_1_ = bf16[512,128]{1,0:T(8,128)(2,1)S(1)} collective-permute-done((bf16[512,128]{1,0:T(8,128)(2,1)S(1)}, bf16[512,128]{1,0:T(8,128)(2,1)S(1)}, u32[]{:S(2)}, u32[]{:S(2)}) %collective-permute-start.9) | collective-permute-done | bytes 131104 | tf_op jit(solution)/shard_map/ppermute | solution.py:56
  17.9 2.6 %collective-permute-start.11 = (bf16[256,128]{1,0:T(8,128)(2,1)S(1)}, bf16[256,128]{1,0:T(8,128)(2,1)S(1)}, u32[]{:S(2)}, u32[]{:S(2)}) collective-permute-start(bf16[256,128]{1,0:T(8,128)(2,1)S(1)} %get-tuple-element.46), channel_id=1, source_target_pairs={{0,16},{1,17},{2,18},{3,19},{4,20},{5,21},{6,22},{7,23},{8,24},{9,... | collective-permute-start | bytes 196616 | tf_op jit(solution)/shard_map/ppermute | solution.py:56
  20.5 1.3 %collective-permute-start.12 = (bf16[256,128]{1,0:T(8,128)(2,1)S(1)}, bf16[256,128]{1,0:T(8,128)(2,1)S(1)}, u32[]{:S(2)}, u32[]{:S(2)}) collective-permute-start(bf16[256,128]{1,0:T(8,128)(2,1)S(1)} %get-tuple-element.47), channel_id=1, source_target_pairs={{0,24},{1,25},{2,26},{3,27},{4,28},{5,29},{6,30},{7,31},{8,16},{9,... | collective-permute-start | bytes 196616 | tf_op jit(solution)/shard_map/ppermute | solution.py:56
  22.6 1.6 %collective-permute-start.7 = (bf16[256,128]{1,0:T(8,128)(2,1)S(1)}, bf16[256,128]{1,0:T(8,128)(2,1)S(1)}, u32[]{:S(2)}, u32[]{:S(2)}) collective-permute-start(bf16[256,128]{1,0:T(8,128)(2,1)S(1)} %get-tuple-element.39), channel_id=1, source_target_pairs={{0,8},{1,9},{2,10},{3,11},{4,12},{5,13},{6,14},{7,15},{8,0},{9,1},... | collective-permute-start | bytes 196616 | tf_op jit(solution)/shard_map/ppermute | solution.py:56
  24.2 1.3 %tiles.1.tiles_ref = bf16[16,256,384]{2,1,0:T(8,128)(2,1)S(1)} custom-call(s32[3,16]{1,0:T(4,128)S(1)} %bitcast.5, s32[16]{0:T(128)S(1)} %copy-done.3, bf16[16,3,128,128]{3,2,1,0:T(8,128)(2,1)S(1)} %copy-done, f32[64,128]{1,0:T(8,128)S(1)} %bitcast.3), custom_call_target="tpu_custom_call" | custom-call | flops 1048576 | bytes 4194304 | tf_op jit(solution)/shard_map/tiles/pallas_call | solution.py:308
  25.5 1.1 %collective-permute-done.12.rest_2_ = bf16[256,128]{1,0:T(8,128)(2,1)S(1)} collective-permute-done((bf16[256,128]{1,0:T(8,128)(2,1)S(1)}, bf16[256,128]{1,0:T(8,128)(2,1)S(1)}, u32[]{:S(2)}, u32[]{:S(2)}) %collective-permute-start.12) | collective-permute-done | bytes 65568 | tf_op jit(solution)/shard_map/ppermute | solution.py:56
  27.3 1.2 %collective-permute-start.18 = (bf16[256,128]{1,0:T(8,128)(2,1)S(1)}, bf16[256,128]{1,0:T(8,128)(2,1)S(1)}, u32[]{:S(2)}, u32[]{:S(2)}) collective-permute-start(bf16[256,128]{1,0:T(8,128)(2,1)S(1)} %get-tuple-element.55), channel_id=1, source_target_pairs={{0,8},{1,9},{2,10},{3,11},{4,12},{5,13},{6,14},{7,15},{8,0},{9,1},... | collective-permute-start | bytes 196616 | tf_op jit(solution)/shard_map/ppermute | solution.py:56
  28.6 2.6 %collective-permute-start.13 = (bf16[256,128]{1,0:T(8,128)(2,1)S(1)}, bf16[256,128]{1,0:T(8,128)(2,1)S(1)}, u32[]{:S(2)}, u32[]{:S(2)}) collective-permute-start(bf16[256,128]{1,0:T(8,128)(2,1)S(1)} %get-tuple-element.55), channel_id=1, source_target_pairs={{0,16},{1,17},{2,18},{3,19},{4,20},{5,21},{6,22},{7,23},{8,24},{9,... | collective-permute-start | bytes 196616 | tf_op jit(solution)/shard_map/ppermute | solution.py:56
  31.9 1.1 %collective-permute-start.19 = (bf16[512,128]{1,0:T(8,128)(2,1)S(1)}, bf16[512,128]{1,0:T(8,128)(2,1)S(1)}, u32[]{:S(2)}, u32[]{:S(2)}) collective-permute-start(bf16[512,128]{1,0:T(8,128)(2,1)S(1)} %constant_dynamic-update-slice_fusion.2.refs_4_.rest_4_), channel_id=1, source_target_pairs={{0,2},{1,3},{2,0},{3,1},{4,6},{5,7},{6,4},{7,5},{8,10},{9,11},{10,... | collective-permute-start | bytes 393224 | tf_op jit(solution)/shard_map/ppermute | solution.py:56
  33.0 1.7 %collective-permute-start.20 = (bf16[512,128]{1,0:T(8,128)(2,1)S(1)}, bf16[512,128]{1,0:T(8,128)(2,1)S(1)}, u32[]{:S(2)}, u32[]{:S(2)}) collective-permute-start(bf16[512,128]{1,0:T(8,128)(2,1)S(1)} %constant_dynamic-update-slice_fusion.2.refs_4_.rest_4_), channel_id=1, source_target_pairs={{0,4},{1,5},{2,6},{3,7},{4,0},{5,1},{6,2},{7,3},{8,12},{9,13},{10,... | collective-permute-start | bytes 393224 | tf_op jit(solution)/shard_map/ppermute | solution.py:56
  34.6 1.4 %collective-permute-start.21 = (bf16[512,128]{1,0:T(8,128)(2,1)S(1)}, bf16[512,128]{1,0:T(8,128)(2,1)S(1)}, u32[]{:S(2)}, u32[]{:S(2)}) collective-permute-start(bf16[512,128]{1,0:T(8,128)(2,1)S(1)} %constant_dynamic-update-slice_fusion.2.refs_4_.rest_4_), channel_id=1, source_target_pairs={{0,6},{1,7},{2,4},{3,5},{4,2},{5,3},{6,0},{7,1},{8,14},{9,15},{10,... | collective-permute-start | bytes 393224 | tf_op jit(solution)/shard_map/ppermute | solution.py:56
  36.0 1.2 %collective-permute-done.14 = bf16[256,128]{1,0:T(8,128)(2,1)S(1)} collective-permute-done((bf16[256,128]{1,0:T(8,128)(2,1)S(1)}, bf16[256,128]{1,0:T(8,128)(2,1)S(1)}, u32[]{:S(2)}, u32[]{:S(2)}) %collective-permute-start.14) | collective-permute-done | bytes 65568 | tf_op jit(solution)/shard_map/ppermute | solution.py:56
  37.3 1.2 %collective-permute-start.15 = (bf16[512,128]{1,0:T(8,128)(2,1)S(1)}, bf16[512,128]{1,0:T(8,128)(2,1)S(1)}, u32[]{:S(2)}, u32[]{:S(2)}) collective-permute-start(bf16[512,128]{1,0:T(8,128)(2,1)S(1)} %constant_dynamic-update-slice_fusion.refs_0_.rest_0_), channel_id=1, source_target_pairs={{0,2},{1,3},{2,0},{3,1},{4,6},{5,7},{6,4},{7,5},{8,10},{9,11},{10,... | collective-permute-start | bytes 393224 | tf_op jit(solution)/shard_map/ppermute | solution.py:56
  38.5 1.1 %collective-permute-start.16 = (bf16[512,128]{1,0:T(8,128)(2,1)S(1)}, bf16[512,128]{1,0:T(8,128)(2,1)S(1)}, u32[]{:S(2)}, u32[]{:S(2)}) collective-permute-start(bf16[512,128]{1,0:T(8,128)(2,1)S(1)} %constant_dynamic-update-slice_fusion.refs_0_.rest_0_), channel_id=1, source_target_pairs={{0,4},{1,5},{2,6},{3,7},{4,0},{5,1},{6,2},{7,3},{8,12},{9,13},{10,... | collective-permute-start | bytes 393224 | tf_op jit(solution)/shard_map/ppermute | solution.py:56
  39.5 2.2 %collective-permute-start.17 = (bf16[512,128]{1,0:T(8,128)(2,1)S(1)}, bf16[512,128]{1,0:T(8,128)(2,1)S(1)}, u32[]{:S(2)}, u32[]{:S(2)}) collective-permute-start(bf16[512,128]{1,0:T(8,128)(2,1)S(1)} %constant_dynamic-update-slice_fusion.refs_0_.rest_0_), channel_id=1, source_target_pairs={{0,6},{1,7},{2,4},{3,5},{4,2},{5,3},{6,0},{7,1},{8,14},{9,15},{10,... | collective-permute-start | bytes 393224 | tf_op jit(solution)/shard_map/ppermute | solution.py:56
  42.2 1.5 %collective-permute-done.15.refs_1_.rest_1_ = bf16[512,128]{1,0:T(8,128)(2,1)S(1)} collective-permute-done((bf16[512,128]{1,0:T(8,128)(2,1)S(1)}, bf16[512,128]{1,0:T(8,128)(2,1)S(1)}, u32[]{:S(2)}, u32[]{:S(2)}) %collective-permute-start.15) | collective-permute-done | bytes 131104 | tf_op jit(solution)/shard_map/ppermute | solution.py:56
  44.6 1.7 %collective-permute-done.17.refs_3_.rest_3_ = bf16[512,128]{1,0:T(8,128)(2,1)S(1)} collective-permute-done((bf16[512,128]{1,0:T(8,128)(2,1)S(1)}, bf16[512,128]{1,0:T(8,128)(2,1)S(1)}, u32[]{:S(2)}, u32[]{:S(2)}) %collective-permute-start.17) | collective-permute-done | bytes 131104 | tf_op jit(solution)/shard_map/ppermute | solution.py:56
  48.2 19.1 %factors.1 = (f32[256,128]{1,0:T(8,128)}, bf16[2048,128]{1,0:T(8,128)(2,1)}) custom-call(s32[3,16]{1,0:T(4,128)S(1)} %bitcast.6, bf16[16,256,384]{2,1,0:T(8,128)(2,1)S(1)} %tiles.1.tiles_ref, f32[256,128]{1,0:T(8,128)S(1)} %get-tuple-element.54.mine_ref, f32[128,128]{1,0:T(8,128)S(1)} %gram.1.early_ref, ...), custom_call_target="tpu_custom_call" | custom-call | tf_op jit(solution)/shard_map/factors/pallas_call | solution.py:389
  (59 shorter events, 8.0 us)
Async XLA Ops:
  4.2 4.4 %collective-permute-start.4 = (bf16[1024,128]{1,0:T(8,128)(2,1)S(1)}, bf16[1024,128]{1,0:T(8,128)(2,1)S(1)}, u32[]{:S(2)}, u32[]{:S(2)}) collective-permute-start(bf16[1024,128]{1,0:T(8,128)(2,1)S(1)} %get-tuple-element.35), channel_id=1, source_target_pairs={{0,1},{1,0},{2,3},{3,2},{4,5},{5,4},{6,7},{7,6},{8,9},{9,8},{10,11... | collective-permute-start | bytes 786440 | tf_op jit(solution)/shard_map/ppermute | solution.py:56
  4.7 5.7 %collective-permute-start.2 = (bf16[1024,128]{1,0:T(8,128)(2,1)S(1)}, bf16[1024,128]{1,0:T(8,128)(2,1)S(1)}, u32[]{:S(2)}, u32[]{:S(2)}) collective-permute-start(bf16[1024,128]{1,0:T(8,128)(2,1)S(1)} %get-tuple-element.33), channel_id=1, source_target_pairs={{0,1},{1,0},{2,3},{3,2},{4,5},{5,4},{6,7},{7,6},{8,9},{9,8},{10,11... | collective-permute-start | bytes 786440 | tf_op jit(solution)/shard_map/ppermute | solution.py:56
  5.7 8.2 %collective-permute-start.10 = (bf16[512,128]{1,0:T(8,128)(2,1)S(1)}, bf16[512,128]{1,0:T(8,128)(2,1)S(1)}, u32[]{:S(2)}, u32[]{:S(2)}) collective-permute-start(bf16[512,128]{1,0:T(8,128)(2,1)S(1)} %get-tuple-element.42), channel_id=1, source_target_pairs={{0,2},{1,3},{2,0},{3,1},{4,6},{5,7},{6,4},{7,5},{8,10},{9,11},{10,... | collective-permute-start | bytes 393224 | tf_op jit(solution)/shard_map/ppermute | solution.py:56
  8.7 9.0 %collective-permute-start.9 = (bf16[512,128]{1,0:T(8,128)(2,1)S(1)}, bf16[512,128]{1,0:T(8,128)(2,1)S(1)}, u32[]{:S(2)}, u32[]{:S(2)}) collective-permute-start(bf16[512,128]{1,0:T(8,128)(2,1)S(1)} %get-tuple-element.41), channel_id=1, source_target_pairs={{0,4},{1,5},{2,6},{3,7},{4,0},{5,1},{6,2},{7,3},{8,12},{9,13},{10,... | collective-permute-start | bytes 393224 | tf_op jit(solution)/shard_map/ppermute | solution.py:56
  10.4 7.4 %collective-permute-start.8 = (bf16[512,128]{1,0:T(8,128)(2,1)S(1)}, bf16[512,128]{1,0:T(8,128)(2,1)S(1)}, u32[]{:S(2)}, u32[]{:S(2)}) collective-permute-start(bf16[512,128]{1,0:T(8,128)(2,1)S(1)} %get-tuple-element.40), channel_id=1, source_target_pairs={{0,6},{1,7},{2,4},{3,5},{4,2},{5,3},{6,0},{7,1},{8,14},{9,15},{10,... | collective-permute-start | bytes 393224 | tf_op jit(solution)/shard_map/ppermute | solution.py:56
  10.6 11.2 %collective-permute-start.6 = (bf16[512,128]{1,0:T(8,128)(2,1)S(1)}, bf16[512,128]{1,0:T(8,128)(2,1)S(1)}, u32[]{:S(2)}, u32[]{:S(2)}) collective-permute-start(bf16[512,128]{1,0:T(8,128)(2,1)S(1)} %get-tuple-element.38), channel_id=1, source_target_pairs={{0,2},{1,3},{2,0},{3,1},{4,6},{5,7},{6,4},{7,5},{8,10},{9,11},{10,... | collective-permute-start | bytes 393224 | tf_op jit(solution)/shard_map/ppermute | solution.py:56
  12.4 10.1 %collective-permute-start.5 = (bf16[512,128]{1,0:T(8,128)(2,1)S(1)}, bf16[512,128]{1,0:T(8,128)(2,1)S(1)}, u32[]{:S(2)}, u32[]{:S(2)}) collective-permute-start(bf16[512,128]{1,0:T(8,128)(2,1)S(1)} %get-tuple-element.36), channel_id=1, source_target_pairs={{0,4},{1,5},{2,6},{3,7},{4,0},{5,1},{6,2},{7,3},{8,12},{9,13},{10,... | collective-permute-start | bytes 393224 | tf_op jit(solution)/shard_map/ppermute | solution.py:56
  13.9 8.6 %collective-permute-start.3 = (bf16[512,128]{1,0:T(8,128)(2,1)S(1)}, bf16[512,128]{1,0:T(8,128)(2,1)S(1)}, u32[]{:S(2)}, u32[]{:S(2)}) collective-permute-start(bf16[512,128]{1,0:T(8,128)(2,1)S(1)} %get-tuple-element.34), channel_id=1, source_target_pairs={{0,6},{1,7},{2,4},{3,5},{4,2},{5,3},{6,0},{7,1},{8,14},{9,15},{10,... | collective-permute-start | bytes 393224 | tf_op jit(solution)/shard_map/ppermute | solution.py:56
  17.9 7.6 %collective-permute-start.11 = (bf16[256,128]{1,0:T(8,128)(2,1)S(1)}, bf16[256,128]{1,0:T(8,128)(2,1)S(1)}, u32[]{:S(2)}, u32[]{:S(2)}) collective-permute-start(bf16[256,128]{1,0:T(8,128)(2,1)S(1)} %get-tuple-element.46), channel_id=1, source_target_pairs={{0,16},{1,17},{2,18},{3,19},{4,20},{5,21},{6,22},{7,23},{8,24},{9,... | collective-permute-start | bytes 196616 | tf_op jit(solution)/shard_map/ppermute | solution.py:56
  20.5 6.1 %collective-permute-start.12 = (bf16[256,128]{1,0:T(8,128)(2,1)S(1)}, bf16[256,128]{1,0:T(8,128)(2,1)S(1)}, u32[]{:S(2)}, u32[]{:S(2)}) collective-permute-start(bf16[256,128]{1,0:T(8,128)(2,1)S(1)} %get-tuple-element.47), channel_id=1, source_target_pairs={{0,24},{1,25},{2,26},{3,27},{4,28},{5,29},{6,30},{7,31},{8,16},{9,... | collective-permute-start | bytes 196616 | tf_op jit(solution)/shard_map/ppermute | solution.py:56
  22.6 4.7 %collective-permute-start.7 = (bf16[256,128]{1,0:T(8,128)(2,1)S(1)}, bf16[256,128]{1,0:T(8,128)(2,1)S(1)}, u32[]{:S(2)}, u32[]{:S(2)}) collective-permute-start(bf16[256,128]{1,0:T(8,128)(2,1)S(1)} %get-tuple-element.39), channel_id=1, source_target_pairs={{0,8},{1,9},{2,10},{3,11},{4,12},{5,13},{6,14},{7,15},{8,0},{9,1},... | collective-permute-start | bytes 196616 | tf_op jit(solution)/shard_map/ppermute | solution.py:56
  27.3 4.5 %collective-permute-start.18 = (bf16[256,128]{1,0:T(8,128)(2,1)S(1)}, bf16[256,128]{1,0:T(8,128)(2,1)S(1)}, u32[]{:S(2)}, u32[]{:S(2)}) collective-permute-start(bf16[256,128]{1,0:T(8,128)(2,1)S(1)} %get-tuple-element.55), channel_id=1, source_target_pairs={{0,8},{1,9},{2,10},{3,11},{4,12},{5,13},{6,14},{7,15},{8,0},{9,1},... | collective-permute-start | bytes 196616 | tf_op jit(solution)/shard_map/ppermute | solution.py:56
  28.6 7.4 %collective-permute-start.13 = (bf16[256,128]{1,0:T(8,128)(2,1)S(1)}, bf16[256,128]{1,0:T(8,128)(2,1)S(1)}, u32[]{:S(2)}, u32[]{:S(2)}) collective-permute-start(bf16[256,128]{1,0:T(8,128)(2,1)S(1)} %get-tuple-element.55), channel_id=1, source_target_pairs={{0,16},{1,17},{2,18},{3,19},{4,20},{5,21},{6,22},{7,23},{8,24},{9,... | collective-permute-start | bytes 196616 | tf_op jit(solution)/shard_map/ppermute | solution.py:56
  31.2 6.1 %collective-permute-start.14 = (bf16[256,128]{1,0:T(8,128)(2,1)S(1)}, bf16[256,128]{1,0:T(8,128)(2,1)S(1)}, u32[]{:S(2)}, u32[]{:S(2)}) collective-permute-start(bf16[256,128]{1,0:T(8,128)(2,1)S(1)} %get-tuple-element.55), channel_id=1, source_target_pairs={{0,24},{1,25},{2,26},{3,27},{4,28},{5,29},{6,30},{7,31},{8,16},{9,... | collective-permute-start | bytes 196616 | tf_op jit(solution)/shard_map/ppermute | solution.py:56
  31.9 6.6 %collective-permute-start.19 = (bf16[512,128]{1,0:T(8,128)(2,1)S(1)}, bf16[512,128]{1,0:T(8,128)(2,1)S(1)}, u32[]{:S(2)}, u32[]{:S(2)}) collective-permute-start(bf16[512,128]{1,0:T(8,128)(2,1)S(1)} %constant_dynamic-update-slice_fusion.2.refs_4_.rest_4_), channel_id=1, source_target_pairs={{0,2},{1,3},{2,0},{3,1},{4,6},{5,7},{6,4},{7,5},{8,10},{9,11},{10,... | collective-permute-start | bytes 393224 | tf_op jit(solution)/shard_map/ppermute | solution.py:56
  33.0 6.6 %collective-permute-start.20 = (bf16[512,128]{1,0:T(8,128)(2,1)S(1)}, bf16[512,128]{1,0:T(8,128)(2,1)S(1)}, u32[]{:S(2)}, u32[]{:S(2)}) collective-permute-start(bf16[512,128]{1,0:T(8,128)(2,1)S(1)} %constant_dynamic-update-slice_fusion.2.refs_4_.rest_4_), channel_id=1, source_target_pairs={{0,4},{1,5},{2,6},{3,7},{4,0},{5,1},{6,2},{7,3},{8,12},{9,13},{10,... | collective-permute-start | bytes 393224 | tf_op jit(solution)/shard_map/ppermute | solution.py:56
  34.6 7.1 %collective-permute-start.21 = (bf16[512,128]{1,0:T(8,128)(2,1)S(1)}, bf16[512,128]{1,0:T(8,128)(2,1)S(1)}, u32[]{:S(2)}, u32[]{:S(2)}) collective-permute-start(bf16[512,128]{1,0:T(8,128)(2,1)S(1)} %constant_dynamic-update-slice_fusion.2.refs_4_.rest_4_), channel_id=1, source_target_pairs={{0,6},{1,7},{2,4},{3,5},{4,2},{5,3},{6,0},{7,1},{8,14},{9,15},{10,... | collective-permute-start | bytes 393224 | tf_op jit(solution)/shard_map/ppermute | solution.py:56
  36.0 5.7 %collective-permute-start.23 = (bf16[512,128]{1,0:T(8,128)(2,1)S(1)}, bf16[512,128]{1,0:T(8,128)(2,1)S(1)}, u32[]{:S(2)}, u32[]{:S(2)}) collective-permute-start(bf16[512,128]{1,0:T(8,128)(2,1)S(1)} %constant_dynamic-update-slice_fusion.2.refs_4_.rest_4_), channel_id=1, source_target_pairs={{0,1},{1,0},{2,3},{3,2},{4,5},{5,4},{6,7},{7,6},{8,9},{9,8},{10,11... | collective-permute-start | bytes 393224 | tf_op jit(solution)/shard_map/ppermute | solution.py:56
  37.3 6.4 %collective-permute-start.15 = (bf16[512,128]{1,0:T(8,128)(2,1)S(1)}, bf16[512,128]{1,0:T(8,128)(2,1)S(1)}, u32[]{:S(2)}, u32[]{:S(2)}) collective-permute-start(bf16[512,128]{1,0:T(8,128)(2,1)S(1)} %constant_dynamic-update-slice_fusion.refs_0_.rest_0_), channel_id=1, source_target_pairs={{0,2},{1,3},{2,0},{3,1},{4,6},{5,7},{6,4},{7,5},{8,10},{9,11},{10,... | collective-permute-start | bytes 393224 | tf_op jit(solution)/shard_map/ppermute | solution.py:56
  38.5 6.1 %collective-permute-start.16 = (bf16[512,128]{1,0:T(8,128)(2,1)S(1)}, bf16[512,128]{1,0:T(8,128)(2,1)S(1)}, u32[]{:S(2)}, u32[]{:S(2)}) collective-permute-start(bf16[512,128]{1,0:T(8,128)(2,1)S(1)} %constant_dynamic-update-slice_fusion.refs_0_.rest_0_), channel_id=1, source_target_pairs={{0,4},{1,5},{2,6},{3,7},{4,0},{5,1},{6,2},{7,3},{8,12},{9,13},{10,... | collective-permute-start | bytes 393224 | tf_op jit(solution)/shard_map/ppermute | solution.py:56
  39.5 6.8 %collective-permute-start.17 = (bf16[512,128]{1,0:T(8,128)(2,1)S(1)}, bf16[512,128]{1,0:T(8,128)(2,1)S(1)}, u32[]{:S(2)}, u32[]{:S(2)}) collective-permute-start(bf16[512,128]{1,0:T(8,128)(2,1)S(1)} %constant_dynamic-update-slice_fusion.refs_0_.rest_0_), channel_id=1, source_target_pairs={{0,6},{1,7},{2,4},{3,5},{4,2},{5,3},{6,0},{7,1},{8,14},{9,15},{10,... | collective-permute-start | bytes 393224 | tf_op jit(solution)/shard_map/ppermute | solution.py:56
  41.7 4.6 %collective-permute-start.22 = (bf16[512,128]{1,0:T(8,128)(2,1)S(1)}, bf16[512,128]{1,0:T(8,128)(2,1)S(1)}, u32[]{:S(2)}, u32[]{:S(2)}) collective-permute-start(bf16[512,128]{1,0:T(8,128)(2,1)S(1)} %constant_dynamic-update-slice_fusion.refs_0_.rest_0_), channel_id=1, source_target_pairs={{0,1},{1,0},{2,3},{3,2},{4,5},{5,4},{6,7},{7,6},{8,9},{9,8},{10,11... | collective-permute-start | bytes 393224 | tf_op jit(solution)/shard_map/ppermute | solution.py:56
  41.7 5.1 %collective-permute-start.24 = (bf16[512,128]{1,0:T(8,128)(2,1)S(1)}, bf16[512,128]{1,0:T(8,128)(2,1)S(1)}, u32[]{:S(2)}, u32[]{:S(2)}) collective-permute-start(bf16[512,128]{1,0:T(8,128)(2,1)S(1)} %collective-permute-done.19.refs_5_.rest_5_), channel_id=1, source_target_pairs={{0,1},{1,0},{2,3},{3,2},{4,5},{5,4},{6,7},{7,6},{8,9},{9,8},{10,11... | collective-permute-start | bytes 393224 | tf_op jit(solution)/shard_map/ppermute | solution.py:56
  43.7 3.2 %collective-permute-start.25 = (bf16[512,128]{1,0:T(8,128)(2,1)S(1)}, bf16[512,128]{1,0:T(8,128)(2,1)S(1)}, u32[]{:S(2)}, u32[]{:S(2)}) collective-permute-start(bf16[512,128]{1,0:T(8,128)(2,1)S(1)} %collective-permute-done.20.refs_6_.rest_6_), channel_id=1, source_target_pairs={{0,1},{1,0},{2,3},{3,2},{4,5},{5,4},{6,7},{7,6},{8,9},{9,8},{10,11... | collective-permute-start | bytes 393224 | tf_op jit(solution)/shard_map/ppermute | solution.py:56
  (10 other events, 36.1 us)

commit v11 on v10

--- a/solution.py
+++ b/solution.py
@@ -62,13 +62,19 @@
         return self.swap(value, member << (1 + self.plane_bits))
 
 
-def sum_kernel(plan, rows_ref, counts_ref, blocks_ref, sketch_ref, total_ref, *rest):
-    send_refs, (tiles_ref, docs_ref, sems) = rest[: plan.plane], rest[plan.plane :]
+def sum_kernel(plan, rows_hbm, counts_hbm, blocks_ref, sketch_ref, total_ref, *rest):
+    send_refs, (tiles_ref, docs_ref, rows_ref, counts_ref, sems, small_sems) = rest[: plan.plane], rest[plan.plane :]
     me = plan.me()
     documents, slots, block, _ = tiles_ref.shape
     half = total_ref.shape[0] // 2
     parts = sems.shape[0]
     per = documents // parts
+    small = (
+        pltpu.make_async_copy(rows_hbm, rows_ref, small_sems.at[0]),
+        pltpu.make_async_copy(counts_hbm, counts_ref, small_sems.at[1]),
+    )
+    for copy in small:
+        copy.start()
     copies = []
     for c in range(parts):
         tiles_at = pl.ds(c * per, per)
@@ -81,6 +87,8 @@
             copy.start()
         copies.append(pair)
     total_ref[...] = jnp.zeros_like(total_ref)
+    for copy in small:
+        copy.wait()
     for c in range(parts):
         for copy in copies[c]:
             copy.wait()
@@ -222,12 +230,12 @@
     across = 1.0 / jnp.sqrt(jnp.sum(diagonal, axis=0, keepdims=True))
     beyond = gram * down * across - eye
     factor = eye - take * beyond
-    for product, product_t in ((dot1, dot_t1), (dot1, dot_t1), (dot3, dot_t3)):
+    for product, product_t in ((dot1, dot_t1), (dot3, dot_t3)):
         left = factor - eye + product(factor, beyond)
         residual = factor.T - eye + product_t(left, factor)
         factor = factor - product(take * residual, factor)
     inverse_ref[...] = factor * across
-    return jnp.max(jnp.sum(jnp.abs(residual), axis=1))
+    return jnp.sum(residual * residual)
 
 
 def gram_kernel(*refs):
@@ -266,7 +274,7 @@
         terms = dot(tiles_ref[d], jnp.concatenate(picked, axis=0))
         product_ref[d * block : (d + 1) * block, :] = terms[:block] + terms[block:]
 
-    @pl.when(jnp.logical_not(residual < 1.5e-2))
+    @pl.when(jnp.logical_not(residual < 1e-3))
     def _():
         gram_ref[...] = gram
         eliminate(gram_ref, inverse_ref)
@@ -293,12 +301,15 @@
     total, *send = pl.pallas_call(
         functools.partial(sum_kernel, plan),
         out_shape=(pltpu.VMEM((features, columns), F32),) + (pltpu.VMEM((chunk, columns), BF16),) * plan.plane,
-        in_specs=[scalars(), scalars(), pl.BlockSpec(memory_space=pltpu.HBM), pl.BlockSpec(memory_space=pltpu.HBM)],
+        in_specs=[pl.BlockSpec(memory_space=pltpu.HBM)] * 4,
         out_specs=(whole(),) * (1 + plan.plane),
         scratch_shapes=[
             pltpu.VMEM(blocks.shape, BF16),
             pltpu.VMEM(sketch.shape, BF16),
+            pltpu.SMEM(rows.shape, jnp.int32),
+            pltpu.SMEM(counts.shape, jnp.int32),
             pltpu.SemaphoreType.DMA((parts, 2)),
+            pltpu.SemaphoreType.DMA((2,)),
         ],
         compiler_params=params,
         name="local_sum",
@@ -328,8 +339,9 @@
     others = range(1, plan.plane)
     got = {p: plan.swap(send[p], 1) for p in (*others, 0)}
     got[1], got[0] = lax.optimization_barrier((got[1], got[0]))
-    chip = {
-        p: pl.pallas_call(
+    chip = {}
+    for p in others:
+        chip[p] = pl.pallas_call(
             functools.partial(chip_kernel, p * chunk),
             out_shape=[shape((middle, columns), BF16)] * 2,
             in_specs=[whole(), whole()],
@@ -337,8 +349,6 @@
             compiler_params=params,
             name="chip_sum",
         )(total, got[p])
-        for p in others
-    }
     far_sent = [plan.swap_plane(chip[p][0], p) for p in reversed(others)]
     near_sent = [plan.swap_plane(chip[p][1], p) for p in reversed(others)]
     far_sent, scale = lax.optimization_barrier((far_sent, scale))

time: 67.5 us -> 66.5 us (0.985)
  Pallas kernels: 24.5 us -> 23.5 us
    pallas_call x1, Pallas kernels: 3 us -> 2.32 us  [body(): pl.pallas_call(functools.partial(sum_kernel, plan), out_shape=(pltpu.VMEM...]
  transfers between devices with their start and end apart: 30 -> 30, of which waited for: 14 -> 14; matrix products, arithmetic and copies ran while one was open for 0% -> 0% of each run, Pallas kernels for 3% -> 4%
where the time goes in v11:
time: 66.5 us; the launch traced here: 66.3 us
  starting transfers between devices  31 us (47%)
  Pallas kernels  23.5 us (35%)
  waiting for transfers between devices  11 us (17%)
  between operations  0.76 us (1%)
    ppermute x30, starting transfers between devices, swap(): return lax.ppermute(value, AXES, [(d, d ^ mask) for d in range(self.count)])  31 us
    pallas_call x1, Pallas kernels, body(): pl.pallas_call(functools.partial(last_kernel, plan, features, late), out_...  18.8 us
    ppermute x30, waiting for transfers between devices, swap(): return lax.ppermute(value, AXES, [(d, d ^ mask) for d in range(self.count)])  11 us
    pallas_call x1, Pallas kernels, body(): pl.pallas_call(functools.partial(sum_kernel, plan), out_shape=(pltpu.VMEM...  2.32 us
  transfers between devices with their start and end apart: 30, of which 14 were waited for; matrix products, arithmetic and copies ran while one was open for 0% of the time, Pallas kernels for 4%

profile of v11, /device:TPU:0, one launch (start us, length us, event | category | flops | bytes accessed | tf_op | source)
XLA Modules:
  0.0 66.3 jit_solution(17984014078320032320)
XLA Ops:
  0.6 2.3 %local_sum.1 = (f32[8192,128]{1,0:T(8,128)S(1)}, bf16[1024,128]{1,0:T(8,128)(2,1)S(1)}, bf16[1024,128]{1,0:T(8,128)(2,1)S(1)}, bf16[1024,128]{1,0:T(8,128)(2,1)S(1)}, bf16[1024,128]{1,0:T(8,128)(2,1)S(1)}) custom-call(s32[3,16]{1,0:T(4,128)} %bitcast.4, s32[16]{0:T(128)} %counts_ref.1, bf16[16,3,128,128]{3,2,1,0:T(8,128)(2,1)} %blocks_ref.3, ...), custom_call_target="tpu_custom_call" | custom-call | tf_op jit(solution)/shard_map/local_sum/pallas_call | solution.py:301
  5.1 2.9 %collective-permute-start.10 = (bf16[512,128]{1,0:T(8,128)(2,1)S(1)}, bf16[512,128]{1,0:T(8,128)(2,1)S(1)}, u32[]{:S(2)}, u32[]{:S(2)}) collective-permute-start(bf16[512,128]{1,0:T(8,128)(2,1)S(1)} %get-tuple-element.42), channel_id=1, source_target_pairs={{0,2},{1,3},{2,0},{3,1},{4,6},{5,7},{6,4},{7,5},{8,10},{9,11},{10,... | collective-permute-start | bytes 393224 | tf_op jit(solution)/shard_map/ppermute | solution.py:56
  8.1 1.6 %collective-permute-start.9 = (bf16[512,128]{1,0:T(8,128)(2,1)S(1)}, bf16[512,128]{1,0:T(8,128)(2,1)S(1)}, u32[]{:S(2)}, u32[]{:S(2)}) collective-permute-start(bf16[512,128]{1,0:T(8,128)(2,1)S(1)} %get-tuple-element.41), channel_id=1, source_target_pairs={{0,4},{1,5},{2,6},{3,7},{4,0},{5,1},{6,2},{7,3},{8,12},{9,13},{10,... | collective-permute-start | bytes 393224 | tf_op jit(solution)/shard_map/ppermute | solution.py:56
  10.0 1.8 %collective-permute-start.6 = (bf16[512,128]{1,0:T(8,128)(2,1)S(1)}, bf16[512,128]{1,0:T(8,128)(2,1)S(1)}, u32[]{:S(2)}, u32[]{:S(2)}) collective-permute-start(bf16[512,128]{1,0:T(8,128)(2,1)S(1)} %get-tuple-element.38), channel_id=1, source_target_pairs={{0,2},{1,3},{2,0},{3,1},{4,6},{5,7},{6,4},{7,5},{8,10},{9,11},{10,... | collective-permute-start | bytes 393224 | tf_op jit(solution)/shard_map/ppermute | solution.py:56
  11.7 1.5 %collective-permute-start.5 = (bf16[512,128]{1,0:T(8,128)(2,1)S(1)}, bf16[512,128]{1,0:T(8,128)(2,1)S(1)}, u32[]{:S(2)}, u32[]{:S(2)}) collective-permute-start(bf16[512,128]{1,0:T(8,128)(2,1)S(1)} %get-tuple-element.36), channel_id=1, source_target_pairs={{0,4},{1,5},{2,6},{3,7},{4,0},{5,1},{6,2},{7,3},{8,12},{9,13},{10,... | collective-permute-start | bytes 393224 | tf_op jit(solution)/shard_map/ppermute | solution.py:56
  13.2 2.0 %collective-permute-start.3 = (bf16[512,128]{1,0:T(8,128)(2,1)S(1)}, bf16[512,128]{1,0:T(8,128)(2,1)S(1)}, u32[]{:S(2)}, u32[]{:S(2)}) collective-permute-start(bf16[512,128]{1,0:T(8,128)(2,1)S(1)} %get-tuple-element.34), channel_id=1, source_target_pairs={{0,6},{1,7},{2,4},{3,5},{4,2},{5,3},{6,0},{7,1},{8,14},{9,15},{10,... | collective-permute-start | bytes 393224 | tf_op jit(solution)/shard_map/ppermute | solution.py:56
  15.4 1.7 %collective-permute-done.9.rest_1_ = bf16[512,128]{1,0:T(8,128)(2,1)S(1)} collective-permute-done((bf16[512,128]{1,0:T(8,128)(2,1)S(1)}, bf16[512,128]{1,0:T(8,128)(2,1)S(1)}, u32[]{:S(2)}, u32[]{:S(2)}) %collective-permute-start.9) | collective-permute-done | bytes 131104 | tf_op jit(solution)/shard_map/ppermute | solution.py:56
  17.2 2.6 %collective-permute-start.11 = (bf16[256,128]{1,0:T(8,128)(2,1)S(1)}, bf16[256,128]{1,0:T(8,128)(2,1)S(1)}, u32[]{:S(2)}, u32[]{:S(2)}) collective-permute-start(bf16[256,128]{1,0:T(8,128)(2,1)S(1)} %get-tuple-element.46), channel_id=1, source_target_pairs={{0,16},{1,17},{2,18},{3,19},{4,20},{5,21},{6,22},{7,23},{8,24},{9,... | collective-permute-start | bytes 196616 | tf_op jit(solution)/shard_map/ppermute | solution.py:56
  19.9 1.3 %collective-permute-start.12 = (bf16[256,128]{1,0:T(8,128)(2,1)S(1)}, bf16[256,128]{1,0:T(8,128)(2,1)S(1)}, u32[]{:S(2)}, u32[]{:S(2)}) collective-permute-start(bf16[256,128]{1,0:T(8,128)(2,1)S(1)} %get-tuple-element.47), channel_id=1, source_target_pairs={{0,24},{1,25},{2,26},{3,27},{4,28},{5,29},{6,30},{7,31},{8,16},{9,... | collective-permute-start | bytes 196616 | tf_op jit(solution)/shard_map/ppermute | solution.py:56
  21.9 1.6 %collective-permute-start.7 = (bf16[256,128]{1,0:T(8,128)(2,1)S(1)}, bf16[256,128]{1,0:T(8,128)(2,1)S(1)}, u32[]{:S(2)}, u32[]{:S(2)}) collective-permute-start(bf16[256,128]{1,0:T(8,128)(2,1)S(1)} %get-tuple-element.39), channel_id=1, source_target_pairs={{0,8},{1,9},{2,10},{3,11},{4,12},{5,13},{6,14},{7,15},{8,0},{9,1},... | collective-permute-start | bytes 196616 | tf_op jit(solution)/shard_map/ppermute | solution.py:56
  23.5 1.3 %tiles.1.tiles_ref = bf16[16,256,384]{2,1,0:T(8,128)(2,1)S(1)} custom-call(s32[3,16]{1,0:T(4,128)S(1)} %bitcast.5, s32[16]{0:T(128)S(1)} %copy-done.3, bf16[16,3,128,128]{3,2,1,0:T(8,128)(2,1)S(1)} %copy-done, f32[64,128]{1,0:T(8,128)S(1)} %bitcast.3), custom_call_target="tpu_custom_call" | custom-call | flops 1048576 | bytes 4194304 | tf_op jit(solution)/shard_map/tiles/pallas_call | solution.py:319
  24.9 1.1 %collective-permute-done.12.rest_2_ = bf16[256,128]{1,0:T(8,128)(2,1)S(1)} collective-permute-done((bf16[256,128]{1,0:T(8,128)(2,1)S(1)}, bf16[256,128]{1,0:T(8,128)(2,1)S(1)}, u32[]{:S(2)}, u32[]{:S(2)}) %collective-permute-start.12) | collective-permute-done | bytes 65568 | tf_op jit(solution)/shard_map/ppermute | solution.py:56
  26.7 1.2 %collective-permute-start.18 = (bf16[256,128]{1,0:T(8,128)(2,1)S(1)}, bf16[256,128]{1,0:T(8,128)(2,1)S(1)}, u32[]{:S(2)}, u32[]{:S(2)}) collective-permute-start(bf16[256,128]{1,0:T(8,128)(2,1)S(1)} %get-tuple-element.55), channel_id=1, source_target_pairs={{0,8},{1,9},{2,10},{3,11},{4,12},{5,13},{6,14},{7,15},{8,0},{9,1},... | collective-permute-start | bytes 196616 | tf_op jit(solution)/shard_map/ppermute | solution.py:56
  27.9 2.6 %collective-permute-start.13 = (bf16[256,128]{1,0:T(8,128)(2,1)S(1)}, bf16[256,128]{1,0:T(8,128)(2,1)S(1)}, u32[]{:S(2)}, u32[]{:S(2)}) collective-permute-start(bf16[256,128]{1,0:T(8,128)(2,1)S(1)} %get-tuple-element.55), channel_id=1, source_target_pairs={{0,16},{1,17},{2,18},{3,19},{4,20},{5,21},{6,22},{7,23},{8,24},{9,... | collective-permute-start | bytes 196616 | tf_op jit(solution)/shard_map/ppermute | solution.py:56
  31.2 1.1 %collective-permute-start.19 = (bf16[512,128]{1,0:T(8,128)(2,1)S(1)}, bf16[512,128]{1,0:T(8,128)(2,1)S(1)}, u32[]{:S(2)}, u32[]{:S(2)}) collective-permute-start(bf16[512,128]{1,0:T(8,128)(2,1)S(1)} %constant_dynamic-update-slice_fusion.2.refs_4_.rest_4_), channel_id=1, source_target_pairs={{0,2},{1,3},{2,0},{3,1},{4,6},{5,7},{6,4},{7,5},{8,10},{9,11},{10,... | collective-permute-start | bytes 393224 | tf_op jit(solution)/shard_map/ppermute | solution.py:56
  32.3 1.7 %collective-permute-start.20 = (bf16[512,128]{1,0:T(8,128)(2,1)S(1)}, bf16[512,128]{1,0:T(8,128)(2,1)S(1)}, u32[]{:S(2)}, u32[]{:S(2)}) collective-permute-start(bf16[512,128]{1,0:T(8,128)(2,1)S(1)} %constant_dynamic-update-slice_fusion.2.refs_4_.rest_4_), channel_id=1, source_target_pairs={{0,4},{1,5},{2,6},{3,7},{4,0},{5,1},{6,2},{7,3},{8,12},{9,13},{10,... | collective-permute-start | bytes 393224 | tf_op jit(solution)/shard_map/ppermute | solution.py:56
  34.0 1.4 %collective-permute-start.21 = (bf16[512,128]{1,0:T(8,128)(2,1)S(1)}, bf16[512,128]{1,0:T(8,128)(2,1)S(1)}, u32[]{:S(2)}, u32[]{:S(2)}) collective-permute-start(bf16[512,128]{1,0:T(8,128)(2,1)S(1)} %constant_dynamic-update-slice_fusion.2.refs_4_.rest_4_), channel_id=1, source_target_pairs={{0,6},{1,7},{2,4},{3,5},{4,2},{5,3},{6,0},{7,1},{8,14},{9,15},{10,... | collective-permute-start | bytes 393224 | tf_op jit(solution)/shard_map/ppermute | solution.py:56
  35.4 1.2 %collective-permute-done.14 = bf16[256,128]{1,0:T(8,128)(2,1)S(1)} collective-permute-done((bf16[256,128]{1,0:T(8,128)(2,1)S(1)}, bf16[256,128]{1,0:T(8,128)(2,1)S(1)}, u32[]{:S(2)}, u32[]{:S(2)}) %collective-permute-start.14) | collective-permute-done | bytes 65568 | tf_op jit(solution)/shard_map/ppermute | solution.py:56
  36.6 1.2 %collective-permute-start.15 = (bf16[512,128]{1,0:T(8,128)(2,1)S(1)}, bf16[512,128]{1,0:T(8,128)(2,1)S(1)}, u32[]{:S(2)}, u32[]{:S(2)}) collective-permute-start(bf16[512,128]{1,0:T(8,128)(2,1)S(1)} %constant_dynamic-update-slice_fusion.refs_0_.rest_0_), channel_id=1, source_target_pairs={{0,2},{1,3},{2,0},{3,1},{4,6},{5,7},{6,4},{7,5},{8,10},{9,11},{10,... | collective-permute-start | bytes 393224 | tf_op jit(solution)/shard_map/ppermute | solution.py:56
  37.8 1.1 %collective-permute-start.16 = (bf16[512,128]{1,0:T(8,128)(2,1)S(1)}, bf16[512,128]{1,0:T(8,128)(2,1)S(1)}, u32[]{:S(2)}, u32[]{:S(2)}) collective-permute-start(bf16[512,128]{1,0:T(8,128)(2,1)S(1)} %constant_dynamic-update-slice_fusion.refs_0_.rest_0_), channel_id=1, source_target_pairs={{0,4},{1,5},{2,6},{3,7},{4,0},{5,1},{6,2},{7,3},{8,12},{9,13},{10,... | collective-permute-start | bytes 393224 | tf_op jit(solution)/shard_map/ppermute | solution.py:56
  38.9 2.2 %collective-permute-start.17 = (bf16[512,128]{1,0:T(8,128)(2,1)S(1)}, bf16[512,128]{1,0:T(8,128)(2,1)S(1)}, u32[]{:S(2)}, u32[]{:S(2)}) collective-permute-start(bf16[512,128]{1,0:T(8,128)(2,1)S(1)} %constant_dynamic-update-slice_fusion.refs_0_.rest_0_), channel_id=1, source_target_pairs={{0,6},{1,7},{2,4},{3,5},{4,2},{5,3},{6,0},{7,1},{8,14},{9,15},{10,... | collective-permute-start | bytes 393224 | tf_op jit(solution)/shard_map/ppermute | solution.py:56
  41.6 1.5 %collective-permute-done.15.refs_1_.rest_1_ = bf16[512,128]{1,0:T(8,128)(2,1)S(1)} collective-permute-done((bf16[512,128]{1,0:T(8,128)(2,1)S(1)}, bf16[512,128]{1,0:T(8,128)(2,1)S(1)}, u32[]{:S(2)}, u32[]{:S(2)}) %collective-permute-start.15) | collective-permute-done | bytes 131104 | tf_op jit(solution)/shard_map/ppermute | solution.py:56
  43.9 1.8 %collective-permute-done.17.refs_3_.rest_3_ = bf16[512,128]{1,0:T(8,128)(2,1)S(1)} collective-permute-done((bf16[512,128]{1,0:T(8,128)(2,1)S(1)}, bf16[512,128]{1,0:T(8,128)(2,1)S(1)}, u32[]{:S(2)}, u32[]{:S(2)}) %collective-permute-start.17) | collective-permute-done | bytes 131104 | tf_op jit(solution)/shard_map/ppermute | solution.py:56
  47.5 18.8 %factors.1 = (f32[256,128]{1,0:T(8,128)}, bf16[2048,128]{1,0:T(8,128)(2,1)}) custom-call(s32[3,16]{1,0:T(4,128)S(1)} %bitcast.6, bf16[16,256,384]{2,1,0:T(8,128)(2,1)S(1)} %tiles.1.tiles_ref, f32[256,128]{1,0:T(8,128)S(1)} %get-tuple-element.54.mine_ref, f32[128,128]{1,0:T(8,128)S(1)} %gram.1.early_ref, ...), custom_call_target="tpu_custom_call" | custom-call | tf_op jit(solution)/shard_map/factors/pallas_call | solution.py:399
  (59 shorter events, 8.0 us)
Async XLA Ops:
  3.6 4.4 %collective-permute-start.4 = (bf16[1024,128]{1,0:T(8,128)(2,1)S(1)}, bf16[1024,128]{1,0:T(8,128)(2,1)S(1)}, u32[]{:S(2)}, u32[]{:S(2)}) collective-permute-start(bf16[1024,128]{1,0:T(8,128)(2,1)S(1)} %get-tuple-element.35), channel_id=1, source_target_pairs={{0,1},{1,0},{2,3},{3,2},{4,5},{5,4},{6,7},{7,6},{8,9},{9,8},{10,11... | collective-permute-start | bytes 786440 | tf_op jit(solution)/shard_map/ppermute | solution.py:56
  4.0 5.7 %collective-permute-start.2 = (bf16[1024,128]{1,0:T(8,128)(2,1)S(1)}, bf16[1024,128]{1,0:T(8,128)(2,1)S(1)}, u32[]{:S(2)}, u32[]{:S(2)}) collective-permute-start(bf16[1024,128]{1,0:T(8,128)(2,1)S(1)} %get-tuple-element.33), channel_id=1, source_target_pairs={{0,1},{1,0},{2,3},{3,2},{4,5},{5,4},{6,7},{7,6},{8,9},{9,8},{10,11... | collective-permute-start | bytes 786440 | tf_op jit(solution)/shard_map/ppermute | solution.py:56
  5.1 8.2 %collective-permute-start.10 = (bf16[512,128]{1,0:T(8,128)(2,1)S(1)}, bf16[512,128]{1,0:T(8,128)(2,1)S(1)}, u32[]{:S(2)}, u32[]{:S(2)}) collective-permute-start(bf16[512,128]{1,0:T(8,128)(2,1)S(1)} %get-tuple-element.42), channel_id=1, source_target_pairs={{0,2},{1,3},{2,0},{3,1},{4,6},{5,7},{6,4},{7,5},{8,10},{9,11},{10,... | collective-permute-start | bytes 393224 | tf_op jit(solution)/shard_map/ppermute | solution.py:56
  8.1 9.0 %collective-permute-start.9 = (bf16[512,128]{1,0:T(8,128)(2,1)S(1)}, bf16[512,128]{1,0:T(8,128)(2,1)S(1)}, u32[]{:S(2)}, u32[]{:S(2)}) collective-permute-start(bf16[512,128]{1,0:T(8,128)(2,1)S(1)} %get-tuple-element.41), channel_id=1, source_target_pairs={{0,4},{1,5},{2,6},{3,7},{4,0},{5,1},{6,2},{7,3},{8,12},{9,13},{10,... | collective-permute-start | bytes 393224 | tf_op jit(solution)/shard_map/ppermute | solution.py:56
  9.7 7.4 %collective-permute-start.8 = (bf16[512,128]{1,0:T(8,128)(2,1)S(1)}, bf16[512,128]{1,0:T(8,128)(2,1)S(1)}, u32[]{:S(2)}, u32[]{:S(2)}) collective-permute-start(bf16[512,128]{1,0:T(8,128)(2,1)S(1)} %get-tuple-element.40), channel_id=1, source_target_pairs={{0,6},{1,7},{2,4},{3,5},{4,2},{5,3},{6,0},{7,1},{8,14},{9,15},{10,... | collective-permute-start | bytes 393224 | tf_op jit(solution)/shard_map/ppermute | solution.py:56
  10.0 11.2 %collective-permute-start.6 = (bf16[512,128]{1,0:T(8,128)(2,1)S(1)}, bf16[512,128]{1,0:T(8,128)(2,1)S(1)}, u32[]{:S(2)}, u32[]{:S(2)}) collective-permute-start(bf16[512,128]{1,0:T(8,128)(2,1)S(1)} %get-tuple-element.38), channel_id=1, source_target_pairs={{0,2},{1,3},{2,0},{3,1},{4,6},{5,7},{6,4},{7,5},{8,10},{9,11},{10,... | collective-permute-start | bytes 393224 | tf_op jit(solution)/shard_map/ppermute | solution.py:56
  11.7 10.1 %collective-permute-start.5 = (bf16[512,128]{1,0:T(8,128)(2,1)S(1)}, bf16[512,128]{1,0:T(8,128)(2,1)S(1)}, u32[]{:S(2)}, u32[]{:S(2)}) collective-permute-start(bf16[512,128]{1,0:T(8,128)(2,1)S(1)} %get-tuple-element.36), channel_id=1, source_target_pairs={{0,4},{1,5},{2,6},{3,7},{4,0},{5,1},{6,2},{7,3},{8,12},{9,13},{10,... | collective-permute-start | bytes 393224 | tf_op jit(solution)/shard_map/ppermute | solution.py:56
  13.2 8.6 %collective-permute-start.3 = (bf16[512,128]{1,0:T(8,128)(2,1)S(1)}, bf16[512,128]{1,0:T(8,128)(2,1)S(1)}, u32[]{:S(2)}, u32[]{:S(2)}) collective-permute-start(bf16[512,128]{1,0:T(8,128)(2,1)S(1)} %get-tuple-element.34), channel_id=1, source_target_pairs={{0,6},{1,7},{2,4},{3,5},{4,2},{5,3},{6,0},{7,1},{8,14},{9,15},{10,... | collective-permute-start | bytes 393224 | tf_op jit(solution)/shard_map/ppermute | solution.py:56
  17.2 7.6 %collective-permute-start.11 = (bf16[256,128]{1,0:T(8,128)(2,1)S(1)}, bf16[256,128]{1,0:T(8,128)(2,1)S(1)}, u32[]{:S(2)}, u32[]{:S(2)}) collective-permute-start(bf16[256,128]{1,0:T(8,128)(2,1)S(1)} %get-tuple-element.46), channel_id=1, source_target_pairs={{0,16},{1,17},{2,18},{3,19},{4,20},{5,21},{6,22},{7,23},{8,24},{9,... | collective-permute-start | bytes 196616 | tf_op jit(solution)/shard_map/ppermute | solution.py:56
  19.9 6.1 %collective-permute-start.12 = (bf16[256,128]{1,0:T(8,128)(2,1)S(1)}, bf16[256,128]{1,0:T(8,128)(2,1)S(1)}, u32[]{:S(2)}, u32[]{:S(2)}) collective-permute-start(bf16[256,128]{1,0:T(8,128)(2,1)S(1)} %get-tuple-element.47), channel_id=1, source_target_pairs={{0,24},{1,25},{2,26},{3,27},{4,28},{5,29},{6,30},{7,31},{8,16},{9,... | collective-permute-start | bytes 196616 | tf_op jit(solution)/shard_map/ppermute | solution.py:56
  21.9 4.7 %collective-permute-start.7 = (bf16[256,128]{1,0:T(8,128)(2,1)S(1)}, bf16[256,128]{1,0:T(8,128)(2,1)S(1)}, u32[]{:S(2)}, u32[]{:S(2)}) collective-permute-start(bf16[256,128]{1,0:T(8,128)(2,1)S(1)} %get-tuple-element.39), channel_id=1, source_target_pairs={{0,8},{1,9},{2,10},{3,11},{4,12},{5,13},{6,14},{7,15},{8,0},{9,1},... | collective-permute-start | bytes 196616 | tf_op jit(solution)/shard_map/ppermute | solution.py:56
  26.7 4.5 %collective-permute-start.18 = (bf16[256,128]{1,0:T(8,128)(2,1)S(1)}, bf16[256,128]{1,0:T(8,128)(2,1)S(1)}, u32[]{:S(2)}, u32[]{:S(2)}) collective-permute-start(bf16[256,128]{1,0:T(8,128)(2,1)S(1)} %get-tuple-element.55), channel_id=1, source_target_pairs={{0,8},{1,9},{2,10},{3,11},{4,12},{5,13},{6,14},{7,15},{8,0},{9,1},... | collective-permute-start | bytes 196616 | tf_op jit(solution)/shard_map/ppermute | solution.py:56
  27.9 7.5 %collective-permute-start.13 = (bf16[256,128]{1,0:T(8,128)(2,1)S(1)}, bf16[256,128]{1,0:T(8,128)(2,1)S(1)}, u32[]{:S(2)}, u32[]{:S(2)}) collective-permute-start(bf16[256,128]{1,0:T(8,128)(2,1)S(1)} %get-tuple-element.55), channel_id=1, source_target_pairs={{0,16},{1,17},{2,18},{3,19},{4,20},{5,21},{6,22},{7,23},{8,24},{9,... | collective-permute-start | bytes 196616 | tf_op jit(solution)/shard_map/ppermute | solution.py:56
  30.5 6.1 %collective-permute-start.14 = (bf16[256,128]{1,0:T(8,128)(2,1)S(1)}, bf16[256,128]{1,0:T(8,128)(2,1)S(1)}, u32[]{:S(2)}, u32[]{:S(2)}) collective-permute-start(bf16[256,128]{1,0:T(8,128)(2,1)S(1)} %get-tuple-element.55), channel_id=1, source_target_pairs={{0,24},{1,25},{2,26},{3,27},{4,28},{5,29},{6,30},{7,31},{8,16},{9,... | collective-permute-start | bytes 196616 | tf_op jit(solution)/shard_map/ppermute | solution.py:56
  31.2 6.6 %collective-permute-start.19 = (bf16[512,128]{1,0:T(8,128)(2,1)S(1)}, bf16[512,128]{1,0:T(8,128)(2,1)S(1)}, u32[]{:S(2)}, u32[]{:S(2)}) collective-permute-start(bf16[512,128]{1,0:T(8,128)(2,1)S(1)} %constant_dynamic-update-slice_fusion.2.refs_4_.rest_4_), channel_id=1, source_target_pairs={{0,2},{1,3},{2,0},{3,1},{4,6},{5,7},{6,4},{7,5},{8,10},{9,11},{10,... | collective-permute-start | bytes 393224 | tf_op jit(solution)/shard_map/ppermute | solution.py:56
  32.3 6.6 %collective-permute-start.20 = (bf16[512,128]{1,0:T(8,128)(2,1)S(1)}, bf16[512,128]{1,0:T(8,128)(2,1)S(1)}, u32[]{:S(2)}, u32[]{:S(2)}) collective-permute-start(bf16[512,128]{1,0:T(8,128)(2,1)S(1)} %constant_dynamic-update-slice_fusion.2.refs_4_.rest_4_), channel_id=1, source_target_pairs={{0,4},{1,5},{2,6},{3,7},{4,0},{5,1},{6,2},{7,3},{8,12},{9,13},{10,... | collective-permute-start | bytes 393224 | tf_op jit(solution)/shard_map/ppermute | solution.py:56
  34.0 7.1 %collective-permute-start.21 = (bf16[512,128]{1,0:T(8,128)(2,1)S(1)}, bf16[512,128]{1,0:T(8,128)(2,1)S(1)}, u32[]{:S(2)}, u32[]{:S(2)}) collective-permute-start(bf16[512,128]{1,0:T(8,128)(2,1)S(1)} %constant_dynamic-update-slice_fusion.2.refs_4_.rest_4_), channel_id=1, source_target_pairs={{0,6},{1,7},{2,4},{3,5},{4,2},{5,3},{6,0},{7,1},{8,14},{9,15},{10,... | collective-permute-start | bytes 393224 | tf_op jit(solution)/shard_map/ppermute | solution.py:56
  35.4 5.7 %collective-permute-start.23 = (bf16[512,128]{1,0:T(8,128)(2,1)S(1)}, bf16[512,128]{1,0:T(8,128)(2,1)S(1)}, u32[]{:S(2)}, u32[]{:S(2)}) collective-permute-start(bf16[512,128]{1,0:T(8,128)(2,1)S(1)} %constant_dynamic-update-slice_fusion.2.refs_4_.rest_4_), channel_id=1, source_target_pairs={{0,1},{1,0},{2,3},{3,2},{4,5},{5,4},{6,7},{7,6},{8,9},{9,8},{10,11... | collective-permute-start | bytes 393224 | tf_op jit(solution)/shard_map/ppermute | solution.py:56
  36.6 6.5 %collective-permute-start.15 = (bf16[512,128]{1,0:T(8,128)(2,1)S(1)}, bf16[512,128]{1,0:T(8,128)(2,1)S(1)}, u32[]{:S(2)}, u32[]{:S(2)}) collective-permute-start(bf16[512,128]{1,0:T(8,128)(2,1)S(1)} %constant_dynamic-update-slice_fusion.refs_0_.rest_0_), channel_id=1, source_target_pairs={{0,2},{1,3},{2,0},{3,1},{4,6},{5,7},{6,4},{7,5},{8,10},{9,11},{10,... | collective-permute-start | bytes 393224 | tf_op jit(solution)/shard_map/ppermute | solution.py:56
  37.8 6.1 %collective-permute-start.16 = (bf16[512,128]{1,0:T(8,128)(2,1)S(1)}, bf16[512,128]{1,0:T(8,128)(2,1)S(1)}, u32[]{:S(2)}, u32[]{:S(2)}) collective-permute-start(bf16[512,128]{1,0:T(8,128)(2,1)S(1)} %constant_dynamic-update-slice_fusion.refs_0_.rest_0_), channel_id=1, source_target_pairs={{0,4},{1,5},{2,6},{3,7},{4,0},{5,1},{6,2},{7,3},{8,12},{9,13},{10,... | collective-permute-start | bytes 393224 | tf_op jit(solution)/shard_map/ppermute | solution.py:56
  38.9 6.8 %collective-permute-start.17 = (bf16[512,128]{1,0:T(8,128)(2,1)S(1)}, bf16[512,128]{1,0:T(8,128)(2,1)S(1)}, u32[]{:S(2)}, u32[]{:S(2)}) collective-permute-start(bf16[512,128]{1,0:T(8,128)(2,1)S(1)} %constant_dynamic-update-slice_fusion.refs_0_.rest_0_), channel_id=1, source_target_pairs={{0,6},{1,7},{2,4},{3,5},{4,2},{5,3},{6,0},{7,1},{8,14},{9,15},{10,... | collective-permute-start | bytes 393224 | tf_op jit(solution)/shard_map/ppermute | solution.py:56
  41.0 4.6 %collective-permute-start.22 = (bf16[512,128]{1,0:T(8,128)(2,1)S(1)}, bf16[512,128]{1,0:T(8,128)(2,1)S(1)}, u32[]{:S(2)}, u32[]{:S(2)}) collective-permute-start(bf16[512,128]{1,0:T(8,128)(2,1)S(1)} %constant_dynamic-update-slice_fusion.refs_0_.rest_0_), channel_id=1, source_target_pairs={{0,1},{1,0},{2,3},{3,2},{4,5},{5,4},{6,7},{7,6},{8,9},{9,8},{10,11... | collective-permute-start | bytes 393224 | tf_op jit(solution)/shard_map/ppermute | solution.py:56
  41.1 5.1 %collective-permute-start.24 = (bf16[512,128]{1,0:T(8,128)(2,1)S(1)}, bf16[512,128]{1,0:T(8,128)(2,1)S(1)}, u32[]{:S(2)}, u32[]{:S(2)}) collective-permute-start(bf16[512,128]{1,0:T(8,128)(2,1)S(1)} %collective-permute-done.19.refs_5_.rest_5_), channel_id=1, source_target_pairs={{0,1},{1,0},{2,3},{3,2},{4,5},{5,4},{6,7},{7,6},{8,9},{9,8},{10,11... | collective-permute-start | bytes 393224 | tf_op jit(solution)/shard_map/ppermute | solution.py:56
  43.0 3.2 %collective-permute-start.25 = (bf16[512,128]{1,0:T(8,128)(2,1)S(1)}, bf16[512,128]{1,0:T(8,128)(2,1)S(1)}, u32[]{:S(2)}, u32[]{:S(2)}) collective-permute-start(bf16[512,128]{1,0:T(8,128)(2,1)S(1)} %collective-permute-done.20.refs_6_.rest_6_), channel_id=1, source_target_pairs={{0,1},{1,0},{2,3},{3,2},{4,5},{5,4},{6,7},{7,6},{8,9},{9,8},{10,11... | collective-permute-start | bytes 393224 | tf_op jit(solution)/shard_map/ppermute | solution.py:56
  (10 other events, 36.1 us)

commit v12 on v11

--- a/solution.py
+++ b/solution.py
@@ -258,6 +258,8 @@
         size = ref.shape[0]
         core, later = divmod(i, 2 * plan.plane)
         near, member = divmod(later, plan.plane)
+        if near and member:
+            member = plan.plane - member
         base = ((core * plan.plane + member) * 2 + 1 - near) * size
         part = ref[...]
         all_ref[base : base + size, :] = part
@@ -338,7 +340,7 @@
     middle = chunk // 2
     others = range(1, plan.plane)
     got = {p: plan.swap(send[p], 1) for p in (*others, 0)}
-    got[1], got[0] = lax.optimization_barrier((got[1], got[0]))
+    got[plan.plane - 1], got[0] = lax.optimization_barrier((got[plan.plane - 1], got[0]))
     chip = {}
     for p in others:
         chip[p] = pl.pallas_call(
@@ -349,8 +351,8 @@
             compiler_params=params,
             name="chip_sum",
         )(total, got[p])
-    far_sent = [plan.swap_plane(chip[p][0], p) for p in reversed(others)]
-    near_sent = [plan.swap_plane(chip[p][1], p) for p in reversed(others)]
+    far_sent = [plan.swap_plane(chip[p][0], p) for p in others]
+    near_sent = [plan.swap_plane(chip[p][1], p) for p in others]
     far_sent, scale = lax.optimization_barrier((far_sent, scale))
 
     def plane_sum(sent, start, dtypes):
@@ -380,7 +382,7 @@
 
     line = [rounded] + [plan.swap_line(rounded, q) for q in range(1, plan.line)]
     near, far = jnp.concatenate(line[:split_at], axis=0), jnp.concatenate(line[split_at:], axis=0)
-    near = [near] + [plan.swap_plane(near, p) for p in others]
+    near = [near] + [plan.swap_plane(near, p) for p in reversed(others)]
     far = [far] + [plan.swap_plane(far, p) for p in others]
     own = far + near
     other = [plan.swap(part, 1) for part in own]

time: 66.5 us -> 66.4 us (level)
  starting transfers between devices: 31 us -> 30.1 us
  waiting for transfers between devices: 11 us -> 11.8 us
    ppermute x30, starting transfers between devices: 31 us -> 30.1 us  [swap(): return lax.ppermute(value, AXES, [(d, d ^ mask) for d in range(self.count)])]
    ppermute x30, waiting for transfers between devices: 11 us -> 11.8 us  [swap(): return lax.ppermute(value, AXES, [(d, d ^ mask) for d in range(self.count)])]
  transfers between devices with their start and end apart: 30 -> 30, of which waited for: 14 -> 13; matrix products, arithmetic and copies ran while one was open for 0% -> 0% of each run, Pallas kernels for 4% -> 4%
where the time goes in v12:
time: 66.4 us; the launch traced here: 66.2 us
  starting transfers between devices  30.1 us (45%)
  Pallas kernels  23.5 us (35%)
  waiting for transfers between devices  11.8 us (18%)
  between operations  0.77 us (1%)
    ppermute x30, starting transfers between devices, swap(): return lax.ppermute(value, AXES, [(d, d ^ mask) for d in range(self.count)])  30.1 us
    pallas_call x1, Pallas kernels, body(): pl.pallas_call(functools.partial(last_kernel, plan, features, late), out_...  18.8 us
    ppermute x30, waiting for transfers between devices, swap(): return lax.ppermute(value, AXES, [(d, d ^ mask) for d in range(self.count)])  11.8 us
    pallas_call x1, Pallas kernels, body(): pl.pallas_call(functools.partial(sum_kernel, plan), out_shape=(pltpu.VMEM...  2.32 us
  transfers between devices with their start and end apart: 30, of which 13 were waited for; matrix products, arithmetic and copies ran while one was open for 0% of the time, Pallas kernels for 4%

profile of v12, /device:TPU:0, one launch (start us, length us, event | category | flops | bytes accessed | tf_op | source)
XLA Modules:
  0.0 66.2 jit_solution(11363898778329677136)
XLA Ops:
  0.6 2.3 %local_sum.1 = (f32[8192,128]{1,0:T(8,128)S(1)}, bf16[1024,128]{1,0:T(8,128)(2,1)S(1)}, bf16[1024,128]{1,0:T(8,128)(2,1)S(1)}, bf16[1024,128]{1,0:T(8,128)(2,1)S(1)}, bf16[1024,128]{1,0:T(8,128)(2,1)S(1)}) custom-call(s32[3,16]{1,0:T(4,128)} %bitcast.4, s32[16]{0:T(128)} %counts_ref.1, bf16[16,3,128,128]{3,2,1,0:T(8,128)(2,1)} %blocks_ref.3, ...), custom_call_target="tpu_custom_call" | custom-call | tf_op jit(solution)/shard_map/local_sum/pallas_call | solution.py:303
  5.1 3.9 %collective-permute-start.10 = (bf16[512,128]{1,0:T(8,128)(2,1)S(1)}, bf16[512,128]{1,0:T(8,128)(2,1)S(1)}, u32[]{:S(2)}, u32[]{:S(2)}) collective-permute-start(bf16[512,128]{1,0:T(8,128)(2,1)S(1)} %get-tuple-element.42), channel_id=1, source_target_pairs={{0,6},{1,7},{2,4},{3,5},{4,2},{5,3},{6,0},{7,1},{8,14},{9,15},{10,... | collective-permute-start | bytes 393224 | tf_op jit(solution)/shard_map/ppermute | solution.py:56
  10.0 2.7 %collective-permute-start.6 = (bf16[512,128]{1,0:T(8,128)(2,1)S(1)}, bf16[512,128]{1,0:T(8,128)(2,1)S(1)}, u32[]{:S(2)}, u32[]{:S(2)}) collective-permute-start(bf16[512,128]{1,0:T(8,128)(2,1)S(1)} %get-tuple-element.38), channel_id=1, source_target_pairs={{0,6},{1,7},{2,4},{3,5},{4,2},{5,3},{6,0},{7,1},{8,14},{9,15},{10,... | collective-permute-start | bytes 393224 | tf_op jit(solution)/shard_map/ppermute | solution.py:56
  13.2 2.0 %collective-permute-start.3 = (bf16[512,128]{1,0:T(8,128)(2,1)S(1)}, bf16[512,128]{1,0:T(8,128)(2,1)S(1)}, u32[]{:S(2)}, u32[]{:S(2)}) collective-permute-start(bf16[512,128]{1,0:T(8,128)(2,1)S(1)} %get-tuple-element.34), channel_id=1, source_target_pairs={{0,2},{1,3},{2,0},{3,1},{4,6},{5,7},{6,4},{7,5},{8,10},{9,11},{10,... | collective-permute-start | bytes 393224 | tf_op jit(solution)/shard_map/ppermute | solution.py:56
  15.3 1.7 %collective-permute-done.9.rest_1_ = bf16[512,128]{1,0:T(8,128)(2,1)S(1)} collective-permute-done((bf16[512,128]{1,0:T(8,128)(2,1)S(1)}, bf16[512,128]{1,0:T(8,128)(2,1)S(1)}, u32[]{:S(2)}, u32[]{:S(2)}) %collective-permute-start.9) | collective-permute-done | bytes 131104 | tf_op jit(solution)/shard_map/ppermute | solution.py:56
  17.2 2.8 %collective-permute-start.11 = (bf16[256,128]{1,0:T(8,128)(2,1)S(1)}, bf16[256,128]{1,0:T(8,128)(2,1)S(1)}, u32[]{:S(2)}, u32[]{:S(2)}) collective-permute-start(bf16[256,128]{1,0:T(8,128)(2,1)S(1)} %get-tuple-element.46), channel_id=1, source_target_pairs={{0,16},{1,17},{2,18},{3,19},{4,20},{5,21},{6,22},{7,23},{8,24},{9,... | collective-permute-start | bytes 196616 | tf_op jit(solution)/shard_map/ppermute | solution.py:56
  20.0 1.4 %collective-permute-start.12 = (bf16[256,128]{1,0:T(8,128)(2,1)S(1)}, bf16[256,128]{1,0:T(8,128)(2,1)S(1)}, u32[]{:S(2)}, u32[]{:S(2)}) collective-permute-start(bf16[256,128]{1,0:T(8,128)(2,1)S(1)} %get-tuple-element.47), channel_id=1, source_target_pairs={{0,24},{1,25},{2,26},{3,27},{4,28},{5,29},{6,30},{7,31},{8,16},{9,... | collective-permute-start | bytes 196616 | tf_op jit(solution)/shard_map/ppermute | solution.py:56
  21.6 1.6 %collective-permute-start.7 = (bf16[256,128]{1,0:T(8,128)(2,1)S(1)}, bf16[256,128]{1,0:T(8,128)(2,1)S(1)}, u32[]{:S(2)}, u32[]{:S(2)}) collective-permute-start(bf16[256,128]{1,0:T(8,128)(2,1)S(1)} %get-tuple-element.39), channel_id=1, source_target_pairs={{0,8},{1,9},{2,10},{3,11},{4,12},{5,13},{6,14},{7,15},{8,0},{9,1},... | collective-permute-start | bytes 196616 | tf_op jit(solution)/shard_map/ppermute | solution.py:56
  23.2 1.3 %tiles.1.tiles_ref = bf16[16,256,384]{2,1,0:T(8,128)(2,1)S(1)} custom-call(s32[3,16]{1,0:T(4,128)S(1)} %bitcast.5, s32[16]{0:T(128)S(1)} %copy-done.3, bf16[16,3,128,128]{3,2,1,0:T(8,128)(2,1)S(1)} %copy-done, f32[64,128]{1,0:T(8,128)S(1)} %bitcast.3), custom_call_target="tpu_custom_call" | custom-call | flops 1048576 | bytes 4194304 | tf_op jit(solution)/shard_map/tiles/pallas_call | solution.py:321
  24.7 1.5 %collective-permute-done.12.rest_2_ = bf16[256,128]{1,0:T(8,128)(2,1)S(1)} collective-permute-done((bf16[256,128]{1,0:T(8,128)(2,1)S(1)}, bf16[256,128]{1,0:T(8,128)(2,1)S(1)}, u32[]{:S(2)}, u32[]{:S(2)}) %collective-permute-start.12) | collective-permute-done | bytes 65568 | tf_op jit(solution)/shard_map/ppermute | solution.py:56
  26.8 0.8 %collective-permute-start.18 = (bf16[256,128]{1,0:T(8,128)(2,1)S(1)}, bf16[256,128]{1,0:T(8,128)(2,1)S(1)}, u32[]{:S(2)}, u32[]{:S(2)}) collective-permute-start(bf16[256,128]{1,0:T(8,128)(2,1)S(1)} %get-tuple-element.55), channel_id=1, source_target_pairs={{0,8},{1,9},{2,10},{3,11},{4,12},{5,13},{6,14},{7,15},{8,0},{9,1},... | collective-permute-start | bytes 196616 | tf_op jit(solution)/shard_map/ppermute | solution.py:56
  27.6 2.9 %collective-permute-start.13 = (bf16[256,128]{1,0:T(8,128)(2,1)S(1)}, bf16[256,128]{1,0:T(8,128)(2,1)S(1)}, u32[]{:S(2)}, u32[]{:S(2)}) collective-permute-start(bf16[256,128]{1,0:T(8,128)(2,1)S(1)} %get-tuple-element.55), channel_id=1, source_target_pairs={{0,16},{1,17},{2,18},{3,19},{4,20},{5,21},{6,22},{7,23},{8,24},{9,... | collective-permute-start | bytes 196616 | tf_op jit(solution)/shard_map/ppermute | solution.py:56
  30.5 0.8 %collective-permute-start.14 = (bf16[256,128]{1,0:T(8,128)(2,1)S(1)}, bf16[256,128]{1,0:T(8,128)(2,1)S(1)}, u32[]{:S(2)}, u32[]{:S(2)}) collective-permute-start(bf16[256,128]{1,0:T(8,128)(2,1)S(1)} %get-tuple-element.55), channel_id=1, source_target_pairs={{0,24},{1,25},{2,26},{3,27},{4,28},{5,29},{6,30},{7,31},{8,16},{9,... | collective-permute-start | bytes 196616 | tf_op jit(solution)/shard_map/ppermute | solution.py:56
  31.8 1.2 %collective-permute-start.19 = (bf16[512,128]{1,0:T(8,128)(2,1)S(1)}, bf16[512,128]{1,0:T(8,128)(2,1)S(1)}, u32[]{:S(2)}, u32[]{:S(2)}) collective-permute-start(bf16[512,128]{1,0:T(8,128)(2,1)S(1)} %constant_dynamic-update-slice_fusion.2.refs_4_.rest_4_), channel_id=1, source_target_pairs={{0,6},{1,7},{2,4},{3,5},{4,2},{5,3},{6,0},{7,1},{8,14},{9,15},{10,... | collective-permute-start | bytes 393224 | tf_op jit(solution)/shard_map/ppermute | solution.py:56
  33.0 1.3 %collective-permute-start.20 = (bf16[512,128]{1,0:T(8,128)(2,1)S(1)}, bf16[512,128]{1,0:T(8,128)(2,1)S(1)}, u32[]{:S(2)}, u32[]{:S(2)}) collective-permute-start(bf16[512,128]{1,0:T(8,128)(2,1)S(1)} %constant_dynamic-update-slice_fusion.2.refs_4_.rest_4_), channel_id=1, source_target_pairs={{0,4},{1,5},{2,6},{3,7},{4,0},{5,1},{6,2},{7,3},{8,12},{9,13},{10,... | collective-permute-start | bytes 393224 | tf_op jit(solution)/shard_map/ppermute | solution.py:56
  34.3 1.1 %collective-permute-start.21 = (bf16[512,128]{1,0:T(8,128)(2,1)S(1)}, bf16[512,128]{1,0:T(8,128)(2,1)S(1)}, u32[]{:S(2)}, u32[]{:S(2)}) collective-permute-start(bf16[512,128]{1,0:T(8,128)(2,1)S(1)} %constant_dynamic-update-slice_fusion.2.refs_4_.rest_4_), channel_id=1, source_target_pairs={{0,2},{1,3},{2,0},{3,1},{4,6},{5,7},{6,4},{7,5},{8,10},{9,11},{10,... | collective-permute-start | bytes 393224 | tf_op jit(solution)/shard_map/ppermute | solution.py:56
  35.4 1.1 %collective-permute-done.14 = bf16[256,128]{1,0:T(8,128)(2,1)S(1)} collective-permute-done((bf16[256,128]{1,0:T(8,128)(2,1)S(1)}, bf16[256,128]{1,0:T(8,128)(2,1)S(1)}, u32[]{:S(2)}, u32[]{:S(2)}) %collective-permute-start.14) | collective-permute-done | bytes 65568 | tf_op jit(solution)/shard_map/ppermute | solution.py:56
  36.5 1.3 %collective-permute-start.15 = (bf16[512,128]{1,0:T(8,128)(2,1)S(1)}, bf16[512,128]{1,0:T(8,128)(2,1)S(1)}, u32[]{:S(2)}, u32[]{:S(2)}) collective-permute-start(bf16[512,128]{1,0:T(8,128)(2,1)S(1)} %constant_dynamic-update-slice_fusion.refs_0_.rest_0_), channel_id=1, source_target_pairs={{0,2},{1,3},{2,0},{3,1},{4,6},{5,7},{6,4},{7,5},{8,10},{9,11},{10,... | collective-permute-start | bytes 393224 | tf_op jit(solution)/shard_map/ppermute | solution.py:56
  37.9 1.1 %collective-permute-start.16 = (bf16[512,128]{1,0:T(8,128)(2,1)S(1)}, bf16[512,128]{1,0:T(8,128)(2,1)S(1)}, u32[]{:S(2)}, u32[]{:S(2)}) collective-permute-start(bf16[512,128]{1,0:T(8,128)(2,1)S(1)} %constant_dynamic-update-slice_fusion.refs_0_.rest_0_), channel_id=1, source_target_pairs={{0,4},{1,5},{2,6},{3,7},{4,0},{5,1},{6,2},{7,3},{8,12},{9,13},{10,... | collective-permute-start | bytes 393224 | tf_op jit(solution)/shard_map/ppermute | solution.py:56
  39.2 1.2 %collective-permute-start.17 = (bf16[512,128]{1,0:T(8,128)(2,1)S(1)}, bf16[512,128]{1,0:T(8,128)(2,1)S(1)}, u32[]{:S(2)}, u32[]{:S(2)}) collective-permute-start(bf16[512,128]{1,0:T(8,128)(2,1)S(1)} %constant_dynamic-update-slice_fusion.refs_0_.rest_0_), channel_id=1, source_target_pairs={{0,6},{1,7},{2,4},{3,5},{4,2},{5,3},{6,0},{7,1},{8,14},{9,15},{10,... | collective-permute-start | bytes 393224 | tf_op jit(solution)/shard_map/ppermute | solution.py:56
  40.9 2.1 %collective-permute-done.15.refs_1_.rest_1_ = bf16[512,128]{1,0:T(8,128)(2,1)S(1)} collective-permute-done((bf16[512,128]{1,0:T(8,128)(2,1)S(1)}, bf16[512,128]{1,0:T(8,128)(2,1)S(1)}, u32[]{:S(2)}, u32[]{:S(2)}) %collective-permute-start.15) | collective-permute-done | bytes 131104 | tf_op jit(solution)/shard_map/ppermute | solution.py:56
  43.0 2.3 %collective-permute-done.16.refs_2_.rest_2_ = bf16[512,128]{1,0:T(8,128)(2,1)S(1)} collective-permute-done((bf16[512,128]{1,0:T(8,128)(2,1)S(1)}, bf16[512,128]{1,0:T(8,128)(2,1)S(1)}, u32[]{:S(2)}, u32[]{:S(2)}) %collective-permute-start.16) | collective-permute-done | bytes 131104 | tf_op jit(solution)/shard_map/ppermute | solution.py:56
  46.7 0.7 gram.1.early_ref
  47.4 18.8 %factors.1 = (f32[256,128]{1,0:T(8,128)}, bf16[2048,128]{1,0:T(8,128)(2,1)}) custom-call(s32[3,16]{1,0:T(4,128)S(1)} %bitcast.6, bf16[16,256,384]{2,1,0:T(8,128)(2,1)S(1)} %tiles.1.tiles_ref, f32[256,128]{1,0:T(8,128)S(1)} %get-tuple-element.54.mine_ref, f32[128,128]{1,0:T(8,128)S(1)} %gram.1.early_ref, ...), custom_call_target="tpu_custom_call" | custom-call | tf_op jit(solution)/shard_map/factors/pallas_call | solution.py:401
  (59 shorter events, 7.7 us)
Async XLA Ops:
  3.6 5.4 %collective-permute-start.4 = (bf16[1024,128]{1,0:T(8,128)(2,1)S(1)}, bf16[1024,128]{1,0:T(8,128)(2,1)S(1)}, u32[]{:S(2)}, u32[]{:S(2)}) collective-permute-start(bf16[1024,128]{1,0:T(8,128)(2,1)S(1)} %get-tuple-element.35), channel_id=1, source_target_pairs={{0,1},{1,0},{2,3},{3,2},{4,5},{5,4},{6,7},{7,6},{8,9},{9,8},{10,11... | collective-permute-start | bytes 786440 | tf_op jit(solution)/shard_map/ppermute | solution.py:56
  4.0 5.6 %collective-permute-start.2 = (bf16[1024,128]{1,0:T(8,128)(2,1)S(1)}, bf16[1024,128]{1,0:T(8,128)(2,1)S(1)}, u32[]{:S(2)}, u32[]{:S(2)}) collective-permute-start(bf16[1024,128]{1,0:T(8,128)(2,1)S(1)} %get-tuple-element.33), channel_id=1, source_target_pairs={{0,1},{1,0},{2,3},{3,2},{4,5},{5,4},{6,7},{7,6},{8,9},{9,8},{10,11... | collective-permute-start | bytes 786440 | tf_op jit(solution)/shard_map/ppermute | solution.py:56
  5.1 8.1 %collective-permute-start.10 = (bf16[512,128]{1,0:T(8,128)(2,1)S(1)}, bf16[512,128]{1,0:T(8,128)(2,1)S(1)}, u32[]{:S(2)}, u32[]{:S(2)}) collective-permute-start(bf16[512,128]{1,0:T(8,128)(2,1)S(1)} %get-tuple-element.42), channel_id=1, source_target_pairs={{0,6},{1,7},{2,4},{3,5},{4,2},{5,3},{6,0},{7,1},{8,14},{9,15},{10,... | collective-permute-start | bytes 393224 | tf_op jit(solution)/shard_map/ppermute | solution.py:56
  9.0 8.0 %collective-permute-start.9 = (bf16[512,128]{1,0:T(8,128)(2,1)S(1)}, bf16[512,128]{1,0:T(8,128)(2,1)S(1)}, u32[]{:S(2)}, u32[]{:S(2)}) collective-permute-start(bf16[512,128]{1,0:T(8,128)(2,1)S(1)} %get-tuple-element.41), channel_id=1, source_target_pairs={{0,4},{1,5},{2,6},{3,7},{4,0},{5,1},{6,2},{7,3},{8,12},{9,13},{10,... | collective-permute-start | bytes 393224 | tf_op jit(solution)/shard_map/ppermute | solution.py:56
  9.6 7.4 %collective-permute-start.8 = (bf16[512,128]{1,0:T(8,128)(2,1)S(1)}, bf16[512,128]{1,0:T(8,128)(2,1)S(1)}, u32[]{:S(2)}, u32[]{:S(2)}) collective-permute-start(bf16[512,128]{1,0:T(8,128)(2,1)S(1)} %get-tuple-element.40), channel_id=1, source_target_pairs={{0,2},{1,3},{2,0},{3,1},{4,6},{5,7},{6,4},{7,5},{8,10},{9,11},{10,... | collective-permute-start | bytes 393224 | tf_op jit(solution)/shard_map/ppermute | solution.py:56
  10.0 11.3 %collective-permute-start.6 = (bf16[512,128]{1,0:T(8,128)(2,1)S(1)}, bf16[512,128]{1,0:T(8,128)(2,1)S(1)}, u32[]{:S(2)}, u32[]{:S(2)}) collective-permute-start(bf16[512,128]{1,0:T(8,128)(2,1)S(1)} %get-tuple-element.38), channel_id=1, source_target_pairs={{0,6},{1,7},{2,4},{3,5},{4,2},{5,3},{6,0},{7,1},{8,14},{9,15},{10,... | collective-permute-start | bytes 393224 | tf_op jit(solution)/shard_map/ppermute | solution.py:56
  12.7 8.6 %collective-permute-start.5 = (bf16[512,128]{1,0:T(8,128)(2,1)S(1)}, bf16[512,128]{1,0:T(8,128)(2,1)S(1)}, u32[]{:S(2)}, u32[]{:S(2)}) collective-permute-start(bf16[512,128]{1,0:T(8,128)(2,1)S(1)} %get-tuple-element.36), channel_id=1, source_target_pairs={{0,4},{1,5},{2,6},{3,7},{4,0},{5,1},{6,2},{7,3},{8,12},{9,13},{10,... | collective-permute-start | bytes 393224 | tf_op jit(solution)/shard_map/ppermute | solution.py:56
  13.2 8.3 %collective-permute-start.3 = (bf16[512,128]{1,0:T(8,128)(2,1)S(1)}, bf16[512,128]{1,0:T(8,128)(2,1)S(1)}, u32[]{:S(2)}, u32[]{:S(2)}) collective-permute-start(bf16[512,128]{1,0:T(8,128)(2,1)S(1)} %get-tuple-element.34), channel_id=1, source_target_pairs={{0,2},{1,3},{2,0},{3,1},{4,6},{5,7},{6,4},{7,5},{8,10},{9,11},{10,... | collective-permute-start | bytes 393224 | tf_op jit(solution)/shard_map/ppermute | solution.py:56
  17.2 7.5 %collective-permute-start.11 = (bf16[256,128]{1,0:T(8,128)(2,1)S(1)}, bf16[256,128]{1,0:T(8,128)(2,1)S(1)}, u32[]{:S(2)}, u32[]{:S(2)}) collective-permute-start(bf16[256,128]{1,0:T(8,128)(2,1)S(1)} %get-tuple-element.46), channel_id=1, source_target_pairs={{0,16},{1,17},{2,18},{3,19},{4,20},{5,21},{6,22},{7,23},{8,24},{9,... | collective-permute-start | bytes 196616 | tf_op jit(solution)/shard_map/ppermute | solution.py:56
  20.0 6.2 %collective-permute-start.12 = (bf16[256,128]{1,0:T(8,128)(2,1)S(1)}, bf16[256,128]{1,0:T(8,128)(2,1)S(1)}, u32[]{:S(2)}, u32[]{:S(2)}) collective-permute-start(bf16[256,128]{1,0:T(8,128)(2,1)S(1)} %get-tuple-element.47), channel_id=1, source_target_pairs={{0,24},{1,25},{2,26},{3,27},{4,28},{5,29},{6,30},{7,31},{8,16},{9,... | collective-permute-start | bytes 196616 | tf_op jit(solution)/shard_map/ppermute | solution.py:56
  21.6 5.2 %collective-permute-start.7 = (bf16[256,128]{1,0:T(8,128)(2,1)S(1)}, bf16[256,128]{1,0:T(8,128)(2,1)S(1)}, u32[]{:S(2)}, u32[]{:S(2)}) collective-permute-start(bf16[256,128]{1,0:T(8,128)(2,1)S(1)} %get-tuple-element.39), channel_id=1, source_target_pairs={{0,8},{1,9},{2,10},{3,11},{4,12},{5,13},{6,14},{7,15},{8,0},{9,1},... | collective-permute-start | bytes 196616 | tf_op jit(solution)/shard_map/ppermute | solution.py:56
  26.8 5.0 %collective-permute-start.18 = (bf16[256,128]{1,0:T(8,128)(2,1)S(1)}, bf16[256,128]{1,0:T(8,128)(2,1)S(1)}, u32[]{:S(2)}, u32[]{:S(2)}) collective-permute-start(bf16[256,128]{1,0:T(8,128)(2,1)S(1)} %get-tuple-element.55), channel_id=1, source_target_pairs={{0,8},{1,9},{2,10},{3,11},{4,12},{5,13},{6,14},{7,15},{8,0},{9,1},... | collective-permute-start | bytes 196616 | tf_op jit(solution)/shard_map/ppermute | solution.py:56
  27.6 7.8 %collective-permute-start.13 = (bf16[256,128]{1,0:T(8,128)(2,1)S(1)}, bf16[256,128]{1,0:T(8,128)(2,1)S(1)}, u32[]{:S(2)}, u32[]{:S(2)}) collective-permute-start(bf16[256,128]{1,0:T(8,128)(2,1)S(1)} %get-tuple-element.55), channel_id=1, source_target_pairs={{0,16},{1,17},{2,18},{3,19},{4,20},{5,21},{6,22},{7,23},{8,24},{9,... | collective-permute-start | bytes 196616 | tf_op jit(solution)/shard_map/ppermute | solution.py:56
  30.5 6.1 %collective-permute-start.14 = (bf16[256,128]{1,0:T(8,128)(2,1)S(1)}, bf16[256,128]{1,0:T(8,128)(2,1)S(1)}, u32[]{:S(2)}, u32[]{:S(2)}) collective-permute-start(bf16[256,128]{1,0:T(8,128)(2,1)S(1)} %get-tuple-element.55), channel_id=1, source_target_pairs={{0,24},{1,25},{2,26},{3,27},{4,28},{5,29},{6,30},{7,31},{8,16},{9,... | collective-permute-start | bytes 196616 | tf_op jit(solution)/shard_map/ppermute | solution.py:56
  31.8 6.0 %collective-permute-start.19 = (bf16[512,128]{1,0:T(8,128)(2,1)S(1)}, bf16[512,128]{1,0:T(8,128)(2,1)S(1)}, u32[]{:S(2)}, u32[]{:S(2)}) collective-permute-start(bf16[512,128]{1,0:T(8,128)(2,1)S(1)} %constant_dynamic-update-slice_fusion.2.refs_4_.rest_4_), channel_id=1, source_target_pairs={{0,6},{1,7},{2,4},{3,5},{4,2},{5,3},{6,0},{7,1},{8,14},{9,15},{10,... | collective-permute-start | bytes 393224 | tf_op jit(solution)/shard_map/ppermute | solution.py:56
  33.0 6.2 %collective-permute-start.20 = (bf16[512,128]{1,0:T(8,128)(2,1)S(1)}, bf16[512,128]{1,0:T(8,128)(2,1)S(1)}, u32[]{:S(2)}, u32[]{:S(2)}) collective-permute-start(bf16[512,128]{1,0:T(8,128)(2,1)S(1)} %constant_dynamic-update-slice_fusion.2.refs_4_.rest_4_), channel_id=1, source_target_pairs={{0,4},{1,5},{2,6},{3,7},{4,0},{5,1},{6,2},{7,3},{8,12},{9,13},{10,... | collective-permute-start | bytes 393224 | tf_op jit(solution)/shard_map/ppermute | solution.py:56
  34.3 6.1 %collective-permute-start.21 = (bf16[512,128]{1,0:T(8,128)(2,1)S(1)}, bf16[512,128]{1,0:T(8,128)(2,1)S(1)}, u32[]{:S(2)}, u32[]{:S(2)}) collective-permute-start(bf16[512,128]{1,0:T(8,128)(2,1)S(1)} %constant_dynamic-update-slice_fusion.2.refs_4_.rest_4_), channel_id=1, source_target_pairs={{0,2},{1,3},{2,0},{3,1},{4,6},{5,7},{6,4},{7,5},{8,10},{9,11},{10,... | collective-permute-start | bytes 393224 | tf_op jit(solution)/shard_map/ppermute | solution.py:56
  35.4 5.0 %collective-permute-start.23 = (bf16[512,128]{1,0:T(8,128)(2,1)S(1)}, bf16[512,128]{1,0:T(8,128)(2,1)S(1)}, u32[]{:S(2)}, u32[]{:S(2)}) collective-permute-start(bf16[512,128]{1,0:T(8,128)(2,1)S(1)} %constant_dynamic-update-slice_fusion.2.refs_4_.rest_4_), channel_id=1, source_target_pairs={{0,1},{1,0},{2,3},{3,2},{4,5},{5,4},{6,7},{7,6},{8,9},{9,8},{10,11... | collective-permute-start | bytes 393224 | tf_op jit(solution)/shard_map/ppermute | solution.py:56
  36.5 6.5 %collective-permute-start.15 = (bf16[512,128]{1,0:T(8,128)(2,1)S(1)}, bf16[512,128]{1,0:T(8,128)(2,1)S(1)}, u32[]{:S(2)}, u32[]{:S(2)}) collective-permute-start(bf16[512,128]{1,0:T(8,128)(2,1)S(1)} %constant_dynamic-update-slice_fusion.refs_0_.rest_0_), channel_id=1, source_target_pairs={{0,2},{1,3},{2,0},{3,1},{4,6},{5,7},{6,4},{7,5},{8,10},{9,11},{10,... | collective-permute-start | bytes 393224 | tf_op jit(solution)/shard_map/ppermute | solution.py:56
  37.9 7.5 %collective-permute-start.16 = (bf16[512,128]{1,0:T(8,128)(2,1)S(1)}, bf16[512,128]{1,0:T(8,128)(2,1)S(1)}, u32[]{:S(2)}, u32[]{:S(2)}) collective-permute-start(bf16[512,128]{1,0:T(8,128)(2,1)S(1)} %constant_dynamic-update-slice_fusion.refs_0_.rest_0_), channel_id=1, source_target_pairs={{0,4},{1,5},{2,6},{3,7},{4,0},{5,1},{6,2},{7,3},{8,12},{9,13},{10,... | collective-permute-start | bytes 393224 | tf_op jit(solution)/shard_map/ppermute | solution.py:56
  39.2 6.2 %collective-permute-start.17 = (bf16[512,128]{1,0:T(8,128)(2,1)S(1)}, bf16[512,128]{1,0:T(8,128)(2,1)S(1)}, u32[]{:S(2)}, u32[]{:S(2)}) collective-permute-start(bf16[512,128]{1,0:T(8,128)(2,1)S(1)} %constant_dynamic-update-slice_fusion.refs_0_.rest_0_), channel_id=1, source_target_pairs={{0,6},{1,7},{2,4},{3,5},{4,2},{5,3},{6,0},{7,1},{8,14},{9,15},{10,... | collective-permute-start | bytes 393224 | tf_op jit(solution)/shard_map/ppermute | solution.py:56
  40.4 5.5 %collective-permute-start.22 = (bf16[512,128]{1,0:T(8,128)(2,1)S(1)}, bf16[512,128]{1,0:T(8,128)(2,1)S(1)}, u32[]{:S(2)}, u32[]{:S(2)}) collective-permute-start(bf16[512,128]{1,0:T(8,128)(2,1)S(1)} %constant_dynamic-update-slice_fusion.refs_0_.rest_0_), channel_id=1, source_target_pairs={{0,1},{1,0},{2,3},{3,2},{4,5},{5,4},{6,7},{7,6},{8,9},{9,8},{10,11... | collective-permute-start | bytes 393224 | tf_op jit(solution)/shard_map/ppermute | solution.py:56
  40.4 5.5 %collective-permute-start.24 = (bf16[512,128]{1,0:T(8,128)(2,1)S(1)}, bf16[512,128]{1,0:T(8,128)(2,1)S(1)}, u32[]{:S(2)}, u32[]{:S(2)}) collective-permute-start(bf16[512,128]{1,0:T(8,128)(2,1)S(1)} %collective-permute-done.19.refs_5_.rest_5_), channel_id=1, source_target_pairs={{0,1},{1,0},{2,3},{3,2},{4,5},{5,4},{6,7},{7,6},{8,9},{9,8},{10,11... | collective-permute-start | bytes 393224 | tf_op jit(solution)/shard_map/ppermute | solution.py:56
  43.0 3.4 %collective-permute-start.25 = (bf16[512,128]{1,0:T(8,128)(2,1)S(1)}, bf16[512,128]{1,0:T(8,128)(2,1)S(1)}, u32[]{:S(2)}, u32[]{:S(2)}) collective-permute-start(bf16[512,128]{1,0:T(8,128)(2,1)S(1)} %collective-permute-done.20.refs_6_.rest_6_), channel_id=1, source_target_pairs={{0,1},{1,0},{2,3},{3,2},{4,5},{5,4},{6,7},{7,6},{8,9},{9,8},{10,11... | collective-permute-start | bytes 393224 | tf_op jit(solution)/shard_map/ppermute | solution.py:56
  (10 other events, 34.0 us)

commit v13 on v12

--- a/solution.py
+++ b/solution.py
@@ -63,7 +63,7 @@
 
 
 def sum_kernel(plan, rows_hbm, counts_hbm, blocks_ref, sketch_ref, total_ref, *rest):
-    send_refs, (tiles_ref, docs_ref, rows_ref, counts_ref, sems, small_sems) = rest[: plan.plane], rest[plan.plane :]
+    first_ref, other_ref, tiles_ref, docs_ref, rows_ref, counts_ref, sems, small_sems = rest
     me = plan.me()
     documents, slots, block, _ = tiles_ref.shape
     half = total_ref.shape[0] // 2
@@ -100,9 +100,9 @@
                 for p in range(plan.pieces):
                     at = pl.ds(plan.start(me, rows_ref[s, d], p), plan.piece)
                     total_ref[at, :] += term[p * plan.piece : (p + 1) * plan.piece]
-    for p, send_ref in enumerate(send_refs):
-        size = send_ref.shape[0]
-        send_ref[...] = total_ref[half + p * size : half + (p + 1) * size, :].astype(BF16)
+    later = other_ref.shape[0]
+    first_ref[...] = total_ref[half + later :, :].astype(BF16)
+    other_ref[...] = total_ref[half : half + later, :].astype(BF16)
 
 
 def tiles_kernel(rows_ref, counts_ref, blocks_ref, weights_ref, out_ref):
@@ -128,11 +128,12 @@
     scale_ref[...] = turned_ref[pl.ds(pl.multiple_of(inside, plan.piece), plan.flat), :]
 
 
-def chip_kernel(start, total_ref, got_ref, far_ref, near_ref):
+def chip_kernel(start, got_start, total_ref, got_ref, far_ref, near_ref):
     middle = near_ref.shape[0]
     for ref, at in ((far_ref, middle), (near_ref, 0)):
         held = total_ref[start + at : start + at + middle, :]
-        ref[...] = (held + got_ref[at : at + middle, :].astype(F32)).astype(BF16)
+        got = got_ref[got_start + at : got_start + at + middle, :]
+        ref[...] = (held + got.astype(F32)).astype(BF16)
 
 
 def plane_kernel(flat, start, total_ref, got_ref, *rest):
@@ -238,33 +239,38 @@
     return jnp.sum(residual * residual)
 
 
-def gram_kernel(*refs):
-    gram = jnp.zeros(refs[-1].shape, F32)
-    for ref in refs[:-1]:
+def place(plan, index, size):
+    core, later = divmod(index, 2 * plan.plane)
+    near, member = divmod(later, plan.plane)
+    if near and member:
+        member = plan.plane - member
+    return ((core * plan.plane + member) * 2 + 1 - near) * size
+
+
+def take(plan, indices, refs, all_ref, gram):
+    for index, ref in zip(indices, refs):
+        size = ref.shape[0]
+        base = place(plan, index, size)
         part = ref[...]
+        all_ref[base : base + size, :] = part
         gram += lax.dot_general(part, part, (((0,), (0,)), ((), ())), preferred_element_type=F32)
-    refs[-1][...] = gram
-
-
-def last_kernel(plan, features, late, rows_ref, tiles_ref, mine_ref, early_ref, *rest):
-    parts, (basis_ref, factors_ref) = rest[: 4 * plan.plane], rest[4 * plan.plane : 4 * plan.plane + 2]
-    all_ref, product_ref, gram_ref, inverse_ref = rest[4 * plan.plane + 2 :]
+    return gram
+
+
+def gather_kernel(plan, indices, before, *refs):
+    parts, (all_ref, gram_ref) = refs[-2 - len(indices) : -2], refs[-2:]
+    gram = refs[1][...] if before else jnp.zeros(gram_ref.shape, F32)
+    gram_ref[...] = take(plan, indices, parts, all_ref, gram)
+
+
+def last_kernel(plan, features, late, rows_ref, tiles_ref, mine_ref, _, early_ref, *rest):
+    parts = rest[: len(late)]
+    basis_ref, factors_ref, all_ref, product_ref, gram_ref, inverse_ref = rest[len(late) :]
     me = plan.me()
     documents = tiles_ref.shape[0]
     block = tiles_ref.shape[1] // 2
     slots = tiles_ref.shape[2] // block
-    gram = early_ref[...]
-    for i, ref in enumerate(parts):
-        size = ref.shape[0]
-        core, later = divmod(i, 2 * plan.plane)
-        near, member = divmod(later, plan.plane)
-        if near and member:
-            member = plan.plane - member
-        base = ((core * plan.plane + member) * 2 + 1 - near) * size
-        part = ref[...]
-        all_ref[base : base + size, :] = part
-        if i in late:
-            gram += lax.dot_general(part, part, (((0,), (0,)), ((), ())), preferred_element_type=F32)
+    gram = take(plan, late, parts, all_ref, early_ref[...])
     gram = gram * (1.0 / features)
     residual = newton(gram, inverse_ref)
     for d in range(documents):
@@ -300,11 +306,15 @@
     rows = rows.T
     parts = min(4, documents)
 
-    total, *send = pl.pallas_call(
+    total, first, later = pl.pallas_call(
         functools.partial(sum_kernel, plan),
-        out_shape=(pltpu.VMEM((features, columns), F32),) + (pltpu.VMEM((chunk, columns), BF16),) * plan.plane,
+        out_shape=(
+            pltpu.VMEM((features, columns), F32),
+            pltpu.VMEM((chunk, columns), BF16),
+            pltpu.VMEM((half - chunk, columns), BF16),
+        ),
         in_specs=[pl.BlockSpec(memory_space=pltpu.HBM)] * 4,
-        out_specs=(whole(),) * (1 + plan.plane),
+        out_specs=(whole(),) * 3,
         scratch_shapes=[
             pltpu.VMEM(blocks.shape, BF16),
             pltpu.VMEM(sketch.shape, BF16),
@@ -339,18 +349,18 @@
 
     middle = chunk // 2
     others = range(1, plan.plane)
-    got = {p: plan.swap(send[p], 1) for p in (*others, 0)}
-    got[plan.plane - 1], got[0] = lax.optimization_barrier((got[plan.plane - 1], got[0]))
+    first, later = plan.swap(first, 1), plan.swap(later, 1)
     chip = {}
     for p in others:
+        last = p == plan.plane - 1
         chip[p] = pl.pallas_call(
-            functools.partial(chip_kernel, p * chunk),
+            functools.partial(chip_kernel, p * chunk, 0 if last else p * chunk),
             out_shape=[shape((middle, columns), BF16)] * 2,
             in_specs=[whole(), whole()],
             out_specs=[whole()] * 2,
             compiler_params=params,
             name="chip_sum",
-        )(total, got[p])
+        )(total, first if last else later)
     far_sent = [plan.swap_plane(chip[p][0], p) for p in others]
     near_sent = [plan.swap_plane(chip[p][1], p) for p in others]
     far_sent, scale = lax.optimization_barrier((far_sent, scale))
@@ -363,14 +373,14 @@
             out_specs=[whole()] * len(dtypes),
             compiler_params=params,
             name="plane_sum",
-        )(total, got[0], *sent)
+        )(total, later, *sent)
 
     split_at = plan.line // 2
     far = plane_sum(far_sent, middle, [BF16] * split_at)
     far = [plan.swap_line(part, split_at + q) for q, part in enumerate(far)]
     held, *near = plane_sum(near_sent, 0, [F32] + [BF16] * (split_at - 1))
     near = [plan.swap_line(part, 1 + q) for q, part in enumerate(near)]
-    near, far, tiles = lax.optimization_barrier((near, far, tiles))
+    far, near, tiles = lax.optimization_barrier((far, near, tiles))
     mine, rounded = pl.pallas_call(
         line_kernel,
         out_shape=(shape((flat, columns), F32), shape((flat, columns), BF16)),
@@ -388,30 +398,42 @@
     other = [plan.swap(part, 1) for part in own]
 
     pieces = own + other
-    late = range(len(own) + 1, len(own) + plan.plane)
-    gram = pl.pallas_call(
-        gram_kernel,
-        out_shape=shape((columns, columns), F32),
-        in_specs=[whole()] * (len(pieces) - len(late)),
-        out_specs=whole(),
-        compiler_params=params,
-        cost_estimate=pl.CostEstimate(flops=2 * features * columns * columns, bytes_accessed=4 << 20, transcendentals=0),
-        name="gram",
-    )(*[piece for i, piece in enumerate(pieces) if i not in late])
-    return pl.pallas_call(
+    count = len(own)
+    gathered = (pltpu.VMEM((features, columns), BF16), pltpu.VMEM((columns, columns), F32))
+
+    def gather(before, indices):
+        return pl.pallas_call(
+            functools.partial(gather_kernel, plan, indices, bool(before)),
+            out_shape=gathered,
+            in_specs=[whole()] * (len(before) + len(indices)),
+            out_specs=(whole(), whole()),
+            input_output_aliases={0: 0} if before else {},
+            compiler_params=params,
+            cost_estimate=pl.CostEstimate(
+                flops=2 * middle * len(indices) * columns * columns, bytes_accessed=2 << 20, transcendentals=0
+            ),
+            name="gram",
+        )(*before, *[pieces[i] for i in indices])
+
+    late = list(range(count + 1, count + plan.plane))
+    early = list(range(plan.plane, count)) + [0]
+    between = [i for i in range(2 * count) if i not in late and i not in early]
+    state = gather(gather((), early), between)
+    basis, factors, _ = pl.pallas_call(
         functools.partial(last_kernel, plan, features, late),
-        out_shape=(shape((flat, columns), F32), shape((documents * block, columns), BF16)),
-        in_specs=[scalars()] + [whole()] * (3 + len(pieces)),
-        out_specs=(whole(), whole()),
+        out_shape=(shape((flat, columns), F32), shape((documents * block, columns), BF16), gathered[0]),
+        in_specs=[scalars()] + [whole()] * (4 + len(late)),
+        out_specs=(whole(),) * 3,
+        input_output_aliases={3: 2},
         scratch_shapes=[
-            pltpu.VMEM((features, columns), BF16),
             pltpu.VMEM((documents * block, columns), F32),
             pltpu.VMEM((columns, columns), F32),
             pltpu.VMEM((columns, columns), F32),
         ],
         compiler_params=params,
         name="factors",
-    )(rows, tiles, mine, gram, *pieces)
+    )(rows, tiles, mine, *state, *[pieces[i] for i in late])
+    return basis, factors
 
 
 def solution(mesh):

time: 66.4 us -> 68 us (1.024)
  waiting for transfers between devices: 11.8 us -> 16.2 us
  starting transfers between devices: 30.1 us -> 27.1 us
    ppermute x30 -> x28, waiting for transfers between devices: 11.8 us -> 16.2 us  [swap(): return lax.ppermute(value, AXES, [(d, d ^ mask) for d in range(self.count)])]
    ppermute x30 -> x28, starting transfers between devices: 30.1 us -> 27.1 us  [swap(): return lax.ppermute(value, AXES, [(d, d ^ mask) for d in range(self.count)])]
  transfers between devices with their start and end apart: 30 -> 28, of which waited for: 13 -> 11; matrix products, arithmetic and copies ran while one was open for 0% -> 0% of each run, Pallas kernels for 4% -> 4%
where the time goes in v13:
time: 68 us; the launch traced here: 67.8 us
  starting transfers between devices  27.1 us (40%)
  Pallas kernels  23.7 us (35%)
  waiting for transfers between devices  16.2 us (24%)
  between operations  0.79 us (1%)
    ppermute x28, starting transfers between devices, swap(): return lax.ppermute(value, AXES, [(d, d ^ mask) for d in range(self.count)])  27.1 us
    pallas_call x1, Pallas kernels, body(): pl.pallas_call(functools.partial(last_kernel, plan, features, late), out_...  18.8 us
    ppermute x28, waiting for transfers between devices, swap(): return lax.ppermute(value, AXES, [(d, d ^ mask) for d in range(self.count)])  16.2 us
    pallas_call x1, Pallas kernels, body(): pl.pallas_call(functools.partial(sum_kernel, plan), out_shape=(pltpu.VMEM...  2.31 us
  transfers between devices with their start and end apart: 28, of which 11 were waited for; matrix products, arithmetic and copies ran while one was open for 0% of the time, Pallas kernels for 4%

profile of v13, /device:TPU:0, one launch (start us, length us, event | category | flops | bytes accessed | tf_op | source)
XLA Modules:
  0.0 67.8 jit_solution(8579182072430331658)
XLA Ops:
  0.6 2.3 %local_sum.1 = (f32[8192,128]{1,0:T(8,128)S(1)}, bf16[1024,128]{1,0:T(8,128)(2,1)S(1)}, bf16[3072,128]{1,0:T(8,128)(2,1)S(1)}) custom-call(s32[3,16]{1,0:T(4,128)} %bitcast.4, s32[16]{0:T(128)} %counts_ref.1, bf16[16,3,128,128]{3,2,1,0:T(8,128)(2,1)} %blocks_ref.3, bf16[2048,128]{1,0:T(8,128)(2,1)} %sketch_ref.1), custom_call_target="tpu_custom_call" | custom-call | tf_op jit(solution)/shard_map/local_sum/pallas_call | solution.py:309
  3.6 2.2 %collective-permute-done.3.got_ref = bf16[1024,128]{1,0:T(8,128)(2,1)S(1)} collective-permute-done((bf16[1024,128]{1,0:T(8,128)(2,1)S(1)}, bf16[1024,128]{1,0:T(8,128)(2,1)S(1)}, u32[]{:S(2)}, u32[]{:S(2)}) %collective-permute-start.3) | collective-permute-done | bytes 262176 | tf_op jit(solution)/shard_map/ppermute | solution.py:56
  5.8 3.9 %collective-permute-start.4 = (bf16[512,128]{1,0:T(8,128)(2,1)S(1)}, bf16[512,128]{1,0:T(8,128)(2,1)S(1)}, u32[]{:S(2)}, u32[]{:S(2)}) collective-permute-start(bf16[512,128]{1,0:T(8,128)(2,1)S(1)} %get-tuple-element.36), channel_id=1, source_target_pairs={{0,6},{1,7},{2,4},{3,5},{4,2},{5,3},{6,0},{7,1},{8,14},{9,15},{10,... | collective-permute-start | bytes 393224 | tf_op jit(solution)/shard_map/ppermute | solution.py:56
  9.8 0.6 collective-permute-start.1
  10.5 2.9 %collective-permute-start.9 = (bf16[512,128]{1,0:T(8,128)(2,1)S(1)}, bf16[512,128]{1,0:T(8,128)(2,1)S(1)}, u32[]{:S(2)}, u32[]{:S(2)}) collective-permute-start(bf16[512,128]{1,0:T(8,128)(2,1)S(1)} %get-tuple-element.44), channel_id=1, source_target_pairs={{0,6},{1,7},{2,4},{3,5},{4,2},{5,3},{6,0},{7,1},{8,14},{9,15},{10,... | collective-permute-start | bytes 393224 | tf_op jit(solution)/shard_map/ppermute | solution.py:56
  14.0 2.0 %collective-permute-start.8 = (bf16[512,128]{1,0:T(8,128)(2,1)S(1)}, bf16[512,128]{1,0:T(8,128)(2,1)S(1)}, u32[]{:S(2)}, u32[]{:S(2)}) collective-permute-start(bf16[512,128]{1,0:T(8,128)(2,1)S(1)} %get-tuple-element.43), channel_id=1, source_target_pairs={{0,4},{1,5},{2,6},{3,7},{4,0},{5,1},{6,2},{7,3},{8,12},{9,13},{10,... | collective-permute-start | bytes 393224 | tf_op jit(solution)/shard_map/ppermute | solution.py:56
  16.1 1.2 %collective-permute-done.1.rest_0_ = bf16[512,128]{1,0:T(8,128)(2,1)S(1)} collective-permute-done((bf16[512,128]{1,0:T(8,128)(2,1)S(1)}, bf16[512,128]{1,0:T(8,128)(2,1)S(1)}, u32[]{:S(2)}, u32[]{:S(2)}) %collective-permute-start.1) | collective-permute-done | bytes 131104 | tf_op jit(solution)/shard_map/ppermute | solution.py:56
  17.3 2.3 %collective-permute-done.2.rest_1_ = bf16[512,128]{1,0:T(8,128)(2,1)S(1)} collective-permute-done((bf16[512,128]{1,0:T(8,128)(2,1)S(1)}, bf16[512,128]{1,0:T(8,128)(2,1)S(1)}, u32[]{:S(2)}, u32[]{:S(2)}) %collective-permute-start.2) | collective-permute-done | bytes 131104 | tf_op jit(solution)/shard_map/ppermute | solution.py:56
  19.7 2.7 %collective-permute-start.5 = (bf16[256,128]{1,0:T(8,128)(2,1)S(1)}, bf16[256,128]{1,0:T(8,128)(2,1)S(1)}, u32[]{:S(2)}, u32[]{:S(2)}) collective-permute-start(bf16[256,128]{1,0:T(8,128)(2,1)S(1)} %get-tuple-element.40), channel_id=1, source_target_pairs={{0,16},{1,17},{2,18},{3,19},{4,20},{5,21},{6,22},{7,23},{8,24},{9,... | collective-permute-start | bytes 196616 | tf_op jit(solution)/shard_map/ppermute | solution.py:56
  22.4 1.3 %collective-permute-start.6 = (bf16[256,128]{1,0:T(8,128)(2,1)S(1)}, bf16[256,128]{1,0:T(8,128)(2,1)S(1)}, u32[]{:S(2)}, u32[]{:S(2)}) collective-permute-start(bf16[256,128]{1,0:T(8,128)(2,1)S(1)} %get-tuple-element.41), channel_id=1, source_target_pairs={{0,24},{1,25},{2,26},{3,27},{4,28},{5,29},{6,30},{7,31},{8,16},{9,... | collective-permute-start | bytes 196616 | tf_op jit(solution)/shard_map/ppermute | solution.py:56
  24.2 1.3 %tiles.1.tiles_ref = bf16[16,256,384]{2,1,0:T(8,128)(2,1)S(1)} custom-call(s32[3,16]{1,0:T(4,128)S(1)} %bitcast.5, s32[16]{0:T(128)S(1)} %copy-done.3, bf16[16,3,128,128]{3,2,1,0:T(8,128)(2,1)S(1)} %copy-done, f32[64,128]{1,0:T(8,128)S(1)} %bitcast.3), custom_call_target="tpu_custom_call" | custom-call | flops 1048576 | bytes 4194304 | tf_op jit(solution)/shard_map/tiles/pallas_call | solution.py:331
  25.5 3.1 %collective-permute-done.6.rest_2_ = bf16[256,128]{1,0:T(8,128)(2,1)S(1)} collective-permute-done((bf16[256,128]{1,0:T(8,128)(2,1)S(1)}, bf16[256,128]{1,0:T(8,128)(2,1)S(1)}, u32[]{:S(2)}, u32[]{:S(2)}) %collective-permute-start.6) | collective-permute-done | bytes 65568 | tf_op jit(solution)/shard_map/ppermute | solution.py:56
  28.6 0.7 collective-permute-done.10.rest_0_
  29.4 2.0 %collective-permute-start.15 = (bf16[256,128]{1,0:T(8,128)(2,1)S(1)}, bf16[256,128]{1,0:T(8,128)(2,1)S(1)}, u32[]{:S(2)}, u32[]{:S(2)}) collective-permute-start(bf16[256,128]{1,0:T(8,128)(2,1)S(1)} %get-tuple-element.53), channel_id=1, source_target_pairs={{0,16},{1,17},{2,18},{3,19},{4,20},{5,21},{6,22},{7,23},{8,24},{9,... | collective-permute-start | bytes 196616 | tf_op jit(solution)/shard_map/ppermute | solution.py:56
  31.4 2.4 %collective-permute-start.16 = (bf16[256,128]{1,0:T(8,128)(2,1)S(1)}, bf16[256,128]{1,0:T(8,128)(2,1)S(1)}, u32[]{:S(2)}, u32[]{:S(2)}) collective-permute-start(bf16[256,128]{1,0:T(8,128)(2,1)S(1)} %get-tuple-element.53), channel_id=1, source_target_pairs={{0,24},{1,25},{2,26},{3,27},{4,28},{5,29},{6,30},{7,31},{8,16},{9,... | collective-permute-start | bytes 196616 | tf_op jit(solution)/shard_map/ppermute | solution.py:56
  33.8 0.7 collective-permute-start.12
  34.5 2.3 %collective-permute-start.13 = (bf16[512,128]{1,0:T(8,128)(2,1)S(1)}, bf16[512,128]{1,0:T(8,128)(2,1)S(1)}, u32[]{:S(2)}, u32[]{:S(2)}) collective-permute-start(bf16[512,128]{1,0:T(8,128)(2,1)S(1)} %constant_dynamic-update-slice_fusion.refs_0_), channel_id=1, source_target_pairs={{0,4},{1,5},{2,6},{3,7},{4,0},{5,1},{6,2},{7,3},{8,12},{9,13},{10,... | collective-permute-start | bytes 393224 | tf_op jit(solution)/shard_map/ppermute | solution.py:56
  37.5 1.5 %collective-permute-start.17 = (bf16[512,128]{1,0:T(8,128)(2,1)S(1)}, bf16[512,128]{1,0:T(8,128)(2,1)S(1)}, u32[]{:S(2)}, u32[]{:S(2)}) collective-permute-start(bf16[512,128]{1,0:T(8,128)(2,1)S(1)} %constant_dynamic-update-slice_fusion.2.refs_4_), channel_id=1, source_target_pairs={{0,2},{1,3},{2,0},{3,1},{4,6},{5,7},{6,4},{7,5},{8,10},{9,11},{10,... | collective-permute-start | bytes 393224 | tf_op jit(solution)/shard_map/ppermute | solution.py:56
  39.0 0.9 %collective-permute-start.18 = (bf16[512,128]{1,0:T(8,128)(2,1)S(1)}, bf16[512,128]{1,0:T(8,128)(2,1)S(1)}, u32[]{:S(2)}, u32[]{:S(2)}) collective-permute-start(bf16[512,128]{1,0:T(8,128)(2,1)S(1)} %constant_dynamic-update-slice_fusion.2.refs_4_), channel_id=1, source_target_pairs={{0,4},{1,5},{2,6},{3,7},{4,0},{5,1},{6,2},{7,3},{8,12},{9,13},{10,... | collective-permute-start | bytes 393224 | tf_op jit(solution)/shard_map/ppermute | solution.py:56
  39.9 1.2 %collective-permute-done.12.refs_1_ = bf16[512,128]{1,0:T(8,128)(2,1)S(1)} collective-permute-done((bf16[512,128]{1,0:T(8,128)(2,1)S(1)}, bf16[512,128]{1,0:T(8,128)(2,1)S(1)}, u32[]{:S(2)}, u32[]{:S(2)}) %collective-permute-start.12) | collective-permute-done | bytes 131104 | tf_op jit(solution)/shard_map/ppermute | solution.py:56
  41.1 2.5 %collective-permute-done.13.refs_2_ = bf16[512,128]{1,0:T(8,128)(2,1)S(1)} collective-permute-done((bf16[512,128]{1,0:T(8,128)(2,1)S(1)}, bf16[512,128]{1,0:T(8,128)(2,1)S(1)}, u32[]{:S(2)}, u32[]{:S(2)}) %collective-permute-start.13) | collective-permute-done | bytes 131104 | tf_op jit(solution)/shard_map/ppermute | solution.py:56
  44.5 0.9 %collective-permute-done.18.refs_3_ = bf16[512,128]{1,0:T(8,128)(2,1)S(1)} collective-permute-done((bf16[512,128]{1,0:T(8,128)(2,1)S(1)}, bf16[512,128]{1,0:T(8,128)(2,1)S(1)}, u32[]{:S(2)}, u32[]{:S(2)}) %collective-permute-start.18) | collective-permute-done | bytes 131104 | tf_op jit(solution)/shard_map/ppermute | solution.py:56
  45.4 1.6 %collective-permute-done.19.refs_4_ = bf16[512,128]{1,0:T(8,128)(2,1)S(1)} collective-permute-done((bf16[512,128]{1,0:T(8,128)(2,1)S(1)}, bf16[512,128]{1,0:T(8,128)(2,1)S(1)}, u32[]{:S(2)}, u32[]{:S(2)}) %collective-permute-start.19) | collective-permute-done | bytes 131104 | tf_op jit(solution)/shard_map/ppermute | solution.py:56
  49.0 18.8 %factors.1 = (f32[256,128]{1,0:T(8,128)}, bf16[2048,128]{1,0:T(8,128)(2,1)}, bf16[8192,128]{1,0:T(8,128)(2,1)S(1)}) custom-call(s32[3,16]{1,0:T(4,128)S(1)} %bitcast.6, bf16[16,256,384]{2,1,0:T(8,128)(2,1)S(1)} %tiles.1.tiles_ref, f32[256,128]{1,0:T(8,128)S(1)} %get-tuple-element.52.mine_ref, ...), custom_call_target="tpu_custom_call", output_to_operand_aliasing={{2}: (3, {})} | custom-call | tf_op jit(solution)/shard_map/factors/pallas_call | solution.py:422
  (56 shorter events, 5.6 us)
Async XLA Ops:
  3.0 6.7 %collective-permute-start = (bf16[3072,128]{1,0:T(8,128)(2,1)S(1)}, bf16[3072,128]{1,0:T(8,128)(2,1)S(1)}, u32[]{:S(2)}, u32[]{:S(2)}) collective-permute-start(bf16[3072,128]{1,0:T(8,128)(2,1)S(1)} %get-tuple-element.32), channel_id=1, source_target_pairs={{0,1},{1,0},{2,3},{3,2},{4,5},{5,4},{6,7},{7,6},{8,9},{9,8},{10,11... | collective-permute-start | bytes 2359304 | tf_op jit(solution)/shard_map/ppermute | solution.py:56
  3.5 2.3 %collective-permute-start.3 = (bf16[1024,128]{1,0:T(8,128)(2,1)S(1)}, bf16[1024,128]{1,0:T(8,128)(2,1)S(1)}, u32[]{:S(2)}, u32[]{:S(2)}) collective-permute-start(bf16[1024,128]{1,0:T(8,128)(2,1)S(1)} %get-tuple-element.35), channel_id=1, source_target_pairs={{0,1},{1,0},{2,3},{3,2},{4,5},{5,4},{6,7},{7,6},{8,9},{9,8},{10,11... | collective-permute-start | bytes 786440 | tf_op jit(solution)/shard_map/ppermute | solution.py:56
  5.8 8.2 %collective-permute-start.4 = (bf16[512,128]{1,0:T(8,128)(2,1)S(1)}, bf16[512,128]{1,0:T(8,128)(2,1)S(1)}, u32[]{:S(2)}, u32[]{:S(2)}) collective-permute-start(bf16[512,128]{1,0:T(8,128)(2,1)S(1)} %get-tuple-element.36), channel_id=1, source_target_pairs={{0,6},{1,7},{2,4},{3,5},{4,2},{5,3},{6,0},{7,1},{8,14},{9,15},{10,... | collective-permute-start | bytes 393224 | tf_op jit(solution)/shard_map/ppermute | solution.py:56
  9.8 7.6 %collective-permute-start.1 = (bf16[512,128]{1,0:T(8,128)(2,1)S(1)}, bf16[512,128]{1,0:T(8,128)(2,1)S(1)}, u32[]{:S(2)}, u32[]{:S(2)}) collective-permute-start(bf16[512,128]{1,0:T(8,128)(2,1)S(1)} %get-tuple-element.33), channel_id=1, source_target_pairs={{0,2},{1,3},{2,0},{3,1},{4,6},{5,7},{6,4},{7,5},{8,10},{9,11},{10,... | collective-permute-start | bytes 393224 | tf_op jit(solution)/shard_map/ppermute | solution.py:56
  10.4 9.2 %collective-permute-start.2 = (bf16[512,128]{1,0:T(8,128)(2,1)S(1)}, bf16[512,128]{1,0:T(8,128)(2,1)S(1)}, u32[]{:S(2)}, u32[]{:S(2)}) collective-permute-start(bf16[512,128]{1,0:T(8,128)(2,1)S(1)} %get-tuple-element.34), channel_id=1, source_target_pairs={{0,4},{1,5},{2,6},{3,7},{4,0},{5,1},{6,2},{7,3},{8,12},{9,13},{10,... | collective-permute-start | bytes 393224 | tf_op jit(solution)/shard_map/ppermute | solution.py:56
  10.5 13.3 %collective-permute-start.9 = (bf16[512,128]{1,0:T(8,128)(2,1)S(1)}, bf16[512,128]{1,0:T(8,128)(2,1)S(1)}, u32[]{:S(2)}, u32[]{:S(2)}) collective-permute-start(bf16[512,128]{1,0:T(8,128)(2,1)S(1)} %get-tuple-element.44), channel_id=1, source_target_pairs={{0,6},{1,7},{2,4},{3,5},{4,2},{5,3},{6,0},{7,1},{8,14},{9,15},{10,... | collective-permute-start | bytes 393224 | tf_op jit(solution)/shard_map/ppermute | solution.py:56
  13.4 10.4 %collective-permute-start.7 = (bf16[512,128]{1,0:T(8,128)(2,1)S(1)}, bf16[512,128]{1,0:T(8,128)(2,1)S(1)}, u32[]{:S(2)}, u32[]{:S(2)}) collective-permute-start(bf16[512,128]{1,0:T(8,128)(2,1)S(1)} %get-tuple-element.42), channel_id=1, source_target_pairs={{0,2},{1,3},{2,0},{3,1},{4,6},{5,7},{6,4},{7,5},{8,10},{9,11},{10,... | collective-permute-start | bytes 393224 | tf_op jit(solution)/shard_map/ppermute | solution.py:56
  14.0 9.8 %collective-permute-start.8 = (bf16[512,128]{1,0:T(8,128)(2,1)S(1)}, bf16[512,128]{1,0:T(8,128)(2,1)S(1)}, u32[]{:S(2)}, u32[]{:S(2)}) collective-permute-start(bf16[512,128]{1,0:T(8,128)(2,1)S(1)} %get-tuple-element.43), channel_id=1, source_target_pairs={{0,4},{1,5},{2,6},{3,7},{4,0},{5,1},{6,2},{7,3},{8,12},{9,13},{10,... | collective-permute-start | bytes 393224 | tf_op jit(solution)/shard_map/ppermute | solution.py:56
  19.7 5.8 %collective-permute-start.5 = (bf16[256,128]{1,0:T(8,128)(2,1)S(1)}, bf16[256,128]{1,0:T(8,128)(2,1)S(1)}, u32[]{:S(2)}, u32[]{:S(2)}) collective-permute-start(bf16[256,128]{1,0:T(8,128)(2,1)S(1)} %get-tuple-element.40), channel_id=1, source_target_pairs={{0,16},{1,17},{2,18},{3,19},{4,20},{5,21},{6,22},{7,23},{8,24},{9,... | collective-permute-start | bytes 196616 | tf_op jit(solution)/shard_map/ppermute | solution.py:56
  22.4 6.2 %collective-permute-start.6 = (bf16[256,128]{1,0:T(8,128)(2,1)S(1)}, bf16[256,128]{1,0:T(8,128)(2,1)S(1)}, u32[]{:S(2)}, u32[]{:S(2)}) collective-permute-start(bf16[256,128]{1,0:T(8,128)(2,1)S(1)} %get-tuple-element.41), channel_id=1, source_target_pairs={{0,24},{1,25},{2,26},{3,27},{4,28},{5,29},{6,30},{7,31},{8,16},{9,... | collective-permute-start | bytes 196616 | tf_op jit(solution)/shard_map/ppermute | solution.py:56
  23.9 5.4 %collective-permute-start.10 = (bf16[256,128]{1,0:T(8,128)(2,1)S(1)}, bf16[256,128]{1,0:T(8,128)(2,1)S(1)}, u32[]{:S(2)}, u32[]{:S(2)}) collective-permute-start(bf16[256,128]{1,0:T(8,128)(2,1)S(1)} %get-tuple-element.45), channel_id=1, source_target_pairs={{0,8},{1,9},{2,10},{3,11},{4,12},{5,13},{6,14},{7,15},{8,0},{9,1},... | collective-permute-start | bytes 196616 | tf_op jit(solution)/shard_map/ppermute | solution.py:56
  29.3 4.5 %collective-permute-start.11 = (bf16[256,128]{1,0:T(8,128)(2,1)S(1)}, bf16[256,128]{1,0:T(8,128)(2,1)S(1)}, u32[]{:S(2)}, u32[]{:S(2)}) collective-permute-start(bf16[256,128]{1,0:T(8,128)(2,1)S(1)} %get-tuple-element.53), channel_id=1, source_target_pairs={{0,8},{1,9},{2,10},{3,11},{4,12},{5,13},{6,14},{7,15},{8,0},{9,1},... | collective-permute-start | bytes 196616 | tf_op jit(solution)/shard_map/ppermute | solution.py:56
  29.4 8.0 %collective-permute-start.15 = (bf16[256,128]{1,0:T(8,128)(2,1)S(1)}, bf16[256,128]{1,0:T(8,128)(2,1)S(1)}, u32[]{:S(2)}, u32[]{:S(2)}) collective-permute-start(bf16[256,128]{1,0:T(8,128)(2,1)S(1)} %get-tuple-element.53), channel_id=1, source_target_pairs={{0,16},{1,17},{2,18},{3,19},{4,20},{5,21},{6,22},{7,23},{8,24},{9,... | collective-permute-start | bytes 196616 | tf_op jit(solution)/shard_map/ppermute | solution.py:56
  31.4 6.1 %collective-permute-start.16 = (bf16[256,128]{1,0:T(8,128)(2,1)S(1)}, bf16[256,128]{1,0:T(8,128)(2,1)S(1)}, u32[]{:S(2)}, u32[]{:S(2)}) collective-permute-start(bf16[256,128]{1,0:T(8,128)(2,1)S(1)} %get-tuple-element.53), channel_id=1, source_target_pairs={{0,24},{1,25},{2,26},{3,27},{4,28},{5,29},{6,30},{7,31},{8,16},{9,... | collective-permute-start | bytes 196616 | tf_op jit(solution)/shard_map/ppermute | solution.py:56
  33.8 7.3 %collective-permute-start.12 = (bf16[512,128]{1,0:T(8,128)(2,1)S(1)}, bf16[512,128]{1,0:T(8,128)(2,1)S(1)}, u32[]{:S(2)}, u32[]{:S(2)}) collective-permute-start(bf16[512,128]{1,0:T(8,128)(2,1)S(1)} %constant_dynamic-update-slice_fusion.refs_0_), channel_id=1, source_target_pairs={{0,6},{1,7},{2,4},{3,5},{4,2},{5,3},{6,0},{7,1},{8,14},{9,15},{10,... | collective-permute-start | bytes 393224 | tf_op jit(solution)/shard_map/ppermute | solution.py:56
  34.5 9.2 %collective-permute-start.13 = (bf16[512,128]{1,0:T(8,128)(2,1)S(1)}, bf16[512,128]{1,0:T(8,128)(2,1)S(1)}, u32[]{:S(2)}, u32[]{:S(2)}) collective-permute-start(bf16[512,128]{1,0:T(8,128)(2,1)S(1)} %constant_dynamic-update-slice_fusion.refs_0_), channel_id=1, source_target_pairs={{0,4},{1,5},{2,6},{3,7},{4,0},{5,1},{6,2},{7,3},{8,12},{9,13},{10,... | collective-permute-start | bytes 393224 | tf_op jit(solution)/shard_map/ppermute | solution.py:56
  36.8 6.8 %collective-permute-start.14 = (bf16[512,128]{1,0:T(8,128)(2,1)S(1)}, bf16[512,128]{1,0:T(8,128)(2,1)S(1)}, u32[]{:S(2)}, u32[]{:S(2)}) collective-permute-start(bf16[512,128]{1,0:T(8,128)(2,1)S(1)} %constant_dynamic-update-slice_fusion.refs_0_), channel_id=1, source_target_pairs={{0,2},{1,3},{2,0},{3,1},{4,6},{5,7},{6,4},{7,5},{8,10},{9,11},{10,... | collective-permute-start | bytes 393224 | tf_op jit(solution)/shard_map/ppermute | solution.py:56
  37.5 7.0 %collective-permute-start.17 = (bf16[512,128]{1,0:T(8,128)(2,1)S(1)}, bf16[512,128]{1,0:T(8,128)(2,1)S(1)}, u32[]{:S(2)}, u32[]{:S(2)}) collective-permute-start(bf16[512,128]{1,0:T(8,128)(2,1)S(1)} %constant_dynamic-update-slice_fusion.2.refs_4_), channel_id=1, source_target_pairs={{0,2},{1,3},{2,0},{3,1},{4,6},{5,7},{6,4},{7,5},{8,10},{9,11},{10,... | collective-permute-start | bytes 393224 | tf_op jit(solution)/shard_map/ppermute | solution.py:56
  39.0 6.3 %collective-permute-start.18 = (bf16[512,128]{1,0:T(8,128)(2,1)S(1)}, bf16[512,128]{1,0:T(8,128)(2,1)S(1)}, u32[]{:S(2)}, u32[]{:S(2)}) collective-permute-start(bf16[512,128]{1,0:T(8,128)(2,1)S(1)} %constant_dynamic-update-slice_fusion.2.refs_4_), channel_id=1, source_target_pairs={{0,4},{1,5},{2,6},{3,7},{4,0},{5,1},{6,2},{7,3},{8,12},{9,13},{10,... | collective-permute-start | bytes 393224 | tf_op jit(solution)/shard_map/ppermute | solution.py:56
  41.1 5.9 %collective-permute-start.19 = (bf16[512,128]{1,0:T(8,128)(2,1)S(1)}, bf16[512,128]{1,0:T(8,128)(2,1)S(1)}, u32[]{:S(2)}, u32[]{:S(2)}) collective-permute-start(bf16[512,128]{1,0:T(8,128)(2,1)S(1)} %constant_dynamic-update-slice_fusion.2.refs_4_), channel_id=1, source_target_pairs={{0,6},{1,7},{2,4},{3,5},{4,2},{5,3},{6,0},{7,1},{8,14},{9,15},{10,... | collective-permute-start | bytes 393224 | tf_op jit(solution)/shard_map/ppermute | solution.py:56
  43.7 3.3 %collective-permute-start.20 = (bf16[512,128]{1,0:T(8,128)(2,1)S(1)}, bf16[512,128]{1,0:T(8,128)(2,1)S(1)}, u32[]{:S(2)}, u32[]{:S(2)}) collective-permute-start(bf16[512,128]{1,0:T(8,128)(2,1)S(1)} %constant_dynamic-update-slice_fusion.2.refs_4_), channel_id=1, source_target_pairs={{0,1},{1,0},{2,3},{3,2},{4,5},{5,4},{6,7},{7,6},{8,9},{9,8},{10,11... | collective-permute-start | bytes 393224 | tf_op jit(solution)/shard_map/ppermute | solution.py:56
  43.7 3.8 %collective-permute-start.21 = (bf16[512,128]{1,0:T(8,128)(2,1)S(1)}, bf16[512,128]{1,0:T(8,128)(2,1)S(1)}, u32[]{:S(2)}, u32[]{:S(2)}) collective-permute-start(bf16[512,128]{1,0:T(8,128)(2,1)S(1)} %constant_dynamic-update-slice_fusion.refs_0_), channel_id=1, source_target_pairs={{0,1},{1,0},{2,3},{3,2},{4,5},{5,4},{6,7},{7,6},{8,9},{9,8},{10,11... | collective-permute-start | bytes 393224 | tf_op jit(solution)/shard_map/ppermute | solution.py:56
  44.5 3.1 %collective-permute-start.22 = (bf16[512,128]{1,0:T(8,128)(2,1)S(1)}, bf16[512,128]{1,0:T(8,128)(2,1)S(1)}, u32[]{:S(2)}, u32[]{:S(2)}) collective-permute-start(bf16[512,128]{1,0:T(8,128)(2,1)S(1)} %collective-permute-done.12.refs_1_), channel_id=1, source_target_pairs={{0,1},{1,0},{2,3},{3,2},{4,5},{5,4},{6,7},{7,6},{8,9},{9,8},{10,11... | collective-permute-start | bytes 393224 | tf_op jit(solution)/shard_map/ppermute | solution.py:56
  45.4 3.1 %collective-permute-start.23 = (bf16[512,128]{1,0:T(8,128)(2,1)S(1)}, bf16[512,128]{1,0:T(8,128)(2,1)S(1)}, u32[]{:S(2)}, u32[]{:S(2)}) collective-permute-start(bf16[512,128]{1,0:T(8,128)(2,1)S(1)} %collective-permute-done.13.refs_2_), channel_id=1, source_target_pairs={{0,1},{1,0},{2,3},{3,2},{4,5},{5,4},{6,7},{7,6},{8,9},{9,8},{10,11... | collective-permute-start | bytes 393224 | tf_op jit(solution)/shard_map/ppermute | solution.py:56
  (8 other events, 18.0 us)

commit v14 on v12

--- a/solution.py
+++ b/solution.py
@@ -248,7 +248,7 @@
 
 def last_kernel(plan, features, late, rows_ref, tiles_ref, mine_ref, early_ref, *rest):
     parts, (basis_ref, factors_ref) = rest[: 4 * plan.plane], rest[4 * plan.plane : 4 * plan.plane + 2]
-    all_ref, product_ref, gram_ref, inverse_ref = rest[4 * plan.plane + 2 :]
+    all_ref, product_ref, gram_ref, inverse_ref, near_basis_ref, near_factors_ref, sems = rest[4 * plan.plane + 2 :]
     me = plan.me()
     documents = tiles_ref.shape[0]
     block = tiles_ref.shape[1] // 2
@@ -282,10 +282,18 @@
         eliminate(gram_ref, inverse_ref)
 
     inverse = inverse_ref[...]
-    basis_ref[...] = dot_t3(mine_ref[...], inverse)
-    size = min(512, documents * block)
-    for at in range(0, documents * block, size):
-        factors_ref[at : at + size, :] = dot_t3(product_ref[at : at + size, :], inverse).astype(BF16)
+    near_basis_ref[...] = dot_t3(mine_ref[...], inverse)
+    copies = [pltpu.make_async_copy(near_basis_ref, basis_ref, sems.at[0])]
+    copies[0].start()
+    steps = sems.shape[0] - 1
+    size = documents * block // steps
+    for i in range(steps):
+        at = pl.ds(i * size, size)
+        near_factors_ref[at, :] = dot_t3(product_ref[at, :], inverse).astype(BF16)
+        copies.append(pltpu.make_async_copy(near_factors_ref.at[at], factors_ref.at[at], sems.at[i + 1]))
+        copies[-1].start()
+    for copy in copies:
+        copy.wait()
 
 
 def body(plan, blocks, rows, counts, sketch, weights):
@@ -388,7 +396,7 @@
     other = [plan.swap(part, 1) for part in own]
 
     pieces = own + other
-    late = range(len(own) + 1, len(own) + plan.plane)
+    late = range(len(own) + plan.plane - 1, len(own) + plan.plane)
     gram = pl.pallas_call(
         gram_kernel,
         out_shape=shape((columns, columns), F32),
@@ -402,12 +410,15 @@
         functools.partial(last_kernel, plan, features, late),
         out_shape=(shape((flat, columns), F32), shape((documents * block, columns), BF16)),
         in_specs=[scalars()] + [whole()] * (3 + len(pieces)),
-        out_specs=(whole(), whole()),
+        out_specs=(pl.BlockSpec(memory_space=pltpu.HBM),) * 2,
         scratch_shapes=[
             pltpu.VMEM((features, columns), BF16),
             pltpu.VMEM((documents * block, columns), F32),
             pltpu.VMEM((columns, columns), F32),
             pltpu.VMEM((columns, columns), F32),
+            pltpu.VMEM((flat, columns), F32),
+            pltpu.VMEM((documents * block, columns), BF16),
+            pltpu.SemaphoreType.DMA((1 + min(4, documents),)),
         ],
         compiler_params=params,
         name="factors",

time: 66.4 us -> 66.8 us (level)
  transfers between devices with their start and end apart: 30 -> 30, of which waited for: 13 -> 15; matrix products, arithmetic and copies ran while one was open for 0% -> 0% of each run, Pallas kernels for 4% -> 4%
where the time goes in v14:
time: 66.8 us; the launch traced here: 66.6 us
  starting transfers between devices  30.1 us (45%)
  Pallas kernels  23.4 us (35%)
  waiting for transfers between devices  12.3 us (18%)
  between operations  0.76 us (1%)
    ppermute x30, starting transfers between devices, swap(): return lax.ppermute(value, AXES, [(d, d ^ mask) for d in range(self.count)])  30.1 us
    pallas_call x1, Pallas kernels, body(): pl.pallas_call(functools.partial(last_kernel, plan, features, late), out_...  18.6 us
    ppermute x30, waiting for transfers between devices, swap(): return lax.ppermute(value, AXES, [(d, d ^ mask) for d in range(self.count)])  12.3 us
    pallas_call x1, Pallas kernels, body(): pl.pallas_call(functools.partial(sum_kernel, plan), out_shape=(pltpu.VMEM...  2.32 us
  transfers between devices with their start and end apart: 30, of which 15 were waited for; matrix products, arithmetic and copies ran while one was open for 0% of the time, Pallas kernels for 4%

profile of v14, /device:TPU:0, one launch (start us, length us, event | category | flops | bytes accessed | tf_op | source)
XLA Modules:
  0.0 66.6 jit_solution(10766441795995116246)
XLA Ops:
  0.6 2.3 %local_sum.1 = (f32[8192,128]{1,0:T(8,128)S(1)}, bf16[1024,128]{1,0:T(8,128)(2,1)S(1)}, bf16[1024,128]{1,0:T(8,128)(2,1)S(1)}, bf16[1024,128]{1,0:T(8,128)(2,1)S(1)}, bf16[1024,128]{1,0:T(8,128)(2,1)S(1)}) custom-call(s32[3,16]{1,0:T(4,128)} %bitcast.4, s32[16]{0:T(128)} %counts_ref.1, bf16[16,3,128,128]{3,2,1,0:T(8,128)(2,1)} %blocks_ref.3, ...), custom_call_target="tpu_custom_call" | custom-call | tf_op jit(solution)/shard_map/local_sum/pallas_call | solution.py:311
  5.1 3.9 %collective-permute-start.10 = (bf16[512,128]{1,0:T(8,128)(2,1)S(1)}, bf16[512,128]{1,0:T(8,128)(2,1)S(1)}, u32[]{:S(2)}, u32[]{:S(2)}) collective-permute-start(bf16[512,128]{1,0:T(8,128)(2,1)S(1)} %get-tuple-element.42), channel_id=1, source_target_pairs={{0,6},{1,7},{2,4},{3,5},{4,2},{5,3},{6,0},{7,1},{8,14},{9,15},{10,... | collective-permute-start | bytes 393224 | tf_op jit(solution)/shard_map/ppermute | solution.py:56
  10.0 2.7 %collective-permute-start.6 = (bf16[512,128]{1,0:T(8,128)(2,1)S(1)}, bf16[512,128]{1,0:T(8,128)(2,1)S(1)}, u32[]{:S(2)}, u32[]{:S(2)}) collective-permute-start(bf16[512,128]{1,0:T(8,128)(2,1)S(1)} %get-tuple-element.38), channel_id=1, source_target_pairs={{0,6},{1,7},{2,4},{3,5},{4,2},{5,3},{6,0},{7,1},{8,14},{9,15},{10,... | collective-permute-start | bytes 393224 | tf_op jit(solution)/shard_map/ppermute | solution.py:56
  13.2 2.0 %collective-permute-start.3 = (bf16[512,128]{1,0:T(8,128)(2,1)S(1)}, bf16[512,128]{1,0:T(8,128)(2,1)S(1)}, u32[]{:S(2)}, u32[]{:S(2)}) collective-permute-start(bf16[512,128]{1,0:T(8,128)(2,1)S(1)} %get-tuple-element.34), channel_id=1, source_target_pairs={{0,2},{1,3},{2,0},{3,1},{4,6},{5,7},{6,4},{7,5},{8,10},{9,11},{10,... | collective-permute-start | bytes 393224 | tf_op jit(solution)/shard_map/ppermute | solution.py:56
  15.3 1.7 %collective-permute-done.9.rest_1_ = bf16[512,128]{1,0:T(8,128)(2,1)S(1)} collective-permute-done((bf16[512,128]{1,0:T(8,128)(2,1)S(1)}, bf16[512,128]{1,0:T(8,128)(2,1)S(1)}, u32[]{:S(2)}, u32[]{:S(2)}) %collective-permute-start.9) | collective-permute-done | bytes 131104 | tf_op jit(solution)/shard_map/ppermute | solution.py:56
  17.2 2.8 %collective-permute-start.11 = (bf16[256,128]{1,0:T(8,128)(2,1)S(1)}, bf16[256,128]{1,0:T(8,128)(2,1)S(1)}, u32[]{:S(2)}, u32[]{:S(2)}) collective-permute-start(bf16[256,128]{1,0:T(8,128)(2,1)S(1)} %get-tuple-element.46), channel_id=1, source_target_pairs={{0,16},{1,17},{2,18},{3,19},{4,20},{5,21},{6,22},{7,23},{8,24},{9,... | collective-permute-start | bytes 196616 | tf_op jit(solution)/shard_map/ppermute | solution.py:56
  20.0 1.4 %collective-permute-start.12 = (bf16[256,128]{1,0:T(8,128)(2,1)S(1)}, bf16[256,128]{1,0:T(8,128)(2,1)S(1)}, u32[]{:S(2)}, u32[]{:S(2)}) collective-permute-start(bf16[256,128]{1,0:T(8,128)(2,1)S(1)} %get-tuple-element.47), channel_id=1, source_target_pairs={{0,24},{1,25},{2,26},{3,27},{4,28},{5,29},{6,30},{7,31},{8,16},{9,... | collective-permute-start | bytes 196616 | tf_op jit(solution)/shard_map/ppermute | solution.py:56
  21.6 1.6 %collective-permute-start.7 = (bf16[256,128]{1,0:T(8,128)(2,1)S(1)}, bf16[256,128]{1,0:T(8,128)(2,1)S(1)}, u32[]{:S(2)}, u32[]{:S(2)}) collective-permute-start(bf16[256,128]{1,0:T(8,128)(2,1)S(1)} %get-tuple-element.39), channel_id=1, source_target_pairs={{0,8},{1,9},{2,10},{3,11},{4,12},{5,13},{6,14},{7,15},{8,0},{9,1},... | collective-permute-start | bytes 196616 | tf_op jit(solution)/shard_map/ppermute | solution.py:56
  23.2 1.3 %tiles.1.tiles_ref = bf16[16,256,384]{2,1,0:T(8,128)(2,1)S(1)} custom-call(s32[3,16]{1,0:T(4,128)S(1)} %bitcast.5, s32[16]{0:T(128)S(1)} %copy-done.3, bf16[16,3,128,128]{3,2,1,0:T(8,128)(2,1)S(1)} %copy-done, f32[64,128]{1,0:T(8,128)S(1)} %bitcast.3), custom_call_target="tpu_custom_call" | custom-call | flops 1048576 | bytes 4194304 | tf_op jit(solution)/shard_map/tiles/pallas_call | solution.py:329
  24.7 1.5 %collective-permute-done.12.rest_2_ = bf16[256,128]{1,0:T(8,128)(2,1)S(1)} collective-permute-done((bf16[256,128]{1,0:T(8,128)(2,1)S(1)}, bf16[256,128]{1,0:T(8,128)(2,1)S(1)}, u32[]{:S(2)}, u32[]{:S(2)}) %collective-permute-start.12) | collective-permute-done | bytes 65568 | tf_op jit(solution)/shard_map/ppermute | solution.py:56
  26.8 0.8 %collective-permute-start.18 = (bf16[256,128]{1,0:T(8,128)(2,1)S(1)}, bf16[256,128]{1,0:T(8,128)(2,1)S(1)}, u32[]{:S(2)}, u32[]{:S(2)}) collective-permute-start(bf16[256,128]{1,0:T(8,128)(2,1)S(1)} %get-tuple-element.55), channel_id=1, source_target_pairs={{0,8},{1,9},{2,10},{3,11},{4,12},{5,13},{6,14},{7,15},{8,0},{9,1},... | collective-permute-start | bytes 196616 | tf_op jit(solution)/shard_map/ppermute | solution.py:56
  27.6 2.9 %collective-permute-start.13 = (bf16[256,128]{1,0:T(8,128)(2,1)S(1)}, bf16[256,128]{1,0:T(8,128)(2,1)S(1)}, u32[]{:S(2)}, u32[]{:S(2)}) collective-permute-start(bf16[256,128]{1,0:T(8,128)(2,1)S(1)} %get-tuple-element.55), channel_id=1, source_target_pairs={{0,16},{1,17},{2,18},{3,19},{4,20},{5,21},{6,22},{7,23},{8,24},{9,... | collective-permute-start | bytes 196616 | tf_op jit(solution)/shard_map/ppermute | solution.py:56
  30.5 0.8 %collective-permute-start.14 = (bf16[256,128]{1,0:T(8,128)(2,1)S(1)}, bf16[256,128]{1,0:T(8,128)(2,1)S(1)}, u32[]{:S(2)}, u32[]{:S(2)}) collective-permute-start(bf16[256,128]{1,0:T(8,128)(2,1)S(1)} %get-tuple-element.55), channel_id=1, source_target_pairs={{0,24},{1,25},{2,26},{3,27},{4,28},{5,29},{6,30},{7,31},{8,16},{9,... | collective-permute-start | bytes 196616 | tf_op jit(solution)/shard_map/ppermute | solution.py:56
  31.8 1.2 %collective-permute-start.19 = (bf16[512,128]{1,0:T(8,128)(2,1)S(1)}, bf16[512,128]{1,0:T(8,128)(2,1)S(1)}, u32[]{:S(2)}, u32[]{:S(2)}) collective-permute-start(bf16[512,128]{1,0:T(8,128)(2,1)S(1)} %constant_dynamic-update-slice_fusion.2.refs_4_.rest_4_), channel_id=1, source_target_pairs={{0,6},{1,7},{2,4},{3,5},{4,2},{5,3},{6,0},{7,1},{8,14},{9,15},{10,... | collective-permute-start | bytes 393224 | tf_op jit(solution)/shard_map/ppermute | solution.py:56
  33.0 1.3 %collective-permute-start.20 = (bf16[512,128]{1,0:T(8,128)(2,1)S(1)}, bf16[512,128]{1,0:T(8,128)(2,1)S(1)}, u32[]{:S(2)}, u32[]{:S(2)}) collective-permute-start(bf16[512,128]{1,0:T(8,128)(2,1)S(1)} %constant_dynamic-update-slice_fusion.2.refs_4_.rest_4_), channel_id=1, source_target_pairs={{0,4},{1,5},{2,6},{3,7},{4,0},{5,1},{6,2},{7,3},{8,12},{9,13},{10,... | collective-permute-start | bytes 393224 | tf_op jit(solution)/shard_map/ppermute | solution.py:56
  34.3 1.1 %collective-permute-start.21 = (bf16[512,128]{1,0:T(8,128)(2,1)S(1)}, bf16[512,128]{1,0:T(8,128)(2,1)S(1)}, u32[]{:S(2)}, u32[]{:S(2)}) collective-permute-start(bf16[512,128]{1,0:T(8,128)(2,1)S(1)} %constant_dynamic-update-slice_fusion.2.refs_4_.rest_4_), channel_id=1, source_target_pairs={{0,2},{1,3},{2,0},{3,1},{4,6},{5,7},{6,4},{7,5},{8,10},{9,11},{10,... | collective-permute-start | bytes 393224 | tf_op jit(solution)/shard_map/ppermute | solution.py:56
  35.4 1.1 %collective-permute-done.14 = bf16[256,128]{1,0:T(8,128)(2,1)S(1)} collective-permute-done((bf16[256,128]{1,0:T(8,128)(2,1)S(1)}, bf16[256,128]{1,0:T(8,128)(2,1)S(1)}, u32[]{:S(2)}, u32[]{:S(2)}) %collective-permute-start.14) | collective-permute-done | bytes 65568 | tf_op jit(solution)/shard_map/ppermute | solution.py:56
  36.5 1.3 %collective-permute-start.15 = (bf16[512,128]{1,0:T(8,128)(2,1)S(1)}, bf16[512,128]{1,0:T(8,128)(2,1)S(1)}, u32[]{:S(2)}, u32[]{:S(2)}) collective-permute-start(bf16[512,128]{1,0:T(8,128)(2,1)S(1)} %constant_dynamic-update-slice_fusion.refs_0_.rest_0_), channel_id=1, source_target_pairs={{0,2},{1,3},{2,0},{3,1},{4,6},{5,7},{6,4},{7,5},{8,10},{9,11},{10,... | collective-permute-start | bytes 393224 | tf_op jit(solution)/shard_map/ppermute | solution.py:56
  37.9 1.1 %collective-permute-start.16 = (bf16[512,128]{1,0:T(8,128)(2,1)S(1)}, bf16[512,128]{1,0:T(8,128)(2,1)S(1)}, u32[]{:S(2)}, u32[]{:S(2)}) collective-permute-start(bf16[512,128]{1,0:T(8,128)(2,1)S(1)} %constant_dynamic-update-slice_fusion.refs_0_.rest_0_), channel_id=1, source_target_pairs={{0,4},{1,5},{2,6},{3,7},{4,0},{5,1},{6,2},{7,3},{8,12},{9,13},{10,... | collective-permute-start | bytes 393224 | tf_op jit(solution)/shard_map/ppermute | solution.py:56
  39.2 1.2 %collective-permute-start.17 = (bf16[512,128]{1,0:T(8,128)(2,1)S(1)}, bf16[512,128]{1,0:T(8,128)(2,1)S(1)}, u32[]{:S(2)}, u32[]{:S(2)}) collective-permute-start(bf16[512,128]{1,0:T(8,128)(2,1)S(1)} %constant_dynamic-update-slice_fusion.refs_0_.rest_0_), channel_id=1, source_target_pairs={{0,6},{1,7},{2,4},{3,5},{4,2},{5,3},{6,0},{7,1},{8,14},{9,15},{10,... | collective-permute-start | bytes 393224 | tf_op jit(solution)/shard_map/ppermute | solution.py:56
  40.9 2.1 %collective-permute-done.15.refs_1_.rest_1_ = bf16[512,128]{1,0:T(8,128)(2,1)S(1)} collective-permute-done((bf16[512,128]{1,0:T(8,128)(2,1)S(1)}, bf16[512,128]{1,0:T(8,128)(2,1)S(1)}, u32[]{:S(2)}, u32[]{:S(2)}) %collective-permute-start.15) | collective-permute-done | bytes 131104 | tf_op jit(solution)/shard_map/ppermute | solution.py:56
  43.0 2.3 %collective-permute-done.16.refs_2_.rest_2_ = bf16[512,128]{1,0:T(8,128)(2,1)S(1)} collective-permute-done((bf16[512,128]{1,0:T(8,128)(2,1)S(1)}, bf16[512,128]{1,0:T(8,128)(2,1)S(1)}, u32[]{:S(2)}, u32[]{:S(2)}) %collective-permute-start.16) | collective-permute-done | bytes 131104 | tf_op jit(solution)/shard_map/ppermute | solution.py:56
  47.2 0.7 %gram.1.early_ref = f32[128,128]{1,0:T(8,128)S(1)} custom-call(bf16[512,128]{1,0:T(8,128)(2,1)S(1)} %constant_dynamic-update-slice_fusion.refs_0_.rest_0_, bf16[512,128]{1,0:T(8,128)(2,1)S(1)} %collective-permute-done.15.refs_1_.rest_1_, bf16[512,128]{1,0:T(8,128)(2,1)S(1)} %collective-permute-done.16.refs_2_.rest_2_, ...), custom_call_target="tpu_custom_call" | custom-call | flops 268435456 | bytes 4194304 | tf_op jit(solution)/shard_map/gram/pallas_call | solution.py:400
  48.0 18.6 %factors.1 = (f32[256,128]{1,0:T(8,128)}, bf16[2048,128]{1,0:T(8,128)(2,1)}) custom-call(s32[3,16]{1,0:T(4,128)S(1)} %bitcast.6, bf16[16,256,384]{2,1,0:T(8,128)(2,1)S(1)} %tiles.1.tiles_ref, f32[256,128]{1,0:T(8,128)S(1)} %get-tuple-element.54.mine_ref, f32[128,128]{1,0:T(8,128)S(1)} %gram.1.early_ref, ...), custom_call_target="tpu_custom_call" | custom-call | tf_op jit(solution)/shard_map/factors/pallas_call | solution.py:409
  (59 shorter events, 8.2 us)
Async XLA Ops:
  3.6 5.4 %collective-permute-start.4 = (bf16[1024,128]{1,0:T(8,128)(2,1)S(1)}, bf16[1024,128]{1,0:T(8,128)(2,1)S(1)}, u32[]{:S(2)}, u32[]{:S(2)}) collective-permute-start(bf16[1024,128]{1,0:T(8,128)(2,1)S(1)} %get-tuple-element.35), channel_id=1, source_target_pairs={{0,1},{1,0},{2,3},{3,2},{4,5},{5,4},{6,7},{7,6},{8,9},{9,8},{10,11... | collective-permute-start | bytes 786440 | tf_op jit(solution)/shard_map/ppermute | solution.py:56
  4.0 5.6 %collective-permute-start.2 = (bf16[1024,128]{1,0:T(8,128)(2,1)S(1)}, bf16[1024,128]{1,0:T(8,128)(2,1)S(1)}, u32[]{:S(2)}, u32[]{:S(2)}) collective-permute-start(bf16[1024,128]{1,0:T(8,128)(2,1)S(1)} %get-tuple-element.33), channel_id=1, source_target_pairs={{0,1},{1,0},{2,3},{3,2},{4,5},{5,4},{6,7},{7,6},{8,9},{9,8},{10,11... | collective-permute-start | bytes 786440 | tf_op jit(solution)/shard_map/ppermute | solution.py:56
  5.1 8.1 %collective-permute-start.10 = (bf16[512,128]{1,0:T(8,128)(2,1)S(1)}, bf16[512,128]{1,0:T(8,128)(2,1)S(1)}, u32[]{:S(2)}, u32[]{:S(2)}) collective-permute-start(bf16[512,128]{1,0:T(8,128)(2,1)S(1)} %get-tuple-element.42), channel_id=1, source_target_pairs={{0,6},{1,7},{2,4},{3,5},{4,2},{5,3},{6,0},{7,1},{8,14},{9,15},{10,... | collective-permute-start | bytes 393224 | tf_op jit(solution)/shard_map/ppermute | solution.py:56
  9.0 8.0 %collective-permute-start.9 = (bf16[512,128]{1,0:T(8,128)(2,1)S(1)}, bf16[512,128]{1,0:T(8,128)(2,1)S(1)}, u32[]{:S(2)}, u32[]{:S(2)}) collective-permute-start(bf16[512,128]{1,0:T(8,128)(2,1)S(1)} %get-tuple-element.41), channel_id=1, source_target_pairs={{0,4},{1,5},{2,6},{3,7},{4,0},{5,1},{6,2},{7,3},{8,12},{9,13},{10,... | collective-permute-start | bytes 393224 | tf_op jit(solution)/shard_map/ppermute | solution.py:56
  9.6 7.4 %collective-permute-start.8 = (bf16[512,128]{1,0:T(8,128)(2,1)S(1)}, bf16[512,128]{1,0:T(8,128)(2,1)S(1)}, u32[]{:S(2)}, u32[]{:S(2)}) collective-permute-start(bf16[512,128]{1,0:T(8,128)(2,1)S(1)} %get-tuple-element.40), channel_id=1, source_target_pairs={{0,2},{1,3},{2,0},{3,1},{4,6},{5,7},{6,4},{7,5},{8,10},{9,11},{10,... | collective-permute-start | bytes 393224 | tf_op jit(solution)/shard_map/ppermute | solution.py:56
  10.0 11.3 %collective-permute-start.6 = (bf16[512,128]{1,0:T(8,128)(2,1)S(1)}, bf16[512,128]{1,0:T(8,128)(2,1)S(1)}, u32[]{:S(2)}, u32[]{:S(2)}) collective-permute-start(bf16[512,128]{1,0:T(8,128)(2,1)S(1)} %get-tuple-element.38), channel_id=1, source_target_pairs={{0,6},{1,7},{2,4},{3,5},{4,2},{5,3},{6,0},{7,1},{8,14},{9,15},{10,... | collective-permute-start | bytes 393224 | tf_op jit(solution)/shard_map/ppermute | solution.py:56
  12.7 8.6 %collective-permute-start.5 = (bf16[512,128]{1,0:T(8,128)(2,1)S(1)}, bf16[512,128]{1,0:T(8,128)(2,1)S(1)}, u32[]{:S(2)}, u32[]{:S(2)}) collective-permute-start(bf16[512,128]{1,0:T(8,128)(2,1)S(1)} %get-tuple-element.36), channel_id=1, source_target_pairs={{0,4},{1,5},{2,6},{3,7},{4,0},{5,1},{6,2},{7,3},{8,12},{9,13},{10,... | collective-permute-start | bytes 393224 | tf_op jit(solution)/shard_map/ppermute | solution.py:56
  13.2 8.3 %collective-permute-start.3 = (bf16[512,128]{1,0:T(8,128)(2,1)S(1)}, bf16[512,128]{1,0:T(8,128)(2,1)S(1)}, u32[]{:S(2)}, u32[]{:S(2)}) collective-permute-start(bf16[512,128]{1,0:T(8,128)(2,1)S(1)} %get-tuple-element.34), channel_id=1, source_target_pairs={{0,2},{1,3},{2,0},{3,1},{4,6},{5,7},{6,4},{7,5},{8,10},{9,11},{10,... | collective-permute-start | bytes 393224 | tf_op jit(solution)/shard_map/ppermute | solution.py:56
  17.2 7.5 %collective-permute-start.11 = (bf16[256,128]{1,0:T(8,128)(2,1)S(1)}, bf16[256,128]{1,0:T(8,128)(2,1)S(1)}, u32[]{:S(2)}, u32[]{:S(2)}) collective-permute-start(bf16[256,128]{1,0:T(8,128)(2,1)S(1)} %get-tuple-element.46), channel_id=1, source_target_pairs={{0,16},{1,17},{2,18},{3,19},{4,20},{5,21},{6,22},{7,23},{8,24},{9,... | collective-permute-start | bytes 196616 | tf_op jit(solution)/shard_map/ppermute | solution.py:56
  20.0 6.2 %collective-permute-start.12 = (bf16[256,128]{1,0:T(8,128)(2,1)S(1)}, bf16[256,128]{1,0:T(8,128)(2,1)S(1)}, u32[]{:S(2)}, u32[]{:S(2)}) collective-permute-start(bf16[256,128]{1,0:T(8,128)(2,1)S(1)} %get-tuple-element.47), channel_id=1, source_target_pairs={{0,24},{1,25},{2,26},{3,27},{4,28},{5,29},{6,30},{7,31},{8,16},{9,... | collective-permute-start | bytes 196616 | tf_op jit(solution)/shard_map/ppermute | solution.py:56
  21.6 5.2 %collective-permute-start.7 = (bf16[256,128]{1,0:T(8,128)(2,1)S(1)}, bf16[256,128]{1,0:T(8,128)(2,1)S(1)}, u32[]{:S(2)}, u32[]{:S(2)}) collective-permute-start(bf16[256,128]{1,0:T(8,128)(2,1)S(1)} %get-tuple-element.39), channel_id=1, source_target_pairs={{0,8},{1,9},{2,10},{3,11},{4,12},{5,13},{6,14},{7,15},{8,0},{9,1},... | collective-permute-start | bytes 196616 | tf_op jit(solution)/shard_map/ppermute | solution.py:56
  26.8 5.0 %collective-permute-start.18 = (bf16[256,128]{1,0:T(8,128)(2,1)S(1)}, bf16[256,128]{1,0:T(8,128)(2,1)S(1)}, u32[]{:S(2)}, u32[]{:S(2)}) collective-permute-start(bf16[256,128]{1,0:T(8,128)(2,1)S(1)} %get-tuple-element.55), channel_id=1, source_target_pairs={{0,8},{1,9},{2,10},{3,11},{4,12},{5,13},{6,14},{7,15},{8,0},{9,1},... | collective-permute-start | bytes 196616 | tf_op jit(solution)/shard_map/ppermute | solution.py:56
  27.6 7.8 %collective-permute-start.13 = (bf16[256,128]{1,0:T(8,128)(2,1)S(1)}, bf16[256,128]{1,0:T(8,128)(2,1)S(1)}, u32[]{:S(2)}, u32[]{:S(2)}) collective-permute-start(bf16[256,128]{1,0:T(8,128)(2,1)S(1)} %get-tuple-element.55), channel_id=1, source_target_pairs={{0,16},{1,17},{2,18},{3,19},{4,20},{5,21},{6,22},{7,23},{8,24},{9,... | collective-permute-start | bytes 196616 | tf_op jit(solution)/shard_map/ppermute | solution.py:56
  30.5 6.1 %collective-permute-start.14 = (bf16[256,128]{1,0:T(8,128)(2,1)S(1)}, bf16[256,128]{1,0:T(8,128)(2,1)S(1)}, u32[]{:S(2)}, u32[]{:S(2)}) collective-permute-start(bf16[256,128]{1,0:T(8,128)(2,1)S(1)} %get-tuple-element.55), channel_id=1, source_target_pairs={{0,24},{1,25},{2,26},{3,27},{4,28},{5,29},{6,30},{7,31},{8,16},{9,... | collective-permute-start | bytes 196616 | tf_op jit(solution)/shard_map/ppermute | solution.py:56
  31.8 6.0 %collective-permute-start.19 = (bf16[512,128]{1,0:T(8,128)(2,1)S(1)}, bf16[512,128]{1,0:T(8,128)(2,1)S(1)}, u32[]{:S(2)}, u32[]{:S(2)}) collective-permute-start(bf16[512,128]{1,0:T(8,128)(2,1)S(1)} %constant_dynamic-update-slice_fusion.2.refs_4_.rest_4_), channel_id=1, source_target_pairs={{0,6},{1,7},{2,4},{3,5},{4,2},{5,3},{6,0},{7,1},{8,14},{9,15},{10,... | collective-permute-start | bytes 393224 | tf_op jit(solution)/shard_map/ppermute | solution.py:56
  33.0 6.2 %collective-permute-start.20 = (bf16[512,128]{1,0:T(8,128)(2,1)S(1)}, bf16[512,128]{1,0:T(8,128)(2,1)S(1)}, u32[]{:S(2)}, u32[]{:S(2)}) collective-permute-start(bf16[512,128]{1,0:T(8,128)(2,1)S(1)} %constant_dynamic-update-slice_fusion.2.refs_4_.rest_4_), channel_id=1, source_target_pairs={{0,4},{1,5},{2,6},{3,7},{4,0},{5,1},{6,2},{7,3},{8,12},{9,13},{10,... | collective-permute-start | bytes 393224 | tf_op jit(solution)/shard_map/ppermute | solution.py:56
  34.3 6.1 %collective-permute-start.21 = (bf16[512,128]{1,0:T(8,128)(2,1)S(1)}, bf16[512,128]{1,0:T(8,128)(2,1)S(1)}, u32[]{:S(2)}, u32[]{:S(2)}) collective-permute-start(bf16[512,128]{1,0:T(8,128)(2,1)S(1)} %constant_dynamic-update-slice_fusion.2.refs_4_.rest_4_), channel_id=1, source_target_pairs={{0,2},{1,3},{2,0},{3,1},{4,6},{5,7},{6,4},{7,5},{8,10},{9,11},{10,... | collective-permute-start | bytes 393224 | tf_op jit(solution)/shard_map/ppermute | solution.py:56
  35.4 5.0 %collective-permute-start.25 = (bf16[512,128]{1,0:T(8,128)(2,1)S(1)}, bf16[512,128]{1,0:T(8,128)(2,1)S(1)}, u32[]{:S(2)}, u32[]{:S(2)}) collective-permute-start(bf16[512,128]{1,0:T(8,128)(2,1)S(1)} %constant_dynamic-update-slice_fusion.2.refs_4_.rest_4_), channel_id=1, source_target_pairs={{0,1},{1,0},{2,3},{3,2},{4,5},{5,4},{6,7},{7,6},{8,9},{9,8},{10,11... | collective-permute-start | bytes 393224 | tf_op jit(solution)/shard_map/ppermute | solution.py:56
  36.5 6.5 %collective-permute-start.15 = (bf16[512,128]{1,0:T(8,128)(2,1)S(1)}, bf16[512,128]{1,0:T(8,128)(2,1)S(1)}, u32[]{:S(2)}, u32[]{:S(2)}) collective-permute-start(bf16[512,128]{1,0:T(8,128)(2,1)S(1)} %constant_dynamic-update-slice_fusion.refs_0_.rest_0_), channel_id=1, source_target_pairs={{0,2},{1,3},{2,0},{3,1},{4,6},{5,7},{6,4},{7,5},{8,10},{9,11},{10,... | collective-permute-start | bytes 393224 | tf_op jit(solution)/shard_map/ppermute | solution.py:56
  37.9 7.5 %collective-permute-start.16 = (bf16[512,128]{1,0:T(8,128)(2,1)S(1)}, bf16[512,128]{1,0:T(8,128)(2,1)S(1)}, u32[]{:S(2)}, u32[]{:S(2)}) collective-permute-start(bf16[512,128]{1,0:T(8,128)(2,1)S(1)} %constant_dynamic-update-slice_fusion.refs_0_.rest_0_), channel_id=1, source_target_pairs={{0,4},{1,5},{2,6},{3,7},{4,0},{5,1},{6,2},{7,3},{8,12},{9,13},{10,... | collective-permute-start | bytes 393224 | tf_op jit(solution)/shard_map/ppermute | solution.py:56
  39.2 6.2 %collective-permute-start.17 = (bf16[512,128]{1,0:T(8,128)(2,1)S(1)}, bf16[512,128]{1,0:T(8,128)(2,1)S(1)}, u32[]{:S(2)}, u32[]{:S(2)}) collective-permute-start(bf16[512,128]{1,0:T(8,128)(2,1)S(1)} %constant_dynamic-update-slice_fusion.refs_0_.rest_0_), channel_id=1, source_target_pairs={{0,6},{1,7},{2,4},{3,5},{4,2},{5,3},{6,0},{7,1},{8,14},{9,15},{10,... | collective-permute-start | bytes 393224 | tf_op jit(solution)/shard_map/ppermute | solution.py:56
  40.4 5.5 %collective-permute-start.22 = (bf16[512,128]{1,0:T(8,128)(2,1)S(1)}, bf16[512,128]{1,0:T(8,128)(2,1)S(1)}, u32[]{:S(2)}, u32[]{:S(2)}) collective-permute-start(bf16[512,128]{1,0:T(8,128)(2,1)S(1)} %constant_dynamic-update-slice_fusion.refs_0_.rest_0_), channel_id=1, source_target_pairs={{0,1},{1,0},{2,3},{3,2},{4,5},{5,4},{6,7},{7,6},{8,9},{9,8},{10,11... | collective-permute-start | bytes 393224 | tf_op jit(solution)/shard_map/ppermute | solution.py:56
  40.4 5.5 %collective-permute-start.26 = (bf16[512,128]{1,0:T(8,128)(2,1)S(1)}, bf16[512,128]{1,0:T(8,128)(2,1)S(1)}, u32[]{:S(2)}, u32[]{:S(2)}) collective-permute-start(bf16[512,128]{1,0:T(8,128)(2,1)S(1)} %collective-permute-done.19.refs_5_.rest_5_), channel_id=1, source_target_pairs={{0,1},{1,0},{2,3},{3,2},{4,5},{5,4},{6,7},{7,6},{8,9},{9,8},{10,11... | collective-permute-start | bytes 393224 | tf_op jit(solution)/shard_map/ppermute | solution.py:56
  43.0 3.4 %collective-permute-start.27 = (bf16[512,128]{1,0:T(8,128)(2,1)S(1)}, bf16[512,128]{1,0:T(8,128)(2,1)S(1)}, u32[]{:S(2)}, u32[]{:S(2)}) collective-permute-start(bf16[512,128]{1,0:T(8,128)(2,1)S(1)} %collective-permute-done.20.refs_6_.rest_6_), channel_id=1, source_target_pairs={{0,1},{1,0},{2,3},{3,2},{4,5},{5,4},{6,7},{7,6},{8,9},{9,8},{10,11... | collective-permute-start | bytes 393224 | tf_op jit(solution)/shard_map/ppermute | solution.py:56
  (10 other events, 33.9 us)

commit v15 on v14

--- a/solution.py
+++ b/solution.py
@@ -63,10 +63,9 @@
 
 
 def sum_kernel(plan, rows_hbm, counts_hbm, blocks_ref, sketch_ref, total_ref, *rest):
-    send_refs, (tiles_ref, docs_ref, rows_ref, counts_ref, sems, small_sems) = rest[: plan.plane], rest[plan.plane :]
+    first_ref, tiles_ref, docs_ref, rows_ref, counts_ref, sems, small_sems = rest
     me = plan.me()
     documents, slots, block, _ = tiles_ref.shape
-    half = total_ref.shape[0] // 2
     parts = sems.shape[0]
     per = documents // parts
     small = (
@@ -100,9 +99,12 @@
                 for p in range(plan.pieces):
                     at = pl.ds(plan.start(me, rows_ref[s, d], p), plan.piece)
                     total_ref[at, :] += term[p * plan.piece : (p + 1) * plan.piece]
-    for p, send_ref in enumerate(send_refs):
-        size = send_ref.shape[0]
-        send_ref[...] = total_ref[half + p * size : half + (p + 1) * size, :].astype(BF16)
+    first_ref[...] = total_ref[total_ref.shape[0] - first_ref.shape[0] :, :].astype(BF16)
+
+
+def later_kernel(total_ref, later_ref):
+    half = total_ref.shape[0] // 2
+    later_ref[...] = total_ref[half : half + later_ref.shape[0], :].astype(BF16)
 
 
 def tiles_kernel(rows_ref, counts_ref, blocks_ref, weights_ref, out_ref):
@@ -128,11 +130,12 @@
     scale_ref[...] = turned_ref[pl.ds(pl.multiple_of(inside, plan.piece), plan.flat), :]
 
 
-def chip_kernel(start, total_ref, got_ref, far_ref, near_ref):
+def chip_kernel(start, got_start, total_ref, got_ref, far_ref, near_ref):
     middle = near_ref.shape[0]
     for ref, at in ((far_ref, middle), (near_ref, 0)):
         held = total_ref[start + at : start + at + middle, :]
-        ref[...] = (held + got_ref[at : at + middle, :].astype(F32)).astype(BF16)
+        got = got_ref[got_start + at : got_start + at + middle, :]
+        ref[...] = (held + got.astype(F32)).astype(BF16)
 
 
 def plane_kernel(flat, start, total_ref, got_ref, *rest):
@@ -308,11 +311,11 @@
     rows = rows.T
     parts = min(4, documents)
 
-    total, *send = pl.pallas_call(
+    total, first = pl.pallas_call(
         functools.partial(sum_kernel, plan),
-        out_shape=(pltpu.VMEM((features, columns), F32),) + (pltpu.VMEM((chunk, columns), BF16),) * plan.plane,
+        out_shape=(pltpu.VMEM((features, columns), F32), pltpu.VMEM((chunk, columns), BF16)),
         in_specs=[pl.BlockSpec(memory_space=pltpu.HBM)] * 4,
-        out_specs=(whole(),) * (1 + plan.plane),
+        out_specs=(whole(), whole()),
         scratch_shapes=[
             pltpu.VMEM(blocks.shape, BF16),
             pltpu.VMEM(sketch.shape, BF16),
@@ -347,18 +350,28 @@
 
     middle = chunk // 2
     others = range(1, plan.plane)
-    got = {p: plan.swap(send[p], 1) for p in (*others, 0)}
-    got[plan.plane - 1], got[0] = lax.optimization_barrier((got[plan.plane - 1], got[0]))
+    first = plan.swap(first, 1)
+    total, first = lax.optimization_barrier((total, first))
+    later = pl.pallas_call(
+        later_kernel,
+        out_shape=shape((half - chunk, columns), BF16),
+        in_specs=[whole()],
+        out_specs=whole(),
+        compiler_params=params,
+        name="later",
+    )(total)
+    later = plan.swap(later, 1)
     chip = {}
     for p in others:
+        last = p == plan.plane - 1
         chip[p] = pl.pallas_call(
-            functools.partial(chip_kernel, p * chunk),
+            functools.partial(chip_kernel, p * chunk, 0 if last else p * chunk),
             out_shape=[shape((middle, columns), BF16)] * 2,
             in_specs=[whole(), whole()],
             out_specs=[whole()] * 2,
             compiler_params=params,
             name="chip_sum",
-        )(total, got[p])
+        )(total, first if last else later)
     far_sent = [plan.swap_plane(chip[p][0], p) for p in others]
     near_sent = [plan.swap_plane(chip[p][1], p) for p in others]
     far_sent, scale = lax.optimization_barrier((far_sent, scale))
@@ -371,14 +384,14 @@
             out_specs=[whole()] * len(dtypes),
             compiler_params=params,
             name="plane_sum",
-        )(total, got[0], *sent)
+        )(total, later, *sent)
 
     split_at = plan.line // 2
     far = plane_sum(far_sent, middle, [BF16] * split_at)
     far = [plan.swap_line(part, split_at + q) for q, part in enumerate(far)]
     held, *near = plane_sum(near_sent, 0, [F32] + [BF16] * (split_at - 1))
     near = [plan.swap_line(part, 1 + q) for q, part in enumerate(near)]
-    near, far, tiles = lax.optimization_barrier((near, far, tiles))
+    far, near, tiles = lax.optimization_barrier((far, near, tiles))
     mine, rounded = pl.pallas_call(
         line_kernel,
         out_shape=(shape((flat, columns), F32), shape((flat, columns), BF16)),
@@ -396,7 +409,7 @@
     other = [plan.swap(part, 1) for part in own]
 
     pieces = own + other
-    late = range(len(own) + plan.plane - 1, len(own) + plan.plane)
+    late = range(len(own) + 1, len(own) + plan.plane)
     gram = pl.pallas_call(
         gram_kernel,
         out_shape=shape((columns, columns), F32),

time: 66.8 us -> 67 us (level)
    ppermute x30 -> x28, waiting for transfers between devices: 12.3 us -> 12.7 us  [swap(): return lax.ppermute(value, AXES, [(d, d ^ mask) for d in range(self.count)])]
    ppermute x30 -> x28, starting transfers between devices: 30.1 us -> 30 us  [swap(): return lax.ppermute(value, AXES, [(d, d ^ mask) for d in range(self.count)])]
  transfers between devices with their start and end apart: 30 -> 28, of which waited for: 15 -> 13; matrix products, arithmetic and copies ran while one was open for 0% -> 0% of each run, Pallas kernels for 4% -> 3%
where the time goes in v15:
time: 67 us; the launch traced here: 66.9 us
  starting transfers between devices  30 us (45%)
  Pallas kernels  23.4 us (35%)
  waiting for transfers between devices  12.7 us (19%)
  between operations  0.77 us (1%)
    ppermute x28, starting transfers between devices, swap(): return lax.ppermute(value, AXES, [(d, d ^ mask) for d in range(self.count)])  30 us
    pallas_call x1, Pallas kernels, body(): pl.pallas_call(functools.partial(last_kernel, plan, features, late), out_...  18.7 us
    ppermute x28, waiting for transfers between devices, swap(): return lax.ppermute(value, AXES, [(d, d ^ mask) for d in range(self.count)])  12.7 us
    pallas_call x1, Pallas kernels, body(): pl.pallas_call(functools.partial(sum_kernel, plan), out_shape=(pltpu.VMEM...  2.24 us
  transfers between devices with their start and end apart: 28, of which 13 were waited for; matrix products, arithmetic and copies ran while one was open for 0% of the time, Pallas kernels for 3%

profile of v15, /device:TPU:0, one launch (start us, length us, event | category | flops | bytes accessed | tf_op | source)
XLA Modules:
  0.0 66.9 jit_solution(10003917444431529000)
XLA Ops:
  0.6 2.2 %local_sum.1 = (f32[8192,128]{1,0:T(8,128)S(1)}, bf16[1024,128]{1,0:T(8,128)(2,1)S(1)}) custom-call(s32[3,16]{1,0:T(4,128)} %bitcast.4, s32[16]{0:T(128)} %counts_ref.1, bf16[16,3,128,128]{3,2,1,0:T(8,128)(2,1)} %blocks_ref.3, bf16[2048,128]{1,0:T(8,128)(2,1)} %sketch_ref.1), custom_call_target="tpu_custom_call" | custom-call | tf_op jit(solution)/shard_map/local_sum/pallas_call | solution.py:314
  3.4 1.2 %collective-permute-done.got_ref = bf16[1024,128]{1,0:T(8,128)(2,1)S(1)} collective-permute-done((bf16[1024,128]{1,0:T(8,128)(2,1)S(1)}, bf16[1024,128]{1,0:T(8,128)(2,1)S(1)}, u32[]{:S(2)}, u32[]{:S(2)}) %collective-permute-start) | collective-permute-done | bytes 262176 | tf_op jit(solution)/shard_map/ppermute | solution.py:56
  5.1 3.7 %collective-permute-start.4 = (bf16[512,128]{1,0:T(8,128)(2,1)S(1)}, bf16[512,128]{1,0:T(8,128)(2,1)S(1)}, u32[]{:S(2)}, u32[]{:S(2)}) collective-permute-start(bf16[512,128]{1,0:T(8,128)(2,1)S(1)} %get-tuple-element.32), channel_id=1, source_target_pairs={{0,6},{1,7},{2,4},{3,5},{4,2},{5,3},{6,0},{7,1},{8,14},{9,15},{10,... | collective-permute-start | bytes 393224 | tf_op jit(solution)/shard_map/ppermute | solution.py:56
  8.8 1.2 %collective-permute-start.3 = (bf16[512,128]{1,0:T(8,128)(2,1)S(1)}, bf16[512,128]{1,0:T(8,128)(2,1)S(1)}, u32[]{:S(2)}, u32[]{:S(2)}) collective-permute-start(bf16[512,128]{1,0:T(8,128)(2,1)S(1)} %get-tuple-element.30), channel_id=1, source_target_pairs={{0,4},{1,5},{2,6},{3,7},{4,0},{5,1},{6,2},{7,3},{8,12},{9,13},{10,... | collective-permute-start | bytes 393224 | tf_op jit(solution)/shard_map/ppermute | solution.py:56
  10.1 1.6 %collective-permute-start.2 = (bf16[512,128]{1,0:T(8,128)(2,1)S(1)}, bf16[512,128]{1,0:T(8,128)(2,1)S(1)}, u32[]{:S(2)}, u32[]{:S(2)}) collective-permute-start(bf16[512,128]{1,0:T(8,128)(2,1)S(1)} %get-tuple-element.29), channel_id=1, source_target_pairs={{0,2},{1,3},{2,0},{3,1},{4,6},{5,7},{6,4},{7,5},{8,10},{9,11},{10,... | collective-permute-start | bytes 393224 | tf_op jit(solution)/shard_map/ppermute | solution.py:56
  11.6 0.9 %collective-permute-start.9 = (bf16[512,128]{1,0:T(8,128)(2,1)S(1)}, bf16[512,128]{1,0:T(8,128)(2,1)S(1)}, u32[]{:S(2)}, u32[]{:S(2)}) collective-permute-start(bf16[512,128]{1,0:T(8,128)(2,1)S(1)} %get-tuple-element.40), channel_id=1, source_target_pairs={{0,6},{1,7},{2,4},{3,5},{4,2},{5,3},{6,0},{7,1},{8,14},{9,15},{10,... | collective-permute-start | bytes 393224 | tf_op jit(solution)/shard_map/ppermute | solution.py:56
  12.5 1.1 %collective-permute-start.8 = (bf16[512,128]{1,0:T(8,128)(2,1)S(1)}, bf16[512,128]{1,0:T(8,128)(2,1)S(1)}, u32[]{:S(2)}, u32[]{:S(2)}) collective-permute-start(bf16[512,128]{1,0:T(8,128)(2,1)S(1)} %get-tuple-element.39), channel_id=1, source_target_pairs={{0,4},{1,5},{2,6},{3,7},{4,0},{5,1},{6,2},{7,3},{8,12},{9,13},{10,... | collective-permute-start | bytes 393224 | tf_op jit(solution)/shard_map/ppermute | solution.py:56
  13.6 1.5 %collective-permute-start.7 = (bf16[512,128]{1,0:T(8,128)(2,1)S(1)}, bf16[512,128]{1,0:T(8,128)(2,1)S(1)}, u32[]{:S(2)}, u32[]{:S(2)}) collective-permute-start(bf16[512,128]{1,0:T(8,128)(2,1)S(1)} %get-tuple-element.38), channel_id=1, source_target_pairs={{0,2},{1,3},{2,0},{3,1},{4,6},{5,7},{6,4},{7,5},{8,10},{9,11},{10,... | collective-permute-start | bytes 393224 | tf_op jit(solution)/shard_map/ppermute | solution.py:56
  15.2 1.6 %collective-permute-done.3.rest_1_ = bf16[512,128]{1,0:T(8,128)(2,1)S(1)} collective-permute-done((bf16[512,128]{1,0:T(8,128)(2,1)S(1)}, bf16[512,128]{1,0:T(8,128)(2,1)S(1)}, u32[]{:S(2)}, u32[]{:S(2)}) %collective-permute-start.3) | collective-permute-done | bytes 131104 | tf_op jit(solution)/shard_map/ppermute | solution.py:56
  16.9 2.9 %collective-permute-start.5 = (bf16[256,128]{1,0:T(8,128)(2,1)S(1)}, bf16[256,128]{1,0:T(8,128)(2,1)S(1)}, u32[]{:S(2)}, u32[]{:S(2)}) collective-permute-start(bf16[256,128]{1,0:T(8,128)(2,1)S(1)} %get-tuple-element.36), channel_id=1, source_target_pairs={{0,16},{1,17},{2,18},{3,19},{4,20},{5,21},{6,22},{7,23},{8,24},{9,... | collective-permute-start | bytes 196616 | tf_op jit(solution)/shard_map/ppermute | solution.py:56
  19.8 1.3 %collective-permute-start.6 = (bf16[256,128]{1,0:T(8,128)(2,1)S(1)}, bf16[256,128]{1,0:T(8,128)(2,1)S(1)}, u32[]{:S(2)}, u32[]{:S(2)}) collective-permute-start(bf16[256,128]{1,0:T(8,128)(2,1)S(1)} %get-tuple-element.37), channel_id=1, source_target_pairs={{0,24},{1,25},{2,26},{3,27},{4,28},{5,29},{6,30},{7,31},{8,16},{9,... | collective-permute-start | bytes 196616 | tf_op jit(solution)/shard_map/ppermute | solution.py:56
  21.6 1.6 %collective-permute-start.10 = (bf16[256,128]{1,0:T(8,128)(2,1)S(1)}, bf16[256,128]{1,0:T(8,128)(2,1)S(1)}, u32[]{:S(2)}, u32[]{:S(2)}) collective-permute-start(bf16[256,128]{1,0:T(8,128)(2,1)S(1)} %get-tuple-element.41), channel_id=1, source_target_pairs={{0,8},{1,9},{2,10},{3,11},{4,12},{5,13},{6,14},{7,15},{8,0},{9,1},... | collective-permute-start | bytes 196616 | tf_op jit(solution)/shard_map/ppermute | solution.py:56
  23.3 1.3 %tiles.1.tiles_ref = bf16[16,256,384]{2,1,0:T(8,128)(2,1)S(1)} custom-call(s32[3,16]{1,0:T(4,128)S(1)} %bitcast.5, s32[16]{0:T(128)S(1)} %copy-done.3, bf16[16,3,128,128]{3,2,1,0:T(8,128)(2,1)S(1)} %copy-done, f32[64,128]{1,0:T(8,128)S(1)} %bitcast.3), custom_call_target="tpu_custom_call" | custom-call | flops 1048576 | bytes 4194304 | tf_op jit(solution)/shard_map/tiles/pallas_call | solution.py:332
  24.6 1.4 %collective-permute-done.6.rest_2_ = bf16[256,128]{1,0:T(8,128)(2,1)S(1)} collective-permute-done((bf16[256,128]{1,0:T(8,128)(2,1)S(1)}, bf16[256,128]{1,0:T(8,128)(2,1)S(1)}, u32[]{:S(2)}, u32[]{:S(2)}) %collective-permute-start.6) | collective-permute-done | bytes 65568 | tf_op jit(solution)/shard_map/ppermute | solution.py:56
  26.7 1.0 %collective-permute-start.16 = (bf16[256,128]{1,0:T(8,128)(2,1)S(1)}, bf16[256,128]{1,0:T(8,128)(2,1)S(1)}, u32[]{:S(2)}, u32[]{:S(2)}) collective-permute-start(bf16[256,128]{1,0:T(8,128)(2,1)S(1)} %get-tuple-element.49), channel_id=1, source_target_pairs={{0,8},{1,9},{2,10},{3,11},{4,12},{5,13},{6,14},{7,15},{8,0},{9,1},... | collective-permute-start | bytes 196616 | tf_op jit(solution)/shard_map/ppermute | solution.py:56
  27.6 2.7 %collective-permute-start.11 = (bf16[256,128]{1,0:T(8,128)(2,1)S(1)}, bf16[256,128]{1,0:T(8,128)(2,1)S(1)}, u32[]{:S(2)}, u32[]{:S(2)}) collective-permute-start(bf16[256,128]{1,0:T(8,128)(2,1)S(1)} %get-tuple-element.49), channel_id=1, source_target_pairs={{0,16},{1,17},{2,18},{3,19},{4,20},{5,21},{6,22},{7,23},{8,24},{9,... | collective-permute-start | bytes 196616 | tf_op jit(solution)/shard_map/ppermute | solution.py:56
  31.7 2.1 %collective-permute-start.17 = (bf16[512,128]{1,0:T(8,128)(2,1)S(1)}, bf16[512,128]{1,0:T(8,128)(2,1)S(1)}, u32[]{:S(2)}, u32[]{:S(2)}) collective-permute-start(bf16[512,128]{1,0:T(8,128)(2,1)S(1)} %constant_dynamic-update-slice_fusion.2.refs_4_.rest_4_), channel_id=1, source_target_pairs={{0,6},{1,7},{2,4},{3,5},{4,2},{5,3},{6,0},{7,1},{8,14},{9,15},{10,... | collective-permute-start | bytes 393224 | tf_op jit(solution)/shard_map/ppermute | solution.py:56
  34.3 0.9 %collective-permute-start.19 = (bf16[512,128]{1,0:T(8,128)(2,1)S(1)}, bf16[512,128]{1,0:T(8,128)(2,1)S(1)}, u32[]{:S(2)}, u32[]{:S(2)}) collective-permute-start(bf16[512,128]{1,0:T(8,128)(2,1)S(1)} %constant_dynamic-update-slice_fusion.2.refs_4_.rest_4_), channel_id=1, source_target_pairs={{0,2},{1,3},{2,0},{3,1},{4,6},{5,7},{6,4},{7,5},{8,10},{9,11},{10,... | collective-permute-start | bytes 393224 | tf_op jit(solution)/shard_map/ppermute | solution.py:56
  35.3 1.1 %collective-permute-done.12 = bf16[256,128]{1,0:T(8,128)(2,1)S(1)} collective-permute-done((bf16[256,128]{1,0:T(8,128)(2,1)S(1)}, bf16[256,128]{1,0:T(8,128)(2,1)S(1)}, u32[]{:S(2)}, u32[]{:S(2)}) %collective-permute-start.12) | collective-permute-done | bytes 65568 | tf_op jit(solution)/shard_map/ppermute | solution.py:56
  36.4 1.5 %collective-permute-start.13 = (bf16[512,128]{1,0:T(8,128)(2,1)S(1)}, bf16[512,128]{1,0:T(8,128)(2,1)S(1)}, u32[]{:S(2)}, u32[]{:S(2)}) collective-permute-start(bf16[512,128]{1,0:T(8,128)(2,1)S(1)} %constant_dynamic-update-slice_fusion.refs_0_.rest_0_), channel_id=1, source_target_pairs={{0,2},{1,3},{2,0},{3,1},{4,6},{5,7},{6,4},{7,5},{8,10},{9,11},{10,... | collective-permute-start | bytes 393224 | tf_op jit(solution)/shard_map/ppermute | solution.py:56
  39.8 1.4 %collective-permute-start.15 = (bf16[512,128]{1,0:T(8,128)(2,1)S(1)}, bf16[512,128]{1,0:T(8,128)(2,1)S(1)}, u32[]{:S(2)}, u32[]{:S(2)}) collective-permute-start(bf16[512,128]{1,0:T(8,128)(2,1)S(1)} %constant_dynamic-update-slice_fusion.refs_0_.rest_0_), channel_id=1, source_target_pairs={{0,6},{1,7},{2,4},{3,5},{4,2},{5,3},{6,0},{7,1},{8,14},{9,15},{10,... | collective-permute-start | bytes 393224 | tf_op jit(solution)/shard_map/ppermute | solution.py:56
  41.8 1.2 %collective-permute-done.13.refs_1_.rest_1_ = bf16[512,128]{1,0:T(8,128)(2,1)S(1)} collective-permute-done((bf16[512,128]{1,0:T(8,128)(2,1)S(1)}, bf16[512,128]{1,0:T(8,128)(2,1)S(1)}, u32[]{:S(2)}, u32[]{:S(2)}) %collective-permute-start.13) | collective-permute-done | bytes 131104 | tf_op jit(solution)/shard_map/ppermute | solution.py:56
  43.0 3.1 %collective-permute-done.14.refs_2_.rest_2_ = bf16[512,128]{1,0:T(8,128)(2,1)S(1)} collective-permute-done((bf16[512,128]{1,0:T(8,128)(2,1)S(1)}, bf16[512,128]{1,0:T(8,128)(2,1)S(1)}, u32[]{:S(2)}, u32[]{:S(2)}) %collective-permute-start.14) | collective-permute-done | bytes 131104 | tf_op jit(solution)/shard_map/ppermute | solution.py:56
  48.2 18.7 %factors.1 = (f32[256,128]{1,0:T(8,128)}, bf16[2048,128]{1,0:T(8,128)(2,1)}) custom-call(s32[3,16]{1,0:T(4,128)S(1)} %bitcast.6, bf16[16,256,384]{2,1,0:T(8,128)(2,1)S(1)} %tiles.1.tiles_ref, f32[256,128]{1,0:T(8,128)S(1)} %get-tuple-element.48.mine_ref, f32[128,128]{1,0:T(8,128)S(1)} %gram.1.early_ref, ...), custom_call_target="tpu_custom_call" | custom-call | tf_op jit(solution)/shard_map/factors/pallas_call | solution.py:422
  (56 shorter events, 9.0 us)
Async XLA Ops:
  4.6 4.1 %collective-permute-start.1 = (bf16[3072,128]{1,0:T(8,128)(2,1)S(1)}, bf16[3072,128]{1,0:T(8,128)(2,1)S(1)}, u32[]{:S(2)}, u32[]{:S(2)}) collective-permute-start(bf16[3072,128]{1,0:T(8,128)(2,1)S(1)} %later.1), channel_id=1, source_target_pairs={{0,1},{1,0},{2,3},{3,2},{4,5},{5,4},{6,7},{7,6},{8,9},{9,8},{10,11... | collective-permute-start | bytes 2359304 | tf_op jit(solution)/shard_map/ppermute | solution.py:56
  5.1 8.5 %collective-permute-start.4 = (bf16[512,128]{1,0:T(8,128)(2,1)S(1)}, bf16[512,128]{1,0:T(8,128)(2,1)S(1)}, u32[]{:S(2)}, u32[]{:S(2)}) collective-permute-start(bf16[512,128]{1,0:T(8,128)(2,1)S(1)} %get-tuple-element.32), channel_id=1, source_target_pairs={{0,6},{1,7},{2,4},{3,5},{4,2},{5,3},{6,0},{7,1},{8,14},{9,15},{10,... | collective-permute-start | bytes 393224 | tf_op jit(solution)/shard_map/ppermute | solution.py:56
  8.8 7.9 %collective-permute-start.3 = (bf16[512,128]{1,0:T(8,128)(2,1)S(1)}, bf16[512,128]{1,0:T(8,128)(2,1)S(1)}, u32[]{:S(2)}, u32[]{:S(2)}) collective-permute-start(bf16[512,128]{1,0:T(8,128)(2,1)S(1)} %get-tuple-element.30), channel_id=1, source_target_pairs={{0,4},{1,5},{2,6},{3,7},{4,0},{5,1},{6,2},{7,3},{8,12},{9,13},{10,... | collective-permute-start | bytes 393224 | tf_op jit(solution)/shard_map/ppermute | solution.py:56
  10.1 6.7 %collective-permute-start.2 = (bf16[512,128]{1,0:T(8,128)(2,1)S(1)}, bf16[512,128]{1,0:T(8,128)(2,1)S(1)}, u32[]{:S(2)}, u32[]{:S(2)}) collective-permute-start(bf16[512,128]{1,0:T(8,128)(2,1)S(1)} %get-tuple-element.29), channel_id=1, source_target_pairs={{0,2},{1,3},{2,0},{3,1},{4,6},{5,7},{6,4},{7,5},{8,10},{9,11},{10,... | collective-permute-start | bytes 393224 | tf_op jit(solution)/shard_map/ppermute | solution.py:56
  11.6 9.5 %collective-permute-start.9 = (bf16[512,128]{1,0:T(8,128)(2,1)S(1)}, bf16[512,128]{1,0:T(8,128)(2,1)S(1)}, u32[]{:S(2)}, u32[]{:S(2)}) collective-permute-start(bf16[512,128]{1,0:T(8,128)(2,1)S(1)} %get-tuple-element.40), channel_id=1, source_target_pairs={{0,6},{1,7},{2,4},{3,5},{4,2},{5,3},{6,0},{7,1},{8,14},{9,15},{10,... | collective-permute-start | bytes 393224 | tf_op jit(solution)/shard_map/ppermute | solution.py:56
  12.5 8.7 %collective-permute-start.8 = (bf16[512,128]{1,0:T(8,128)(2,1)S(1)}, bf16[512,128]{1,0:T(8,128)(2,1)S(1)}, u32[]{:S(2)}, u32[]{:S(2)}) collective-permute-start(bf16[512,128]{1,0:T(8,128)(2,1)S(1)} %get-tuple-element.39), channel_id=1, source_target_pairs={{0,4},{1,5},{2,6},{3,7},{4,0},{5,1},{6,2},{7,3},{8,12},{9,13},{10,... | collective-permute-start | bytes 393224 | tf_op jit(solution)/shard_map/ppermute | solution.py:56
  13.6 7.9 %collective-permute-start.7 = (bf16[512,128]{1,0:T(8,128)(2,1)S(1)}, bf16[512,128]{1,0:T(8,128)(2,1)S(1)}, u32[]{:S(2)}, u32[]{:S(2)}) collective-permute-start(bf16[512,128]{1,0:T(8,128)(2,1)S(1)} %get-tuple-element.38), channel_id=1, source_target_pairs={{0,2},{1,3},{2,0},{3,1},{4,6},{5,7},{6,4},{7,5},{8,10},{9,11},{10,... | collective-permute-start | bytes 393224 | tf_op jit(solution)/shard_map/ppermute | solution.py:56
  16.9 7.7 %collective-permute-start.5 = (bf16[256,128]{1,0:T(8,128)(2,1)S(1)}, bf16[256,128]{1,0:T(8,128)(2,1)S(1)}, u32[]{:S(2)}, u32[]{:S(2)}) collective-permute-start(bf16[256,128]{1,0:T(8,128)(2,1)S(1)} %get-tuple-element.36), channel_id=1, source_target_pairs={{0,16},{1,17},{2,18},{3,19},{4,20},{5,21},{6,22},{7,23},{8,24},{9,... | collective-permute-start | bytes 196616 | tf_op jit(solution)/shard_map/ppermute | solution.py:56
  19.8 6.2 %collective-permute-start.6 = (bf16[256,128]{1,0:T(8,128)(2,1)S(1)}, bf16[256,128]{1,0:T(8,128)(2,1)S(1)}, u32[]{:S(2)}, u32[]{:S(2)}) collective-permute-start(bf16[256,128]{1,0:T(8,128)(2,1)S(1)} %get-tuple-element.37), channel_id=1, source_target_pairs={{0,24},{1,25},{2,26},{3,27},{4,28},{5,29},{6,30},{7,31},{8,16},{9,... | collective-permute-start | bytes 196616 | tf_op jit(solution)/shard_map/ppermute | solution.py:56
  21.6 5.0 %collective-permute-start.10 = (bf16[256,128]{1,0:T(8,128)(2,1)S(1)}, bf16[256,128]{1,0:T(8,128)(2,1)S(1)}, u32[]{:S(2)}, u32[]{:S(2)}) collective-permute-start(bf16[256,128]{1,0:T(8,128)(2,1)S(1)} %get-tuple-element.41), channel_id=1, source_target_pairs={{0,8},{1,9},{2,10},{3,11},{4,12},{5,13},{6,14},{7,15},{8,0},{9,1},... | collective-permute-start | bytes 196616 | tf_op jit(solution)/shard_map/ppermute | solution.py:56
  26.7 5.0 %collective-permute-start.16 = (bf16[256,128]{1,0:T(8,128)(2,1)S(1)}, bf16[256,128]{1,0:T(8,128)(2,1)S(1)}, u32[]{:S(2)}, u32[]{:S(2)}) collective-permute-start(bf16[256,128]{1,0:T(8,128)(2,1)S(1)} %get-tuple-element.49), channel_id=1, source_target_pairs={{0,8},{1,9},{2,10},{3,11},{4,12},{5,13},{6,14},{7,15},{8,0},{9,1},... | collective-permute-start | bytes 196616 | tf_op jit(solution)/shard_map/ppermute | solution.py:56
  27.6 7.6 %collective-permute-start.11 = (bf16[256,128]{1,0:T(8,128)(2,1)S(1)}, bf16[256,128]{1,0:T(8,128)(2,1)S(1)}, u32[]{:S(2)}, u32[]{:S(2)}) collective-permute-start(bf16[256,128]{1,0:T(8,128)(2,1)S(1)} %get-tuple-element.49), channel_id=1, source_target_pairs={{0,16},{1,17},{2,18},{3,19},{4,20},{5,21},{6,22},{7,23},{8,24},{9,... | collective-permute-start | bytes 196616 | tf_op jit(solution)/shard_map/ppermute | solution.py:56
  30.3 6.1 %collective-permute-start.12 = (bf16[256,128]{1,0:T(8,128)(2,1)S(1)}, bf16[256,128]{1,0:T(8,128)(2,1)S(1)}, u32[]{:S(2)}, u32[]{:S(2)}) collective-permute-start(bf16[256,128]{1,0:T(8,128)(2,1)S(1)} %get-tuple-element.49), channel_id=1, source_target_pairs={{0,24},{1,25},{2,26},{3,27},{4,28},{5,29},{6,30},{7,31},{8,16},{9,... | collective-permute-start | bytes 196616 | tf_op jit(solution)/shard_map/ppermute | solution.py:56
  31.7 6.7 %collective-permute-start.17 = (bf16[512,128]{1,0:T(8,128)(2,1)S(1)}, bf16[512,128]{1,0:T(8,128)(2,1)S(1)}, u32[]{:S(2)}, u32[]{:S(2)}) collective-permute-start(bf16[512,128]{1,0:T(8,128)(2,1)S(1)} %constant_dynamic-update-slice_fusion.2.refs_4_.rest_4_), channel_id=1, source_target_pairs={{0,6},{1,7},{2,4},{3,5},{4,2},{5,3},{6,0},{7,1},{8,14},{9,15},{10,... | collective-permute-start | bytes 393224 | tf_op jit(solution)/shard_map/ppermute | solution.py:56
  33.8 6.0 %collective-permute-start.18 = (bf16[512,128]{1,0:T(8,128)(2,1)S(1)}, bf16[512,128]{1,0:T(8,128)(2,1)S(1)}, u32[]{:S(2)}, u32[]{:S(2)}) collective-permute-start(bf16[512,128]{1,0:T(8,128)(2,1)S(1)} %constant_dynamic-update-slice_fusion.2.refs_4_.rest_4_), channel_id=1, source_target_pairs={{0,4},{1,5},{2,6},{3,7},{4,0},{5,1},{6,2},{7,3},{8,12},{9,13},{10,... | collective-permute-start | bytes 393224 | tf_op jit(solution)/shard_map/ppermute | solution.py:56
  34.3 6.9 %collective-permute-start.19 = (bf16[512,128]{1,0:T(8,128)(2,1)S(1)}, bf16[512,128]{1,0:T(8,128)(2,1)S(1)}, u32[]{:S(2)}, u32[]{:S(2)}) collective-permute-start(bf16[512,128]{1,0:T(8,128)(2,1)S(1)} %constant_dynamic-update-slice_fusion.2.refs_4_.rest_4_), channel_id=1, source_target_pairs={{0,2},{1,3},{2,0},{3,1},{4,6},{5,7},{6,4},{7,5},{8,10},{9,11},{10,... | collective-permute-start | bytes 393224 | tf_op jit(solution)/shard_map/ppermute | solution.py:56
  35.3 6.0 %collective-permute-start.21 = (bf16[512,128]{1,0:T(8,128)(2,1)S(1)}, bf16[512,128]{1,0:T(8,128)(2,1)S(1)}, u32[]{:S(2)}, u32[]{:S(2)}) collective-permute-start(bf16[512,128]{1,0:T(8,128)(2,1)S(1)} %constant_dynamic-update-slice_fusion.2.refs_4_.rest_4_), channel_id=1, source_target_pairs={{0,1},{1,0},{2,3},{3,2},{4,5},{5,4},{6,7},{7,6},{8,9},{9,8},{10,11... | collective-permute-start | bytes 393224 | tf_op jit(solution)/shard_map/ppermute | solution.py:56
  36.4 6.7 %collective-permute-start.13 = (bf16[512,128]{1,0:T(8,128)(2,1)S(1)}, bf16[512,128]{1,0:T(8,128)(2,1)S(1)}, u32[]{:S(2)}, u32[]{:S(2)}) collective-permute-start(bf16[512,128]{1,0:T(8,128)(2,1)S(1)} %constant_dynamic-update-slice_fusion.refs_0_.rest_0_), channel_id=1, source_target_pairs={{0,2},{1,3},{2,0},{3,1},{4,6},{5,7},{6,4},{7,5},{8,10},{9,11},{10,... | collective-permute-start | bytes 393224 | tf_op jit(solution)/shard_map/ppermute | solution.py:56
  38.4 7.7 %collective-permute-start.14 = (bf16[512,128]{1,0:T(8,128)(2,1)S(1)}, bf16[512,128]{1,0:T(8,128)(2,1)S(1)}, u32[]{:S(2)}, u32[]{:S(2)}) collective-permute-start(bf16[512,128]{1,0:T(8,128)(2,1)S(1)} %constant_dynamic-update-slice_fusion.refs_0_.rest_0_), channel_id=1, source_target_pairs={{0,4},{1,5},{2,6},{3,7},{4,0},{5,1},{6,2},{7,3},{8,12},{9,13},{10,... | collective-permute-start | bytes 393224 | tf_op jit(solution)/shard_map/ppermute | solution.py:56
  39.8 6.3 %collective-permute-start.15 = (bf16[512,128]{1,0:T(8,128)(2,1)S(1)}, bf16[512,128]{1,0:T(8,128)(2,1)S(1)}, u32[]{:S(2)}, u32[]{:S(2)}) collective-permute-start(bf16[512,128]{1,0:T(8,128)(2,1)S(1)} %constant_dynamic-update-slice_fusion.refs_0_.rest_0_), channel_id=1, source_target_pairs={{0,6},{1,7},{2,4},{3,5},{4,2},{5,3},{6,0},{7,1},{8,14},{9,15},{10,... | collective-permute-start | bytes 393224 | tf_op jit(solution)/shard_map/ppermute | solution.py:56
  41.3 5.4 %collective-permute-start.20 = (bf16[512,128]{1,0:T(8,128)(2,1)S(1)}, bf16[512,128]{1,0:T(8,128)(2,1)S(1)}, u32[]{:S(2)}, u32[]{:S(2)}) collective-permute-start(bf16[512,128]{1,0:T(8,128)(2,1)S(1)} %constant_dynamic-update-slice_fusion.refs_0_.rest_0_), channel_id=1, source_target_pairs={{0,1},{1,0},{2,3},{3,2},{4,5},{5,4},{6,7},{7,6},{8,9},{9,8},{10,11... | collective-permute-start | bytes 393224 | tf_op jit(solution)/shard_map/ppermute | solution.py:56
  41.3 5.4 %collective-permute-start.22 = (bf16[512,128]{1,0:T(8,128)(2,1)S(1)}, bf16[512,128]{1,0:T(8,128)(2,1)S(1)}, u32[]{:S(2)}, u32[]{:S(2)}) collective-permute-start(bf16[512,128]{1,0:T(8,128)(2,1)S(1)} %collective-permute-done.17.refs_5_.rest_5_), channel_id=1, source_target_pairs={{0,1},{1,0},{2,3},{3,2},{4,5},{5,4},{6,7},{7,6},{8,9},{9,8},{10,11... | collective-permute-start | bytes 393224 | tf_op jit(solution)/shard_map/ppermute | solution.py:56
  43.0 4.1 %collective-permute-start.23 = (bf16[512,128]{1,0:T(8,128)(2,1)S(1)}, bf16[512,128]{1,0:T(8,128)(2,1)S(1)}, u32[]{:S(2)}, u32[]{:S(2)}) collective-permute-start(bf16[512,128]{1,0:T(8,128)(2,1)S(1)} %collective-permute-done.18.refs_6_.rest_6_), channel_id=1, source_target_pairs={{0,1},{1,0},{2,3},{3,2},{4,5},{5,4},{6,7},{7,6},{8,9},{9,8},{10,11... | collective-permute-start | bytes 393224 | tf_op jit(solution)/shard_map/ppermute | solution.py:56
  46.1 2.0 %collective-permute-start.25 = (bf16[512,128]{1,0:T(8,128)(2,1)S(1)}, bf16[512,128]{1,0:T(8,128)(2,1)S(1)}, u32[]{:S(2)}, u32[]{:S(2)}) collective-permute-start(bf16[512,128]{1,0:T(8,128)(2,1)S(1)} %collective-permute-done.13.refs_1_.rest_1_), channel_id=1, source_target_pairs={{0,1},{1,0},{2,3},{3,2},{4,5},{5,4},{6,7},{7,6},{8,9},{9,8},{10,11... | collective-permute-start | bytes 393224 | tf_op jit(solution)/shard_map/ppermute | solution.py:56
  (8 other events, 31.5 us)

commit v16 on v14

--- a/solution.py
+++ b/solution.py
@@ -396,7 +396,7 @@
     other = [plan.swap(part, 1) for part in own]
 
     pieces = own + other
-    late = range(len(own) + plan.plane - 1, len(own) + plan.plane)
+    late = range(len(own) + 1, len(own) + plan.plane)
     gram = pl.pallas_call(
         gram_kernel,
         out_shape=shape((columns, columns), F32),

time: 66.8 us -> 66.3 us (level)
  transfers between devices with their start and end apart: 30 -> 30, of which waited for: 15 -> 13; matrix products, arithmetic and copies ran while one was open for 0% -> 0% of each run, Pallas kernels for 4% -> 4%
where the time goes in v16:
time: 66.3 us; the launch traced here: 66.1 us
  starting transfers between devices  30.1 us (45%)
  Pallas kernels  23.4 us (35%)
  waiting for transfers between devices  11.8 us (18%)
  between operations  0.77 us (1%)
    ppermute x30, starting transfers between devices, swap(): return lax.ppermute(value, AXES, [(d, d ^ mask) for d in range(self.count)])  30.1 us
    pallas_call x1, Pallas kernels, body(): pl.pallas_call(functools.partial(last_kernel, plan, features, late), out_...  18.7 us
    ppermute x30, waiting for transfers between devices, swap(): return lax.ppermute(value, AXES, [(d, d ^ mask) for d in range(self.count)])  11.8 us
    pallas_call x1, Pallas kernels, body(): pl.pallas_call(functools.partial(sum_kernel, plan), out_shape=(pltpu.VMEM...  2.32 us
  transfers between devices with their start and end apart: 30, of which 13 were waited for; matrix products, arithmetic and copies ran while one was open for 0% of the time, Pallas kernels for 4%

profile of v16, /device:TPU:0, one launch (start us, length us, event | category | flops | bytes accessed | tf_op | source)
XLA Modules:
  0.0 66.1 jit_solution(16594928365882740649)
XLA Ops:
  0.6 2.3 %local_sum.1 = (f32[8192,128]{1,0:T(8,128)S(1)}, bf16[1024,128]{1,0:T(8,128)(2,1)S(1)}, bf16[1024,128]{1,0:T(8,128)(2,1)S(1)}, bf16[1024,128]{1,0:T(8,128)(2,1)S(1)}, bf16[1024,128]{1,0:T(8,128)(2,1)S(1)}) custom-call(s32[3,16]{1,0:T(4,128)} %bitcast.4, s32[16]{0:T(128)} %counts_ref.1, bf16[16,3,128,128]{3,2,1,0:T(8,128)(2,1)} %blocks_ref.3, ...), custom_call_target="tpu_custom_call" | custom-call | tf_op jit(solution)/shard_map/local_sum/pallas_call | solution.py:311
  5.1 3.9 %collective-permute-start.10 = (bf16[512,128]{1,0:T(8,128)(2,1)S(1)}, bf16[512,128]{1,0:T(8,128)(2,1)S(1)}, u32[]{:S(2)}, u32[]{:S(2)}) collective-permute-start(bf16[512,128]{1,0:T(8,128)(2,1)S(1)} %get-tuple-element.42), channel_id=1, source_target_pairs={{0,6},{1,7},{2,4},{3,5},{4,2},{5,3},{6,0},{7,1},{8,14},{9,15},{10,... | collective-permute-start | bytes 393224 | tf_op jit(solution)/shard_map/ppermute | solution.py:56
  10.0 2.7 %collective-permute-start.6 = (bf16[512,128]{1,0:T(8,128)(2,1)S(1)}, bf16[512,128]{1,0:T(8,128)(2,1)S(1)}, u32[]{:S(2)}, u32[]{:S(2)}) collective-permute-start(bf16[512,128]{1,0:T(8,128)(2,1)S(1)} %get-tuple-element.38), channel_id=1, source_target_pairs={{0,6},{1,7},{2,4},{3,5},{4,2},{5,3},{6,0},{7,1},{8,14},{9,15},{10,... | collective-permute-start | bytes 393224 | tf_op jit(solution)/shard_map/ppermute | solution.py:56
  13.2 2.0 %collective-permute-start.3 = (bf16[512,128]{1,0:T(8,128)(2,1)S(1)}, bf16[512,128]{1,0:T(8,128)(2,1)S(1)}, u32[]{:S(2)}, u32[]{:S(2)}) collective-permute-start(bf16[512,128]{1,0:T(8,128)(2,1)S(1)} %get-tuple-element.34), channel_id=1, source_target_pairs={{0,2},{1,3},{2,0},{3,1},{4,6},{5,7},{6,4},{7,5},{8,10},{9,11},{10,... | collective-permute-start | bytes 393224 | tf_op jit(solution)/shard_map/ppermute | solution.py:56
  15.3 1.7 %collective-permute-done.9.rest_1_ = bf16[512,128]{1,0:T(8,128)(2,1)S(1)} collective-permute-done((bf16[512,128]{1,0:T(8,128)(2,1)S(1)}, bf16[512,128]{1,0:T(8,128)(2,1)S(1)}, u32[]{:S(2)}, u32[]{:S(2)}) %collective-permute-start.9) | collective-permute-done | bytes 131104 | tf_op jit(solution)/shard_map/ppermute | solution.py:56
  17.2 2.8 %collective-permute-start.11 = (bf16[256,128]{1,0:T(8,128)(2,1)S(1)}, bf16[256,128]{1,0:T(8,128)(2,1)S(1)}, u32[]{:S(2)}, u32[]{:S(2)}) collective-permute-start(bf16[256,128]{1,0:T(8,128)(2,1)S(1)} %get-tuple-element.46), channel_id=1, source_target_pairs={{0,16},{1,17},{2,18},{3,19},{4,20},{5,21},{6,22},{7,23},{8,24},{9,... | collective-permute-start | bytes 196616 | tf_op jit(solution)/shard_map/ppermute | solution.py:56
  20.0 1.4 %collective-permute-start.12 = (bf16[256,128]{1,0:T(8,128)(2,1)S(1)}, bf16[256,128]{1,0:T(8,128)(2,1)S(1)}, u32[]{:S(2)}, u32[]{:S(2)}) collective-permute-start(bf16[256,128]{1,0:T(8,128)(2,1)S(1)} %get-tuple-element.47), channel_id=1, source_target_pairs={{0,24},{1,25},{2,26},{3,27},{4,28},{5,29},{6,30},{7,31},{8,16},{9,... | collective-permute-start | bytes 196616 | tf_op jit(solution)/shard_map/ppermute | solution.py:56
  21.6 1.6 %collective-permute-start.7 = (bf16[256,128]{1,0:T(8,128)(2,1)S(1)}, bf16[256,128]{1,0:T(8,128)(2,1)S(1)}, u32[]{:S(2)}, u32[]{:S(2)}) collective-permute-start(bf16[256,128]{1,0:T(8,128)(2,1)S(1)} %get-tuple-element.39), channel_id=1, source_target_pairs={{0,8},{1,9},{2,10},{3,11},{4,12},{5,13},{6,14},{7,15},{8,0},{9,1},... | collective-permute-start | bytes 196616 | tf_op jit(solution)/shard_map/ppermute | solution.py:56
  23.2 1.3 %tiles.1.tiles_ref = bf16[16,256,384]{2,1,0:T(8,128)(2,1)S(1)} custom-call(s32[3,16]{1,0:T(4,128)S(1)} %bitcast.5, s32[16]{0:T(128)S(1)} %copy-done.3, bf16[16,3,128,128]{3,2,1,0:T(8,128)(2,1)S(1)} %copy-done, f32[64,128]{1,0:T(8,128)S(1)} %bitcast.3), custom_call_target="tpu_custom_call" | custom-call | flops 1048576 | bytes 4194304 | tf_op jit(solution)/shard_map/tiles/pallas_call | solution.py:329
  24.7 1.5 %collective-permute-done.12.rest_2_ = bf16[256,128]{1,0:T(8,128)(2,1)S(1)} collective-permute-done((bf16[256,128]{1,0:T(8,128)(2,1)S(1)}, bf16[256,128]{1,0:T(8,128)(2,1)S(1)}, u32[]{:S(2)}, u32[]{:S(2)}) %collective-permute-start.12) | collective-permute-done | bytes 65568 | tf_op jit(solution)/shard_map/ppermute | solution.py:56
  26.8 0.8 %collective-permute-start.18 = (bf16[256,128]{1,0:T(8,128)(2,1)S(1)}, bf16[256,128]{1,0:T(8,128)(2,1)S(1)}, u32[]{:S(2)}, u32[]{:S(2)}) collective-permute-start(bf16[256,128]{1,0:T(8,128)(2,1)S(1)} %get-tuple-element.55), channel_id=1, source_target_pairs={{0,8},{1,9},{2,10},{3,11},{4,12},{5,13},{6,14},{7,15},{8,0},{9,1},... | collective-permute-start | bytes 196616 | tf_op jit(solution)/shard_map/ppermute | solution.py:56
  27.6 2.9 %collective-permute-start.13 = (bf16[256,128]{1,0:T(8,128)(2,1)S(1)}, bf16[256,128]{1,0:T(8,128)(2,1)S(1)}, u32[]{:S(2)}, u32[]{:S(2)}) collective-permute-start(bf16[256,128]{1,0:T(8,128)(2,1)S(1)} %get-tuple-element.55), channel_id=1, source_target_pairs={{0,16},{1,17},{2,18},{3,19},{4,20},{5,21},{6,22},{7,23},{8,24},{9,... | collective-permute-start | bytes 196616 | tf_op jit(solution)/shard_map/ppermute | solution.py:56
  30.5 0.8 %collective-permute-start.14 = (bf16[256,128]{1,0:T(8,128)(2,1)S(1)}, bf16[256,128]{1,0:T(8,128)(2,1)S(1)}, u32[]{:S(2)}, u32[]{:S(2)}) collective-permute-start(bf16[256,128]{1,0:T(8,128)(2,1)S(1)} %get-tuple-element.55), channel_id=1, source_target_pairs={{0,24},{1,25},{2,26},{3,27},{4,28},{5,29},{6,30},{7,31},{8,16},{9,... | collective-permute-start | bytes 196616 | tf_op jit(solution)/shard_map/ppermute | solution.py:56
  31.8 1.2 %collective-permute-start.19 = (bf16[512,128]{1,0:T(8,128)(2,1)S(1)}, bf16[512,128]{1,0:T(8,128)(2,1)S(1)}, u32[]{:S(2)}, u32[]{:S(2)}) collective-permute-start(bf16[512,128]{1,0:T(8,128)(2,1)S(1)} %constant_dynamic-update-slice_fusion.2.refs_4_.rest_4_), channel_id=1, source_target_pairs={{0,6},{1,7},{2,4},{3,5},{4,2},{5,3},{6,0},{7,1},{8,14},{9,15},{10,... | collective-permute-start | bytes 393224 | tf_op jit(solution)/shard_map/ppermute | solution.py:56
  33.0 1.3 %collective-permute-start.20 = (bf16[512,128]{1,0:T(8,128)(2,1)S(1)}, bf16[512,128]{1,0:T(8,128)(2,1)S(1)}, u32[]{:S(2)}, u32[]{:S(2)}) collective-permute-start(bf16[512,128]{1,0:T(8,128)(2,1)S(1)} %constant_dynamic-update-slice_fusion.2.refs_4_.rest_4_), channel_id=1, source_target_pairs={{0,4},{1,5},{2,6},{3,7},{4,0},{5,1},{6,2},{7,3},{8,12},{9,13},{10,... | collective-permute-start | bytes 393224 | tf_op jit(solution)/shard_map/ppermute | solution.py:56
  34.3 1.1 %collective-permute-start.21 = (bf16[512,128]{1,0:T(8,128)(2,1)S(1)}, bf16[512,128]{1,0:T(8,128)(2,1)S(1)}, u32[]{:S(2)}, u32[]{:S(2)}) collective-permute-start(bf16[512,128]{1,0:T(8,128)(2,1)S(1)} %constant_dynamic-update-slice_fusion.2.refs_4_.rest_4_), channel_id=1, source_target_pairs={{0,2},{1,3},{2,0},{3,1},{4,6},{5,7},{6,4},{7,5},{8,10},{9,11},{10,... | collective-permute-start | bytes 393224 | tf_op jit(solution)/shard_map/ppermute | solution.py:56
  35.4 1.1 %collective-permute-done.14 = bf16[256,128]{1,0:T(8,128)(2,1)S(1)} collective-permute-done((bf16[256,128]{1,0:T(8,128)(2,1)S(1)}, bf16[256,128]{1,0:T(8,128)(2,1)S(1)}, u32[]{:S(2)}, u32[]{:S(2)}) %collective-permute-start.14) | collective-permute-done | bytes 65568 | tf_op jit(solution)/shard_map/ppermute | solution.py:56
  36.5 1.3 %collective-permute-start.15 = (bf16[512,128]{1,0:T(8,128)(2,1)S(1)}, bf16[512,128]{1,0:T(8,128)(2,1)S(1)}, u32[]{:S(2)}, u32[]{:S(2)}) collective-permute-start(bf16[512,128]{1,0:T(8,128)(2,1)S(1)} %constant_dynamic-update-slice_fusion.refs_0_.rest_0_), channel_id=1, source_target_pairs={{0,2},{1,3},{2,0},{3,1},{4,6},{5,7},{6,4},{7,5},{8,10},{9,11},{10,... | collective-permute-start | bytes 393224 | tf_op jit(solution)/shard_map/ppermute | solution.py:56
  37.9 1.1 %collective-permute-start.16 = (bf16[512,128]{1,0:T(8,128)(2,1)S(1)}, bf16[512,128]{1,0:T(8,128)(2,1)S(1)}, u32[]{:S(2)}, u32[]{:S(2)}) collective-permute-start(bf16[512,128]{1,0:T(8,128)(2,1)S(1)} %constant_dynamic-update-slice_fusion.refs_0_.rest_0_), channel_id=1, source_target_pairs={{0,4},{1,5},{2,6},{3,7},{4,0},{5,1},{6,2},{7,3},{8,12},{9,13},{10,... | collective-permute-start | bytes 393224 | tf_op jit(solution)/shard_map/ppermute | solution.py:56
  39.2 1.2 %collective-permute-start.17 = (bf16[512,128]{1,0:T(8,128)(2,1)S(1)}, bf16[512,128]{1,0:T(8,128)(2,1)S(1)}, u32[]{:S(2)}, u32[]{:S(2)}) collective-permute-start(bf16[512,128]{1,0:T(8,128)(2,1)S(1)} %constant_dynamic-update-slice_fusion.refs_0_.rest_0_), channel_id=1, source_target_pairs={{0,6},{1,7},{2,4},{3,5},{4,2},{5,3},{6,0},{7,1},{8,14},{9,15},{10,... | collective-permute-start | bytes 393224 | tf_op jit(solution)/shard_map/ppermute | solution.py:56
  40.9 2.1 %collective-permute-done.15.refs_1_.rest_1_ = bf16[512,128]{1,0:T(8,128)(2,1)S(1)} collective-permute-done((bf16[512,128]{1,0:T(8,128)(2,1)S(1)}, bf16[512,128]{1,0:T(8,128)(2,1)S(1)}, u32[]{:S(2)}, u32[]{:S(2)}) %collective-permute-start.15) | collective-permute-done | bytes 131104 | tf_op jit(solution)/shard_map/ppermute | solution.py:56
  43.0 2.3 %collective-permute-done.16.refs_2_.rest_2_ = bf16[512,128]{1,0:T(8,128)(2,1)S(1)} collective-permute-done((bf16[512,128]{1,0:T(8,128)(2,1)S(1)}, bf16[512,128]{1,0:T(8,128)(2,1)S(1)}, u32[]{:S(2)}, u32[]{:S(2)}) %collective-permute-start.16) | collective-permute-done | bytes 131104 | tf_op jit(solution)/shard_map/ppermute | solution.py:56
  46.7 0.7 gram.1.early_ref
  47.4 18.7 %factors.1 = (f32[256,128]{1,0:T(8,128)}, bf16[2048,128]{1,0:T(8,128)(2,1)}) custom-call(s32[3,16]{1,0:T(4,128)S(1)} %bitcast.6, bf16[16,256,384]{2,1,0:T(8,128)(2,1)S(1)} %tiles.1.tiles_ref, f32[256,128]{1,0:T(8,128)S(1)} %get-tuple-element.54.mine_ref, f32[128,128]{1,0:T(8,128)S(1)} %gram.1.early_ref, ...), custom_call_target="tpu_custom_call" | custom-call | tf_op jit(solution)/shard_map/factors/pallas_call | solution.py:409
  (59 shorter events, 7.7 us)
Async XLA Ops:
  3.6 5.4 %collective-permute-start.4 = (bf16[1024,128]{1,0:T(8,128)(2,1)S(1)}, bf16[1024,128]{1,0:T(8,128)(2,1)S(1)}, u32[]{:S(2)}, u32[]{:S(2)}) collective-permute-start(bf16[1024,128]{1,0:T(8,128)(2,1)S(1)} %get-tuple-element.35), channel_id=1, source_target_pairs={{0,1},{1,0},{2,3},{3,2},{4,5},{5,4},{6,7},{7,6},{8,9},{9,8},{10,11... | collective-permute-start | bytes 786440 | tf_op jit(solution)/shard_map/ppermute | solution.py:56
  4.0 5.6 %collective-permute-start.2 = (bf16[1024,128]{1,0:T(8,128)(2,1)S(1)}, bf16[1024,128]{1,0:T(8,128)(2,1)S(1)}, u32[]{:S(2)}, u32[]{:S(2)}) collective-permute-start(bf16[1024,128]{1,0:T(8,128)(2,1)S(1)} %get-tuple-element.33), channel_id=1, source_target_pairs={{0,1},{1,0},{2,3},{3,2},{4,5},{5,4},{6,7},{7,6},{8,9},{9,8},{10,11... | collective-permute-start | bytes 786440 | tf_op jit(solution)/shard_map/ppermute | solution.py:56
  5.1 8.1 %collective-permute-start.10 = (bf16[512,128]{1,0:T(8,128)(2,1)S(1)}, bf16[512,128]{1,0:T(8,128)(2,1)S(1)}, u32[]{:S(2)}, u32[]{:S(2)}) collective-permute-start(bf16[512,128]{1,0:T(8,128)(2,1)S(1)} %get-tuple-element.42), channel_id=1, source_target_pairs={{0,6},{1,7},{2,4},{3,5},{4,2},{5,3},{6,0},{7,1},{8,14},{9,15},{10,... | collective-permute-start | bytes 393224 | tf_op jit(solution)/shard_map/ppermute | solution.py:56
  9.0 8.0 %collective-permute-start.9 = (bf16[512,128]{1,0:T(8,128)(2,1)S(1)}, bf16[512,128]{1,0:T(8,128)(2,1)S(1)}, u32[]{:S(2)}, u32[]{:S(2)}) collective-permute-start(bf16[512,128]{1,0:T(8,128)(2,1)S(1)} %get-tuple-element.41), channel_id=1, source_target_pairs={{0,4},{1,5},{2,6},{3,7},{4,0},{5,1},{6,2},{7,3},{8,12},{9,13},{10,... | collective-permute-start | bytes 393224 | tf_op jit(solution)/shard_map/ppermute | solution.py:56
  9.6 7.4 %collective-permute-start.8 = (bf16[512,128]{1,0:T(8,128)(2,1)S(1)}, bf16[512,128]{1,0:T(8,128)(2,1)S(1)}, u32[]{:S(2)}, u32[]{:S(2)}) collective-permute-start(bf16[512,128]{1,0:T(8,128)(2,1)S(1)} %get-tuple-element.40), channel_id=1, source_target_pairs={{0,2},{1,3},{2,0},{3,1},{4,6},{5,7},{6,4},{7,5},{8,10},{9,11},{10,... | collective-permute-start | bytes 393224 | tf_op jit(solution)/shard_map/ppermute | solution.py:56
  10.0 11.3 %collective-permute-start.6 = (bf16[512,128]{1,0:T(8,128)(2,1)S(1)}, bf16[512,128]{1,0:T(8,128)(2,1)S(1)}, u32[]{:S(2)}, u32[]{:S(2)}) collective-permute-start(bf16[512,128]{1,0:T(8,128)(2,1)S(1)} %get-tuple-element.38), channel_id=1, source_target_pairs={{0,6},{1,7},{2,4},{3,5},{4,2},{5,3},{6,0},{7,1},{8,14},{9,15},{10,... | collective-permute-start | bytes 393224 | tf_op jit(solution)/shard_map/ppermute | solution.py:56
  12.7 8.6 %collective-permute-start.5 = (bf16[512,128]{1,0:T(8,128)(2,1)S(1)}, bf16[512,128]{1,0:T(8,128)(2,1)S(1)}, u32[]{:S(2)}, u32[]{:S(2)}) collective-permute-start(bf16[512,128]{1,0:T(8,128)(2,1)S(1)} %get-tuple-element.36), channel_id=1, source_target_pairs={{0,4},{1,5},{2,6},{3,7},{4,0},{5,1},{6,2},{7,3},{8,12},{9,13},{10,... | collective-permute-start | bytes 393224 | tf_op jit(solution)/shard_map/ppermute | solution.py:56
  13.2 8.3 %collective-permute-start.3 = (bf16[512,128]{1,0:T(8,128)(2,1)S(1)}, bf16[512,128]{1,0:T(8,128)(2,1)S(1)}, u32[]{:S(2)}, u32[]{:S(2)}) collective-permute-start(bf16[512,128]{1,0:T(8,128)(2,1)S(1)} %get-tuple-element.34), channel_id=1, source_target_pairs={{0,2},{1,3},{2,0},{3,1},{4,6},{5,7},{6,4},{7,5},{8,10},{9,11},{10,... | collective-permute-start | bytes 393224 | tf_op jit(solution)/shard_map/ppermute | solution.py:56
  17.2 7.5 %collective-permute-start.11 = (bf16[256,128]{1,0:T(8,128)(2,1)S(1)}, bf16[256,128]{1,0:T(8,128)(2,1)S(1)}, u32[]{:S(2)}, u32[]{:S(2)}) collective-permute-start(bf16[256,128]{1,0:T(8,128)(2,1)S(1)} %get-tuple-element.46), channel_id=1, source_target_pairs={{0,16},{1,17},{2,18},{3,19},{4,20},{5,21},{6,22},{7,23},{8,24},{9,... | collective-permute-start | bytes 196616 | tf_op jit(solution)/shard_map/ppermute | solution.py:56
  20.0 6.2 %collective-permute-start.12 = (bf16[256,128]{1,0:T(8,128)(2,1)S(1)}, bf16[256,128]{1,0:T(8,128)(2,1)S(1)}, u32[]{:S(2)}, u32[]{:S(2)}) collective-permute-start(bf16[256,128]{1,0:T(8,128)(2,1)S(1)} %get-tuple-element.47), channel_id=1, source_target_pairs={{0,24},{1,25},{2,26},{3,27},{4,28},{5,29},{6,30},{7,31},{8,16},{9,... | collective-permute-start | bytes 196616 | tf_op jit(solution)/shard_map/ppermute | solution.py:56
  21.6 5.2 %collective-permute-start.7 = (bf16[256,128]{1,0:T(8,128)(2,1)S(1)}, bf16[256,128]{1,0:T(8,128)(2,1)S(1)}, u32[]{:S(2)}, u32[]{:S(2)}) collective-permute-start(bf16[256,128]{1,0:T(8,128)(2,1)S(1)} %get-tuple-element.39), channel_id=1, source_target_pairs={{0,8},{1,9},{2,10},{3,11},{4,12},{5,13},{6,14},{7,15},{8,0},{9,1},... | collective-permute-start | bytes 196616 | tf_op jit(solution)/shard_map/ppermute | solution.py:56
  26.8 5.0 %collective-permute-start.18 = (bf16[256,128]{1,0:T(8,128)(2,1)S(1)}, bf16[256,128]{1,0:T(8,128)(2,1)S(1)}, u32[]{:S(2)}, u32[]{:S(2)}) collective-permute-start(bf16[256,128]{1,0:T(8,128)(2,1)S(1)} %get-tuple-element.55), channel_id=1, source_target_pairs={{0,8},{1,9},{2,10},{3,11},{4,12},{5,13},{6,14},{7,15},{8,0},{9,1},... | collective-permute-start | bytes 196616 | tf_op jit(solution)/shard_map/ppermute | solution.py:56
  27.6 7.8 %collective-permute-start.13 = (bf16[256,128]{1,0:T(8,128)(2,1)S(1)}, bf16[256,128]{1,0:T(8,128)(2,1)S(1)}, u32[]{:S(2)}, u32[]{:S(2)}) collective-permute-start(bf16[256,128]{1,0:T(8,128)(2,1)S(1)} %get-tuple-element.55), channel_id=1, source_target_pairs={{0,16},{1,17},{2,18},{3,19},{4,20},{5,21},{6,22},{7,23},{8,24},{9,... | collective-permute-start | bytes 196616 | tf_op jit(solution)/shard_map/ppermute | solution.py:56
  30.5 6.1 %collective-permute-start.14 = (bf16[256,128]{1,0:T(8,128)(2,1)S(1)}, bf16[256,128]{1,0:T(8,128)(2,1)S(1)}, u32[]{:S(2)}, u32[]{:S(2)}) collective-permute-start(bf16[256,128]{1,0:T(8,128)(2,1)S(1)} %get-tuple-element.55), channel_id=1, source_target_pairs={{0,24},{1,25},{2,26},{3,27},{4,28},{5,29},{6,30},{7,31},{8,16},{9,... | collective-permute-start | bytes 196616 | tf_op jit(solution)/shard_map/ppermute | solution.py:56
  31.8 6.0 %collective-permute-start.19 = (bf16[512,128]{1,0:T(8,128)(2,1)S(1)}, bf16[512,128]{1,0:T(8,128)(2,1)S(1)}, u32[]{:S(2)}, u32[]{:S(2)}) collective-permute-start(bf16[512,128]{1,0:T(8,128)(2,1)S(1)} %constant_dynamic-update-slice_fusion.2.refs_4_.rest_4_), channel_id=1, source_target_pairs={{0,6},{1,7},{2,4},{3,5},{4,2},{5,3},{6,0},{7,1},{8,14},{9,15},{10,... | collective-permute-start | bytes 393224 | tf_op jit(solution)/shard_map/ppermute | solution.py:56
  33.0 6.2 %collective-permute-start.20 = (bf16[512,128]{1,0:T(8,128)(2,1)S(1)}, bf16[512,128]{1,0:T(8,128)(2,1)S(1)}, u32[]{:S(2)}, u32[]{:S(2)}) collective-permute-start(bf16[512,128]{1,0:T(8,128)(2,1)S(1)} %constant_dynamic-update-slice_fusion.2.refs_4_.rest_4_), channel_id=1, source_target_pairs={{0,4},{1,5},{2,6},{3,7},{4,0},{5,1},{6,2},{7,3},{8,12},{9,13},{10,... | collective-permute-start | bytes 393224 | tf_op jit(solution)/shard_map/ppermute | solution.py:56
  34.3 6.1 %collective-permute-start.21 = (bf16[512,128]{1,0:T(8,128)(2,1)S(1)}, bf16[512,128]{1,0:T(8,128)(2,1)S(1)}, u32[]{:S(2)}, u32[]{:S(2)}) collective-permute-start(bf16[512,128]{1,0:T(8,128)(2,1)S(1)} %constant_dynamic-update-slice_fusion.2.refs_4_.rest_4_), channel_id=1, source_target_pairs={{0,2},{1,3},{2,0},{3,1},{4,6},{5,7},{6,4},{7,5},{8,10},{9,11},{10,... | collective-permute-start | bytes 393224 | tf_op jit(solution)/shard_map/ppermute | solution.py:56
  35.4 5.0 %collective-permute-start.23 = (bf16[512,128]{1,0:T(8,128)(2,1)S(1)}, bf16[512,128]{1,0:T(8,128)(2,1)S(1)}, u32[]{:S(2)}, u32[]{:S(2)}) collective-permute-start(bf16[512,128]{1,0:T(8,128)(2,1)S(1)} %constant_dynamic-update-slice_fusion.2.refs_4_.rest_4_), channel_id=1, source_target_pairs={{0,1},{1,0},{2,3},{3,2},{4,5},{5,4},{6,7},{7,6},{8,9},{9,8},{10,11... | collective-permute-start | bytes 393224 | tf_op jit(solution)/shard_map/ppermute | solution.py:56
  36.5 6.5 %collective-permute-start.15 = (bf16[512,128]{1,0:T(8,128)(2,1)S(1)}, bf16[512,128]{1,0:T(8,128)(2,1)S(1)}, u32[]{:S(2)}, u32[]{:S(2)}) collective-permute-start(bf16[512,128]{1,0:T(8,128)(2,1)S(1)} %constant_dynamic-update-slice_fusion.refs_0_.rest_0_), channel_id=1, source_target_pairs={{0,2},{1,3},{2,0},{3,1},{4,6},{5,7},{6,4},{7,5},{8,10},{9,11},{10,... | collective-permute-start | bytes 393224 | tf_op jit(solution)/shard_map/ppermute | solution.py:56
  37.9 7.5 %collective-permute-start.16 = (bf16[512,128]{1,0:T(8,128)(2,1)S(1)}, bf16[512,128]{1,0:T(8,128)(2,1)S(1)}, u32[]{:S(2)}, u32[]{:S(2)}) collective-permute-start(bf16[512,128]{1,0:T(8,128)(2,1)S(1)} %constant_dynamic-update-slice_fusion.refs_0_.rest_0_), channel_id=1, source_target_pairs={{0,4},{1,5},{2,6},{3,7},{4,0},{5,1},{6,2},{7,3},{8,12},{9,13},{10,... | collective-permute-start | bytes 393224 | tf_op jit(solution)/shard_map/ppermute | solution.py:56
  39.2 6.2 %collective-permute-start.17 = (bf16[512,128]{1,0:T(8,128)(2,1)S(1)}, bf16[512,128]{1,0:T(8,128)(2,1)S(1)}, u32[]{:S(2)}, u32[]{:S(2)}) collective-permute-start(bf16[512,128]{1,0:T(8,128)(2,1)S(1)} %constant_dynamic-update-slice_fusion.refs_0_.rest_0_), channel_id=1, source_target_pairs={{0,6},{1,7},{2,4},{3,5},{4,2},{5,3},{6,0},{7,1},{8,14},{9,15},{10,... | collective-permute-start | bytes 393224 | tf_op jit(solution)/shard_map/ppermute | solution.py:56
  40.4 5.5 %collective-permute-start.22 = (bf16[512,128]{1,0:T(8,128)(2,1)S(1)}, bf16[512,128]{1,0:T(8,128)(2,1)S(1)}, u32[]{:S(2)}, u32[]{:S(2)}) collective-permute-start(bf16[512,128]{1,0:T(8,128)(2,1)S(1)} %constant_dynamic-update-slice_fusion.refs_0_.rest_0_), channel_id=1, source_target_pairs={{0,1},{1,0},{2,3},{3,2},{4,5},{5,4},{6,7},{7,6},{8,9},{9,8},{10,11... | collective-permute-start | bytes 393224 | tf_op jit(solution)/shard_map/ppermute | solution.py:56
  40.4 5.5 %collective-permute-start.24 = (bf16[512,128]{1,0:T(8,128)(2,1)S(1)}, bf16[512,128]{1,0:T(8,128)(2,1)S(1)}, u32[]{:S(2)}, u32[]{:S(2)}) collective-permute-start(bf16[512,128]{1,0:T(8,128)(2,1)S(1)} %collective-permute-done.19.refs_5_.rest_5_), channel_id=1, source_target_pairs={{0,1},{1,0},{2,3},{3,2},{4,5},{5,4},{6,7},{7,6},{8,9},{9,8},{10,11... | collective-permute-start | bytes 393224 | tf_op jit(solution)/shard_map/ppermute | solution.py:56
  43.0 3.4 %collective-permute-start.25 = (bf16[512,128]{1,0:T(8,128)(2,1)S(1)}, bf16[512,128]{1,0:T(8,128)(2,1)S(1)}, u32[]{:S(2)}, u32[]{:S(2)}) collective-permute-start(bf16[512,128]{1,0:T(8,128)(2,1)S(1)} %collective-permute-done.20.refs_6_.rest_6_), channel_id=1, source_target_pairs={{0,1},{1,0},{2,3},{3,2},{4,5},{5,4},{6,7},{7,6},{8,9},{9,8},{10,11... | collective-permute-start | bytes 393224 | tf_op jit(solution)/shard_map/ppermute | solution.py:56
  (10 other events, 34.0 us)

commit v17 on v16

--- a/solution.py
+++ b/solution.py
@@ -348,7 +348,6 @@
     middle = chunk // 2
     others = range(1, plan.plane)
     got = {p: plan.swap(send[p], 1) for p in (*others, 0)}
-    got[plan.plane - 1], got[0] = lax.optimization_barrier((got[plan.plane - 1], got[0]))
     chip = {}
     for p in others:
         chip[p] = pl.pallas_call(

time: 66.3 us -> 66.9 us (level)
  starting transfers between devices: 30.1 us -> 30.9 us
    ppermute x30, starting transfers between devices: 30.1 us -> 30.9 us  [swap(): return lax.ppermute(value, AXES, [(d, d ^ mask) for d in range(self.count)])]
  transfers between devices with their start and end apart: 30 -> 30, of which waited for: 13 -> 11; matrix products, arithmetic and copies ran while one was open for 0% -> 0% of each run, Pallas kernels for 4% -> 4%
where the time goes in v17:
time: 66.9 us; the launch traced here: 66.7 us
  starting transfers between devices  30.9 us (46%)
  Pallas kernels  23.4 us (35%)
  waiting for transfers between devices  11.5 us (17%)
  between operations  0.79 us (1%)
    ppermute x30, starting transfers between devices, swap(): return lax.ppermute(value, AXES, [(d, d ^ mask) for d in range(self.count)])  30.9 us
    pallas_call x1, Pallas kernels, body(): pl.pallas_call(functools.partial(last_kernel, plan, features, late), out_...  18.7 us
    ppermute x30, waiting for transfers between devices, swap(): return lax.ppermute(value, AXES, [(d, d ^ mask) for d in range(self.count)])  11.5 us
    pallas_call x1, Pallas kernels, body(): pl.pallas_call(functools.partial(sum_kernel, plan), out_shape=(pltpu.VMEM...  2.32 us
  transfers between devices with their start and end apart: 30, of which 11 were waited for; matrix products, arithmetic and copies ran while one was open for 0% of the time, Pallas kernels for 4%

profile of v17, /device:TPU:0, one launch (start us, length us, event | category | flops | bytes accessed | tf_op | source)
XLA Modules:
  0.0 66.7 jit_solution(11782430730275471879)
XLA Ops:
  0.6 2.3 %local_sum.1 = (f32[8192,128]{1,0:T(8,128)S(1)}, bf16[1024,128]{1,0:T(8,128)(2,1)S(1)}, bf16[1024,128]{1,0:T(8,128)(2,1)S(1)}, bf16[1024,128]{1,0:T(8,128)(2,1)S(1)}, bf16[1024,128]{1,0:T(8,128)(2,1)S(1)}) custom-call(s32[3,16]{1,0:T(4,128)} %bitcast.4, s32[16]{0:T(128)} %counts_ref.1, bf16[16,3,128,128]{3,2,1,0:T(8,128)(2,1)} %blocks_ref.3, ...), custom_call_target="tpu_custom_call" | custom-call | tf_op jit(solution)/shard_map/local_sum/pallas_call | solution.py:311
  4.7 3.9 %collective-permute-start.10 = (bf16[512,128]{1,0:T(8,128)(2,1)S(1)}, bf16[512,128]{1,0:T(8,128)(2,1)S(1)}, u32[]{:S(2)}, u32[]{:S(2)}) collective-permute-start(bf16[512,128]{1,0:T(8,128)(2,1)S(1)} %get-tuple-element.38), channel_id=1, source_target_pairs={{0,6},{1,7},{2,4},{3,5},{4,2},{5,3},{6,0},{7,1},{8,14},{9,15},{10,... | collective-permute-start | bytes 393224 | tf_op jit(solution)/shard_map/ppermute | solution.py:56
  9.6 2.7 %collective-permute-start.6 = (bf16[512,128]{1,0:T(8,128)(2,1)S(1)}, bf16[512,128]{1,0:T(8,128)(2,1)S(1)}, u32[]{:S(2)}, u32[]{:S(2)}) collective-permute-start(bf16[512,128]{1,0:T(8,128)(2,1)S(1)} %get-tuple-element.34), channel_id=1, source_target_pairs={{0,6},{1,7},{2,4},{3,5},{4,2},{5,3},{6,0},{7,1},{8,14},{9,15},{10,... | collective-permute-start | bytes 393224 | tf_op jit(solution)/shard_map/ppermute | solution.py:56
  12.5 2.4 %collective-permute-start.4 = (bf16[512,128]{1,0:T(8,128)(2,1)S(1)}, bf16[512,128]{1,0:T(8,128)(2,1)S(1)}, u32[]{:S(2)}, u32[]{:S(2)}) collective-permute-start(bf16[512,128]{1,0:T(8,128)(2,1)S(1)} %get-tuple-element.32), channel_id=1, source_target_pairs={{0,4},{1,5},{2,6},{3,7},{4,0},{5,1},{6,2},{7,3},{8,12},{9,13},{10,... | collective-permute-start | bytes 393224 | tf_op jit(solution)/shard_map/ppermute | solution.py:56
  14.9 1.8 %collective-permute-done.9.rest_1_ = bf16[512,128]{1,0:T(8,128)(2,1)S(1)} collective-permute-done((bf16[512,128]{1,0:T(8,128)(2,1)S(1)}, bf16[512,128]{1,0:T(8,128)(2,1)S(1)}, u32[]{:S(2)}, u32[]{:S(2)}) %collective-permute-start.9) | collective-permute-done | bytes 131104 | tf_op jit(solution)/shard_map/ppermute | solution.py:56
  16.7 1.0 %collective-permute-start.2 = (bf16[512,128]{1,0:T(8,128)(2,1)S(1)}, bf16[512,128]{1,0:T(8,128)(2,1)S(1)}, u32[]{:S(2)}, u32[]{:S(2)}) collective-permute-start(bf16[512,128]{1,0:T(8,128)(2,1)S(1)} %get-tuple-element.30), channel_id=1, source_target_pairs={{0,2},{1,3},{2,0},{3,1},{4,6},{5,7},{6,4},{7,5},{8,10},{9,11},{10,... | collective-permute-start | bytes 393224 | tf_op jit(solution)/shard_map/ppermute | solution.py:56
  18.0 2.7 %collective-permute-start.11 = (bf16[256,128]{1,0:T(8,128)(2,1)S(1)}, bf16[256,128]{1,0:T(8,128)(2,1)S(1)}, u32[]{:S(2)}, u32[]{:S(2)}) collective-permute-start(bf16[256,128]{1,0:T(8,128)(2,1)S(1)} %get-tuple-element.42), channel_id=1, source_target_pairs={{0,16},{1,17},{2,18},{3,19},{4,20},{5,21},{6,22},{7,23},{8,24},{9,... | collective-permute-start | bytes 196616 | tf_op jit(solution)/shard_map/ppermute | solution.py:56
  20.7 1.3 %collective-permute-start.12 = (bf16[256,128]{1,0:T(8,128)(2,1)S(1)}, bf16[256,128]{1,0:T(8,128)(2,1)S(1)}, u32[]{:S(2)}, u32[]{:S(2)}) collective-permute-start(bf16[256,128]{1,0:T(8,128)(2,1)S(1)} %get-tuple-element.43), channel_id=1, source_target_pairs={{0,24},{1,25},{2,26},{3,27},{4,28},{5,29},{6,30},{7,31},{8,16},{9,... | collective-permute-start | bytes 196616 | tf_op jit(solution)/shard_map/ppermute | solution.py:56
  22.1 1.6 %collective-permute-start.7 = (bf16[256,128]{1,0:T(8,128)(2,1)S(1)}, bf16[256,128]{1,0:T(8,128)(2,1)S(1)}, u32[]{:S(2)}, u32[]{:S(2)}) collective-permute-start(bf16[256,128]{1,0:T(8,128)(2,1)S(1)} %get-tuple-element.35), channel_id=1, source_target_pairs={{0,8},{1,9},{2,10},{3,11},{4,12},{5,13},{6,14},{7,15},{8,0},{9,1},... | collective-permute-start | bytes 196616 | tf_op jit(solution)/shard_map/ppermute | solution.py:56
  23.8 1.3 %tiles.1.tiles_ref = bf16[16,256,384]{2,1,0:T(8,128)(2,1)S(1)} custom-call(s32[3,16]{1,0:T(4,128)S(1)} %bitcast.5, s32[16]{0:T(128)S(1)} %copy-done.3, bf16[16,3,128,128]{3,2,1,0:T(8,128)(2,1)S(1)} %copy-done, f32[64,128]{1,0:T(8,128)S(1)} %bitcast.3), custom_call_target="tpu_custom_call" | custom-call | flops 1048576 | bytes 4194304 | tf_op jit(solution)/shard_map/tiles/pallas_call | solution.py:329
  25.1 2.1 %collective-permute-done.12.rest_2_ = bf16[256,128]{1,0:T(8,128)(2,1)S(1)} collective-permute-done((bf16[256,128]{1,0:T(8,128)(2,1)S(1)}, bf16[256,128]{1,0:T(8,128)(2,1)S(1)}, u32[]{:S(2)}, u32[]{:S(2)}) %collective-permute-start.12) | collective-permute-done | bytes 65568 | tf_op jit(solution)/shard_map/ppermute | solution.py:56
  27.2 0.9 %collective-permute-start.18 = (bf16[256,128]{1,0:T(8,128)(2,1)S(1)}, bf16[256,128]{1,0:T(8,128)(2,1)S(1)}, u32[]{:S(2)}, u32[]{:S(2)}) collective-permute-start(bf16[256,128]{1,0:T(8,128)(2,1)S(1)} %get-tuple-element.51), channel_id=1, source_target_pairs={{0,8},{1,9},{2,10},{3,11},{4,12},{5,13},{6,14},{7,15},{8,0},{9,1},... | collective-permute-start | bytes 196616 | tf_op jit(solution)/shard_map/ppermute | solution.py:56
  28.1 2.7 %collective-permute-start.13 = (bf16[256,128]{1,0:T(8,128)(2,1)S(1)}, bf16[256,128]{1,0:T(8,128)(2,1)S(1)}, u32[]{:S(2)}, u32[]{:S(2)}) collective-permute-start(bf16[256,128]{1,0:T(8,128)(2,1)S(1)} %get-tuple-element.51), channel_id=1, source_target_pairs={{0,16},{1,17},{2,18},{3,19},{4,20},{5,21},{6,22},{7,23},{8,24},{9,... | collective-permute-start | bytes 196616 | tf_op jit(solution)/shard_map/ppermute | solution.py:56
  30.9 0.8 %collective-permute-start.14 = (bf16[256,128]{1,0:T(8,128)(2,1)S(1)}, bf16[256,128]{1,0:T(8,128)(2,1)S(1)}, u32[]{:S(2)}, u32[]{:S(2)}) collective-permute-start(bf16[256,128]{1,0:T(8,128)(2,1)S(1)} %get-tuple-element.51), channel_id=1, source_target_pairs={{0,24},{1,25},{2,26},{3,27},{4,28},{5,29},{6,30},{7,31},{8,16},{9,... | collective-permute-start | bytes 196616 | tf_op jit(solution)/shard_map/ppermute | solution.py:56
  32.3 1.5 %collective-permute-start.19 = (bf16[512,128]{1,0:T(8,128)(2,1)S(1)}, bf16[512,128]{1,0:T(8,128)(2,1)S(1)}, u32[]{:S(2)}, u32[]{:S(2)}) collective-permute-start(bf16[512,128]{1,0:T(8,128)(2,1)S(1)} %constant_dynamic-update-slice_fusion.2.refs_4_.rest_4_), channel_id=1, source_target_pairs={{0,6},{1,7},{2,4},{3,5},{4,2},{5,3},{6,0},{7,1},{8,14},{9,15},{10,... | collective-permute-start | bytes 393224 | tf_op jit(solution)/shard_map/ppermute | solution.py:56
  33.8 1.3 %collective-permute-start.20 = (bf16[512,128]{1,0:T(8,128)(2,1)S(1)}, bf16[512,128]{1,0:T(8,128)(2,1)S(1)}, u32[]{:S(2)}, u32[]{:S(2)}) collective-permute-start(bf16[512,128]{1,0:T(8,128)(2,1)S(1)} %constant_dynamic-update-slice_fusion.2.refs_4_.rest_4_), channel_id=1, source_target_pairs={{0,4},{1,5},{2,6},{3,7},{4,0},{5,1},{6,2},{7,3},{8,12},{9,13},{10,... | collective-permute-start | bytes 393224 | tf_op jit(solution)/shard_map/ppermute | solution.py:56
  35.0 0.8 %collective-permute-start.21 = (bf16[512,128]{1,0:T(8,128)(2,1)S(1)}, bf16[512,128]{1,0:T(8,128)(2,1)S(1)}, u32[]{:S(2)}, u32[]{:S(2)}) collective-permute-start(bf16[512,128]{1,0:T(8,128)(2,1)S(1)} %constant_dynamic-update-slice_fusion.2.refs_4_.rest_4_), channel_id=1, source_target_pairs={{0,2},{1,3},{2,0},{3,1},{4,6},{5,7},{6,4},{7,5},{8,10},{9,11},{10,... | collective-permute-start | bytes 393224 | tf_op jit(solution)/shard_map/ppermute | solution.py:56
  35.9 1.1 %collective-permute-done.14 = bf16[256,128]{1,0:T(8,128)(2,1)S(1)} collective-permute-done((bf16[256,128]{1,0:T(8,128)(2,1)S(1)}, bf16[256,128]{1,0:T(8,128)(2,1)S(1)}, u32[]{:S(2)}, u32[]{:S(2)}) %collective-permute-start.14) | collective-permute-done | bytes 65568 | tf_op jit(solution)/shard_map/ppermute | solution.py:56
  36.9 1.1 %collective-permute-start.15 = (bf16[512,128]{1,0:T(8,128)(2,1)S(1)}, bf16[512,128]{1,0:T(8,128)(2,1)S(1)}, u32[]{:S(2)}, u32[]{:S(2)}) collective-permute-start(bf16[512,128]{1,0:T(8,128)(2,1)S(1)} %constant_dynamic-update-slice_fusion.refs_0_.rest_0_), channel_id=1, source_target_pairs={{0,2},{1,3},{2,0},{3,1},{4,6},{5,7},{6,4},{7,5},{8,10},{9,11},{10,... | collective-permute-start | bytes 393224 | tf_op jit(solution)/shard_map/ppermute | solution.py:56
  38.3 0.7 %collective-permute-start.16 = (bf16[512,128]{1,0:T(8,128)(2,1)S(1)}, bf16[512,128]{1,0:T(8,128)(2,1)S(1)}, u32[]{:S(2)}, u32[]{:S(2)}) collective-permute-start(bf16[512,128]{1,0:T(8,128)(2,1)S(1)} %constant_dynamic-update-slice_fusion.refs_0_.rest_0_), channel_id=1, source_target_pairs={{0,4},{1,5},{2,6},{3,7},{4,0},{5,1},{6,2},{7,3},{8,12},{9,13},{10,... | collective-permute-start | bytes 393224 | tf_op jit(solution)/shard_map/ppermute | solution.py:56
  39.6 1.8 %collective-permute-start.17 = (bf16[512,128]{1,0:T(8,128)(2,1)S(1)}, bf16[512,128]{1,0:T(8,128)(2,1)S(1)}, u32[]{:S(2)}, u32[]{:S(2)}) collective-permute-start(bf16[512,128]{1,0:T(8,128)(2,1)S(1)} %constant_dynamic-update-slice_fusion.refs_0_.rest_0_), channel_id=1, source_target_pairs={{0,6},{1,7},{2,4},{3,5},{4,2},{5,3},{6,0},{7,1},{8,14},{9,15},{10,... | collective-permute-start | bytes 393224 | tf_op jit(solution)/shard_map/ppermute | solution.py:56
  41.9 1.9 %collective-permute-done.15.refs_1_.rest_1_ = bf16[512,128]{1,0:T(8,128)(2,1)S(1)} collective-permute-done((bf16[512,128]{1,0:T(8,128)(2,1)S(1)}, bf16[512,128]{1,0:T(8,128)(2,1)S(1)}, u32[]{:S(2)}, u32[]{:S(2)}) %collective-permute-start.15) | collective-permute-done | bytes 131104 | tf_op jit(solution)/shard_map/ppermute | solution.py:56
  43.8 2.1 %collective-permute-done.16.refs_2_.rest_2_ = bf16[512,128]{1,0:T(8,128)(2,1)S(1)} collective-permute-done((bf16[512,128]{1,0:T(8,128)(2,1)S(1)}, bf16[512,128]{1,0:T(8,128)(2,1)S(1)}, u32[]{:S(2)}, u32[]{:S(2)}) %collective-permute-start.16) | collective-permute-done | bytes 131104 | tf_op jit(solution)/shard_map/ppermute | solution.py:56
  48.0 18.7 %factors.1 = (f32[256,128]{1,0:T(8,128)}, bf16[2048,128]{1,0:T(8,128)(2,1)}) custom-call(s32[3,16]{1,0:T(4,128)S(1)} %bitcast.6, bf16[16,256,384]{2,1,0:T(8,128)(2,1)S(1)} %tiles.1.tiles_ref, f32[256,128]{1,0:T(8,128)S(1)} %get-tuple-element.50.mine_ref, f32[128,128]{1,0:T(8,128)S(1)} %gram.1.early_ref, ...), custom_call_target="tpu_custom_call" | custom-call | tf_op jit(solution)/shard_map/factors/pallas_call | solution.py:408
  (59 shorter events, 7.2 us)
Async XLA Ops:
  3.5 5.1 %collective-permute-start.3 = (bf16[1024,128]{1,0:T(8,128)(2,1)S(1)}, bf16[1024,128]{1,0:T(8,128)(2,1)S(1)}, u32[]{:S(2)}, u32[]{:S(2)}) collective-permute-start(bf16[1024,128]{1,0:T(8,128)(2,1)S(1)} %get-tuple-element.31), channel_id=1, source_target_pairs={{0,1},{1,0},{2,3},{3,2},{4,5},{5,4},{6,7},{7,6},{8,9},{9,8},{10,11... | collective-permute-start | bytes 786440 | tf_op jit(solution)/shard_map/ppermute | solution.py:56
  3.6 5.7 %collective-permute-start.1 = (bf16[1024,128]{1,0:T(8,128)(2,1)S(1)}, bf16[1024,128]{1,0:T(8,128)(2,1)S(1)}, u32[]{:S(2)}, u32[]{:S(2)}) collective-permute-start(bf16[1024,128]{1,0:T(8,128)(2,1)S(1)} %get-tuple-element.29), channel_id=1, source_target_pairs={{0,1},{1,0},{2,3},{3,2},{4,5},{5,4},{6,7},{7,6},{8,9},{9,8},{10,11... | collective-permute-start | bytes 786440 | tf_op jit(solution)/shard_map/ppermute | solution.py:56
  4.0 13.9 %collective-permute-start = (bf16[1024,128]{1,0:T(8,128)(2,1)S(1)}, bf16[1024,128]{1,0:T(8,128)(2,1)S(1)}, u32[]{:S(2)}, u32[]{:S(2)}) collective-permute-start(bf16[1024,128]{1,0:T(8,128)(2,1)S(1)} %get-tuple-element.28), channel_id=1, source_target_pairs={{0,1},{1,0},{2,3},{3,2},{4,5},{5,4},{6,7},{7,6},{8,9},{9,8},{10,11... | collective-permute-start | bytes 786440 | tf_op jit(solution)/shard_map/ppermute | solution.py:56
  4.7 7.8 %collective-permute-start.10 = (bf16[512,128]{1,0:T(8,128)(2,1)S(1)}, bf16[512,128]{1,0:T(8,128)(2,1)S(1)}, u32[]{:S(2)}, u32[]{:S(2)}) collective-permute-start(bf16[512,128]{1,0:T(8,128)(2,1)S(1)} %get-tuple-element.38), channel_id=1, source_target_pairs={{0,6},{1,7},{2,4},{3,5},{4,2},{5,3},{6,0},{7,1},{8,14},{9,15},{10,... | collective-permute-start | bytes 393224 | tf_op jit(solution)/shard_map/ppermute | solution.py:56
  8.6 8.1 %collective-permute-start.9 = (bf16[512,128]{1,0:T(8,128)(2,1)S(1)}, bf16[512,128]{1,0:T(8,128)(2,1)S(1)}, u32[]{:S(2)}, u32[]{:S(2)}) collective-permute-start(bf16[512,128]{1,0:T(8,128)(2,1)S(1)} %get-tuple-element.37), channel_id=1, source_target_pairs={{0,4},{1,5},{2,6},{3,7},{4,0},{5,1},{6,2},{7,3},{8,12},{9,13},{10,... | collective-permute-start | bytes 393224 | tf_op jit(solution)/shard_map/ppermute | solution.py:56
  9.3 8.6 %collective-permute-start.8 = (bf16[512,128]{1,0:T(8,128)(2,1)S(1)}, bf16[512,128]{1,0:T(8,128)(2,1)S(1)}, u32[]{:S(2)}, u32[]{:S(2)}) collective-permute-start(bf16[512,128]{1,0:T(8,128)(2,1)S(1)} %get-tuple-element.36), channel_id=1, source_target_pairs={{0,2},{1,3},{2,0},{3,1},{4,6},{5,7},{6,4},{7,5},{8,10},{9,11},{10,... | collective-permute-start | bytes 393224 | tf_op jit(solution)/shard_map/ppermute | solution.py:56
  9.6 12.4 %collective-permute-start.6 = (bf16[512,128]{1,0:T(8,128)(2,1)S(1)}, bf16[512,128]{1,0:T(8,128)(2,1)S(1)}, u32[]{:S(2)}, u32[]{:S(2)}) collective-permute-start(bf16[512,128]{1,0:T(8,128)(2,1)S(1)} %get-tuple-element.34), channel_id=1, source_target_pairs={{0,6},{1,7},{2,4},{3,5},{4,2},{5,3},{6,0},{7,1},{8,14},{9,15},{10,... | collective-permute-start | bytes 393224 | tf_op jit(solution)/shard_map/ppermute | solution.py:56
  12.5 9.5 %collective-permute-start.4 = (bf16[512,128]{1,0:T(8,128)(2,1)S(1)}, bf16[512,128]{1,0:T(8,128)(2,1)S(1)}, u32[]{:S(2)}, u32[]{:S(2)}) collective-permute-start(bf16[512,128]{1,0:T(8,128)(2,1)S(1)} %get-tuple-element.32), channel_id=1, source_target_pairs={{0,4},{1,5},{2,6},{3,7},{4,0},{5,1},{6,2},{7,3},{8,12},{9,13},{10,... | collective-permute-start | bytes 393224 | tf_op jit(solution)/shard_map/ppermute | solution.py:56
  16.7 5.3 %collective-permute-start.2 = (bf16[512,128]{1,0:T(8,128)(2,1)S(1)}, bf16[512,128]{1,0:T(8,128)(2,1)S(1)}, u32[]{:S(2)}, u32[]{:S(2)}) collective-permute-start(bf16[512,128]{1,0:T(8,128)(2,1)S(1)} %get-tuple-element.30), channel_id=1, source_target_pairs={{0,2},{1,3},{2,0},{3,1},{4,6},{5,7},{6,4},{7,5},{8,10},{9,11},{10,... | collective-permute-start | bytes 393224 | tf_op jit(solution)/shard_map/ppermute | solution.py:56
  18.0 7.1 %collective-permute-start.11 = (bf16[256,128]{1,0:T(8,128)(2,1)S(1)}, bf16[256,128]{1,0:T(8,128)(2,1)S(1)}, u32[]{:S(2)}, u32[]{:S(2)}) collective-permute-start(bf16[256,128]{1,0:T(8,128)(2,1)S(1)} %get-tuple-element.42), channel_id=1, source_target_pairs={{0,16},{1,17},{2,18},{3,19},{4,20},{5,21},{6,22},{7,23},{8,24},{9,... | collective-permute-start | bytes 196616 | tf_op jit(solution)/shard_map/ppermute | solution.py:56
  20.7 6.5 %collective-permute-start.12 = (bf16[256,128]{1,0:T(8,128)(2,1)S(1)}, bf16[256,128]{1,0:T(8,128)(2,1)S(1)}, u32[]{:S(2)}, u32[]{:S(2)}) collective-permute-start(bf16[256,128]{1,0:T(8,128)(2,1)S(1)} %get-tuple-element.43), channel_id=1, source_target_pairs={{0,24},{1,25},{2,26},{3,27},{4,28},{5,29},{6,30},{7,31},{8,16},{9,... | collective-permute-start | bytes 196616 | tf_op jit(solution)/shard_map/ppermute | solution.py:56
  22.1 5.1 %collective-permute-start.7 = (bf16[256,128]{1,0:T(8,128)(2,1)S(1)}, bf16[256,128]{1,0:T(8,128)(2,1)S(1)}, u32[]{:S(2)}, u32[]{:S(2)}) collective-permute-start(bf16[256,128]{1,0:T(8,128)(2,1)S(1)} %get-tuple-element.35), channel_id=1, source_target_pairs={{0,8},{1,9},{2,10},{3,11},{4,12},{5,13},{6,14},{7,15},{8,0},{9,1},... | collective-permute-start | bytes 196616 | tf_op jit(solution)/shard_map/ppermute | solution.py:56
  27.2 5.0 %collective-permute-start.18 = (bf16[256,128]{1,0:T(8,128)(2,1)S(1)}, bf16[256,128]{1,0:T(8,128)(2,1)S(1)}, u32[]{:S(2)}, u32[]{:S(2)}) collective-permute-start(bf16[256,128]{1,0:T(8,128)(2,1)S(1)} %get-tuple-element.51), channel_id=1, source_target_pairs={{0,8},{1,9},{2,10},{3,11},{4,12},{5,13},{6,14},{7,15},{8,0},{9,1},... | collective-permute-start | bytes 196616 | tf_op jit(solution)/shard_map/ppermute | solution.py:56
  28.1 7.7 %collective-permute-start.13 = (bf16[256,128]{1,0:T(8,128)(2,1)S(1)}, bf16[256,128]{1,0:T(8,128)(2,1)S(1)}, u32[]{:S(2)}, u32[]{:S(2)}) collective-permute-start(bf16[256,128]{1,0:T(8,128)(2,1)S(1)} %get-tuple-element.51), channel_id=1, source_target_pairs={{0,16},{1,17},{2,18},{3,19},{4,20},{5,21},{6,22},{7,23},{8,24},{9,... | collective-permute-start | bytes 196616 | tf_op jit(solution)/shard_map/ppermute | solution.py:56
  30.9 6.1 %collective-permute-start.14 = (bf16[256,128]{1,0:T(8,128)(2,1)S(1)}, bf16[256,128]{1,0:T(8,128)(2,1)S(1)}, u32[]{:S(2)}, u32[]{:S(2)}) collective-permute-start(bf16[256,128]{1,0:T(8,128)(2,1)S(1)} %get-tuple-element.51), channel_id=1, source_target_pairs={{0,24},{1,25},{2,26},{3,27},{4,28},{5,29},{6,30},{7,31},{8,16},{9,... | collective-permute-start | bytes 196616 | tf_op jit(solution)/shard_map/ppermute | solution.py:56
  32.3 6.0 %collective-permute-start.19 = (bf16[512,128]{1,0:T(8,128)(2,1)S(1)}, bf16[512,128]{1,0:T(8,128)(2,1)S(1)}, u32[]{:S(2)}, u32[]{:S(2)}) collective-permute-start(bf16[512,128]{1,0:T(8,128)(2,1)S(1)} %constant_dynamic-update-slice_fusion.2.refs_4_.rest_4_), channel_id=1, source_target_pairs={{0,6},{1,7},{2,4},{3,5},{4,2},{5,3},{6,0},{7,1},{8,14},{9,15},{10,... | collective-permute-start | bytes 393224 | tf_op jit(solution)/shard_map/ppermute | solution.py:56
  33.8 5.8 %collective-permute-start.20 = (bf16[512,128]{1,0:T(8,128)(2,1)S(1)}, bf16[512,128]{1,0:T(8,128)(2,1)S(1)}, u32[]{:S(2)}, u32[]{:S(2)}) collective-permute-start(bf16[512,128]{1,0:T(8,128)(2,1)S(1)} %constant_dynamic-update-slice_fusion.2.refs_4_.rest_4_), channel_id=1, source_target_pairs={{0,4},{1,5},{2,6},{3,7},{4,0},{5,1},{6,2},{7,3},{8,12},{9,13},{10,... | collective-permute-start | bytes 393224 | tf_op jit(solution)/shard_map/ppermute | solution.py:56
  35.0 6.4 %collective-permute-start.21 = (bf16[512,128]{1,0:T(8,128)(2,1)S(1)}, bf16[512,128]{1,0:T(8,128)(2,1)S(1)}, u32[]{:S(2)}, u32[]{:S(2)}) collective-permute-start(bf16[512,128]{1,0:T(8,128)(2,1)S(1)} %constant_dynamic-update-slice_fusion.2.refs_4_.rest_4_), channel_id=1, source_target_pairs={{0,2},{1,3},{2,0},{3,1},{4,6},{5,7},{6,4},{7,5},{8,10},{9,11},{10,... | collective-permute-start | bytes 393224 | tf_op jit(solution)/shard_map/ppermute | solution.py:56
  35.8 5.6 %collective-permute-start.23 = (bf16[512,128]{1,0:T(8,128)(2,1)S(1)}, bf16[512,128]{1,0:T(8,128)(2,1)S(1)}, u32[]{:S(2)}, u32[]{:S(2)}) collective-permute-start(bf16[512,128]{1,0:T(8,128)(2,1)S(1)} %constant_dynamic-update-slice_fusion.2.refs_4_.rest_4_), channel_id=1, source_target_pairs={{0,1},{1,0},{2,3},{3,2},{4,5},{5,4},{6,7},{7,6},{8,9},{9,8},{10,11... | collective-permute-start | bytes 393224 | tf_op jit(solution)/shard_map/ppermute | solution.py:56
  36.9 6.9 %collective-permute-start.15 = (bf16[512,128]{1,0:T(8,128)(2,1)S(1)}, bf16[512,128]{1,0:T(8,128)(2,1)S(1)}, u32[]{:S(2)}, u32[]{:S(2)}) collective-permute-start(bf16[512,128]{1,0:T(8,128)(2,1)S(1)} %constant_dynamic-update-slice_fusion.refs_0_.rest_0_), channel_id=1, source_target_pairs={{0,2},{1,3},{2,0},{3,1},{4,6},{5,7},{6,4},{7,5},{8,10},{9,11},{10,... | collective-permute-start | bytes 393224 | tf_op jit(solution)/shard_map/ppermute | solution.py:56
  38.3 7.7 %collective-permute-start.16 = (bf16[512,128]{1,0:T(8,128)(2,1)S(1)}, bf16[512,128]{1,0:T(8,128)(2,1)S(1)}, u32[]{:S(2)}, u32[]{:S(2)}) collective-permute-start(bf16[512,128]{1,0:T(8,128)(2,1)S(1)} %constant_dynamic-update-slice_fusion.refs_0_.rest_0_), channel_id=1, source_target_pairs={{0,4},{1,5},{2,6},{3,7},{4,0},{5,1},{6,2},{7,3},{8,12},{9,13},{10,... | collective-permute-start | bytes 393224 | tf_op jit(solution)/shard_map/ppermute | solution.py:56
  39.6 6.4 %collective-permute-start.17 = (bf16[512,128]{1,0:T(8,128)(2,1)S(1)}, bf16[512,128]{1,0:T(8,128)(2,1)S(1)}, u32[]{:S(2)}, u32[]{:S(2)}) collective-permute-start(bf16[512,128]{1,0:T(8,128)(2,1)S(1)} %constant_dynamic-update-slice_fusion.refs_0_.rest_0_), channel_id=1, source_target_pairs={{0,6},{1,7},{2,4},{3,5},{4,2},{5,3},{6,0},{7,1},{8,14},{9,15},{10,... | collective-permute-start | bytes 393224 | tf_op jit(solution)/shard_map/ppermute | solution.py:56
  41.4 5.1 %collective-permute-start.22 = (bf16[512,128]{1,0:T(8,128)(2,1)S(1)}, bf16[512,128]{1,0:T(8,128)(2,1)S(1)}, u32[]{:S(2)}, u32[]{:S(2)}) collective-permute-start(bf16[512,128]{1,0:T(8,128)(2,1)S(1)} %constant_dynamic-update-slice_fusion.refs_0_.rest_0_), channel_id=1, source_target_pairs={{0,1},{1,0},{2,3},{3,2},{4,5},{5,4},{6,7},{7,6},{8,9},{9,8},{10,11... | collective-permute-start | bytes 393224 | tf_op jit(solution)/shard_map/ppermute | solution.py:56
  41.4 5.1 %collective-permute-start.24 = (bf16[512,128]{1,0:T(8,128)(2,1)S(1)}, bf16[512,128]{1,0:T(8,128)(2,1)S(1)}, u32[]{:S(2)}, u32[]{:S(2)}) collective-permute-start(bf16[512,128]{1,0:T(8,128)(2,1)S(1)} %collective-permute-done.19.refs_5_.rest_5_), channel_id=1, source_target_pairs={{0,1},{1,0},{2,3},{3,2},{4,5},{5,4},{6,7},{7,6},{8,9},{9,8},{10,11... | collective-permute-start | bytes 393224 | tf_op jit(solution)/shard_map/ppermute | solution.py:56
  (10 other events, 37.6 us)

commit v18 on v16

--- a/solution.py
+++ b/solution.py
@@ -218,7 +218,7 @@
     lax.fori_loop(0, size, step, 0)
 
 
-def newton(gram, inverse_ref):
+def newton(gram, inverse_ref, fill):
     size = gram.shape[0]
     line = lax.broadcasted_iota(jnp.int32, (size, size), 0)
     lane = lax.broadcasted_iota(jnp.int32, (size, size), 1)
@@ -232,8 +232,11 @@
     factor = eye - take * beyond
     for product, product_t in ((dot1, dot_t1), (dot3, dot_t3)):
         left = factor - eye + product(factor, beyond)
+        fill()
         residual = factor.T - eye + product_t(left, factor)
+        fill()
         factor = factor - product(take * residual, factor)
+        fill()
     inverse_ref[...] = factor * across
     return jnp.sum(residual * residual)
 
@@ -266,15 +269,22 @@
         if i in late:
             gram += lax.dot_general(part, part, (((0,), (0,)), ((), ())), preferred_element_type=F32)
     gram = gram * (1.0 / features)
-    residual = newton(gram, inverse_ref)
-    for d in range(documents):
-        picked = []
-        for s in range(slots):
-            for p in range(plan.pieces):
-                at = pl.ds(plan.start(me, rows_ref[s, d], p), plan.piece)
-                picked.append(all_ref[at, :])
-        terms = dot(tiles_ref[d], jnp.concatenate(picked, axis=0))
-        product_ref[d * block : (d + 1) * block, :] = terms[:block] + terms[block:]
+    left = list(range(documents))
+    share = -(-documents // 6)
+
+    def fill():
+        for d in left[:share]:
+            picked = []
+            for s in range(slots):
+                for p in range(plan.pieces):
+                    at = pl.ds(plan.start(me, rows_ref[s, d], p), plan.piece)
+                    picked.append(all_ref[at, :])
+            terms = dot(tiles_ref[d], jnp.concatenate(picked, axis=0))
+            product_ref[d * block : (d + 1) * block, :] = terms[:block] + terms[block:]
+        del left[:share]
+
+    residual = newton(gram, inverse_ref, fill)
+    assert not left
 
     @pl.when(jnp.logical_not(residual < 1e-3))
     def _():

time: 66.3 us -> 65.8 us (level)
  no operation moved by 1% of the time
where the time goes in v18:
time: 65.8 us; the launch traced here: 65.6 us
  starting transfers between devices  30 us (46%)
  Pallas kernels  22.9 us (35%)
  waiting for transfers between devices  11.9 us (18%)
  between operations  0.77 us (1%)
    ppermute x30, starting transfers between devices, swap(): return lax.ppermute(value, AXES, [(d, d ^ mask) for d in range(self.count)])  30 us
    pallas_call x1, Pallas kernels, body(): pl.pallas_call(functools.partial(last_kernel, plan, features, late), out_...  18.2 us
    ppermute x30, waiting for transfers between devices, swap(): return lax.ppermute(value, AXES, [(d, d ^ mask) for d in range(self.count)])  11.9 us
    pallas_call x1, Pallas kernels, body(): pl.pallas_call(functools.partial(sum_kernel, plan), out_shape=(pltpu.VMEM...  2.32 us
  transfers between devices with their start and end apart: 30, of which 13 were waited for; matrix products, arithmetic and copies ran while one was open for 0% of the time, Pallas kernels for 4%

profile of v18, /device:TPU:0, one launch (start us, length us, event | category | flops | bytes accessed | tf_op | source)
XLA Modules:
  0.0 65.6 jit_solution(1241195049626475145)
XLA Ops:
  0.6 2.3 %local_sum.1 = (f32[8192,128]{1,0:T(8,128)S(1)}, bf16[1024,128]{1,0:T(8,128)(2,1)S(1)}, bf16[1024,128]{1,0:T(8,128)(2,1)S(1)}, bf16[1024,128]{1,0:T(8,128)(2,1)S(1)}, bf16[1024,128]{1,0:T(8,128)(2,1)S(1)}) custom-call(s32[3,16]{1,0:T(4,128)} %bitcast.4, s32[16]{0:T(128)} %counts_ref.1, bf16[16,3,128,128]{3,2,1,0:T(8,128)(2,1)} %blocks_ref.3, ...), custom_call_target="tpu_custom_call" | custom-call | tf_op jit(solution)/shard_map/local_sum/pallas_call | solution.py:321
  5.1 3.9 %collective-permute-start.10 = (bf16[512,128]{1,0:T(8,128)(2,1)S(1)}, bf16[512,128]{1,0:T(8,128)(2,1)S(1)}, u32[]{:S(2)}, u32[]{:S(2)}) collective-permute-start(bf16[512,128]{1,0:T(8,128)(2,1)S(1)} %get-tuple-element.42), channel_id=1, source_target_pairs={{0,6},{1,7},{2,4},{3,5},{4,2},{5,3},{6,0},{7,1},{8,14},{9,15},{10,... | collective-permute-start | bytes 393224 | tf_op jit(solution)/shard_map/ppermute | solution.py:56
  10.0 2.7 %collective-permute-start.6 = (bf16[512,128]{1,0:T(8,128)(2,1)S(1)}, bf16[512,128]{1,0:T(8,128)(2,1)S(1)}, u32[]{:S(2)}, u32[]{:S(2)}) collective-permute-start(bf16[512,128]{1,0:T(8,128)(2,1)S(1)} %get-tuple-element.38), channel_id=1, source_target_pairs={{0,6},{1,7},{2,4},{3,5},{4,2},{5,3},{6,0},{7,1},{8,14},{9,15},{10,... | collective-permute-start | bytes 393224 | tf_op jit(solution)/shard_map/ppermute | solution.py:56
  13.2 2.0 %collective-permute-start.3 = (bf16[512,128]{1,0:T(8,128)(2,1)S(1)}, bf16[512,128]{1,0:T(8,128)(2,1)S(1)}, u32[]{:S(2)}, u32[]{:S(2)}) collective-permute-start(bf16[512,128]{1,0:T(8,128)(2,1)S(1)} %get-tuple-element.34), channel_id=1, source_target_pairs={{0,2},{1,3},{2,0},{3,1},{4,6},{5,7},{6,4},{7,5},{8,10},{9,11},{10,... | collective-permute-start | bytes 393224 | tf_op jit(solution)/shard_map/ppermute | solution.py:56
  15.3 1.7 %collective-permute-done.9.rest_1_ = bf16[512,128]{1,0:T(8,128)(2,1)S(1)} collective-permute-done((bf16[512,128]{1,0:T(8,128)(2,1)S(1)}, bf16[512,128]{1,0:T(8,128)(2,1)S(1)}, u32[]{:S(2)}, u32[]{:S(2)}) %collective-permute-start.9) | collective-permute-done | bytes 131104 | tf_op jit(solution)/shard_map/ppermute | solution.py:56
  17.2 2.8 %collective-permute-start.11 = (bf16[256,128]{1,0:T(8,128)(2,1)S(1)}, bf16[256,128]{1,0:T(8,128)(2,1)S(1)}, u32[]{:S(2)}, u32[]{:S(2)}) collective-permute-start(bf16[256,128]{1,0:T(8,128)(2,1)S(1)} %get-tuple-element.46), channel_id=1, source_target_pairs={{0,16},{1,17},{2,18},{3,19},{4,20},{5,21},{6,22},{7,23},{8,24},{9,... | collective-permute-start | bytes 196616 | tf_op jit(solution)/shard_map/ppermute | solution.py:56
  20.0 1.3 %collective-permute-start.12 = (bf16[256,128]{1,0:T(8,128)(2,1)S(1)}, bf16[256,128]{1,0:T(8,128)(2,1)S(1)}, u32[]{:S(2)}, u32[]{:S(2)}) collective-permute-start(bf16[256,128]{1,0:T(8,128)(2,1)S(1)} %get-tuple-element.47), channel_id=1, source_target_pairs={{0,24},{1,25},{2,26},{3,27},{4,28},{5,29},{6,30},{7,31},{8,16},{9,... | collective-permute-start | bytes 196616 | tf_op jit(solution)/shard_map/ppermute | solution.py:56
  21.6 1.6 %collective-permute-start.7 = (bf16[256,128]{1,0:T(8,128)(2,1)S(1)}, bf16[256,128]{1,0:T(8,128)(2,1)S(1)}, u32[]{:S(2)}, u32[]{:S(2)}) collective-permute-start(bf16[256,128]{1,0:T(8,128)(2,1)S(1)} %get-tuple-element.39), channel_id=1, source_target_pairs={{0,8},{1,9},{2,10},{3,11},{4,12},{5,13},{6,14},{7,15},{8,0},{9,1},... | collective-permute-start | bytes 196616 | tf_op jit(solution)/shard_map/ppermute | solution.py:56
  23.2 1.3 %tiles.1.tiles_ref = bf16[16,256,384]{2,1,0:T(8,128)(2,1)S(1)} custom-call(s32[3,16]{1,0:T(4,128)S(1)} %bitcast.5, s32[16]{0:T(128)S(1)} %copy-done.3, bf16[16,3,128,128]{3,2,1,0:T(8,128)(2,1)S(1)} %copy-done, f32[64,128]{1,0:T(8,128)S(1)} %bitcast.3), custom_call_target="tpu_custom_call" | custom-call | flops 1048576 | bytes 4194304 | tf_op jit(solution)/shard_map/tiles/pallas_call | solution.py:339
  24.7 1.5 %collective-permute-done.12.rest_2_ = bf16[256,128]{1,0:T(8,128)(2,1)S(1)} collective-permute-done((bf16[256,128]{1,0:T(8,128)(2,1)S(1)}, bf16[256,128]{1,0:T(8,128)(2,1)S(1)}, u32[]{:S(2)}, u32[]{:S(2)}) %collective-permute-start.12) | collective-permute-done | bytes 65568 | tf_op jit(solution)/shard_map/ppermute | solution.py:56
  26.8 0.8 %collective-permute-start.18 = (bf16[256,128]{1,0:T(8,128)(2,1)S(1)}, bf16[256,128]{1,0:T(8,128)(2,1)S(1)}, u32[]{:S(2)}, u32[]{:S(2)}) collective-permute-start(bf16[256,128]{1,0:T(8,128)(2,1)S(1)} %get-tuple-element.55), channel_id=1, source_target_pairs={{0,8},{1,9},{2,10},{3,11},{4,12},{5,13},{6,14},{7,15},{8,0},{9,1},... | collective-permute-start | bytes 196616 | tf_op jit(solution)/shard_map/ppermute | solution.py:56
  27.6 2.9 %collective-permute-start.13 = (bf16[256,128]{1,0:T(8,128)(2,1)S(1)}, bf16[256,128]{1,0:T(8,128)(2,1)S(1)}, u32[]{:S(2)}, u32[]{:S(2)}) collective-permute-start(bf16[256,128]{1,0:T(8,128)(2,1)S(1)} %get-tuple-element.55), channel_id=1, source_target_pairs={{0,16},{1,17},{2,18},{3,19},{4,20},{5,21},{6,22},{7,23},{8,24},{9,... | collective-permute-start | bytes 196616 | tf_op jit(solution)/shard_map/ppermute | solution.py:56
  30.5 0.8 %collective-permute-start.14 = (bf16[256,128]{1,0:T(8,128)(2,1)S(1)}, bf16[256,128]{1,0:T(8,128)(2,1)S(1)}, u32[]{:S(2)}, u32[]{:S(2)}) collective-permute-start(bf16[256,128]{1,0:T(8,128)(2,1)S(1)} %get-tuple-element.55), channel_id=1, source_target_pairs={{0,24},{1,25},{2,26},{3,27},{4,28},{5,29},{6,30},{7,31},{8,16},{9,... | collective-permute-start | bytes 196616 | tf_op jit(solution)/shard_map/ppermute | solution.py:56
  31.8 1.2 %collective-permute-start.19 = (bf16[512,128]{1,0:T(8,128)(2,1)S(1)}, bf16[512,128]{1,0:T(8,128)(2,1)S(1)}, u32[]{:S(2)}, u32[]{:S(2)}) collective-permute-start(bf16[512,128]{1,0:T(8,128)(2,1)S(1)} %constant_dynamic-update-slice_fusion.2.refs_4_.rest_4_), channel_id=1, source_target_pairs={{0,6},{1,7},{2,4},{3,5},{4,2},{5,3},{6,0},{7,1},{8,14},{9,15},{10,... | collective-permute-start | bytes 393224 | tf_op jit(solution)/shard_map/ppermute | solution.py:56
  33.0 1.3 %collective-permute-start.20 = (bf16[512,128]{1,0:T(8,128)(2,1)S(1)}, bf16[512,128]{1,0:T(8,128)(2,1)S(1)}, u32[]{:S(2)}, u32[]{:S(2)}) collective-permute-start(bf16[512,128]{1,0:T(8,128)(2,1)S(1)} %constant_dynamic-update-slice_fusion.2.refs_4_.rest_4_), channel_id=1, source_target_pairs={{0,4},{1,5},{2,6},{3,7},{4,0},{5,1},{6,2},{7,3},{8,12},{9,13},{10,... | collective-permute-start | bytes 393224 | tf_op jit(solution)/shard_map/ppermute | solution.py:56
  34.3 1.1 %collective-permute-start.21 = (bf16[512,128]{1,0:T(8,128)(2,1)S(1)}, bf16[512,128]{1,0:T(8,128)(2,1)S(1)}, u32[]{:S(2)}, u32[]{:S(2)}) collective-permute-start(bf16[512,128]{1,0:T(8,128)(2,1)S(1)} %constant_dynamic-update-slice_fusion.2.refs_4_.rest_4_), channel_id=1, source_target_pairs={{0,2},{1,3},{2,0},{3,1},{4,6},{5,7},{6,4},{7,5},{8,10},{9,11},{10,... | collective-permute-start | bytes 393224 | tf_op jit(solution)/shard_map/ppermute | solution.py:56
  35.4 1.1 %collective-permute-done.14 = bf16[256,128]{1,0:T(8,128)(2,1)S(1)} collective-permute-done((bf16[256,128]{1,0:T(8,128)(2,1)S(1)}, bf16[256,128]{1,0:T(8,128)(2,1)S(1)}, u32[]{:S(2)}, u32[]{:S(2)}) %collective-permute-start.14) | collective-permute-done | bytes 65568 | tf_op jit(solution)/shard_map/ppermute | solution.py:56
  36.5 1.3 %collective-permute-start.15 = (bf16[512,128]{1,0:T(8,128)(2,1)S(1)}, bf16[512,128]{1,0:T(8,128)(2,1)S(1)}, u32[]{:S(2)}, u32[]{:S(2)}) collective-permute-start(bf16[512,128]{1,0:T(8,128)(2,1)S(1)} %constant_dynamic-update-slice_fusion.refs_0_.rest_0_), channel_id=1, source_target_pairs={{0,2},{1,3},{2,0},{3,1},{4,6},{5,7},{6,4},{7,5},{8,10},{9,11},{10,... | collective-permute-start | bytes 393224 | tf_op jit(solution)/shard_map/ppermute | solution.py:56
  37.9 1.1 %collective-permute-start.16 = (bf16[512,128]{1,0:T(8,128)(2,1)S(1)}, bf16[512,128]{1,0:T(8,128)(2,1)S(1)}, u32[]{:S(2)}, u32[]{:S(2)}) collective-permute-start(bf16[512,128]{1,0:T(8,128)(2,1)S(1)} %constant_dynamic-update-slice_fusion.refs_0_.rest_0_), channel_id=1, source_target_pairs={{0,4},{1,5},{2,6},{3,7},{4,0},{5,1},{6,2},{7,3},{8,12},{9,13},{10,... | collective-permute-start | bytes 393224 | tf_op jit(solution)/shard_map/ppermute | solution.py:56
  39.2 1.2 %collective-permute-start.17 = (bf16[512,128]{1,0:T(8,128)(2,1)S(1)}, bf16[512,128]{1,0:T(8,128)(2,1)S(1)}, u32[]{:S(2)}, u32[]{:S(2)}) collective-permute-start(bf16[512,128]{1,0:T(8,128)(2,1)S(1)} %constant_dynamic-update-slice_fusion.refs_0_.rest_0_), channel_id=1, source_target_pairs={{0,6},{1,7},{2,4},{3,5},{4,2},{5,3},{6,0},{7,1},{8,14},{9,15},{10,... | collective-permute-start | bytes 393224 | tf_op jit(solution)/shard_map/ppermute | solution.py:56
  40.9 2.1 %collective-permute-done.15.refs_1_.rest_1_ = bf16[512,128]{1,0:T(8,128)(2,1)S(1)} collective-permute-done((bf16[512,128]{1,0:T(8,128)(2,1)S(1)}, bf16[512,128]{1,0:T(8,128)(2,1)S(1)}, u32[]{:S(2)}, u32[]{:S(2)}) %collective-permute-start.15) | collective-permute-done | bytes 131104 | tf_op jit(solution)/shard_map/ppermute | solution.py:56
  43.0 2.3 %collective-permute-done.16.refs_2_.rest_2_ = bf16[512,128]{1,0:T(8,128)(2,1)S(1)} collective-permute-done((bf16[512,128]{1,0:T(8,128)(2,1)S(1)}, bf16[512,128]{1,0:T(8,128)(2,1)S(1)}, u32[]{:S(2)}, u32[]{:S(2)}) %collective-permute-start.16) | collective-permute-done | bytes 131104 | tf_op jit(solution)/shard_map/ppermute | solution.py:56
  46.7 0.7 %gram.1.early_ref = f32[128,128]{1,0:T(8,128)S(1)} custom-call(bf16[512,128]{1,0:T(8,128)(2,1)S(1)} %constant_dynamic-update-slice_fusion.refs_0_.rest_0_, bf16[512,128]{1,0:T(8,128)(2,1)S(1)} %collective-permute-done.15.refs_1_.rest_1_, bf16[512,128]{1,0:T(8,128)(2,1)S(1)} %collective-permute-done.16.refs_2_.rest_2_, ...), custom_call_target="tpu_custom_call" | custom-call | flops 268435456 | bytes 4194304 | tf_op jit(solution)/shard_map/gram/pallas_call | solution.py:410
  47.4 18.2 %factors.1 = (f32[256,128]{1,0:T(8,128)}, bf16[2048,128]{1,0:T(8,128)(2,1)}) custom-call(s32[3,16]{1,0:T(4,128)S(1)} %bitcast.6, bf16[16,256,384]{2,1,0:T(8,128)(2,1)S(1)} %tiles.1.tiles_ref, f32[256,128]{1,0:T(8,128)S(1)} %get-tuple-element.54.mine_ref, f32[128,128]{1,0:T(8,128)S(1)} %gram.1.early_ref, ...), custom_call_target="tpu_custom_call" | custom-call | tf_op jit(solution)/shard_map/factors/pallas_call | solution.py:419
  (59 shorter events, 7.7 us)
Async XLA Ops:
  3.6 5.4 %collective-permute-start.4 = (bf16[1024,128]{1,0:T(8,128)(2,1)S(1)}, bf16[1024,128]{1,0:T(8,128)(2,1)S(1)}, u32[]{:S(2)}, u32[]{:S(2)}) collective-permute-start(bf16[1024,128]{1,0:T(8,128)(2,1)S(1)} %get-tuple-element.35), channel_id=1, source_target_pairs={{0,1},{1,0},{2,3},{3,2},{4,5},{5,4},{6,7},{7,6},{8,9},{9,8},{10,11... | collective-permute-start | bytes 786440 | tf_op jit(solution)/shard_map/ppermute | solution.py:56
  4.0 5.6 %collective-permute-start.2 = (bf16[1024,128]{1,0:T(8,128)(2,1)S(1)}, bf16[1024,128]{1,0:T(8,128)(2,1)S(1)}, u32[]{:S(2)}, u32[]{:S(2)}) collective-permute-start(bf16[1024,128]{1,0:T(8,128)(2,1)S(1)} %get-tuple-element.33), channel_id=1, source_target_pairs={{0,1},{1,0},{2,3},{3,2},{4,5},{5,4},{6,7},{7,6},{8,9},{9,8},{10,11... | collective-permute-start | bytes 786440 | tf_op jit(solution)/shard_map/ppermute | solution.py:56
  5.1 8.1 %collective-permute-start.10 = (bf16[512,128]{1,0:T(8,128)(2,1)S(1)}, bf16[512,128]{1,0:T(8,128)(2,1)S(1)}, u32[]{:S(2)}, u32[]{:S(2)}) collective-permute-start(bf16[512,128]{1,0:T(8,128)(2,1)S(1)} %get-tuple-element.42), channel_id=1, source_target_pairs={{0,6},{1,7},{2,4},{3,5},{4,2},{5,3},{6,0},{7,1},{8,14},{9,15},{10,... | collective-permute-start | bytes 393224 | tf_op jit(solution)/shard_map/ppermute | solution.py:56
  9.0 8.0 %collective-permute-start.9 = (bf16[512,128]{1,0:T(8,128)(2,1)S(1)}, bf16[512,128]{1,0:T(8,128)(2,1)S(1)}, u32[]{:S(2)}, u32[]{:S(2)}) collective-permute-start(bf16[512,128]{1,0:T(8,128)(2,1)S(1)} %get-tuple-element.41), channel_id=1, source_target_pairs={{0,4},{1,5},{2,6},{3,7},{4,0},{5,1},{6,2},{7,3},{8,12},{9,13},{10,... | collective-permute-start | bytes 393224 | tf_op jit(solution)/shard_map/ppermute | solution.py:56
  9.6 7.4 %collective-permute-start.8 = (bf16[512,128]{1,0:T(8,128)(2,1)S(1)}, bf16[512,128]{1,0:T(8,128)(2,1)S(1)}, u32[]{:S(2)}, u32[]{:S(2)}) collective-permute-start(bf16[512,128]{1,0:T(8,128)(2,1)S(1)} %get-tuple-element.40), channel_id=1, source_target_pairs={{0,2},{1,3},{2,0},{3,1},{4,6},{5,7},{6,4},{7,5},{8,10},{9,11},{10,... | collective-permute-start | bytes 393224 | tf_op jit(solution)/shard_map/ppermute | solution.py:56
  10.0 11.3 %collective-permute-start.6 = (bf16[512,128]{1,0:T(8,128)(2,1)S(1)}, bf16[512,128]{1,0:T(8,128)(2,1)S(1)}, u32[]{:S(2)}, u32[]{:S(2)}) collective-permute-start(bf16[512,128]{1,0:T(8,128)(2,1)S(1)} %get-tuple-element.38), channel_id=1, source_target_pairs={{0,6},{1,7},{2,4},{3,5},{4,2},{5,3},{6,0},{7,1},{8,14},{9,15},{10,... | collective-permute-start | bytes 393224 | tf_op jit(solution)/shard_map/ppermute | solution.py:56
  12.7 8.6 %collective-permute-start.5 = (bf16[512,128]{1,0:T(8,128)(2,1)S(1)}, bf16[512,128]{1,0:T(8,128)(2,1)S(1)}, u32[]{:S(2)}, u32[]{:S(2)}) collective-permute-start(bf16[512,128]{1,0:T(8,128)(2,1)S(1)} %get-tuple-element.36), channel_id=1, source_target_pairs={{0,4},{1,5},{2,6},{3,7},{4,0},{5,1},{6,2},{7,3},{8,12},{9,13},{10,... | collective-permute-start | bytes 393224 | tf_op jit(solution)/shard_map/ppermute | solution.py:56
  13.2 8.3 %collective-permute-start.3 = (bf16[512,128]{1,0:T(8,128)(2,1)S(1)}, bf16[512,128]{1,0:T(8,128)(2,1)S(1)}, u32[]{:S(2)}, u32[]{:S(2)}) collective-permute-start(bf16[512,128]{1,0:T(8,128)(2,1)S(1)} %get-tuple-element.34), channel_id=1, source_target_pairs={{0,2},{1,3},{2,0},{3,1},{4,6},{5,7},{6,4},{7,5},{8,10},{9,11},{10,... | collective-permute-start | bytes 393224 | tf_op jit(solution)/shard_map/ppermute | solution.py:56
  17.2 7.5 %collective-permute-start.11 = (bf16[256,128]{1,0:T(8,128)(2,1)S(1)}, bf16[256,128]{1,0:T(8,128)(2,1)S(1)}, u32[]{:S(2)}, u32[]{:S(2)}) collective-permute-start(bf16[256,128]{1,0:T(8,128)(2,1)S(1)} %get-tuple-element.46), channel_id=1, source_target_pairs={{0,16},{1,17},{2,18},{3,19},{4,20},{5,21},{6,22},{7,23},{8,24},{9,... | collective-permute-start | bytes 196616 | tf_op jit(solution)/shard_map/ppermute | solution.py:56
  20.0 6.2 %collective-permute-start.12 = (bf16[256,128]{1,0:T(8,128)(2,1)S(1)}, bf16[256,128]{1,0:T(8,128)(2,1)S(1)}, u32[]{:S(2)}, u32[]{:S(2)}) collective-permute-start(bf16[256,128]{1,0:T(8,128)(2,1)S(1)} %get-tuple-element.47), channel_id=1, source_target_pairs={{0,24},{1,25},{2,26},{3,27},{4,28},{5,29},{6,30},{7,31},{8,16},{9,... | collective-permute-start | bytes 196616 | tf_op jit(solution)/shard_map/ppermute | solution.py:56
  21.6 5.2 %collective-permute-start.7 = (bf16[256,128]{1,0:T(8,128)(2,1)S(1)}, bf16[256,128]{1,0:T(8,128)(2,1)S(1)}, u32[]{:S(2)}, u32[]{:S(2)}) collective-permute-start(bf16[256,128]{1,0:T(8,128)(2,1)S(1)} %get-tuple-element.39), channel_id=1, source_target_pairs={{0,8},{1,9},{2,10},{3,11},{4,12},{5,13},{6,14},{7,15},{8,0},{9,1},... | collective-permute-start | bytes 196616 | tf_op jit(solution)/shard_map/ppermute | solution.py:56
  26.8 5.0 %collective-permute-start.18 = (bf16[256,128]{1,0:T(8,128)(2,1)S(1)}, bf16[256,128]{1,0:T(8,128)(2,1)S(1)}, u32[]{:S(2)}, u32[]{:S(2)}) collective-permute-start(bf16[256,128]{1,0:T(8,128)(2,1)S(1)} %get-tuple-element.55), channel_id=1, source_target_pairs={{0,8},{1,9},{2,10},{3,11},{4,12},{5,13},{6,14},{7,15},{8,0},{9,1},... | collective-permute-start | bytes 196616 | tf_op jit(solution)/shard_map/ppermute | solution.py:56
  27.6 7.8 %collective-permute-start.13 = (bf16[256,128]{1,0:T(8,128)(2,1)S(1)}, bf16[256,128]{1,0:T(8,128)(2,1)S(1)}, u32[]{:S(2)}, u32[]{:S(2)}) collective-permute-start(bf16[256,128]{1,0:T(8,128)(2,1)S(1)} %get-tuple-element.55), channel_id=1, source_target_pairs={{0,16},{1,17},{2,18},{3,19},{4,20},{5,21},{6,22},{7,23},{8,24},{9,... | collective-permute-start | bytes 196616 | tf_op jit(solution)/shard_map/ppermute | solution.py:56
  30.5 6.1 %collective-permute-start.14 = (bf16[256,128]{1,0:T(8,128)(2,1)S(1)}, bf16[256,128]{1,0:T(8,128)(2,1)S(1)}, u32[]{:S(2)}, u32[]{:S(2)}) collective-permute-start(bf16[256,128]{1,0:T(8,128)(2,1)S(1)} %get-tuple-element.55), channel_id=1, source_target_pairs={{0,24},{1,25},{2,26},{3,27},{4,28},{5,29},{6,30},{7,31},{8,16},{9,... | collective-permute-start | bytes 196616 | tf_op jit(solution)/shard_map/ppermute | solution.py:56
  31.8 6.0 %collective-permute-start.19 = (bf16[512,128]{1,0:T(8,128)(2,1)S(1)}, bf16[512,128]{1,0:T(8,128)(2,1)S(1)}, u32[]{:S(2)}, u32[]{:S(2)}) collective-permute-start(bf16[512,128]{1,0:T(8,128)(2,1)S(1)} %constant_dynamic-update-slice_fusion.2.refs_4_.rest_4_), channel_id=1, source_target_pairs={{0,6},{1,7},{2,4},{3,5},{4,2},{5,3},{6,0},{7,1},{8,14},{9,15},{10,... | collective-permute-start | bytes 393224 | tf_op jit(solution)/shard_map/ppermute | solution.py:56
  33.0 6.2 %collective-permute-start.20 = (bf16[512,128]{1,0:T(8,128)(2,1)S(1)}, bf16[512,128]{1,0:T(8,128)(2,1)S(1)}, u32[]{:S(2)}, u32[]{:S(2)}) collective-permute-start(bf16[512,128]{1,0:T(8,128)(2,1)S(1)} %constant_dynamic-update-slice_fusion.2.refs_4_.rest_4_), channel_id=1, source_target_pairs={{0,4},{1,5},{2,6},{3,7},{4,0},{5,1},{6,2},{7,3},{8,12},{9,13},{10,... | collective-permute-start | bytes 393224 | tf_op jit(solution)/shard_map/ppermute | solution.py:56
  34.3 6.1 %collective-permute-start.21 = (bf16[512,128]{1,0:T(8,128)(2,1)S(1)}, bf16[512,128]{1,0:T(8,128)(2,1)S(1)}, u32[]{:S(2)}, u32[]{:S(2)}) collective-permute-start(bf16[512,128]{1,0:T(8,128)(2,1)S(1)} %constant_dynamic-update-slice_fusion.2.refs_4_.rest_4_), channel_id=1, source_target_pairs={{0,2},{1,3},{2,0},{3,1},{4,6},{5,7},{6,4},{7,5},{8,10},{9,11},{10,... | collective-permute-start | bytes 393224 | tf_op jit(solution)/shard_map/ppermute | solution.py:56
  35.4 5.0 %collective-permute-start.23 = (bf16[512,128]{1,0:T(8,128)(2,1)S(1)}, bf16[512,128]{1,0:T(8,128)(2,1)S(1)}, u32[]{:S(2)}, u32[]{:S(2)}) collective-permute-start(bf16[512,128]{1,0:T(8,128)(2,1)S(1)} %constant_dynamic-update-slice_fusion.2.refs_4_.rest_4_), channel_id=1, source_target_pairs={{0,1},{1,0},{2,3},{3,2},{4,5},{5,4},{6,7},{7,6},{8,9},{9,8},{10,11... | collective-permute-start | bytes 393224 | tf_op jit(solution)/shard_map/ppermute | solution.py:56
  36.5 6.5 %collective-permute-start.15 = (bf16[512,128]{1,0:T(8,128)(2,1)S(1)}, bf16[512,128]{1,0:T(8,128)(2,1)S(1)}, u32[]{:S(2)}, u32[]{:S(2)}) collective-permute-start(bf16[512,128]{1,0:T(8,128)(2,1)S(1)} %constant_dynamic-update-slice_fusion.refs_0_.rest_0_), channel_id=1, source_target_pairs={{0,2},{1,3},{2,0},{3,1},{4,6},{5,7},{6,4},{7,5},{8,10},{9,11},{10,... | collective-permute-start | bytes 393224 | tf_op jit(solution)/shard_map/ppermute | solution.py:56
  37.9 7.5 %collective-permute-start.16 = (bf16[512,128]{1,0:T(8,128)(2,1)S(1)}, bf16[512,128]{1,0:T(8,128)(2,1)S(1)}, u32[]{:S(2)}, u32[]{:S(2)}) collective-permute-start(bf16[512,128]{1,0:T(8,128)(2,1)S(1)} %constant_dynamic-update-slice_fusion.refs_0_.rest_0_), channel_id=1, source_target_pairs={{0,4},{1,5},{2,6},{3,7},{4,0},{5,1},{6,2},{7,3},{8,12},{9,13},{10,... | collective-permute-start | bytes 393224 | tf_op jit(solution)/shard_map/ppermute | solution.py:56
  39.2 6.2 %collective-permute-start.17 = (bf16[512,128]{1,0:T(8,128)(2,1)S(1)}, bf16[512,128]{1,0:T(8,128)(2,1)S(1)}, u32[]{:S(2)}, u32[]{:S(2)}) collective-permute-start(bf16[512,128]{1,0:T(8,128)(2,1)S(1)} %constant_dynamic-update-slice_fusion.refs_0_.rest_0_), channel_id=1, source_target_pairs={{0,6},{1,7},{2,4},{3,5},{4,2},{5,3},{6,0},{7,1},{8,14},{9,15},{10,... | collective-permute-start | bytes 393224 | tf_op jit(solution)/shard_map/ppermute | solution.py:56
  40.4 5.5 %collective-permute-start.22 = (bf16[512,128]{1,0:T(8,128)(2,1)S(1)}, bf16[512,128]{1,0:T(8,128)(2,1)S(1)}, u32[]{:S(2)}, u32[]{:S(2)}) collective-permute-start(bf16[512,128]{1,0:T(8,128)(2,1)S(1)} %constant_dynamic-update-slice_fusion.refs_0_.rest_0_), channel_id=1, source_target_pairs={{0,1},{1,0},{2,3},{3,2},{4,5},{5,4},{6,7},{7,6},{8,9},{9,8},{10,11... | collective-permute-start | bytes 393224 | tf_op jit(solution)/shard_map/ppermute | solution.py:56
  40.4 5.6 %collective-permute-start.24 = (bf16[512,128]{1,0:T(8,128)(2,1)S(1)}, bf16[512,128]{1,0:T(8,128)(2,1)S(1)}, u32[]{:S(2)}, u32[]{:S(2)}) collective-permute-start(bf16[512,128]{1,0:T(8,128)(2,1)S(1)} %collective-permute-done.19.refs_5_.rest_5_), channel_id=1, source_target_pairs={{0,1},{1,0},{2,3},{3,2},{4,5},{5,4},{6,7},{7,6},{8,9},{9,8},{10,11... | collective-permute-start | bytes 393224 | tf_op jit(solution)/shard_map/ppermute | solution.py:56
  43.0 3.4 %collective-permute-start.25 = (bf16[512,128]{1,0:T(8,128)(2,1)S(1)}, bf16[512,128]{1,0:T(8,128)(2,1)S(1)}, u32[]{:S(2)}, u32[]{:S(2)}) collective-permute-start(bf16[512,128]{1,0:T(8,128)(2,1)S(1)} %collective-permute-done.20.refs_6_.rest_6_), channel_id=1, source_target_pairs={{0,1},{1,0},{2,3},{3,2},{4,5},{5,4},{6,7},{7,6},{8,9},{9,8},{10,11... | collective-permute-start | bytes 393224 | tf_op jit(solution)/shard_map/ppermute | solution.py:56
  (10 other events, 34.0 us)
